TPU v7x, 128 devices: a whole 4x4x4 slice. The times are simulated.
128 devices in a mesh: col: 8 (over z, core), dp: 16 (over x, y).
Axes of the slice: x: 4, y: 4, z: 4, core: 2. Of those that a mesh axis runs over, the one named last changes fastest.
Arguments:
- tokens: bfloat16 [1024, 8192], P('col', 'dp'), may hold values from -6 to 6
- cotangent: bfloat16 [1024, 8192], P('col', 'dp'), may hold values from -0.1796875 to 0.1796875
- gate_weight: bfloat16 [8192, 14336], P('dp', 'col'), may hold values from -0.09375 to 0.09375
- up_weight: bfloat16 [8192, 14336], P('dp', 'col'), may hold values from -0.09375 to 0.09375
- down_weight: bfloat16 [14336, 8192], P('col', 'dp'), may hold values from -0.0625 to 0.0625
- gate_mask: int32 [64, 112], P('dp', 'col'), may hold values 0 or 1
- up_mask: int32 [64, 112], P('dp', 'col'), may hold values 0 or 1
- down_mask: int32 [112, 64], P('col', 'dp'), may hold values 0 or 1
- counts: int32 [8], P('col'), may hold values from 1 to 128, 768 in all
Outputs:
- output: bfloat16 [1024, 8192], P('col', 'dp')
- gate_grad: float32 [8192, 14336], P('dp', 'col')
- up_grad: float32 [8192, 14336], P('dp', 'col')
- down_grad: float32 [14336, 8192], P('col', 'dp')
Inputs may be any that keep to these rules, and one draw needn't show every extreme that they name: `counts`: the largest count equals 128.
All inputs are finite; a program needn't handle non-finite values. No bound on the sum of `gate_mask` or of `up_mask` or of `down_mask` or of `counts` on one device may be relied on, other than what follows from the above.
Results may differ from a plain program's by a relative error of at most 0.039.
Values may be sent and summed in bfloat16 or wider, within the bound.
No kernel may reach another device: no remote copies, remote signals or barrier semaphores. Data moves between devices by JAX's collectives and lax.ppermute only.
A program may use at most 128 MiB of HBM per device.

v0:
```python
import jax
import jax.numpy as jnp
from jax import lax
from jax.sharding import PartitionSpec as P


def widen(mask, weight):
    rows, cols = mask.shape
    height = weight.shape[0] // rows
    breadth = weight.shape[1] // cols
    shaped = weight.reshape(rows, height, cols, breadth)
    keep = (mask > 0)[:, None, :, None]
    return jnp.where(keep, shaped, jnp.zeros_like(shaped)).reshape(weight.shape)


def activate(gate_up, units):
    gate = gate_up[:, :units]
    upward = gate_up[:, units:]
    sigma = jax.nn.sigmoid(gate)
    active = gate * sigma
    hidden = (active * upward).astype(jnp.bfloat16)
    return (gate, upward, sigma, active, hidden)


def derive(gate, upward, sigma, active, back):
    d_gate = (back * upward * sigma * (1.0 + gate * (1.0 - sigma))).astype(jnp.bfloat16)
    d_up = (back * active).astype(jnp.bfloat16)
    return jnp.concatenate([d_gate, d_up], axis=1)


def on_device(
    tokens, cotangent, gate_weight, up_weight, down_weight, gate_mask, up_mask, down_mask, counts
):
    tok_dev = tokens.shape[0]
    live = (lax.iota(jnp.int32, tok_dev) < counts[0])[:, None]
    g_live = jnp.where(live, cotangent, jnp.zeros_like(cotangent))
    tok_all, grad_all = (
        lax.all_gather(tokens, "col", axis=0, tiled=True),
        lax.all_gather(g_live, "col", axis=0, tiled=True),
    )
    w_gate = widen(gate_mask, gate_weight)
    w_up = widen(up_mask, up_weight)
    w_down = widen(down_mask, down_weight)
    w_both = jnp.concatenate([w_gate, w_up], axis=1)
    units = gate_weight.shape[1]
    contract_rows = (((0,), (0,)), ((), ()))
    contract_cols = (((1,), (1,)), ((), ()))
    block = tok_all
    gate_up = lax.psum_scatter(
        jnp.dot(block, w_both, preferred_element_type=jnp.float32).astype(jnp.bfloat16),
        "dp",
        scatter_dimension=0,
        tiled=True,
    ).astype(jnp.float32)
    gate, upward, sigma, active, hidden_mine = activate(gate_up, units)
    hidden_all = lax.all_gather(hidden_mine, "dp", axis=0, tiled=True)
    block = grad_all
    back = lax.psum_scatter(
        lax.dot_general(block, w_down, contract_cols, preferred_element_type=jnp.float32).astype(
            jnp.bfloat16
        ),
        "dp",
        scatter_dimension=0,
        tiled=True,
    ).astype(jnp.float32)
    d_mine = derive(gate, upward, sigma, active, back)
    block = tok_all
    grads = lax.dot_general(
        block,
        lax.all_gather(d_mine, "dp", axis=0, tiled=True),
        contract_rows,
        preferred_element_type=jnp.float32,
    )
    block = hidden_all
    mixed = lax.psum_scatter(
        jnp.dot(block, w_down, preferred_element_type=jnp.float32).astype(jnp.bfloat16),
        "col",
        scatter_dimension=0,
        tiled=True,
    ).astype(jnp.float32)
    output = jnp.where(live, mixed, jnp.zeros_like(mixed)).astype(jnp.bfloat16)
    down_full = lax.dot_general(
        hidden_all, grad_all, contract_rows, preferred_element_type=jnp.float32
    )
    gate_grad = widen(gate_mask, grads[:, :units])
    up_grad = widen(up_mask, grads[:, units:])
    down_grad = widen(down_mask, down_full)
    return (output, gate_grad, up_grad, down_grad)


def solution(mesh):
    in_specs = (
        P("col", "dp"),
        P("col", "dp"),
        P("dp", "col"),
        P("dp", "col"),
        P("col", "dp"),
        P("dp", "col"),
        P("dp", "col"),
        P("col", "dp"),
        P("col"),
    )
    out_specs = (P("col", "dp"), P("dp", "col"), P("dp", "col"), P("col", "dp"))
    return jax.shard_map(
        on_device, mesh=mesh, in_specs=in_specs, out_specs=out_specs, check_vma=False
    )
```

profile of v0, /device:TPU:1, one launch (start us, length us, event | category | flops | bytes accessed | tf_op | source)
XLA Modules:
  0.0 412.8 jit_solution(5790270918840601619)
XLA Ops:
  7.2 0.0 copy-start
  7.2 0.0 all-gather.5.cloned.1.call-start
  7.2 0.7 all-gather.5.cloned.1.call-update
  7.9 0.0 all-gather.9.cloned.1.call-start
  8.6 1.6 broadcast_select_fusion
  10.3 0.0 all-gather.9.cloned.1.call-update
  10.3 0.0 reduce-scatter.10.cloned.1.call-start
  10.3 0.7 broadcast_compare_fusion.1
  11.0 0.1 copy.33
  11.1 0.7 broadcast_compare_fusion.2
  11.8 0.1 copy.31
  11.9 3.8 copy.32
  15.8 0.0 copy-done
  15.8 2.3 copy.34
  18.1 0.5 broadcast_in_dim.76
  18.6 0.5 broadcast_in_dim.78
  19.2 4.8 %bitcast_select_fusion.2 = (bf16[512,1792]{0,1:T(8,128)(2,1)}, bf16[512,1792]{0,1:T(8,128)(2,1)}) fusion(bf16[512,1792]{0,1:T(8,128)(2,1)} %copy.34, pred[224,8,4,128]{3,2,1,0:T(4,128)(4,1)S(1)} %bitcast.38, bf16[512,1792]{0,1:T(8,128)(2,1)} %copy.32, pred[224,8,4,128]{3,2,1,0:T(4,128)(4,1)S(1)} %bitcast.36), kind=kLoop, calls=%fused_computation.11 | loop fusion | flops 1835008 | bytes 9175040 | tf_op jit(solution)/shard_map/jit(_where)/select_n | solution.py:13
  24.0 13.0 %all-gather.5.cloned.1.call-done = bf16[1024,512]{1,0:T(8,128)(2,1)} async-done(((bf16[128,512]{1,0:T(8,128)(2,1)}), bf16[1024,512]{1,0:T(8,128)(2,1)}) %all-gather.5.cloned.1.call-update) | async-done | bytes 1048592 | tf_op jit(solution)/shard_map/all_gather | solution.py:38
  37.0 9.4 %fusion = bf16[1024,3584]{0,1:T(8,128)(2,1)} fusion(bf16[1024,512]{1,0:T(8,128)(2,1)} %all-gather.5.cloned.1.call-done, bf16[512,1792]{0,1:T(8,128)(2,1)} %get-tuple-element.21, bf16[512,1792]{0,1:T(8,128)(2,1)} %get-tuple-element.22), kind=kOutput, calls=%fused_computation.1 | convolution fusion | flops 3769106432 | bytes 12058624 | tf_op jit(solution)/shard_map/dot_general | solution.py:50
  46.3 10.1 %copy.41 = bf16[1024,3584]{1,0:T(8,128)(2,1)} copy(bf16[1024,3584]{0,1:T(8,128)(2,1)} %fusion) | data formatting | bytes 14680064
  56.4 0.0 copy-start.3
  56.4 0.0 reduce-scatter.10.cloned.1.call-update
  56.4 0.0 reduce-scatter.12.cloned.1.call-start
  56.5 0.6 copy-done.3
  57.1 0.1 copy.36
  57.2 5.5 %all-gather.9.cloned.1.call-done = bf16[1024,512]{1,0:T(8,128)(2,1)} async-done(((bf16[128,512]{1,0:T(8,128)(2,1)}), bf16[1024,512]{1,0:T(8,128)(2,1)}) %all-gather.9.cloned.1.call-update) | async-done | bytes 1048592 | tf_op jit(solution)/shard_map/all_gather | solution.py:39
  62.8 0.5 broadcast_in_dim.80
  63.3 0.0 copy-start.1
  63.3 0.9 copy-done.1
  64.2 5.8 %convolution_convert_fusion.1 = bf16[1024,1792]{1,0:T(8,128)(2,1)} fusion(bf16[1024,512]{1,0:T(8,128)(2,1)} %all-gather.9.cloned.1.call-done, bf16[1792,512]{1,0:T(8,128)(2,1)} %param.13, pred[224,8,4,128]{3,2,1,0:T(4,128)(4,1)S(1)} %bitcast.40), kind=kOutput, calls=%fused_computation.3 | convolution fusion | flops 1881800704 | bytes 7471104 | tf_op jit(solution)/shard_map/dot_general | solution.py:59
  70.0 0.0 reduce-scatter.12.cloned.1.call-update
  70.0 0.0 all-gather.7.cloned.1.call-start
  70.1 77.4 %reduce-scatter.10.cloned.1.call-done = bf16[64,3584]{1,0:T(8,128)(2,1)} async-done(((bf16[1024,3584]{1,0:T(8,128)(2,1)}), bf16[64,3584]{1,0:T(8,128)(2,1)}) %reduce-scatter.10.cloned.1.call-update) | async-done | bytes 458768 | tf_op jit(solution)/shard_map/reduce_scatter | solution.py:49
  147.5 1.1 convert_element_type.35
  148.6 78.2 %reduce-scatter.12.cloned.1.call-done = bf16[64,1792]{1,0:T(8,128)(2,1)} async-done(((bf16[1024,1792]{1,0:T(8,128)(2,1)}), bf16[64,1792]{1,0:T(8,128)(2,1)}) %reduce-scatter.12.cloned.1.call-update) | async-done | bytes 229392 | tf_op jit(solution)/shard_map/reduce_scatter | solution.py:58
  226.8 1.9 fusion.8
  228.7 0.0 all-gather.7.cloned.1.call-update
  228.7 0.0 copy-start.2
  228.7 0.2 reduce-scatter.8.cloned.1.call-start
  229.0 50.9 %all-gather.7.cloned.1.call-done = bf16[1024,1792]{1,0:T(8,128)(2,1)} async-done(((bf16[64,1792]{1,0:T(8,128)(2,1)}), bf16[1024,1792]{1,0:T(8,128)(2,1)}) %all-gather.7.cloned.1.call-update) | async-done | bytes 3670032 | tf_op jit(solution)/shard_map/all_gather | solution.py:56
  279.9 5.9 %convolution_convert_fusion.2 = bf16[1024,512]{1,0:T(8,128)(2,1)} fusion(bf16[1024,1792]{1,0:T(8,128)(2,1)} %all-gather.7.cloned.1.call-done, bf16[1792,512]{1,0:T(8,128)(2,1)} %param.13, pred[224,8,4,128]{3,2,1,0:T(4,128)(4,1)} %bitcast.41), kind=kOutput, calls=%fused_computation.13 | convolution fusion | flops 1880489984 | bytes 7471104 | tf_op jit(solution)/shard_map/dot_general | solution.py:76
  285.7 0.0 reduce-scatter.8.cloned.1.call-update
  285.8 0.0 all-gather.11.cloned.1.call-start
  285.8 0.8 pad_maximum_fusion
  286.6 0.0 all-gather.11.cloned.1.call-update
  286.6 0.0 copy-done.2
  286.7 6.3 %bitcast_select_fusion = f32[1792,512]{1,0:T(8,128)} fusion(bf16[1024,1792]{1,0:T(8,128)(2,1)} %all-gather.7.cloned.1.call-done, bf16[1024,512]{1,0:T(8,128)(2,1)} %all-gather.9.cloned.1.call-done, pred[224,8,4,128]{3,2,1,0:T(4,128)(4,1)S(1)} %bitcast.42), kind=kOutput, calls=%fused_computation.9 | convolution fusion | flops 1879965696 | bytes 9306112 | tf_op jit(solution)/shard_map/dot_general | solution.py:82
  293.0 21.6 %reduce-scatter.8.cloned.1.call-done = bf16[128,512]{1,0:T(8,128)(2,1)} async-done(((bf16[1024,512]{1,0:T(8,128)(2,1)}), bf16[128,512]{1,0:T(8,128)(2,1)}) %reduce-scatter.8.cloned.1.call-update) | async-done | bytes 131088 | tf_op jit(solution)/shard_map/reduce_scatter | solution.py:75
  314.6 1.6 select_convert_fusion
  316.2 68.5 %all-gather.11.cloned.1.call-done = bf16[1024,3584]{1,0:T(8,128)(2,1)} async-done(((bf16[64,3584]{1,0:T(8,128)(2,1)}), bf16[1024,3584]{1,0:T(8,128)(2,1)}) %all-gather.11.cloned.1.call-update) | async-done | bytes 7340048 | tf_op jit(solution)/shard_map/all_gather | solution.py:70
  384.8 6.6 %convolution_bitcast_fusion = f32[512,3584]{0,1:T(8,128)S(1)} fusion(bf16[1024,3584]{1,0:T(8,128)(2,1)} %all-gather.11.cloned.1.call-done, bf16[1024,512]{1,0:T(8,128)(2,1)} %all-gather.5.cloned.1.call-done), kind=kOutput, calls=%fused_computation.2 | convolution fusion | flops 3758096384 | bytes 15728640 | tf_op jit(solution)/shard_map/dot_general | solution.py:68
  391.4 4.3 %slice_select_fusion = (f32[512,1792]{0,1:T(8,128)}, f32[512,1792]{0,1:T(8,128)}) fusion(f32[512,3584]{0,1:T(8,128)S(1)} %convolution_bitcast_fusion, pred[224,8,4,128]{3,2,1,0:T(4,128)(4,1)S(1)} %bitcast.39, pred[224,8,4,128]{3,2,1,0:T(4,128)(4,1)S(1)} %bitcast.37), kind=kLoop, calls=%fused_computation.4 | loop fusion | flops 1835008 | bytes 16515072 | tf_op jit(solution)/shard_map/jit(_where)/select_n | solution.py:13
  395.7 5.1 %copy.40 = f32[512,1792]{1,0:T(8,128)} copy(f32[512,1792]{0,1:T(8,128)} %get-tuple-element.16) | data formatting | bytes 7340032
  400.8 5.1 %copy.39 = f32[512,1792]{1,0:T(8,128)} copy(f32[512,1792]{0,1:T(8,128)} %get-tuple-element.17) | data formatting | bytes 7340032
  (2 shorter events, 0.0 us)
Async XLA Ops:
  7.2 8.6 %copy-start = (bf16[512,1792]{1,0:T(8,128)(2,1)S(1)}, bf16[512,1792]{1,0:T(8,128)(2,1)}, u32[]{:S(2)}) copy-start(bf16[512,1792]{1,0:T(8,128)(2,1)} %param.12) | copy-start | bytes 5505028
  7.2 29.8 %all-gather.5.cloned.1.call-start = ((), (), s32[]{:S(2)}) async-start(), calls=%async_computation.3 | async-start | bytes 1179648 | tf_op jit(solution)/shard_map/all_gather | solution.py:38
  7.9 54.8 %all-gather.9.cloned.1.call-start = ((), (), s32[]{:S(2)}) async-start(), calls=%async_computation.6 | async-start | bytes 1179648 | tf_op jit(solution)/shard_map/all_gather | solution.py:39
  10.3 137.3 %reduce-scatter.10.cloned.1.call-start = ((), (), s32[]{:S(2)}) async-start(), calls=%async_computation.8 | async-start | bytes 7798784 | tf_op jit(solution)/shard_map/reduce_scatter | solution.py:49
  56.4 0.7 copy-start.3
  56.4 170.4 %reduce-scatter.12.cloned.1.call-start = ((), (), s32[]{:S(2)}) async-start(), calls=%async_computation.9 | async-start | bytes 3899392 | tf_op jit(solution)/shard_map/reduce_scatter | solution.py:58
  63.3 0.9 copy-start.1
  70.0 209.8 %all-gather.7.cloned.1.call-start = ((), (), s32[]{:S(2)}) async-start(), calls=%async_computation.4 | async-start | bytes 3899392 | tf_op jit(solution)/shard_map/all_gather | solution.py:56
  228.7 57.9 %copy-start.2 = (pred[14,128,4,128]{3,2,1,0:T(4,128)(4,1)S(1)}, pred[14,128,4,128]{3,2,1,0:T(4,128)(4,1)}, u32[]{:S(2)}) copy-start(pred[14,128,4,128]{3,2,1,0:T(4,128)(4,1)} %copy-done.1) | copy-start | bytes 2752516
  228.7 85.9 %reduce-scatter.8.cloned.1.call-start = ((), (), s32[]{:S(2)}) async-start(), calls=%async_computation.5 | async-start | bytes 1179648 | tf_op jit(solution)/shard_map/reduce_scatter | solution.py:75
  285.8 99.0 %all-gather.11.cloned.1.call-start = ((), (), s32[]{:S(2)}) async-start(), calls=%async_computation.7 | async-start | bytes 7798784 | tf_op jit(solution)/shard_map/all_gather | solution.py:70
Sparse Core Ops, SparseCore 0:
  9.7 27.2 all-gather.4
  39.3 23.4 all-gather.8
  66.2 81.2 reduce-scatter.9
  151.7 75.0 reduce-scatter.11
  229.7 50.1 all-gather.6
  285.9 28.6 reduce-scatter.7
  317.0 67.7 all-gather.10
where the time goes:
time: 414 us; the launch traced here: 413 us
  waiting for transfers between devices  316 us (76%)
  matrix products  34 us (8%)
  local copies, waits for them, and re-layouts  29.9 us (7%)
  other arithmetic  17.6 us (4%)
  between operations  14.9 us (4%)
    reduce_scatter x1, waiting for transfers between devices, on_device(): lax.psum_scatter(lax.dot_general(block, w_down, contract_cols, preferred_...  78.2 us
    reduce_scatter x1, waiting for transfers between devices, on_device(): lax.psum_scatter(jnp.dot(block, w_both, preferred_element_type=jnp.float3...  77.4 us
    all_gather x1, waiting for transfers between devices, on_device(): lax.all_gather(d_mine, 'dp', axis=0, tiled=True)  68.5 us
    all_gather x1, waiting for transfers between devices, on_device(): hidden_all = lax.all_gather(hidden_mine, 'dp', axis=0, tiled=True)  50.9 us
    unnamed x13, local copies, waits for them, and re-layouts  28 us
    reduce_scatter x1, waiting for transfers between devices, on_device(): lax.psum_scatter(jnp.dot(block, w_down, preferred_element_type=jnp.float3...  21.6 us
    all_gather x1, waiting for transfers between devices, on_device(): lax.all_gather(tokens, 'col', axis=0, tiled=True)  13 us
    dot_general x1, matrix products, on_device(): jnp.dot(block, w_both, preferred_element_type=jnp.float32)  9.36 us
  transfers between devices with their start and end apart: 7, of which 7 were waited for; matrix products, arithmetic and copies ran while one was open for 12% of the time, Pallas kernels for 0%

commit v1 on v0

v1 whole, which is shorter than its diff:
```python
import functools

import jax
import jax.numpy as jnp
from jax import lax
from jax.experimental import pallas as pl
from jax.experimental.pallas import tpu as pltpu
from jax.sharding import PartitionSpec as P

BF = jnp.bfloat16
F32 = jnp.float32
LIVE = 768
PAD = 144
SIDE = 4
BLK = 128
UNITS = 1792
HALF = UNITS // 2
STEPS = HALF // BLK
FEAT = 512
SLOTS = 1024

MASKS = {"xA": (1, 0), "xB": (3, 0), "yA": (0, 1), "yB": (0, 3)}
ROUNDS = {
    (0, 0): (("xA", 0), ("xB", 1), ("yA", 2), ("yB", 3)),
    (0, 1): (("xB", 0), ("xA", 1), ("yB", 2), ("yA", 3)),
    (1, 0): (("yA", 2), ("yB", 3), ("xA", 0), ("xB", 1)),
    (1, 1): (("yB", 2), ("yA", 3), ("xB", 0), ("xA", 1)),
}
GROUPS = tuple(ROUNDS)


def partners(name):
    dx, dy = MASKS[name]
    return [
        (x * SIDE + y, (x ^ dx) * SIDE + (y ^ dy)) for x in range(SIDE) for y in range(SIDE)
    ]


def shift(dz, dc):
    return [
        (z * 2 + c, ((z + dz) % SIDE) * 2 + (c + dc) % 2) for z in range(SIDE) for c in range(2)
    ]


def logical_rows():
    place = lax.axis_index("dp")
    x, y = place // SIDE, place % SIDE

    def sides(v):
        high = v // 2
        return (v % 2) ^ high, high

    xa, xb = sides(x)
    ya, yb = sides(y)
    first = xa * 8 + xb * 4 + ya * 2 + yb
    second = xb * 8 + xa * 4 + yb * 2 + ya
    row = lax.iota(jnp.int32, LIVE)
    half, block, rest = row // 384, (row % 384) // 24, row % 24
    return half * 384 + (block ^ jnp.where(half > 0, second, first)) * 24 + rest


def kept(mask_ref, row, col, value):
    return jnp.where(mask_ref[row, col] > 0, value, jnp.zeros_like(value))


def compact_kernel(offs, cnts, rows_ref, all_ref, x_ref, g_ref, xt_ref):
    rows = rows_ref[...]
    slot = lax.broadcasted_iota(jnp.int32, (LIVE, BLK), 1)
    total = None
    for pair in range(4):
        picks = []
        for c in (2 * pair, 2 * pair + 1):
            hit = (rows - offs[c] == slot) & (slot < cnts[c])
            picks.append(jnp.where(hit, 1.0, 0.0).astype(BF))
        pick = jnp.concatenate(picks, axis=1)
        source = jnp.concatenate(
            [all_ref[2 * pair, :BLK, :], all_ref[2 * pair + 1, :BLK, :]], axis=0
        )
        part = jnp.dot(pick, source, preferred_element_type=F32)
        total = part if total is None else total + part
    x_ref[...] = total[:, :FEAT].astype(BF)
    g_ref[...] = total[:, FEAT:].astype(BF)
    xt_ref[...] = total[:, :FEAT].T.astype(BF)


def compact(offs, cnts, rows, gathered):
    smem = pl.BlockSpec(memory_space=pltpu.SMEM)
    vmem = pl.BlockSpec(memory_space=pltpu.VMEM)
    return pl.pallas_call(
        compact_kernel,
        out_shape=(
            jax.ShapeDtypeStruct((LIVE, FEAT), BF),
            jax.ShapeDtypeStruct((LIVE, FEAT), BF),
            jax.ShapeDtypeStruct((FEAT, LIVE), BF),
        ),
        in_specs=[smem, smem, vmem, vmem],
        out_specs=(vmem, vmem, vmem),
        compiler_params=pltpu.CompilerParams(vmem_limit_bytes=48 << 20),
        cost_estimate=pl.CostEstimate(
            flops=2 * LIVE * SLOTS * SLOTS, bytes_accessed=5 << 20, transcendentals=0
        ),
        name="compact",
    )(offs, cnts, rows, gathered)


def masked_columns(mask_ref, ref, col):
    return jnp.concatenate(
        [kept(mask_ref, r, col, ref[r * BLK : (r + 1) * BLK, :]) for r in range(4)], axis=0
    )


def masked_rows(mask_ref, ref, row):
    return jnp.concatenate(
        [kept(mask_ref, row, c, ref[:, c * BLK : (c + 1) * BLK]) for c in range(4)], axis=1
    )


def partial_kernel(
    gm, um, dm, x_ref, g_ref, wga, wgb, wua, wub, wda, wdb, as0, ak0, as1, ak1, bs0, bk0, bs1, bk1
):
    j = pl.program_id(0)
    w_gate = jnp.concatenate(
        [masked_columns(gm, wga, j), masked_columns(gm, wgb, STEPS + j)], axis=1
    )
    w_up = jnp.concatenate(
        [masked_columns(um, wua, j), masked_columns(um, wub, STEPS + j)], axis=1
    )
    w_down = jnp.concatenate([masked_rows(dm, wda, j), masked_rows(dm, wdb, STEPS + j)], axis=0)
    x, g = x_ref[...], g_ref[...]
    results = (
        jnp.dot(x, w_gate, preferred_element_type=F32),
        jnp.dot(x, w_up, preferred_element_type=F32),
        lax.dot_general(g, w_down, (((1,), (1,)), ((), ())), preferred_element_type=F32),
    )
    for which, result in enumerate(results):
        left, right = result[:, :BLK], result[:, BLK:]
        for q, (send, keep) in enumerate(((as0, ak0), (as1, ak1))):
            keep[which] = left[q * 384 : q * 384 + 192].astype(BF)
            send[which] = left[q * 384 + 192 : q * 384 + 384].astype(BF)
        for q, (send, keep) in enumerate(((bs0, bk0), (bs1, bk1))):
            for t in range(4):
                at = q * 384 + t * 96
                keep[which, t] = right[at : at + 48].astype(BF)
                send[which, t] = right[at + 48 : at + 96].astype(BF)


def weight_specs():
    return [
        pl.BlockSpec((FEAT, BLK), lambda j: (0, j)),
        pl.BlockSpec((FEAT, BLK), lambda j: (0, STEPS + j)),
        pl.BlockSpec((FEAT, BLK), lambda j: (0, j)),
        pl.BlockSpec((FEAT, BLK), lambda j: (0, STEPS + j)),
        pl.BlockSpec((BLK, FEAT), lambda j: (j, 0)),
        pl.BlockSpec((BLK, FEAT), lambda j: (STEPS + j, 0)),
    ]


def partials(gm, um, dm, x, g, wg, wu, wd):
    smem = pl.BlockSpec(memory_space=pltpu.SMEM)
    whole = pl.BlockSpec((LIVE, FEAT), lambda j: (0, 0))
    a_spec = pl.BlockSpec((3, 192, BLK), lambda j: (0, 0, j))
    b_spec = pl.BlockSpec((3, 4, 48, BLK), lambda j: (0, 0, 0, j))
    a_out = jax.ShapeDtypeStruct((3, 192, HALF), BF)
    b_out = jax.ShapeDtypeStruct((3, 4, 48, HALF), BF)
    return pl.pallas_call(
        partial_kernel,
        grid=(STEPS,),
        out_shape=(a_out,) * 4 + (b_out,) * 4,
        in_specs=[smem, smem, smem, whole, whole] + weight_specs(),
        out_specs=(a_spec,) * 4 + (b_spec,) * 4,
        compiler_params=pltpu.CompilerParams(vmem_limit_bytes=48 << 20),
        cost_estimate=pl.CostEstimate(
            flops=2 * LIVE * FEAT * 3 * UNITS, bytes_accessed=16 << 20, transcendentals=0
        ),
        name="partials",
    )(gm, um, dm, x, g, wg, wg, wu, wu, wd, wd)


def rows_a(own, far, which):
    return [own[which], far[which]]


def rows_b(own, far, which):
    return [piece for t in range(4) for piece in (own[which, t], far[which, t])]


def output_kernel(
    offs, cnts, dm, rows_ref, a0, a0f, a1, a1f, b0, b0f, b1, b1f, wda, wdb, out_ref, total
):
    j = pl.program_id(0)
    left = jnp.concatenate(rows_a(a0, a0f, 0) + rows_a(a1, a1f, 0), axis=0)
    right = jnp.concatenate(rows_b(b0, b0f, 0) + rows_b(b1, b1f, 0), axis=0)
    hidden = jnp.concatenate([left, right], axis=1)
    w_down = jnp.concatenate([masked_rows(dm, wda, j), masked_rows(dm, wdb, STEPS + j)], axis=0)
    part = jnp.dot(hidden, w_down, preferred_element_type=F32)

    @pl.when(j == 0)
    def _():
        total[...] = part

    @pl.when(j > 0)
    def _():
        total[...] += part

    @pl.when(j == STEPS - 1)
    def _():
        mixed = total[...].astype(BF)
        rows = rows_ref[...]
        slot = lax.broadcasted_iota(jnp.int32, (BLK, LIVE), 0)
        for k in range(8):
            hit = (rows - offs[k] == slot) & (slot < cnts[k])
            pick = jnp.where(hit, 1.0, 0.0).astype(BF)
            out_ref[k // 4, k % 4] = jnp.dot(pick, mixed, preferred_element_type=F32).astype(BF)


def output_rows(offs, cnts, dm, rows, parts, wd):
    smem = pl.BlockSpec(memory_space=pltpu.SMEM)
    a_spec = pl.BlockSpec((1, 192, BLK), lambda j: (0, 0, j))
    b_spec = pl.BlockSpec((1, 4, 48, BLK), lambda j: (0, 0, 0, j))
    return pl.pallas_call(
        output_kernel,
        grid=(STEPS,),
        out_shape=jax.ShapeDtypeStruct((2, 4, BLK, FEAT), BF),
        in_specs=[smem, smem, smem, pl.BlockSpec((1, LIVE), lambda j: (0, 0))]
        + [a_spec] * 4
        + [b_spec] * 4
        + weight_specs()[4:],
        out_specs=pl.BlockSpec((2, 4, BLK, FEAT), lambda j: (0, 0, 0, 0)),
        scratch_shapes=[pltpu.VMEM((LIVE, FEAT), F32)],
        compiler_params=pltpu.CompilerParams(vmem_limit_bytes=48 << 20),
        cost_estimate=pl.CostEstimate(
            flops=2 * LIVE * FEAT * (UNITS + SLOTS), bytes_accessed=6 << 20, transcendentals=0
        ),
        name="output_rows",
    )(offs, cnts, dm, rows, *parts, wd, wd)


def grad_kernel(
    gm, um, dm, xt_ref, g_ref, a0, a0f, a1, a1f, b0, b0f, b1, b1f, gate_out, up_out, down_out
):
    k = pl.program_id(0)

    def work(rows, first, second):
        hidden, d_gate, d_up = [
            jnp.concatenate(rows(*first, which) + rows(*second, which), axis=0)
            for which in range(3)
        ]
        both = jnp.dot(
            xt_ref[...], jnp.concatenate([d_gate, d_up], axis=1), preferred_element_type=F32
        )
        down = lax.dot_general(
            hidden, g_ref[...], (((0,), (0,)), ((), ())), preferred_element_type=F32
        )
        for r in range(4):
            at = slice(r * BLK, (r + 1) * BLK)
            gate_out[at, :] = kept(gm, r, k, both[at, :BLK])
            up_out[at, :] = kept(um, r, k, both[at, BLK:])
            down_out[:, at] = kept(dm, k, r, down[:, at])

    @pl.when(k < STEPS)
    def _():
        work(rows_a, (a0, a0f), (a1, a1f))

    @pl.when(k >= STEPS)
    def _():
        work(rows_b, (b0, b0f), (b1, b1f))


def gradients(gm, um, dm, xt, g, parts):
    smem = pl.BlockSpec(memory_space=pltpu.SMEM)
    a_spec = pl.BlockSpec((3, 192, BLK), lambda k: (0, 0, jnp.minimum(k, STEPS - 1)))
    b_spec = pl.BlockSpec((3, 4, 48, BLK), lambda k: (0, 0, 0, jnp.maximum(k - STEPS, 0)))
    return pl.pallas_call(
        grad_kernel,
        grid=(2 * STEPS,),
        out_shape=(
            jax.ShapeDtypeStruct((FEAT, UNITS), F32),
            jax.ShapeDtypeStruct((FEAT, UNITS), F32),
            jax.ShapeDtypeStruct((UNITS, FEAT), F32),
        ),
        in_specs=[
            smem,
            smem,
            smem,
            pl.BlockSpec((FEAT, LIVE), lambda k: (0, 0)),
            pl.BlockSpec((LIVE, FEAT), lambda k: (0, 0)),
        ]
        + [a_spec] * 4
        + [b_spec] * 4,
        out_specs=(
            pl.BlockSpec((FEAT, BLK), lambda k: (0, k)),
            pl.BlockSpec((FEAT, BLK), lambda k: (0, k)),
            pl.BlockSpec((BLK, FEAT), lambda k: (k, 0)),
        ),
        compiler_params=pltpu.CompilerParams(vmem_limit_bytes=48 << 20),
        cost_estimate=pl.CostEstimate(
            flops=2 * LIVE * FEAT * 3 * UNITS, bytes_accessed=20 << 20, transcendentals=0
        ),
        name="gradients",
    )(gm, um, dm, xt, g, *parts)


def split(value, axis):
    lower = lax.slice_in_dim(value, 0, 1, axis=axis)
    upper = lax.slice_in_dim(value, 1, 2, axis=axis)
    return lower, upper


def activate(total):
    gate, upward, back = total[0], total[1], total[2]
    sigma = jax.nn.sigmoid(gate)
    active = gate * sigma
    hidden = (active * upward).astype(BF)
    d_gate = (back * upward * sigma * (1.0 + gate * (1.0 - sigma))).astype(BF)
    d_up = (back * active).astype(BF)
    return jnp.stack([hidden, d_gate, d_up])


def on_device(
    tokens, cotangent, gate_weight, up_weight, down_weight, gate_mask, up_mask, down_mask, counts
):
    tok_dev = tokens.shape[0]
    live = (lax.iota(jnp.int32, tok_dev) < counts[0])[:, None]
    tail = jnp.full((PAD - tok_dev, 2 * FEAT), counts[0], F32).astype(BF)
    mine = jnp.concatenate([jnp.concatenate([tokens, cotangent], axis=1), tail], axis=0)
    gathered = lax.all_gather(mine, "col", axis=0, tiled=False)
    cnts = gathered[:, tok_dev, 0].astype(jnp.int32)
    offs = jnp.cumsum(cnts) - cnts
    rows = logical_rows()
    x, g, xt = compact(offs, cnts, rows[:, None], gathered)
    as0, ak0, as1, ak1, bs0, bk0, bs1, bk1 = partials(
        gate_mask, up_mask, down_mask, x, g, gate_weight, up_weight, down_weight
    )

    def spread(value, bit):
        sizes = [1 if b == bit else 2 for b in range(4)]
        return value.reshape((3, *sizes, 24, HALF))

    send = {
        (0, 0): spread(as0, 0),
        (0, 1): spread(as1, 0),
        (1, 0): spread(bs0, 2),
        (1, 1): spread(bs1, 2),
    }
    keep = {
        (0, 0): spread(ak0, 0),
        (0, 1): spread(ak1, 0),
        (1, 0): spread(bk0, 2),
        (1, 1): spread(bk1, 2),
    }
    for number in range(4):
        come = {
            s: lax.ppermute(send[s], "dp", partners(ROUNDS[s][number][0])) for s in GROUPS
        }
        for s in GROUPS:
            total = keep[s].astype(F32) + come[s].astype(F32)
            if number < 3:
                lower, upper = split(total, 1 + ROUNDS[s][number + 1][1])
                keep[s], send[s] = lower.astype(BF), upper.astype(BF)
            else:
                keep[s] = activate(total)
    for number in (3, 2, 1, 0):
        come = {
            s: lax.ppermute(keep[s], "dp", partners(ROUNDS[s][number][0])) for s in GROUPS
        }
        if number > 0:
            for s in GROUPS:
                keep[s] = jnp.concatenate([keep[s], come[s]], axis=1 + ROUNDS[s][number][1])
    parts = []
    for s in GROUPS:
        shape = (3, 192, HALF) if s[0] == 0 else (3, 4, 48, HALF)
        parts += [keep[s].reshape(shape), come[s].reshape(shape)]

    place = lax.axis_index("col")
    order = jnp.arange(8)
    owner = ((place // 2 + order % 4) % SIDE) * 2 + ((place % 2) ^ (order // 4))
    expanded = output_rows(offs[owner], cnts[owner], down_mask, rows[None, :], parts, down_weight)
    other = lax.ppermute(expanded[1], "col", shift(0, 1))
    summed = expanded[0].astype(F32) + other.astype(F32)
    near, up, far, down = [summed[k].astype(BF) for k in range(4)]
    mixed = (
        near.astype(F32)
        + lax.ppermute(up, "col", shift(1, 0)).astype(F32)
        + lax.ppermute(down, "col", shift(-1, 0)).astype(F32)
        + lax.ppermute(far, "col", shift(2, 0)).astype(F32)
    )
    output = jnp.where(live, mixed, jnp.zeros_like(mixed)).astype(BF)
    gate_grad, up_grad, down_grad = gradients(gate_mask, up_mask, down_mask, xt, g, parts)
    return (output, gate_grad, up_grad, down_grad)


def solution(mesh):
    in_specs = (
        P("col", "dp"),
        P("col", "dp"),
        P("dp", "col"),
        P("dp", "col"),
        P("col", "dp"),
        P("dp", "col"),
        P("dp", "col"),
        P("col", "dp"),
        P("col"),
    )
    out_specs = (P("col", "dp"), P("dp", "col"), P("dp", "col"), P("col", "dp"))
    return jax.shard_map(
        on_device, mesh=mesh, in_specs=in_specs, out_specs=out_specs, check_vma=False
    )
```

time: 414 us -> 207 us (0.50)
  waiting for transfers between devices: 316 us -> 91.1 us
  starting transfers between devices: 0.47 us -> 42.6 us
  Pallas kernels: 0 us -> 35 us
  matrix products: 34 us -> 0 us
  local copies, waits for them, and re-layouts: 29.9 us -> 10.9 us
  other arithmetic: 17.6 us -> 11.6 us
    reduce_scatter x3 -> x0, waiting for transfers between devices: 177 us -> none  [the longest x1 78.2 us: on_device(): lax.psum_scatter(lax.dot_general(block, w_down, contract_cols, preferred_...]
    all_gather x4 -> x1, waiting for transfers between devices: 138 us -> 28.7 us  [on_device(): gathered = lax.all_gather(mine, 'col', axis=0, tiled=False)]
    ppermute x0 -> x36, waiting for transfers between devices: none -> 62.3 us  [the longest x16 33.5 us: on_device(): lax.ppermute(send[s], 'dp', partners(ROUNDS[s][number][0]))]
    ppermute x0 -> x36, starting transfers between devices: none -> 42.5 us  [the longest x16 20.5 us: on_device(): lax.ppermute(send[s], 'dp', partners(ROUNDS[s][number][0]))]
    pallas_call x0 -> x4, Pallas kernels: none -> 35 us  [the longest x1 13.5 us: gradients(): pl.pallas_call(grad_kernel, grid=(2 * STEPS,), out_shape=(jax.ShapeDtypeS...]
    dot_general x5 -> x0, matrix products: 34 us -> none  [the longest x1 9.36 us: on_device(): jnp.dot(block, w_both, preferred_element_type=jnp.float32)]
    unnamed x13 -> x19, local copies, waits for them, and re-layouts: 28 us -> 2.77 us
    select_n x3 -> x1, other arithmetic: 10.8 us -> 0.02 us  [on_device(): offs[owner]]
  transfers between devices with their start and end apart: 7 -> 37, of which waited for: 7 -> 16; matrix products, arithmetic and copies ran while one was open for 12% -> 7% of each run, Pallas kernels for 0% -> 7%
where the time goes in v1:
time: 207 us
  waiting for transfers between devices  91.1 us (44%)
  starting transfers between devices  42.6 us (21%)
  Pallas kernels  35 us (17%)
  between operations  15.3 us (7%)
  other arithmetic  11.6 us (6%)
  local copies, waits for them, and re-layouts  10.9 us (5%)
    ppermute x16, waiting for transfers between devices, on_device(): lax.ppermute(send[s], 'dp', partners(ROUNDS[s][number][0]))  33.5 us
    all_gather x1, waiting for transfers between devices, on_device(): gathered = lax.all_gather(mine, 'col', axis=0, tiled=False)  28.7 us
    ppermute x16, waiting for transfers between devices, on_device(): lax.ppermute(keep[s], 'dp', partners(ROUNDS[s][number][0]))  27.3 us
    ppermute x16, starting transfers between devices, on_device(): lax.ppermute(send[s], 'dp', partners(ROUNDS[s][number][0]))  20.5 us
    pallas_call x1, Pallas kernels, gradients(): pl.pallas_call(grad_kernel, grid=(2 * STEPS,), out_shape=(jax.ShapeDtypeS...  13.5 us
    ppermute x16, starting transfers between devices, on_device(): lax.ppermute(keep[s], 'dp', partners(ROUNDS[s][number][0]))  12.4 us
    pallas_call x1, Pallas kernels, partials(): pl.pallas_call(partial_kernel, grid=(STEPS,), out_shape=(a_out,) * 4 + (b...  10.2 us
    pallas_call x1, Pallas kernels, output_rows(): pl.pallas_call(output_kernel, grid=(STEPS,), out_shape=jax.ShapeDtypeStru...  8.84 us
  transfers between devices with their start and end apart: 37, of which 16 were waited for; matrix products, arithmetic and copies ran while one was open for 7% of the time, Pallas kernels for 7%

profile of v1, /device:TPU:1, one launch (start us, length us, event | category | flops | bytes accessed | tf_op | source)
XLA Modules:
  0.0 206.5 jit_solution(7764133306806606285)
XLA Ops:
  7.9 1.7 fusion.27
  9.7 0.8 copy.33.dm
  10.5 0.6 fusion.16.rows_ref
  11.0 28.7 %all-gather.3.cloned.1.call-done = bf16[1152,1024]{1,0:T(8,128)(2,1)} async-done(((bf16[144,1024]{1,0:T(8,128)(2,1)}), bf16[1152,1024]{1,0:T(8,128)(2,1)}) %all-gather.3.cloned.1.call-update) | async-done | bytes 2359312 | tf_op jit(solution)/shard_map/all_gather | solution.py:326
  39.8 1.0 fusion.36.cnts
  40.9 1.7 copy-done.2
  42.6 2.5 %compact.1 = (bf16[768,512]{1,0:T(8,128)(2,1)S(1)}, bf16[768,512]{1,0:T(8,128)(2,1)S(1)}, bf16[512,768]{1,0:T(8,128)(2,1)S(1)}) custom-call(s32[8]{0:T(128)S(1)} %bitcast_subtract_fusion.offs, s32[8]{0:T(128)S(1)} %fusion.36.cnts, s32[768,1]{1,0:T(8,128)S(1)} %fusion.16.rows_ref, bf16[8,144,1024]{2,1,0:T(8,128)(2,1)S(1)} %bitcast.65), custom_call_target="tpu_custom_call" | custom-call | flops 1610612736 | bytes 5242880 | tf_op jit(solution)/shard_map/compact/pallas_call | solution.py:89
  45.2 10.2 %partials.1 = (bf16[3,192,896]{2,1,0:T(8,128)(2,1)S(1)}, bf16[3,192,896]{2,1,0:T(8,128)(2,1)S(1)}, bf16[3,192,896]{2,1,0:T(8,128)(2,1)S(1)}, bf16[3,192,896]{2,1...) custom-call(s32[4,14]{1,0:T(4,128)S(1)} %copy-done.3, ...), custom_call_target="tpu_custom_call" | custom-call | flops 4227858432 | bytes 16777216 | tf_op jit(solution)/shard_map/partials/pallas_call | solution.py:165
  55.3 2.5 %collective-permute-start.24 = (bf16[3,2,2,1,2,24,896]{6,5,4,2,1,0,3:T(8,128)(2,1)}, bf16[3,2,2,1,2,24,896]{6,5,4,2,1,0,3:T(8,128)(2,1)S(1)}, u32[]{:S(2)}, u32[]{:S(2)}) collective-permute-start(bf16[3,2,2,1,2,24,896]{6,5,4,2,1,0,3:T(8,128)(2,1)} %bitcast.69), channel_id=1, source_target_pairs={{0,3},{1,2},{2,1},{3,0},{4,7},{5,6},{6,5},{7,4},{8,11},{9,10},{10,... | collective-permute-start | bytes 3096584 | tf_op jit(solution)/shard_map/ppermute | solution.py:353
  58.0 2.5 %collective-permute-start.8 = (bf16[3,1,2,2,2,24,896]{6,5,4,2,1,0,3:T(8,128)(2,1)S(1)}, bf16[3,1,2,2,2,24,896]{6,5,4,2,1,0,3:T(8,128)(2,1)S(1)}, u32[]{:S(2)}, u32[]{:S(2)}) collective-permute-start(bf16[3,1,2,2,2,24,896]{6,5,4,2,1,0,3:T(8,128)(2,1)S(1)} %copy.29), channel_id=1, source_target_pairs={{0,12},{1,13},{2,14},{3,15},{4,8},{5,9},{6,10},{7,11},{8,4},{9,5},... | collective-permute-start | bytes 3096584 | tf_op jit(solution)/shard_map/ppermute | solution.py:353
  60.6 20.3 %collective-permute-done.24 = bf16[3,2,2,1,2,24,896]{6,5,4,2,1,0,3:T(8,128)(2,1)S(1)} collective-permute-done((bf16[3,2,2,1,2,24,896]{6,5,4,2,1,0,3:T(8,128)(2,1)}, bf16[3,2,2,1,2,24,896]{6,5,4,2,1,0,3:T(8,128)(2,1)S(1)}, u32[]{:S(2)}, u32[]{:S(2)}) %collective-permute-start.24) | collective-permute-done | bytes 1032224 | tf_op jit(solution)/shard_map/ppermute | solution.py:353
  81.4 0.5 collective-permute-done.16
  81.9 0.3 copy-done.7
  82.5 2.5 %collective-permute-start.17 = (bf16[3,2,2,1,1,24,896]{6,5,4,2,1,0,3:T(8,128)(2,1)S(1)}, bf16[3,2,2,1,1,24,896]{6,5,4,2,1,0,3:T(8,128)(2,1)S(1)}, u32[]{:S(2)}, u32[]{:S(2)}) collective-permute-start(bf16[3,2,2,1,1,24,896]{6,5,4,2,1,0,3:T(8,128)(2,1)S(1)} %slice.224), channel_id=1, source_target_pairs={{0,3},{1,2},{2,1},{3,0},{4,7},{5,6},{6,5},{7,4},{8,11},{9,10},{10,... | collective-permute-start | bytes 1548296 | tf_op jit(solution)/shard_map/ppermute | solution.py:353
  85.1 0.3 fusion.2
  85.4 1.3 collective-permute-start.9
  86.6 0.3 fusion.3
  87.0 1.9 collective-permute-start.1
  88.9 4.7 %collective-permute-done.25 = bf16[3,2,2,1,1,24,896]{6,5,4,2,1,0,3:T(8,128)(2,1)S(1)} collective-permute-done((bf16[3,2,2,1,1,24,896]{6,5,4,2,1,0,3:T(8,128)(2,1)S(1)}, bf16[3,2,2,1,1,24,896]{6,5,4,2,1,0,3:T(8,128)(2,1)S(1)}, u32[]{:S(2)}, u32[]{:S(2)}) %collective-permute-start.25) | collective-permute-done | bytes 516128 | tf_op jit(solution)/shard_map/ppermute | solution.py:353
  93.7 2.5 %collective-permute-start.26 = (bf16[3,1,2,1,1,24,896]{6,5,4,2,1,0,3:T(8,128)(2,1)S(1)}, bf16[3,1,2,1,1,24,896]{6,5,4,2,1,0,3:T(8,128)(2,1)S(1)}, u32[]{:S(2)}, u32[]{:S(2)}) collective-permute-start(bf16[3,1,2,1,1,24,896]{6,5,4,2,1,0,3:T(8,128)(2,1)S(1)} %slice.235), channel_id=1, source_target_pairs={{0,12},{1,13},{2,14},{3,15},{4,8},{5,9},{6,10},{7,11},{8,4},{9,5},... | collective-permute-start | bytes 774152 | tf_op jit(solution)/shard_map/ppermute | solution.py:353
  96.4 1.0 collective-permute-start.18
  97.6 2.5 %collective-permute-start.10 = (bf16[3,1,1,1,2,24,896]{6,5,4,2,1,0,3:T(8,128)(2,1)S(1)}, bf16[3,1,1,1,2,24,896]{6,5,4,2,1,0,3:T(8,128)(2,1)S(1)}, u32[]{:S(2)}, u32[]{:S(2)}) collective-permute-start(bf16[3,1,1,1,2,24,896]{6,5,4,2,1,0,3:T(8,128)(2,1)S(1)} %slice.217), channel_id=1, source_target_pairs={{0,3},{1,2},{2,1},{3,0},{4,7},{5,6},{6,5},{7,4},{8,11},{9,10},{10,... | collective-permute-start | bytes 774152 | tf_op jit(solution)/shard_map/ppermute | solution.py:353
  100.4 5.0 %collective-permute-done.26 = bf16[3,1,2,1,1,24,896]{6,5,4,2,1,0,3:T(8,128)(2,1)S(1)} collective-permute-done((bf16[3,1,2,1,1,24,896]{6,5,4,2,1,0,3:T(8,128)(2,1)S(1)}, bf16[3,1,2,1,1,24,896]{6,5,4,2,1,0,3:T(8,128)(2,1)S(1)}, u32[]{:S(2)}, u32[]{:S(2)}) %collective-permute-start.26) | collective-permute-done | bytes 258080 | tf_op jit(solution)/shard_map/ppermute | solution.py:353
  105.7 1.9 collective-permute-start.19
  107.9 1.3 collective-permute-start.3
  109.2 0.5 collective-permute-done.27
  109.8 0.5 collective-permute-start.28
  110.2 1.9 collective-permute-done.11
  112.3 0.4 collective-permute-start.12
  112.7 0.6 collective-permute-done.3
  113.4 1.3 collective-permute-start.4
  114.9 1.1 collective-permute-start.29
  116.0 1.7 collective-permute-start.20
  117.8 1.7 collective-permute-start.13
  119.6 1.7 collective-permute-done.29
  121.5 1.5 collective-permute-done.20
  123.1 2.8 %collective-permute-done.13 = bf16[3,1,1,1,2,24,896]{6,5,4,2,1,0,3:T(8,128)(2,1)S(1)} collective-permute-done((bf16[3,1,1,1,2,24,896]{6,5,4,2,1,0,3:T(8,128)(2,1)S(1)}, bf16[3,1,1,1,2,24,896]{6,5,4,2,1,0,3:T(8,128)(2,1)S(1)}, u32[]{:S(2)}, u32[]{:S(2)}) %collective-permute-start.13) | collective-permute-done | bytes 258080 | tf_op jit(solution)/shard_map/ppermute | solution.py:364
  126.2 0.9 collective-permute-start.6
  127.1 1.5 collective-permute-done.21
  128.7 1.7 collective-permute-start.22
  130.4 1.3 collective-permute-done.30
  131.6 1.1 pad_maximum_fusion.3
  132.8 2.4 %collective-permute-start.31 = (bf16[3,2,2,1,2,24,896]{6,5,4,2,1,0,3:T(8,128)(2,1)}, bf16[3,2,2,1,2,24,896]{6,5,4,2,1,0,3:T(8,128)(2,1)}, u32[]{:S(2)}, u32[]{:S(2)}) collective-permute-start(bf16[3,2,2,1,2,24,896]{6,5,4,2,1,0,3:T(8,128)(2,1)} %pad_maximum_fusion.3), channel_id=1, source_target_pairs={{0,3},{1,2},{2,1},{3,0},{4,7},{5,6},{6,5},{7,4},{8,11},{9,10},{10,... | collective-permute-start | bytes 3096584 | tf_op jit(solution)/shard_map/ppermute | solution.py:364
  135.1 1.1 collective-permute-done.14
  136.3 1.1 pad_maximum_fusion.1
  137.4 1.1 pad_maximum_fusion
  138.5 0.3 collective-permute-start.7
  139.1 0.6 gather_fusion
  139.7 0.6 gather_fusion.1
  140.4 1.3 copy.31
  141.7 1.3 copy.27
  143.0 17.3 %collective-permute-done.15 = bf16[3,1,2,2,2,24,896]{6,5,4,2,1,0,3:T(8,128)(2,1)} collective-permute-done((bf16[3,1,2,2,2,24,896]{6,5,4,2,1,0,3:T(8,128)(2,1)}, bf16[3,1,2,2,2,24,896]{6,5,4,2,1,0,3:T(8,128)(2,1)}, u32[]{:S(2)}, u32[]{:S(2)}) %collective-permute-start.15) | collective-permute-done | bytes 1032224 | tf_op jit(solution)/shard_map/ppermute | solution.py:364
  160.4 1.3 copy.32
  161.7 1.3 copy.28
  163.0 8.8 %output_rows.1 = bf16[2,4,128,512]{3,2,1,0:T(8,128)(2,1)} custom-call(s32[8]{0:T(128)S(1)} %gather_fusion, s32[8]{0:T(128)S(1)} %gather_fusion.1, s32[14,4]{1,0:T(8,128)S(1)} %copy.33.dm, s32[1,768]{1,0:T(1,128)S(1)} %fusion.37.rows_ref, bf16[3,192,896]{2,1,0:T(8,128)(2,1)S(1)} %bitcast.52, bf16[3,192,896]{2,1,0:T(8,128)(2,1)S(1)} %bitcast.56, ...), custom_call_target="tpu_custom_call" | custom-call | flops 2214592512 | bytes 6291456 | tf_op jit(solution)/shard_map/output_rows/pallas_call | solution.py:220
  171.9 1.2 slice_bitcast_fusion
  173.0 6.2 %collective-permute-start.32 = (bf16[4,128,512]{2,1,0:T(8,128)(2,1)S(1)}, bf16[4,128,512]{2,1,0:T(8,128)(2,1)S(1)}, u32[]{:S(2)}, u32[]{:S(2)}) collective-permute-start(bf16[4,128,512]{2,1,0:T(8,128)(2,1)S(1)} %slice_bitcast_fusion), channel_id=1, source_target_pairs={{0,16},{16,0},{32,48},{48,32},{64,80},{80,64},{96,112},{112,96},{1... | collective-permute-start | bytes 1572872 | tf_op jit(solution)/shard_map/ppermute | solution.py:378
  179.2 1.5 collective-permute-done.32
  180.7 1.2 fusion.4
  181.9 0.3 collective-permute-start.33
  182.2 2.5 %collective-permute-start.34 = (bf16[128,512]{1,0:T(8,128)(2,1)S(1)}, bf16[128,512]{1,0:T(8,128)(2,1)S(1)}, u32[]{:S(2)}, u32[]{:S(2)}) collective-permute-start(bf16[128,512]{1,0:T(8,128)(2,1)S(1)} %get-tuple-element.34), channel_id=1, source_target_pairs={{0,96},{16,112},{32,0},{48,16},{64,32},{80,48},{96,64},{112,80},{1... | collective-permute-start | bytes 393224 | tf_op jit(solution)/shard_map/ppermute | solution.py:384
  184.7 0.7 collective-permute-start.35
  185.4 13.5 %gradients.1 = (f32[512,1792]{1,0:T(8,128)}, f32[512,1792]{1,0:T(8,128)}, f32[1792,512]{1,0:T(8,128)}) custom-call(s32[4,14]{1,0:T(4,128)S(1)} %copy-done.3, s32[4,14]{1,0:T(4,128)S(1)} %copy-done.4, s32[14,4]{1,0:T(8,128)S(1)} %copy.33.dm, bf16[512,768]{1,0:T(8,128)(2,1)S(1)} %copy-done.6, bf16[768,512]{1,0:T(8,128)(2,1)S(1)} %get-tuple-element.19.g_ref, ...), custom_call_target="tpu_custom_call" | custom-call | flops 4227858432 | bytes 20971520 | tf_op jit(solution)/shard_map/gradients/pallas_call | solution.py:273
  198.9 0.7 fusion.31
  (103 shorter events, 4.1 us)
Async XLA Ops:
  7.2 32.6 %all-gather.3.cloned.1.call-start = ((), (), s32[]{:S(2)}) async-start(), calls=%async_computation | async-start | bytes 2654208 | tf_op jit(solution)/shard_map/all_gather | solution.py:326
  40.9 1.7 copy-start.2
  42.6 2.6 %copy-start.3 = (s32[4,14]{1,0:T(4,128)S(1)}, s32[4,14]{1,0:T(4,128)}, u32[]{:S(2)}) copy-start(s32[4,14]{1,0:T(4,128)} %gm.3) | copy-start | bytes 676
  42.6 2.6 %copy-start.4 = (s32[4,14]{1,0:T(4,128)S(1)}, s32[4,14]{1,0:T(4,128)}, u32[]{:S(2)}) copy-start(s32[4,14]{1,0:T(4,128)} %um.3) | copy-start | bytes 676
  45.1 10.2 %copy-start.5 = (bf16[512,768]{1,0:T(8,128)(2,1)}, bf16[512,768]{1,0:T(8,128)(2,1)S(1)}, u32[]{:S(2)}) copy-start(bf16[512,768]{1,0:T(8,128)(2,1)S(1)} %get-tuple-element.28.xt_ref) | copy-start | bytes 2359300
  55.3 25.6 %collective-permute-start.24 = (bf16[3,2,2,1,2,24,896]{6,5,4,2,1,0,3:T(8,128)(2,1)}, bf16[3,2,2,1,2,24,896]{6,5,4,2,1,0,3:T(8,128)(2,1)S(1)}, u32[]{:S(2)}, u32[]{:S(2)}) collective-permute-start(bf16[3,2,2,1,2,24,896]{6,5,4,2,1,0,3:T(8,128)(2,1)} %bitcast.69), channel_id=1, source_target_pairs={{0,3},{1,2},{2,1},{3,0},{4,7},{5,6},{6,5},{7,4},{8,11},{9,10},{10,... | collective-permute-start | bytes 3096584 | tf_op jit(solution)/shard_map/ppermute | solution.py:353
  57.9 24.0 %collective-permute-start.16 = (bf16[3,2,2,1,2,24,896]{6,5,4,2,1,0,3:T(8,128)(2,1)}, bf16[3,2,2,1,2,24,896]{6,5,4,2,1,0,3:T(8,128)(2,1)S(1)}, u32[]{:S(2)}, u32[]{:S(2)}) collective-permute-start(bf16[3,2,2,1,2,24,896]{6,5,4,2,1,0,3:T(8,128)(2,1)} %bitcast.68), channel_id=1, source_target_pairs={{0,1},{1,0},{2,3},{3,2},{4,5},{5,4},{6,7},{7,6},{8,9},{9,8},{10,11... | collective-permute-start | bytes 3096584 | tf_op jit(solution)/shard_map/ppermute | solution.py:353
  57.9 23.1 %copy-start.8 = (bf16[3,4,48,896]{3,2,1,0:T(8,128)(2,1)S(1)}, bf16[3,4,48,896]{3,2,1,0:T(8,128)(2,1)}, u32[]{:S(2)}) copy-start(bf16[3,4,48,896]{3,2,1,0:T(8,128)(2,1)} %get-tuple-element.26) | copy-start | bytes 3096580
  58.0 27.1 %collective-permute-start.8 = (bf16[3,1,2,2,2,24,896]{6,5,4,2,1,0,3:T(8,128)(2,1)S(1)}, bf16[3,1,2,2,2,24,896]{6,5,4,2,1,0,3:T(8,128)(2,1)S(1)}, u32[]{:S(2)}, u32[]{:S(2)}) collective-permute-start(bf16[3,1,2,2,2,24,896]{6,5,4,2,1,0,3:T(8,128)(2,1)S(1)} %copy.29), channel_id=1, source_target_pairs={{0,12},{1,13},{2,14},{3,15},{4,8},{5,9},{6,10},{7,11},{8,4},{9,5},... | collective-permute-start | bytes 3096584 | tf_op jit(solution)/shard_map/ppermute | solution.py:353
  60.5 26.1 %collective-permute-start = (bf16[3,1,2,2,2,24,896]{6,5,4,2,1,0,3:T(8,128)(2,1)S(1)}, bf16[3,1,2,2,2,24,896]{6,5,4,2,1,0,3:T(8,128)(2,1)S(1)}, u32[]{:S(2)}, u32[]{:S(2)}) collective-permute-start(bf16[3,1,2,2,2,24,896]{6,5,4,2,1,0,3:T(8,128)(2,1)S(1)} %copy.25), channel_id=1, source_target_pairs={{0,4},{1,5},{2,6},{3,7},{4,0},{5,1},{6,2},{7,3},{8,12},{9,13},{10,... | collective-permute-start | bytes 3096584 | tf_op jit(solution)/shard_map/ppermute | solution.py:353
  81.0 1.2 copy-start.7
  81.3 12.2 %collective-permute-start.25 = (bf16[3,2,2,1,1,24,896]{6,5,4,2,1,0,3:T(8,128)(2,1)S(1)}, bf16[3,2,2,1,1,24,896]{6,5,4,2,1,0,3:T(8,128)(2,1)S(1)}, u32[]{:S(2)}, u32[]{:S(2)}) collective-permute-start(bf16[3,2,2,1,1,24,896]{6,5,4,2,1,0,3:T(8,128)(2,1)S(1)} %slice.233), channel_id=1, source_target_pairs={{0,1},{1,0},{2,3},{3,2},{4,5},{5,4},{6,7},{7,6},{8,9},{9,8},{10,11... | collective-permute-start | bytes 1548296 | tf_op jit(solution)/shard_map/ppermute | solution.py:353
  82.5 13.7 %collective-permute-start.17 = (bf16[3,2,2,1,1,24,896]{6,5,4,2,1,0,3:T(8,128)(2,1)S(1)}, bf16[3,2,2,1,1,24,896]{6,5,4,2,1,0,3:T(8,128)(2,1)S(1)}, u32[]{:S(2)}, u32[]{:S(2)}) collective-permute-start(bf16[3,2,2,1,1,24,896]{6,5,4,2,1,0,3:T(8,128)(2,1)S(1)} %slice.224), channel_id=1, source_target_pairs={{0,3},{1,2},{2,1},{3,0},{4,7},{5,6},{6,5},{7,4},{8,11},{9,10},{10,... | collective-permute-start | bytes 1548296 | tf_op jit(solution)/shard_map/ppermute | solution.py:353
  85.4 12.0 %collective-permute-start.9 = (bf16[3,1,1,2,2,24,896]{6,5,4,2,1,0,3:T(8,128)(2,1)S(1)}, bf16[3,1,1,2,2,24,896]{6,5,4,2,1,0,3:T(8,128)(2,1)S(1)}, u32[]{:S(2)}, u32[]{:S(2)}) collective-permute-start(bf16[3,1,1,2,2,24,896]{6,5,4,2,1,0,3:T(8,128)(2,1)S(1)} %slice.215), channel_id=1, source_target_pairs={{0,4},{1,5},{2,6},{3,7},{4,0},{5,1},{6,2},{7,3},{8,12},{9,13},{10,... | collective-permute-start | bytes 1548296 | tf_op jit(solution)/shard_map/ppermute | solution.py:353
  87.0 13.2 %collective-permute-start.1 = (bf16[3,1,1,2,2,24,896]{6,5,4,2,1,0,3:T(8,128)(2,1)S(1)}, bf16[3,1,1,2,2,24,896]{6,5,4,2,1,0,3:T(8,128)(2,1)S(1)}, u32[]{:S(2)}, u32[]{:S(2)}) collective-permute-start(bf16[3,1,1,2,2,24,896]{6,5,4,2,1,0,3:T(8,128)(2,1)S(1)} %slice.206), channel_id=1, source_target_pairs={{0,12},{1,13},{2,14},{3,15},{4,8},{5,9},{6,10},{7,11},{8,4},{9,5},... | collective-permute-start | bytes 1548296 | tf_op jit(solution)/shard_map/ppermute | solution.py:353
  93.7 11.7 %collective-permute-start.26 = (bf16[3,1,2,1,1,24,896]{6,5,4,2,1,0,3:T(8,128)(2,1)S(1)}, bf16[3,1,2,1,1,24,896]{6,5,4,2,1,0,3:T(8,128)(2,1)S(1)}, u32[]{:S(2)}, u32[]{:S(2)}) collective-permute-start(bf16[3,1,2,1,1,24,896]{6,5,4,2,1,0,3:T(8,128)(2,1)S(1)} %slice.235), channel_id=1, source_target_pairs={{0,12},{1,13},{2,14},{3,15},{4,8},{5,9},{6,10},{7,11},{8,4},{9,5},... | collective-permute-start | bytes 774152 | tf_op jit(solution)/shard_map/ppermute | solution.py:353
  96.4 9.2 %collective-permute-start.18 = (bf16[3,1,2,1,1,24,896]{6,5,4,2,1,0,3:T(8,128)(2,1)S(1)}, bf16[3,1,2,1,1,24,896]{6,5,4,2,1,0,3:T(8,128)(2,1)S(1)}, u32[]{:S(2)}, u32[]{:S(2)}) collective-permute-start(bf16[3,1,2,1,1,24,896]{6,5,4,2,1,0,3:T(8,128)(2,1)S(1)} %slice.226), channel_id=1, source_target_pairs={{0,4},{1,5},{2,6},{3,7},{4,0},{5,1},{6,2},{7,3},{8,12},{9,13},{10,... | collective-permute-start | bytes 774152 | tf_op jit(solution)/shard_map/ppermute | solution.py:353
  97.6 10.0 %collective-permute-start.10 = (bf16[3,1,1,1,2,24,896]{6,5,4,2,1,0,3:T(8,128)(2,1)S(1)}, bf16[3,1,1,1,2,24,896]{6,5,4,2,1,0,3:T(8,128)(2,1)S(1)}, u32[]{:S(2)}, u32[]{:S(2)}) collective-permute-start(bf16[3,1,1,1,2,24,896]{6,5,4,2,1,0,3:T(8,128)(2,1)S(1)} %slice.217), channel_id=1, source_target_pairs={{0,3},{1,2},{2,1},{3,0},{4,7},{5,6},{6,5},{7,4},{8,11},{9,10},{10,... | collective-permute-start | bytes 774152 | tf_op jit(solution)/shard_map/ppermute | solution.py:353
  100.3 7.5 %collective-permute-start.2 = (bf16[3,1,1,1,2,24,896]{6,5,4,2,1,0,3:T(8,128)(2,1)S(1)}, bf16[3,1,1,1,2,24,896]{6,5,4,2,1,0,3:T(8,128)(2,1)S(1)}, u32[]{:S(2)}, u32[]{:S(2)}) collective-permute-start(bf16[3,1,1,1,2,24,896]{6,5,4,2,1,0,3:T(8,128)(2,1)S(1)} %slice.208), channel_id=1, source_target_pairs={{0,1},{1,0},{2,3},{3,2},{4,5},{5,4},{6,7},{7,6},{8,9},{9,8},{10,11... | collective-permute-start | bytes 774152 | tf_op jit(solution)/shard_map/ppermute | solution.py:353
  105.5 4.2 %collective-permute-start.27 = (bf16[3,1,1,1,1,24,896]{6,5,4,2,1,0,3:T(8,128)(2,1)S(1)}, bf16[3,1,1,1,1,24,896]{6,5,4,2,1,0,3:T(8,128)(2,1)S(1)}, u32[]{:S(2)}, u32[]{:S(2)}) collective-permute-start(bf16[3,1,1,1,1,24,896]{6,5,4,2,1,0,3:T(8,128)(2,1)S(1)} %slice.237), channel_id=1, source_target_pairs={{0,4},{1,5},{2,6},{3,7},{4,0},{5,1},{6,2},{7,3},{8,12},{9,13},{10,... | collective-permute-start | bytes 387080 | tf_op jit(solution)/shard_map/ppermute | solution.py:353
  105.7 9.0 %collective-permute-start.19 = (bf16[3,1,1,1,1,24,896]{6,5,4,2,1,0,3:T(8,128)(2,1)S(1)}, bf16[3,1,1,1,1,24,896]{6,5,4,2,1,0,3:T(8,128)(2,1)S(1)}, u32[]{:S(2)}, u32[]{:S(2)}) collective-permute-start(bf16[3,1,1,1,1,24,896]{6,5,4,2,1,0,3:T(8,128)(2,1)S(1)} %slice.228), channel_id=1, source_target_pairs={{0,12},{1,13},{2,14},{3,15},{4,8},{5,9},{6,10},{7,11},{8,4},{9,5},... | collective-permute-start | bytes 387080 | tf_op jit(solution)/shard_map/ppermute | solution.py:353
  107.7 4.5 %collective-permute-start.11 = (bf16[3,1,1,1,1,24,896]{6,5,4,2,1,0,3:T(8,128)(2,1)S(1)}, bf16[3,1,1,1,1,24,896]{6,5,4,2,1,0,3:T(8,128)(2,1)S(1)}, u32[]{:S(2)}, u32[]{:S(2)}) collective-permute-start(bf16[3,1,1,1,1,24,896]{6,5,4,2,1,0,3:T(8,128)(2,1)S(1)} %slice.219), channel_id=1, source_target_pairs={{0,1},{1,0},{2,3},{3,2},{4,5},{5,4},{6,7},{7,6},{8,9},{9,8},{10,11... | collective-permute-start | bytes 387080 | tf_op jit(solution)/shard_map/ppermute | solution.py:353
  107.9 5.4 %collective-permute-start.3 = (bf16[3,1,1,1,1,24,896]{6,5,4,2,1,0,3:T(8,128)(2,1)S(1)}, bf16[3,1,1,1,1,24,896]{6,5,4,2,1,0,3:T(8,128)(2,1)S(1)}, u32[]{:S(2)}, u32[]{:S(2)}) collective-permute-start(bf16[3,1,1,1,1,24,896]{6,5,4,2,1,0,3:T(8,128)(2,1)S(1)} %slice.210), channel_id=1, source_target_pairs={{0,3},{1,2},{2,1},{3,0},{4,7},{5,6},{6,5},{7,4},{8,11},{9,10},{10,... | collective-permute-start | bytes 387080 | tf_op jit(solution)/shard_map/ppermute | solution.py:353
  109.8 5.0 %collective-permute-start.28 = (bf16[3,1,1,1,1,24,896]{6,5,4,2,1,0,3:T(8,128)(2,1)S(1)}, bf16[3,1,1,1,1,24,896]{6,5,4,2,1,0,3:T(8,128)(2,1)S(1)}, u32[]{:S(2)}, u32[]{:S(2)}) collective-permute-start(bf16[3,1,1,1,1,24,896]{6,5,4,2,1,0,3:T(8,128)(2,1)S(1)} %pad_maximum_fusion.15), channel_id=1, source_target_pairs={{0,4},{1,5},{2,6},{3,7},{4,0},{5,1},{6,2},{7,3},{8,12},{9,13},{10,... | collective-permute-start | bytes 387080 | tf_op jit(solution)/shard_map/ppermute | solution.py:364
  112.3 5.4 %collective-permute-start.12 = (bf16[3,1,1,1,1,24,896]{6,5,4,2,1,0,3:T(8,128)(2,1)S(1)}, bf16[3,1,1,1,1,24,896]{6,5,4,2,1,0,3:T(8,128)(2,1)S(1)}, u32[]{:S(2)}, u32[]{:S(2)}) collective-permute-start(bf16[3,1,1,1,1,24,896]{6,5,4,2,1,0,3:T(8,128)(2,1)S(1)} %pad_maximum_fusion.13), channel_id=1, source_target_pairs={{0,1},{1,0},{2,3},{3,2},{4,5},{5,4},{6,7},{7,6},{8,9},{9,8},{10,11... | collective-permute-start | bytes 387080 | tf_op jit(solution)/shard_map/ppermute | solution.py:364
  113.4 6.1 %collective-permute-start.4 = (bf16[3,1,1,1,1,24,896]{6,5,4,2,1,0,3:T(8,128)(2,1)S(1)}, bf16[3,1,1,1,1,24,896]{6,5,4,2,1,0,3:T(8,128)(2,1)S(1)}, u32[]{:S(2)}, u32[]{:S(2)}) collective-permute-start(bf16[3,1,1,1,1,24,896]{6,5,4,2,1,0,3:T(8,128)(2,1)S(1)} %pad_maximum_fusion.12), channel_id=1, source_target_pairs={{0,3},{1,2},{2,1},{3,0},{4,7},{5,6},{6,5},{7,4},{8,11},{9,10},{10,... | collective-permute-start | bytes 387080 | tf_op jit(solution)/shard_map/ppermute | solution.py:364
  114.9 6.5 %collective-permute-start.29 = (bf16[3,1,2,1,1,24,896]{6,5,4,2,1,0,3:T(8,128)(2,1)S(1)}, bf16[3,1,2,1,1,24,896]{6,5,4,2,1,0,3:T(8,128)(2,1)S(1)}, u32[]{:S(2)}, u32[]{:S(2)}) collective-permute-start(bf16[3,1,2,1,1,24,896]{6,5,4,2,1,0,3:T(8,128)(2,1)S(1)} %pad_maximum_fusion.11), channel_id=1, source_target_pairs={{0,12},{1,13},{2,14},{3,15},{4,8},{5,9},{6,10},{7,11},{8,4},{9,5},... | collective-permute-start | bytes 774152 | tf_op jit(solution)/shard_map/ppermute | solution.py:364
  116.0 7.0 %collective-permute-start.20 = (bf16[3,1,1,1,1,24,896]{6,5,4,2,1,0,3:T(8,128)(2,1)S(1)}, bf16[3,1,1,1,1,24,896]{6,5,4,2,1,0,3:T(8,128)(2,1)S(1)}, u32[]{:S(2)}, u32[]{:S(2)}) collective-permute-start(bf16[3,1,1,1,1,24,896]{6,5,4,2,1,0,3:T(8,128)(2,1)S(1)} %pad_maximum_fusion.14), channel_id=1, source_target_pairs={{0,12},{1,13},{2,14},{3,15},{4,8},{5,9},{6,10},{7,11},{8,4},{9,5},... | collective-permute-start | bytes 387080 | tf_op jit(solution)/shard_map/ppermute | solution.py:364
  117.8 8.1 %collective-permute-start.13 = (bf16[3,1,1,1,2,24,896]{6,5,4,2,1,0,3:T(8,128)(2,1)S(1)}, bf16[3,1,1,1,2,24,896]{6,5,4,2,1,0,3:T(8,128)(2,1)S(1)}, u32[]{:S(2)}, u32[]{:S(2)}) collective-permute-start(bf16[3,1,1,1,2,24,896]{6,5,4,2,1,0,3:T(8,128)(2,1)S(1)} %pad_maximum_fusion.9), channel_id=1, source_target_pairs={{0,3},{1,2},{2,1},{3,0},{4,7},{5,6},{6,5},{7,4},{8,11},{9,10},{10,... | collective-permute-start | bytes 774152 | tf_op jit(solution)/shard_map/ppermute | solution.py:364
  119.5 6.6 %collective-permute-start.5 = (bf16[3,1,1,1,2,24,896]{6,5,4,2,1,0,3:T(8,128)(2,1)S(1)}, bf16[3,1,1,1,2,24,896]{6,5,4,2,1,0,3:T(8,128)(2,1)S(1)}, u32[]{:S(2)}, u32[]{:S(2)}) collective-permute-start(bf16[3,1,1,1,2,24,896]{6,5,4,2,1,0,3:T(8,128)(2,1)S(1)} %pad_maximum_fusion.8), channel_id=1, source_target_pairs={{0,1},{1,0},{2,3},{3,2},{4,5},{5,4},{6,7},{7,6},{8,9},{9,8},{10,11... | collective-permute-start | bytes 774152 | tf_op jit(solution)/shard_map/ppermute | solution.py:364
  121.4 10.2 %collective-permute-start.30 = (bf16[3,2,2,1,1,24,896]{6,5,4,2,1,0,3:T(8,128)(2,1)S(1)}, bf16[3,2,2,1,1,24,896]{6,5,4,2,1,0,3:T(8,128)(2,1)S(1)}, u32[]{:S(2)}, u32[]{:S(2)}) collective-permute-start(bf16[3,2,2,1,1,24,896]{6,5,4,2,1,0,3:T(8,128)(2,1)S(1)} %pad_maximum_fusion.7), channel_id=1, source_target_pairs={{0,1},{1,0},{2,3},{3,2},{4,5},{5,4},{6,7},{7,6},{8,9},{9,8},{10,11... | collective-permute-start | bytes 1548296 | tf_op jit(solution)/shard_map/ppermute | solution.py:364
  123.0 5.6 %collective-permute-start.21 = (bf16[3,1,2,1,1,24,896]{6,5,4,2,1,0,3:T(8,128)(2,1)S(1)}, bf16[3,1,2,1,1,24,896]{6,5,4,2,1,0,3:T(8,128)(2,1)S(1)}, u32[]{:S(2)}, u32[]{:S(2)}) collective-permute-start(bf16[3,1,2,1,1,24,896]{6,5,4,2,1,0,3:T(8,128)(2,1)S(1)} %pad_maximum_fusion.10), channel_id=1, source_target_pairs={{0,4},{1,5},{2,6},{3,7},{4,0},{5,1},{6,2},{7,3},{8,12},{9,13},{10,... | collective-permute-start | bytes 774152 | tf_op jit(solution)/shard_map/ppermute | solution.py:364
  126.0 10.3 %collective-permute-start.14 = (bf16[3,1,1,2,2,24,896]{6,5,4,2,1,0,3:T(8,128)(2,1)S(1)}, bf16[3,1,1,2,2,24,896]{6,5,4,2,1,0,3:T(8,128)(2,1)S(1)}, u32[]{:S(2)}, u32[]{:S(2)}) collective-permute-start(bf16[3,1,1,2,2,24,896]{6,5,4,2,1,0,3:T(8,128)(2,1)S(1)} %pad_maximum_fusion.5), channel_id=1, source_target_pairs={{0,4},{1,5},{2,6},{3,7},{4,0},{5,1},{6,2},{7,3},{8,12},{9,13},{10,... | collective-permute-start | bytes 1548296 | tf_op jit(solution)/shard_map/ppermute | solution.py:364
  126.2 11.2 %collective-permute-start.6 = (bf16[3,1,1,2,2,24,896]{6,5,4,2,1,0,3:T(8,128)(2,1)S(1)}, bf16[3,1,1,2,2,24,896]{6,5,4,2,1,0,3:T(8,128)(2,1)S(1)}, u32[]{:S(2)}, u32[]{:S(2)}) collective-permute-start(bf16[3,1,1,2,2,24,896]{6,5,4,2,1,0,3:T(8,128)(2,1)S(1)} %pad_maximum_fusion.4), channel_id=1, source_target_pairs={{0,12},{1,13},{2,14},{3,15},{4,8},{5,9},{6,10},{7,11},{8,4},{9,5},... | collective-permute-start | bytes 1548296 | tf_op jit(solution)/shard_map/ppermute | solution.py:364
  128.7 10.1 %collective-permute-start.22 = (bf16[3,2,2,1,1,24,896]{6,5,4,2,1,0,3:T(8,128)(2,1)S(1)}, bf16[3,2,2,1,1,24,896]{6,5,4,2,1,0,3:T(8,128)(2,1)S(1)}, u32[]{:S(2)}, u32[]{:S(2)}) collective-permute-start(bf16[3,2,2,1,1,24,896]{6,5,4,2,1,0,3:T(8,128)(2,1)S(1)} %pad_maximum_fusion.6), channel_id=1, source_target_pairs={{0,3},{1,2},{2,1},{3,0},{4,7},{5,6},{6,5},{7,4},{8,11},{9,10},{10,... | collective-permute-start | bytes 1548296 | tf_op jit(solution)/shard_map/ppermute | solution.py:364
  132.8 30.2 %collective-permute-start.31 = (bf16[3,2,2,1,2,24,896]{6,5,4,2,1,0,3:T(8,128)(2,1)}, bf16[3,2,2,1,2,24,896]{6,5,4,2,1,0,3:T(8,128)(2,1)}, u32[]{:S(2)}, u32[]{:S(2)}) collective-permute-start(bf16[3,2,2,1,2,24,896]{6,5,4,2,1,0,3:T(8,128)(2,1)} %pad_maximum_fusion.3), channel_id=1, source_target_pairs={{0,3},{1,2},{2,1},{3,0},{4,7},{5,6},{6,5},{7,4},{8,11},{9,10},{10,... | collective-permute-start | bytes 3096584 | tf_op jit(solution)/shard_map/ppermute | solution.py:364
  137.4 23.0 %collective-permute-start.15 = (bf16[3,1,2,2,2,24,896]{6,5,4,2,1,0,3:T(8,128)(2,1)}, bf16[3,1,2,2,2,24,896]{6,5,4,2,1,0,3:T(8,128)(2,1)}, u32[]{:S(2)}, u32[]{:S(2)}) collective-permute-start(bf16[3,1,2,2,2,24,896]{6,5,4,2,1,0,3:T(8,128)(2,1)} %pad_maximum_fusion.1), channel_id=1, source_target_pairs={{0,12},{1,13},{2,14},{3,15},{4,8},{5,9},{6,10},{7,11},{8,4},{9,5},... | collective-permute-start | bytes 3096584 | tf_op jit(solution)/shard_map/ppermute | solution.py:364
  138.5 23.2 %collective-permute-start.7 = (bf16[3,1,2,2,2,24,896]{6,5,4,2,1,0,3:T(8,128)(2,1)}, bf16[3,1,2,2,2,24,896]{6,5,4,2,1,0,3:T(8,128)(2,1)}, u32[]{:S(2)}, u32[]{:S(2)}) collective-permute-start(bf16[3,1,2,2,2,24,896]{6,5,4,2,1,0,3:T(8,128)(2,1)} %pad_maximum_fusion), channel_id=1, source_target_pairs={{0,4},{1,5},{2,6},{3,7},{4,0},{5,1},{6,2},{7,3},{8,12},{9,13},{10,... | collective-permute-start | bytes 3096584 | tf_op jit(solution)/shard_map/ppermute | solution.py:364
  138.9 24.1 %copy-start = (bf16[3,2,2,1,2,24,896]{6,5,4,2,1,0,3:T(8,128)(2,1)}, bf16[3,2,2,1,2,24,896]{6,5,4,2,1,0,3:T(8,128)(2,1)S(1)}, u32[]{:S(2)}) copy-start(bf16[3,2,2,1,2,24,896]{6,5,4,2,1,0,3:T(8,128)(2,1)S(1)} %pad_maximum_fusion.2) | copy-start | bytes 3096580
  138.9 24.1 %collective-permute-start.23 = (bf16[3,2,2,1,2,24,896]{6,5,4,2,1,0,3:T(8,128)(2,1)S(1)}, bf16[3,2,2,1,2,24,896]{6,5,4,2,1,0,3:T(8,128)(2,1)S(1)}, u32[]{:S(2)}, u32[]{:S(2)}) collective-permute-start(bf16[3,2,2,1,2,24,896]{6,5,4,2,1,0,3:T(8,128)(2,1)S(1)} %pad_maximum_fusion.2), channel_id=1, source_target_pairs={{0,1},{1,0},{2,3},{3,2},{4,5},{5,4},{6,7},{7,6},{8,9},{9,8},{10,11... | collective-permute-start | bytes 3096584 | tf_op jit(solution)/shard_map/ppermute | solution.py:364
  163.0 8.9 %copy-start.1 = (bf16[3,2,2,1,2,24,896]{6,5,4,2,1,0,3:T(8,128)(2,1)}, bf16[3,2,2,1,2,24,896]{6,5,4,2,1,0,3:T(8,128)(2,1)S(1)}, u32[]{:S(2)}) copy-start(bf16[3,2,2,1,2,24,896]{6,5,4,2,1,0,3:T(8,128)(2,1)S(1)} %collective-permute-done.23) | copy-start | bytes 3096580
  171.9 13.6 %copy-start.6 = (bf16[512,768]{1,0:T(8,128)(2,1)S(1)}, bf16[512,768]{1,0:T(8,128)(2,1)}, u32[]{:S(2)}) copy-start(bf16[512,768]{1,0:T(8,128)(2,1)} %copy-done.5) | copy-start | bytes 2359300
  173.0 7.7 %collective-permute-start.32 = (bf16[4,128,512]{2,1,0:T(8,128)(2,1)S(1)}, bf16[4,128,512]{2,1,0:T(8,128)(2,1)S(1)}, u32[]{:S(2)}, u32[]{:S(2)}) collective-permute-start(bf16[4,128,512]{2,1,0:T(8,128)(2,1)S(1)} %slice_bitcast_fusion), channel_id=1, source_target_pairs={{0,16},{16,0},{32,48},{48,32},{64,80},{80,64},{96,112},{112,96},{1... | collective-permute-start | bytes 1572872 | tf_op jit(solution)/shard_map/ppermute | solution.py:378
  181.9 17.0 %collective-permute-start.33 = (bf16[128,512]{1,0:T(8,128)(2,1)S(1)}, bf16[128,512]{1,0:T(8,128)(2,1)S(1)}, u32[]{:S(2)}, u32[]{:S(2)}) collective-permute-start(bf16[128,512]{1,0:T(8,128)(2,1)S(1)} %get-tuple-element.32), channel_id=1, source_target_pairs={{0,32},{16,48},{32,64},{48,80},{64,96},{80,112},{96,0},{112,16},{1... | collective-permute-start | bytes 393224 | tf_op jit(solution)/shard_map/ppermute | solution.py:383
  182.2 16.7 %collective-permute-start.34 = (bf16[128,512]{1,0:T(8,128)(2,1)S(1)}, bf16[128,512]{1,0:T(8,128)(2,1)S(1)}, u32[]{:S(2)}, u32[]{:S(2)}) collective-permute-start(bf16[128,512]{1,0:T(8,128)(2,1)S(1)} %get-tuple-element.34), channel_id=1, source_target_pairs={{0,96},{16,112},{32,0},{48,16},{64,32},{80,48},{96,64},{112,80},{1... | collective-permute-start | bytes 393224 | tf_op jit(solution)/shard_map/ppermute | solution.py:384
  184.7 14.2 %collective-permute-start.35 = (bf16[128,512]{1,0:T(8,128)(2,1)S(1)}, bf16[128,512]{1,0:T(8,128)(2,1)S(1)}, u32[]{:S(2)}, u32[]{:S(2)}) collective-permute-start(bf16[128,512]{1,0:T(8,128)(2,1)S(1)} %get-tuple-element.33), channel_id=1, source_target_pairs={{0,64},{16,80},{32,96},{48,112},{64,0},{80,16},{96,32},{112,48},{1... | collective-permute-start | bytes 393224 | tf_op jit(solution)/shard_map/ppermute | solution.py:385
Sparse Core Ops, SparseCore 0:
  10.3 29.4 all-gather.2

commit v2 on v0

v2 whole, which is shorter than its diff:
```python
import functools

import jax
import jax.numpy as jnp
from jax import lax
from jax.experimental import pallas as pl
from jax.experimental.pallas import tpu as pltpu
from jax.sharding import PartitionSpec as P

BF = jnp.bfloat16
F32 = jnp.float32
LIVE = 768
PAD = 144
SIDE = 4
BLK = 128
PAIR = 2 * BLK
UNITS = 1792
HALF = UNITS // 2
STEPS = UNITS // PAIR
FEAT = 512
SLOTS = 1024
CUT = 96
FIRST = 576
LAST = LIVE - FIRST
VMEM = 48 << 20

MASKS = {"xA": (1, 0), "xB": (3, 0), "yA": (0, 1), "yB": (0, 3)}
ROUNDS = {
    (0, 0): (("xA", 0), ("xB", 1), ("yA", 2), ("yB", 3)),
    (0, 1): (("xB", 1), ("xA", 0), ("yB", 3), ("yA", 2)),
    (1, 0): (("yA", 0), ("yB", 1), ("xA", 2), ("xB", 3)),
    (1, 1): (("yB", 1), ("yA", 0), ("xB", 3), ("xA", 2)),
}
GROUPS = tuple(ROUNDS)


def partners(name):
    dx, dy = MASKS[name]
    return [
        (x * SIDE + y, (x ^ dx) * SIDE + (y ^ dy)) for x in range(SIDE) for y in range(SIDE)
    ]


def shift(dz, dc):
    return [
        (z * 2 + c, ((z + dz) % SIDE) * 2 + (c + dc) % 2) for z in range(SIDE) for c in range(2)
    ]


def logical_rows():
    place = lax.axis_index("dp")
    x, y = place // SIDE, place % SIDE

    def sides(v):
        high = v // 2
        return (v % 2) ^ high, high

    xa, xb = sides(x)
    ya, yb = sides(y)
    first = xa * 8 + xb * 4 + ya * 2 + yb
    second = ya * 8 + yb * 4 + xa * 2 + xb
    row = lax.iota(jnp.int32, LIVE)
    early = row < FIRST
    half = jnp.where(early, row // 288, (row - FIRST) // CUT)
    piece = jnp.where(early, (row % 288) // CUT, 3)
    block, rest = piece * 4 + (row % CUT) // 24, row % 24
    return half * 384 + (block ^ jnp.where(half > 0, second, first)) * 24 + rest


def kept(mask_ref, row, col, value):
    return jnp.where(mask_ref[row, col] > 0, value, jnp.zeros_like(value))


def smem():
    return pl.BlockSpec(memory_space=pltpu.SMEM)


def whole(shape):
    return pl.BlockSpec(shape, lambda j: (0,) * len(shape))


def call(kernel, name, flops, moved, **rest):
    return pl.pallas_call(
        kernel,
        compiler_params=pltpu.CompilerParams(vmem_limit_bytes=VMEM),
        cost_estimate=pl.CostEstimate(flops=flops, bytes_accessed=moved, transcendentals=0),
        name=name,
        **rest,
    )


def pack_kernel(tok_ref, cot_ref, count_ref, out_ref):
    out_ref[:BLK, :FEAT] = tok_ref[...]
    out_ref[:BLK, FEAT:] = cot_ref[...]
    count = jnp.full((PAD - BLK, 2 * FEAT), count_ref[0], jnp.int32)
    out_ref[BLK:, :] = count.astype(F32).astype(BF)


def pack(tokens, cotangent, counts):
    vmem = pl.BlockSpec(memory_space=pltpu.VMEM)
    return call(
        pack_kernel,
        "pack",
        0,
        1 << 19,
        out_shape=jax.ShapeDtypeStruct((PAD, 2 * FEAT), BF),
        in_specs=[vmem, vmem, smem()],
        out_specs=vmem,
    )(tokens, cotangent, counts)


def prepare_kernel(gm, um, dm, wg, wu, wd, wx_ref, wdt_ref, wd_ref):
    j = pl.program_id(0)
    for which, (mask, ref) in enumerate(((gm, wg), (um, wu))):
        for r in range(4):
            for b in range(2):
                at = slice(r * BLK, (r + 1) * BLK)
                wx_ref[0, at, which * PAIR + b * BLK : which * PAIR + (b + 1) * BLK] = kept(
                    mask, r, 2 * j + b, ref[at, b * BLK : (b + 1) * BLK]
                )
    down = jnp.concatenate(
        [
            jnp.concatenate(
                [
                    kept(dm, 2 * j + b, c, wd[b * BLK : (b + 1) * BLK, c * BLK : (c + 1) * BLK])
                    for c in range(4)
                ],
                axis=1,
            )
            for b in range(2)
        ],
        axis=0,
    )
    wd_ref[...] = down
    wdt_ref[0] = down.T


def prepare(gm, um, dm, wg, wu, wd):
    return call(
        prepare_kernel,
        "prepare",
        0,
        13 << 20,
        grid=(STEPS,),
        out_shape=(
            jax.ShapeDtypeStruct((STEPS, FEAT, 2 * PAIR), BF),
            jax.ShapeDtypeStruct((STEPS, FEAT, PAIR), BF),
            jax.ShapeDtypeStruct((UNITS, FEAT), BF),
        ),
        in_specs=[
            smem(),
            smem(),
            smem(),
            pl.BlockSpec((FEAT, PAIR), lambda j: (0, j)),
            pl.BlockSpec((FEAT, PAIR), lambda j: (0, j)),
            pl.BlockSpec((PAIR, FEAT), lambda j: (j, 0)),
        ],
        out_specs=(
            pl.BlockSpec((1, FEAT, 2 * PAIR), lambda j: (j, 0, 0)),
            pl.BlockSpec((1, FEAT, PAIR), lambda j: (j, 0, 0)),
            pl.BlockSpec((PAIR, FEAT), lambda j: (j, 0)),
        ),
    )(gm, um, dm, wg, wu, wd)


def compact_kernel(shard, rows_ref, *refs):
    sources, (x_ref, g_ref, xt_first, xt_last, offs_ref, cnts_ref) = refs[:8], refs[8:]
    rows = rows_ref[...]
    slot = lax.broadcasted_iota(jnp.int32, (LIVE, BLK), 1)
    cnts = [ref[BLK : BLK + 1, 0:1].astype(F32).astype(jnp.int32) for ref in sources]
    total = None
    for pair in range(4):
        picks = []
        for k in (2 * pair, 2 * pair + 1):
            offset = jnp.zeros((1, 1), jnp.int32)
            for other in range(8):
                if other != k:
                    offset += jnp.where(shard[other] < shard[k], cnts[other], 0)
            offs_ref[k] = jnp.broadcast_to(offset, (8, BLK))
            cnts_ref[k] = jnp.broadcast_to(cnts[k], (8, BLK))
            hit = (rows - offset == slot) & (slot < cnts[k])
            picks.append(jnp.where(hit, 1.0, 0.0).astype(BF))
        source = jnp.concatenate(
            [sources[2 * pair][:BLK, :], sources[2 * pair + 1][:BLK, :]], axis=0
        )
        part = jnp.dot(jnp.concatenate(picks, axis=1), source, preferred_element_type=F32)
        total = part if total is None else total + part
    x_ref[...] = total[:, :FEAT].astype(BF)
    g_ref[...] = total[:, FEAT:].astype(BF)
    xt_first[...] = total[:FIRST, :FEAT].T.astype(BF)
    xt_last[...] = total[FIRST:, :FEAT].T.astype(BF)


def compact(shard, rows, sources):
    vmem = pl.BlockSpec(memory_space=pltpu.VMEM)
    return call(
        compact_kernel,
        "compact",
        2 * LIVE * SLOTS * SLOTS,
        5 << 20,
        out_shape=(
            jax.ShapeDtypeStruct((LIVE, FEAT), BF),
            jax.ShapeDtypeStruct((LIVE, FEAT), BF),
            jax.ShapeDtypeStruct((FEAT, FIRST), BF),
            jax.ShapeDtypeStruct((FEAT, LAST), BF),
            jax.ShapeDtypeStruct((8, 8, BLK), jnp.int32),
            jax.ShapeDtypeStruct((8, 8, BLK), jnp.int32),
        ),
        in_specs=[smem(), vmem] + [vmem] * 8,
        out_specs=(vmem,) * 6,
    )(shard, rows, *sources)


def partial_kernel(start, pieces, x_ref, g_ref, wx_ref, wdt_ref, *outs):
    count = 2 * pieces * CUT
    x, g = x_ref[start : start + count, :], g_ref[start : start + count, :]
    both = jnp.dot(x, wx_ref[0], preferred_element_type=F32)
    back = jnp.dot(g, wdt_ref[0], preferred_element_type=F32)
    for which, result in enumerate((both[:, :PAIR], both[:, PAIR:], back)):
        result = result.astype(BF)
        for h in range(2):
            for piece in range(pieces):
                at = (h * pieces + piece) * CUT
                for q in range(2):
                    outs[(piece * 2 + h) * 2 + q][which] = result[
                        at : at + CUT, q * BLK : (q + 1) * BLK
                    ]


def partials(start, pieces, x, g, wx, wdt):
    count = 2 * pieces * CUT
    return call(
        functools.partial(partial_kernel, start, pieces),
        "partials",
        2 * count * FEAT * 3 * UNITS,
        7 << 20,
        grid=(STEPS,),
        out_shape=(jax.ShapeDtypeStruct((3, CUT, HALF), BF),) * (4 * pieces),
        in_specs=[
            whole((LIVE, FEAT)),
            whole((LIVE, FEAT)),
            pl.BlockSpec((1, FEAT, 2 * PAIR), lambda j: (j, 0, 0)),
            pl.BlockSpec((1, FEAT, PAIR), lambda j: (j, 0, 0)),
        ],
        out_specs=(pl.BlockSpec((3, CUT, BLK), lambda j: (0, 0, j)),) * (4 * pieces),
    )(x, g, wx, wdt)


def stacked(refs, which, pieces):
    return jnp.concatenate(
        [
            jnp.concatenate([refs[(p * 2 + h) * 2 + q][which] for q in range(2)], axis=1)
            for h in range(2)
            for p in pieces
        ],
        axis=0,
    )


def picked(rows, offs, cnts, k, slot):
    hit = (rows - offs[k, 0:1, 0:1] == slot) & (slot < cnts[k, 0:1, 0:1])
    return jnp.where(hit, 1.0, 0.0).astype(BF)


def first_output_kernel(rows_ref, offs, cnts, wd_ref, *refs):
    parts, (out_ref, total) = refs[:12], refs[12:]
    j = pl.program_id(0)
    part = jnp.dot(stacked(parts, 0, range(3)), wd_ref[...], preferred_element_type=F32)

    @pl.when(j == 0)
    def _():
        total[...] = part

    @pl.when(j > 0)
    def _():
        total[...] += part

    @pl.when(j == STEPS - 1)
    def _():
        mixed = total[...].astype(BF)
        rows = rows_ref[0:1, :]
        slot = lax.broadcasted_iota(jnp.int32, (BLK, FIRST), 0)
        for k in range(8):
            pick = picked(rows, offs, cnts, k, slot)
            out_ref[k] = jnp.dot(pick, mixed, preferred_element_type=F32).astype(BF)


def first_output(rows, offs, cnts, wd, parts):
    return call(
        first_output_kernel,
        "first_output",
        2 * FIRST * FEAT * (UNITS + SLOTS),
        5 << 20,
        grid=(STEPS,),
        out_shape=jax.ShapeDtypeStruct((8, BLK, FEAT), BF),
        in_specs=[whole((1, FIRST)), whole((8, 8, BLK)), whole((8, 8, BLK))]
        + [pl.BlockSpec((PAIR, FEAT), lambda j: (j, 0))]
        + [pl.BlockSpec((1, CUT, BLK), lambda j: (0, 0, j))] * 12,
        out_specs=whole((8, BLK, FEAT)),
        scratch_shapes=[pltpu.VMEM((FIRST, FEAT), F32)],
    )(rows, offs, cnts, wd, *parts)


def last_output_kernel(rows_ref, offs, cnts, early_ref, wd_ref, *refs):
    parts, (near_ref, away_ref) = refs[:4], refs[4:]
    mixed = None
    for j in range(STEPS):
        hidden = jnp.concatenate(
            [
                jnp.concatenate(
                    [parts[h * 2 + q][0, :, j * BLK : (j + 1) * BLK] for q in range(2)], axis=1
                )
                for h in range(2)
            ],
            axis=0,
        )
        part = jnp.dot(
            hidden, wd_ref[j * PAIR : (j + 1) * PAIR, :], preferred_element_type=F32
        )
        mixed = part if mixed is None else mixed + part
    mixed = mixed.astype(BF)
    rows = rows_ref[0:1, :]
    slot = lax.broadcasted_iota(jnp.int32, (BLK, LAST), 0)
    for k in range(8):
        pick = picked(rows, offs, cnts, k, slot)
        late = jnp.dot(pick, mixed, preferred_element_type=F32)
        target = near_ref if k < 4 else away_ref
        target[k % 4] = (early_ref[k].astype(F32) + late).astype(BF)


def last_output(rows, offs, cnts, early, wd, parts):
    return call(
        last_output_kernel,
        "last_output",
        2 * LAST * FEAT * (UNITS + SLOTS),
        5 << 20,
        grid=(1,),
        out_shape=(jax.ShapeDtypeStruct((4, BLK, FEAT), BF),) * 2,
        in_specs=[
            whole((1, LAST)),
            whole((8, 8, BLK)),
            whole((8, 8, BLK)),
            whole((8, BLK, FEAT)),
            whole((UNITS, FEAT)),
        ]
        + [whole((1, CUT, HALF))] * 4,
        out_specs=(whole((4, BLK, FEAT)),) * 2,
    )(rows, offs, cnts, early, wd, *parts)


def grad_kernel(gm, um, dm, xt_first, xt_last, g_ref, *refs):
    parts, (gate_out, up_out, down_out) = refs[:16], refs[16:]
    j = pl.program_id(0)

    def side(which):
        return stacked(parts, which, range(3)), stacked(parts, which, (3,))

    (hidden, hidden_l), (d_gate, d_gate_l), (d_up, d_up_l) = [side(which) for which in range(3)]
    xt, xt_l = xt_first[...], xt_last[...]
    gate = jnp.dot(xt, d_gate, preferred_element_type=F32) + jnp.dot(
        xt_l, d_gate_l, preferred_element_type=F32
    )
    up = jnp.dot(xt, d_up, preferred_element_type=F32) + jnp.dot(
        xt_l, d_up_l, preferred_element_type=F32
    )
    down = lax.dot_general(
        jnp.concatenate([hidden, hidden_l], axis=0),
        g_ref[...],
        (((0,), (0,)), ((), ())),
        preferred_element_type=F32,
    )
    for r in range(4):
        for b in range(2):
            at, by = slice(r * BLK, (r + 1) * BLK), slice(b * BLK, (b + 1) * BLK)
            gate_out[at, by] = kept(gm, r, 2 * j + b, gate[at, by])
            up_out[at, by] = kept(um, r, 2 * j + b, up[at, by])
            down_out[by, at] = kept(dm, 2 * j + b, r, down[by, at])


def gradients(gm, um, dm, xt_first, xt_last, g, parts):
    return call(
        grad_kernel,
        "gradients",
        2 * LIVE * FEAT * 3 * UNITS,
        20 << 20,
        grid=(STEPS,),
        out_shape=(
            jax.ShapeDtypeStruct((FEAT, UNITS), F32),
            jax.ShapeDtypeStruct((FEAT, UNITS), F32),
            jax.ShapeDtypeStruct((UNITS, FEAT), F32),
        ),
        in_specs=[
            smem(),
            smem(),
            smem(),
            whole((FEAT, FIRST)),
            whole((FEAT, LAST)),
            whole((LIVE, FEAT)),
        ]
        + [pl.BlockSpec((3, CUT, BLK), lambda j: (0, 0, j))] * 16,
        out_specs=(
            pl.BlockSpec((FEAT, PAIR), lambda j: (0, j)),
            pl.BlockSpec((FEAT, PAIR), lambda j: (0, j)),
            pl.BlockSpec((PAIR, FEAT), lambda j: (j, 0)),
        ),
    )(gm, um, dm, xt_first, xt_last, g, *parts)


def split(value, axis):
    lower = lax.slice_in_dim(value, 0, 1, axis=axis)
    upper = lax.slice_in_dim(value, 1, 2, axis=axis)
    return lower, upper


def activate(total):
    gate, upward, back = total[0], total[1], total[2]
    sigma = jax.nn.sigmoid(gate)
    active = gate * sigma
    hidden = (active * upward).astype(BF)
    d_gate = (back * upward * sigma * (1.0 + gate * (1.0 - sigma))).astype(BF)
    d_up = (back * active).astype(BF)
    return jnp.stack([hidden, d_gate, d_up])


def exchange(values, number):
    return {
        s: lax.ppermute(values[s], "dp", partners(ROUNDS[s][number][0])) for s in GROUPS
    }


def on_device(
    tokens, cotangent, gate_weight, up_weight, down_weight, gate_mask, up_mask, down_mask, counts
):
    live = (lax.iota(jnp.int32, tokens.shape[0]) < counts[0])[:, None]
    place = lax.axis_index("col")
    order = jnp.arange(8)
    shard = ((place // 2 + order % 4) % SIDE) * 2 + ((place % 2) ^ (order // 4))
    own = pack(tokens, cotangent, counts)
    column = [own] + [lax.ppermute(own, "col", shift(-dz, 0)) for dz in (1, 2, 3)]
    beside = [lax.ppermute(value, "col", shift(0, 1)) for value in column]
    wx, wdt, wd = prepare(gate_mask, up_mask, down_mask, gate_weight, up_weight, down_weight)
    rows = logical_rows()
    x, g, xt_first, xt_last, offs, cnts = compact(shard, rows[:, None], column + beside)

    early = partials(FIRST, 1, x, g, wx, wdt)
    late = partials(0, 3, x, g, wx, wdt)
    piece = {}
    for s in GROUPS:
        at = s[0] * 2 + s[1]
        piece[s] = (late[at], late[4 + at], late[8 + at], early[at])
    other = {s: tuple(2 - ROUNDS[s][n][1] for n in range(2)) for s in GROUPS}

    come = exchange({s: piece[s][3] for s in GROUPS}, 0)
    second = {
        s: (piece[s][other[s][1]].astype(F32) + come[s].astype(F32)).astype(BF) for s in GROUPS
    }
    come_rest = exchange({s: piece[s][other[s][0]] for s in GROUPS}, 0)
    come_second = exchange(second, 1)
    keep, send = {}, {}
    for s in GROUPS:
        total = (
            piece[s][0].astype(F32) + come_rest[s].astype(F32) + come_second[s].astype(F32)
        ).reshape(3, 2, 2, 24, HALF)
        keep[s], upper = split(total, ROUNDS[s][2][1] - 1)
        send[s] = upper.astype(BF)
    come = exchange(send, 2)
    for s in GROUPS:
        total = keep[s] + come[s].astype(F32)
        keep[s], upper = split(total, ROUNDS[s][3][1] - 1)
        send[s] = upper.astype(BF)
    come = exchange(send, 3)
    held = {s: activate(keep[s] + come[s].astype(F32)) for s in GROUPS}
    for number in (3, 2):
        come = exchange(held, number)
        held = {
            s: jnp.concatenate([held[s], come[s]], axis=ROUNDS[s][number][1] - 1)
            for s in GROUPS
        }
    held = {s: held[s].reshape(3, CUT, HALF) for s in GROUPS}
    near = exchange(held, 1)
    far = exchange(held, 0)
    last = exchange(near, 0)
    parts = [[], [], [], []]
    for s in GROUPS:
        given = {0: held[s], other[s][1]: near[s], other[s][0]: far[s], 3: last[s]}
        for p in range(4):
            parts[p].append(given[p])

    early_rows, last_rows = rows[None, :FIRST], rows[None, FIRST:]
    begun = first_output(early_rows, offs, cnts, wd, parts[0] + parts[1] + parts[2])
    mine, away = last_output(last_rows, offs, cnts, begun, wd, parts[3])
    summed = mine.astype(F32) + lax.ppermute(away, "col", shift(0, 1)).astype(F32)
    terms = [summed[k].astype(BF) for k in range(4)]
    mixed = terms[0].astype(F32)
    for dz in (1, 2, 3):
        mixed += lax.ppermute(terms[dz], "col", shift(dz, 0)).astype(F32)
    output = jnp.where(live, mixed, jnp.zeros_like(mixed)).astype(BF)
    gate_grad, up_grad, down_grad = gradients(
        gate_mask,
        up_mask,
        down_mask,
        xt_first,
        xt_last,
        g,
        parts[0] + parts[1] + parts[2] + parts[3],
    )
    return (output, gate_grad, up_grad, down_grad)


def solution(mesh):
    in_specs = (
        P("col", "dp"),
        P("col", "dp"),
        P("dp", "col"),
        P("dp", "col"),
        P("col", "dp"),
        P("dp", "col"),
        P("dp", "col"),
        P("col", "dp"),
        P("col"),
    )
    out_specs = (P("col", "dp"), P("dp", "col"), P("dp", "col"), P("col", "dp"))
    return jax.shard_map(
        on_device, mesh=mesh, in_specs=in_specs, out_specs=out_specs, check_vma=False
    )
```

time: 414 us -> 202 us (0.49)
  waiting for transfers between devices: 316 us -> 67.7 us
  starting transfers between devices: 0.47 us -> 75.6 us
  Pallas kernels: 0 us -> 42.8 us
  matrix products: 34 us -> 0 us
  local copies, waits for them, and re-layouts: 29.9 us -> 8.42 us
  other arithmetic: 17.6 us -> 4.13 us
  between operations: 14.9 us -> 1.97 us
    reduce_scatter x3 -> x0, waiting for transfers between devices: 177 us -> none  [the longest x1 78.2 us: on_device(): lax.psum_scatter(lax.dot_general(block, w_down, contract_cols, preferred_...]
    all_gather x4 -> x0, waiting for transfers between devices: 138 us -> none  [the longest x1 68.5 us: on_device(): lax.all_gather(d_mine, 'dp', axis=0, tiled=True)]
    ppermute x0 -> x51, starting transfers between devices: none -> 75.6 us  [the longest x40 43.2 us: exchange(): lax.ppermute(values[s], 'dp', partners(ROUNDS[s][number][0]))]
    ppermute x0 -> x51, waiting for transfers between devices: none -> 67.7 us  [the longest x40 56.9 us: exchange(): lax.ppermute(values[s], 'dp', partners(ROUNDS[s][number][0]))]
    pallas_call x0 -> x8, Pallas kernels: none -> 42.8 us  [the longest x2 14.3 us: partials(): call(functools.partial(partial_kernel, start, pieces), 'partials', 2 * co...]
    dot_general x5 -> x0, matrix products: 34 us -> none  [the longest x1 9.36 us: on_device(): jnp.dot(block, w_both, preferred_element_type=jnp.float32)]
    unnamed x13 -> x39, local copies, waits for them, and re-layouts: 28 us -> 8.12 us
    select_n x3 -> x0, other arithmetic: 10.8 us -> none  [the longest x2 9.16 us: widen(): return jnp.where(keep, shaped, jnp.zeros_like(shaped)).reshape(weight.shape)]
  transfers between devices with their start and end apart: 7 -> 51, of which waited for: 7 -> 18; matrix products, arithmetic and copies ran while one was open for 12% -> 2% of each run, Pallas kernels for 0% -> 16%
where the time goes in v2:
time: 202 us; the launch traced here: 201 us
  starting transfers between devices  75.6 us (37%)
  waiting for transfers between devices  67.7 us (34%)
  Pallas kernels  42.8 us (21%)
  local copies, waits for them, and re-layouts  8.42 us (4%)
  other arithmetic  4.13 us (2%)
    ppermute x40, waiting for transfers between devices, exchange(): lax.ppermute(values[s], 'dp', partners(ROUNDS[s][number][0]))  56.9 us
    ppermute x40, starting transfers between devices, exchange(): lax.ppermute(values[s], 'dp', partners(ROUNDS[s][number][0]))  43.2 us
    pallas_call x2, Pallas kernels, partials(): call(functools.partial(partial_kernel, start, pieces), 'partials', 2 * co...  14.3 us
    ppermute x1, starting transfers between devices, on_device(): lax.ppermute(away, 'col', shift(0, 1)).astype(F32)  14.3 us
    pallas_call x1, Pallas kernels, gradients(): call(grad_kernel, 'gradients', 2 * LIVE * FEAT * 3 * UNITS, 20 << 20, gri...  10.6 us
    ppermute x3, waiting for transfers between devices, on_device(): lax.ppermute(own, 'col', shift(-dz, 0))  9.26 us
    unnamed x39, local copies, waits for them, and re-layouts  8.12 us
    pallas_call x1, Pallas kernels, first_output(): call(first_output_kernel, 'first_output', 2 * FIRST * FEAT * (UNITS + SLO...  7.72 us
  transfers between devices with their start and end apart: 51, of which 18 were waited for; matrix products, arithmetic and copies ran while one was open for 2% of the time, Pallas kernels for 16%

profile of v2, /device:TPU:1, one launch (start us, length us, event | category | flops | bytes accessed | tf_op | source)
XLA Modules:
  0.0 200.6 jit_solution(5552122312084819974)
XLA Ops:
  1.3 0.9 copy-done.11
  2.2 0.9 copy-done.12
  3.1 2.5 %collective-permute-start.2 = (bf16[144,1024]{1,0:T(8,128)(2,1)S(1)}, bf16[144,1024]{1,0:T(8,128)(2,1)S(1)}, u32[]{:S(2)}, u32[]{:S(2)}) collective-permute-start(bf16[144,1024]{1,0:T(8,128)(2,1)S(1)} %pack.1.refs_0_), channel_id=1, source_target_pairs={{0,32},{16,48},{32,64},{48,80},{64,96},{80,112},{96,0},{112,16},{1... | collective-permute-start | bytes 884744 | tf_op jit(solution)/shard_map/ppermute | solution.py:439
  5.6 3.3 %collective-permute-start.1 = (bf16[144,1024]{1,0:T(8,128)(2,1)S(1)}, bf16[144,1024]{1,0:T(8,128)(2,1)S(1)}, u32[]{:S(2)}, u32[]{:S(2)}) collective-permute-start(bf16[144,1024]{1,0:T(8,128)(2,1)S(1)} %pack.1.refs_0_), channel_id=1, source_target_pairs={{0,64},{16,80},{32,96},{48,112},{64,0},{80,16},{96,32},{112,48},{1... | collective-permute-start | bytes 884744 | tf_op jit(solution)/shard_map/ppermute | solution.py:439
  9.7 1.5 collective-permute-start.3
  11.2 3.3 %collective-permute-done.2.refs_3_ = bf16[144,1024]{1,0:T(8,128)(2,1)S(1)} collective-permute-done((bf16[144,1024]{1,0:T(8,128)(2,1)S(1)}, bf16[144,1024]{1,0:T(8,128)(2,1)S(1)}, u32[]{:S(2)}, u32[]{:S(2)}) %collective-permute-start.2) | collective-permute-done | bytes 294944 | tf_op jit(solution)/shard_map/ppermute | solution.py:439
  14.5 1.2 collective-permute-start.6
  15.7 5.9 %collective-permute-done.1.refs_2_ = bf16[144,1024]{1,0:T(8,128)(2,1)S(1)} collective-permute-done((bf16[144,1024]{1,0:T(8,128)(2,1)S(1)}, bf16[144,1024]{1,0:T(8,128)(2,1)S(1)}, u32[]{:S(2)}, u32[]{:S(2)}) %collective-permute-start.1) | collective-permute-done | bytes 294944 | tf_op jit(solution)/shard_map/ppermute | solution.py:439
  21.7 1.5 collective-permute-start.5
  23.3 0.8 copy.17.dm
  24.1 1.5 copy-done.3
  27.0 6.6 %prepare.1 = (bf16[7,512,512]{2,1,0:T(8,128)(2,1)}, bf16[7,512,256]{2,1,0:T(8,128)(2,1)S(1)}, bf16[1792,512]{1,0:T(8,128)(2,1)S(1)}) custom-call(s32[4,14]{1,0:T(4,128)S(1)} %copy-done.13, s32[4,14]{1,0:T(4,128)S(1)} %copy-done.15, s32[14,4]{1,0:T(8,128)S(1)} %copy.17.dm, bf16[512,1792]{1,0:T(8,128)(2,1)S(1)} %copy-done.3, bf16[512,1792]{1,0:T(8,128)(2,1)} %wu.1, ...), custom_call_target="tpu_custom_call" | custom-call | bytes 13631488 | tf_op jit(solution)/shard_map/prepare/pallas_call | solution.py:139
  33.5 1.2 copy-done
  34.8 0.9 fusion.16.rows_ref
  35.7 2.6 %compact.1 = (bf16[768,512]{1,0:T(8,128)(2,1)S(1)}, bf16[768,512]{1,0:T(8,128)(2,1)S(1)}, bf16[512,576]{1,0:T(8,128)(2,1)S(1)}, bf16[512,192]{1,0:T(8,128)(2,1)S...) custom-call(s32[8]{0:T(128)S(1)} %fusion.78.shard, s32[768,1]{1,0:T(8,128)S(1)} %fusion.16.rows_ref, ...), custom_call_target="tpu_custom_call" | custom-call | flops 1610612736 | bytes 5242880 | tf_op jit(solution)/shard_map/compact/pallas_call | solution.py:196
  38.4 6.2 %partials.3 = (bf16[3,96,896]{2,1,0:T(8,128)(2,1)S(1)}, bf16[3,96,896]{2,1,0:T(8,128)(2,1)S(1)}, bf16[3,96,896]{2,1,0:T(8,128)(2,1)S(1)}, bf16[3,96,896]{2,1,0:T(8,128)(2,1)S(1)}) custom-call(bf16[768,512]{1,0:T(8,128)(2,1)S(1)} %get-tuple-element.37.x_ref, bf16[768,512]{1,0:T(8,128)(2,1)S(1)} %get-tuple-element.38.g_ref, ...), custom_call_target="tpu_custom_call" | custom-call | flops 1056964608 | bytes 7340032 | tf_op jit(solution)/shard_map/partials/pallas_call | solution.py:232
  44.6 1.3 collective-permute-start.8
  45.9 1.8 collective-permute-start.15
  47.7 1.3 collective-permute-start.22
  49.0 1.9 collective-permute-start.29
  50.9 8.2 %partials.2 = (bf16[3,96,896]{2,1,0:T(8,128)(2,1)S(1)}, bf16[3,96,896]{2,1,0:T(8,128)(2,1)S(1)}, bf16[3,96,896]{2,1,0:T(8,128)(2,1)S(1)}, bf16[3,96,896]{2,1,0:T...) custom-call(bf16[768,512]{1,0:T(8,128)(2,1)} %copy-done.6, ...), custom_call_target="tpu_custom_call" | custom-call | flops 3170893824 | bytes 7340032 | tf_op jit(solution)/shard_map/partials/pallas_call | solution.py:232
  60.3 1.2 collective-permute-start.21
  61.6 1.4 collective-permute-start.9
  63.4 7.4 %collective-permute-done.7 = bf16[3,96,896]{2,1,0:T(8,128)(2,1)S(1)} collective-permute-done((bf16[3,96,896]{2,1,0:T(8,128)(2,1)S(1)}, bf16[3,96,896]{2,1,0:T(8,128)(2,1)S(1)}, u32[]{:S(2)}, u32[]{:S(2)}) %collective-permute-start.7) | collective-permute-done | bytes 516128 | tf_op jit(solution)/shard_map/ppermute | solution.py:427
  70.8 0.8 collective-permute-start.28
  71.5 11.5 %collective-permute-done.9 = bf16[3,96,896]{2,1,0:T(8,128)(2,1)S(1)} collective-permute-done((bf16[3,96,896]{2,1,0:T(8,128)(2,1)S(1)}, bf16[3,96,896]{2,1,0:T(8,128)(2,1)S(1)}, u32[]{:S(2)}, u32[]{:S(2)}) %collective-permute-start.9) | collective-permute-done | bytes 516128 | tf_op jit(solution)/shard_map/ppermute | solution.py:427
  83.1 0.8 collective-permute-start.23
  84.5 1.1 collective-permute-start.10
  85.8 2.0 collective-permute-start.17
  87.8 6.9 %collective-permute-done.23 = bf16[3,96,896]{2,1,0:T(8,128)(2,1)S(1)} collective-permute-done((bf16[3,96,896]{2,1,0:T(8,128)(2,1)S(1)}, bf16[3,96,896]{2,1,0:T(8,128)(2,1)S(1)}, u32[]{:S(2)}, u32[]{:S(2)}) %collective-permute-start.23) | collective-permute-done | bytes 516128 | tf_op jit(solution)/shard_map/ppermute | solution.py:427
  95.4 2.5 %collective-permute-start.31 = (bf16[3,2,1,24,896]{4,3,2,1,0:T(8,128)(2,1)S(1)}, bf16[3,2,1,24,896]{4,3,2,1,0:T(8,128)(2,1)S(1)}, u32[]{:S(2)}, u32[]{:S(2)}) collective-permute-start(bf16[3,2,1,24,896]{4,3,2,1,0:T(8,128)(2,1)S(1)} %slice.242), channel_id=1, source_target_pairs={{0,12},{1,13},{2,14},{3,15},{4,8},{5,9},{6,10},{7,11},{8,4},{9,5},... | collective-permute-start | bytes 774152 | tf_op jit(solution)/shard_map/ppermute | solution.py:427
  98.0 1.8 collective-permute-done.10
  99.9 2.0 %collective-permute-start.11 = (bf16[3,1,1,24,896]{4,3,2,1,0:T(8,128)(2,1)S(1)}, bf16[3,1,1,24,896]{4,3,2,1,0:T(8,128)(2,1)S(1)}, u32[]{:S(2)}, u32[]{:S(2)}) collective-permute-start(bf16[3,1,1,24,896]{4,3,2,1,0:T(8,128)(2,1)S(1)} %slice.249), channel_id=1, source_target_pairs={{0,3},{1,2},{2,1},{3,0},{4,7},{5,6},{6,5},{7,4},{8,11},{9,10},{10,... | collective-permute-start | bytes 387080 | tf_op jit(solution)/shard_map/ppermute | solution.py:427
  102.2 1.7 collective-permute-start.25
  104.1 0.9 collective-permute-done.11
  105.1 2.0 %collective-permute-start.12 = (bf16[3,1,1,24,896]{4,3,2,1,0:T(8,128)(2,1)S(1)}, bf16[3,1,1,24,896]{4,3,2,1,0:T(8,128)(2,1)S(1)}, u32[]{:S(2)}, u32[]{:S(2)}) collective-permute-start(bf16[3,1,1,24,896]{4,3,2,1,0:T(8,128)(2,1)S(1)} %pad_maximum_fusion.8), channel_id=1, source_target_pairs={{0,3},{1,2},{2,1},{3,0},{4,7},{5,6},{6,5},{7,4},{8,11},{9,10},{10,... | collective-permute-start | bytes 387080 | tf_op jit(solution)/shard_map/ppermute | solution.py:427
  107.8 0.8 collective-permute-done.25
  108.7 1.2 collective-permute-start.26
  110.0 1.9 collective-permute-done.12
  112.4 2.2 %collective-permute-start.20 = (bf16[3,2,1,24,896]{4,3,2,1,0:T(8,128)(2,1)S(1)}, bf16[3,2,1,24,896]{4,3,2,1,0:T(8,128)(2,1)S(1)}, u32[]{:S(2)}, u32[]{:S(2)}) collective-permute-start(bf16[3,2,1,24,896]{4,3,2,1,0:T(8,128)(2,1)S(1)} %pad_maximum_fusion.5), channel_id=1, source_target_pairs={{0,3},{1,2},{2,1},{3,0},{4,7},{5,6},{6,5},{7,4},{8,11},{9,10},{10,... | collective-permute-start | bytes 774152 | tf_op jit(solution)/shard_map/ppermute | solution.py:427
  114.6 2.8 %collective-permute-done.13 = bf16[3,1,2,24,896]{4,3,2,1,0:T(8,128)(2,1)S(1)} collective-permute-done((bf16[3,1,2,24,896]{4,3,2,1,0:T(8,128)(2,1)S(1)}, bf16[3,1,2,24,896]{4,3,2,1,0:T(8,128)(2,1)S(1)}, u32[]{:S(2)}, u32[]{:S(2)}) %collective-permute-start.13) | collective-permute-done | bytes 258080 | tf_op jit(solution)/shard_map/ppermute | solution.py:427
  117.6 2.8 %collective-permute-start.35 = (bf16[3,96,896]{2,1,0:T(8,128)(2,1)S(1)}, bf16[3,96,896]{2,1,0:T(8,128)(2,1)S(1)}, u32[]{:S(2)}, u32[]{:S(2)}) collective-permute-start(bf16[3,96,896]{2,1,0:T(8,128)(2,1)S(1)} %bitcast.24), channel_id=1, source_target_pairs={{0,12},{1,13},{2,14},{3,15},{4,8},{5,9},{6,10},{7,11},{8,4},{9,5},... | collective-permute-start | bytes 1548296 | tf_op jit(solution)/shard_map/ppermute | solution.py:427
  120.4 0.8 collective-permute-start.27
  122.2 7.9 %collective-permute-done.27 = bf16[3,1,2,24,896]{4,3,2,1,0:T(8,128)(2,1)S(1)} collective-permute-done((bf16[3,1,2,24,896]{4,3,2,1,0:T(8,128)(2,1)S(1)}, bf16[3,1,2,24,896]{4,3,2,1,0:T(8,128)(2,1)S(1)}, u32[]{:S(2)}, u32[]{:S(2)}) %collective-permute-start.27) | collective-permute-done | bytes 258080 | tf_op jit(solution)/shard_map/ppermute | solution.py:427
  130.2 4.4 %collective-permute-start.36 = (bf16[3,96,896]{2,1,0:T(8,128)(2,1)S(1)}, bf16[3,96,896]{2,1,0:T(8,128)(2,1)S(1)}, u32[]{:S(2)}, u32[]{:S(2)}) collective-permute-start(bf16[3,96,896]{2,1,0:T(8,128)(2,1)S(1)} %bitcast.28), channel_id=1, source_target_pairs={{0,12},{1,13},{2,14},{3,15},{4,8},{5,9},{6,10},{7,11},{8,4},{9,5},... | collective-permute-start | bytes 1548296 | tf_op jit(solution)/shard_map/ppermute | solution.py:427
  134.7 0.9 collective-permute-start.41
  136.5 4.7 %collective-permute-done.40.refs_9_ = bf16[3,96,896]{2,1,0:T(8,128)(2,1)S(1)} collective-permute-done((bf16[3,96,896]{2,1,0:T(8,128)(2,1)S(1)}, bf16[3,96,896]{2,1,0:T(8,128)(2,1)S(1)}, u32[]{:S(2)}, u32[]{:S(2)}) %collective-permute-start.40) | collective-permute-done | bytes 516128 | tf_op jit(solution)/shard_map/ppermute | solution.py:427
  141.2 1.7 collective-permute-start.38
  142.9 1.6 collective-permute-done.36.refs_5_
  145.3 1.3 collective-permute-start.44
  146.8 1.7 collective-permute-done.42.refs_11_
  148.9 1.9 collective-permute-done.38.refs_7_
  150.8 7.7 %first_output.1.early_ref = bf16[8,128,512]{2,1,0:T(8,128)(2,1)} custom-call(s32[1,576]{1,0:T(1,128)S(1)} %broadcast_in_dim.45.rows_ref, s32[8,8,128]{2,1,0:T(8,128)S(1)} %get-tuple-element.34.offs, s32[8,8,128]{2,1,0:T(8,128)S(1)} %get-tuple-element.35.cnts, bf16[1792,512]{1,0:T(8,128)(2,1)} %copy-done, bf16[3,96,896]{2,1,0:T(8,128)(2,1)S(1)} %bitcast.25, ...), custom_call_target="tpu_custom_call" | custom-call | flops 1660944384 | bytes 5242880 | tf_op jit(solution)/shard_map/first_output/pallas_call | solution.py:289
  158.5 1.1 collective-permute-done.44.refs_1_.refs_13_
  159.6 3.9 %collective-permute-done.46.refs_3_.refs_15_ = bf16[3,96,896]{2,1,0:T(8,128)(2,1)S(1)} collective-permute-done((bf16[3,96,896]{2,1,0:T(8,128)(2,1)S(1)}, bf16[3,96,896]{2,1,0:T(8,128)(2,1)S(1)}, u32[]{:S(2)}, u32[]{:S(2)}) %collective-permute-start.46) | collective-permute-done | bytes 516128 | tf_op jit(solution)/shard_map/ppermute | solution.py:427
  163.5 1.4 copy-done.2
  164.9 1.0 last_output.1
  166.0 14.3 %collective-permute-start.47 = (bf16[4,128,512]{2,1,0:T(8,128)(2,1)S(1)}, bf16[4,128,512]{2,1,0:T(8,128)(2,1)S(1)}, u32[]{:S(2)}, u32[]{:S(2)}) collective-permute-start(bf16[4,128,512]{2,1,0:T(8,128)(2,1)S(1)} %get-tuple-element.58), channel_id=1, source_target_pairs={{0,16},{16,0},{32,48},{48,32},{64,80},{80,64},{96,112},{112,96},{1... | collective-permute-start | bytes 1572872 | tf_op jit(solution)/shard_map/ppermute | solution.py:492
  180.3 1.5 collective-permute-done.47
  182.0 4.8 %collective-permute-start.48 = (bf16[128,512]{1,0:T(8,128)(2,1)S(1)}, bf16[128,512]{1,0:T(8,128)(2,1)S(1)}, u32[]{:S(2)}, u32[]{:S(2)}) collective-permute-start(bf16[128,512]{1,0:T(8,128)(2,1)S(1)} %get-tuple-element.64), channel_id=1, source_target_pairs={{0,32},{16,48},{32,64},{48,80},{64,96},{80,112},{96,0},{112,16},{1... | collective-permute-start | bytes 393224 | tf_op jit(solution)/shard_map/ppermute | solution.py:496
  186.8 1.0 collective-permute-start.50
  187.8 1.5 collective-permute-start.49
  189.3 10.6 %gradients.1 = (f32[512,1792]{1,0:T(8,128)}, f32[512,1792]{1,0:T(8,128)}, f32[1792,512]{1,0:T(8,128)}) custom-call(s32[4,14]{1,0:T(4,128)S(1)} %copy-done.14, s32[4,14]{1,0:T(4,128)S(1)} %copy-done.16, s32[14,4]{1,0:T(8,128)S(1)} %copy.17.dm, bf16[512,576]{1,0:T(8,128)(2,1)} %copy-done.17, bf16[512,192]{1,0:T(8,128)(2,1)S(1)} %get-tuple-element.60.xt_last, ...), custom_call_target="tpu_custom_call" | custom-call | flops 4227858432 | bytes 20971520 | tf_op jit(solution)/shard_map/gradients/pallas_call | solution.py:381
  199.9 0.7 fusion.37
  (134 shorter events, 11.0 us)
Async XLA Ops:
  3.1 11.4 %collective-permute-start.2 = (bf16[144,1024]{1,0:T(8,128)(2,1)S(1)}, bf16[144,1024]{1,0:T(8,128)(2,1)S(1)}, u32[]{:S(2)}, u32[]{:S(2)}) collective-permute-start(bf16[144,1024]{1,0:T(8,128)(2,1)S(1)} %pack.1.refs_0_), channel_id=1, source_target_pairs={{0,32},{16,48},{32,64},{48,80},{64,96},{80,112},{96,0},{112,16},{1... | collective-permute-start | bytes 884744 | tf_op jit(solution)/shard_map/ppermute | solution.py:439
  5.6 16.0 %collective-permute-start.1 = (bf16[144,1024]{1,0:T(8,128)(2,1)S(1)}, bf16[144,1024]{1,0:T(8,128)(2,1)S(1)}, u32[]{:S(2)}, u32[]{:S(2)}) collective-permute-start(bf16[144,1024]{1,0:T(8,128)(2,1)S(1)} %pack.1.refs_0_), channel_id=1, source_target_pairs={{0,64},{16,80},{32,96},{48,112},{64,0},{80,16},{96,32},{112,48},{1... | collective-permute-start | bytes 884744 | tf_op jit(solution)/shard_map/ppermute | solution.py:439
  9.0 14.3 %collective-permute-start = (bf16[144,1024]{1,0:T(8,128)(2,1)S(1)}, bf16[144,1024]{1,0:T(8,128)(2,1)S(1)}, u32[]{:S(2)}, u32[]{:S(2)}) collective-permute-start(bf16[144,1024]{1,0:T(8,128)(2,1)S(1)} %pack.1.refs_0_), channel_id=1, source_target_pairs={{0,96},{16,112},{32,0},{48,16},{64,32},{80,48},{96,64},{112,80},{1... | collective-permute-start | bytes 884744 | tf_op jit(solution)/shard_map/ppermute | solution.py:439
  9.7 26.0 %collective-permute-start.3 = (bf16[144,1024]{1,0:T(8,128)(2,1)S(1)}, bf16[144,1024]{1,0:T(8,128)(2,1)S(1)}, u32[]{:S(2)}, u32[]{:S(2)}) collective-permute-start(bf16[144,1024]{1,0:T(8,128)(2,1)S(1)} %pack.1.refs_0_), channel_id=1, source_target_pairs={{0,16},{16,0},{32,48},{48,32},{64,80},{80,64},{96,112},{112,96},{1... | collective-permute-start | bytes 884744 | tf_op jit(solution)/shard_map/ppermute | solution.py:440
  14.5 21.2 %collective-permute-start.6 = (bf16[144,1024]{1,0:T(8,128)(2,1)S(1)}, bf16[144,1024]{1,0:T(8,128)(2,1)S(1)}, u32[]{:S(2)}, u32[]{:S(2)}) collective-permute-start(bf16[144,1024]{1,0:T(8,128)(2,1)S(1)} %collective-permute-done.2.refs_3_), channel_id=1, source_target_pairs={{0,16},{16,0},{32,48},{48,32},{64,80},{80,64},{96,112},{112,96},{1... | collective-permute-start | bytes 884744 | tf_op jit(solution)/shard_map/ppermute | solution.py:440
  21.7 14.0 %collective-permute-start.5 = (bf16[144,1024]{1,0:T(8,128)(2,1)S(1)}, bf16[144,1024]{1,0:T(8,128)(2,1)S(1)}, u32[]{:S(2)}, u32[]{:S(2)}) collective-permute-start(bf16[144,1024]{1,0:T(8,128)(2,1)S(1)} %collective-permute-done.1.refs_2_), channel_id=1, source_target_pairs={{0,16},{16,0},{32,48},{48,32},{64,80},{80,64},{96,112},{112,96},{1... | collective-permute-start | bytes 884744 | tf_op jit(solution)/shard_map/ppermute | solution.py:440
  23.2 12.5 %collective-permute-start.4 = (bf16[144,1024]{1,0:T(8,128)(2,1)S(1)}, bf16[144,1024]{1,0:T(8,128)(2,1)S(1)}, u32[]{:S(2)}, u32[]{:S(2)}) collective-permute-start(bf16[144,1024]{1,0:T(8,128)(2,1)S(1)} %collective-permute-done.refs_1_), channel_id=1, source_target_pairs={{0,16},{16,0},{32,48},{48,32},{64,80},{80,64},{96,112},{112,96},{1... | collective-permute-start | bytes 884744 | tf_op jit(solution)/shard_map/ppermute | solution.py:440
  24.1 1.5 copy-start.3
  34.8 3.6 %copy-start.4 = (bf16[7,512,256]{2,1,0:T(8,128)(2,1)}, bf16[7,512,256]{2,1,0:T(8,128)(2,1)S(1)}, u32[]{:S(2)}) copy-start(bf16[7,512,256]{2,1,0:T(8,128)(2,1)S(1)} %get-tuple-element.40.wdt_ref) | copy-start | bytes 5505028
  38.3 6.2 %copy-start.5 = (bf16[768,512]{1,0:T(8,128)(2,1)}, bf16[768,512]{1,0:T(8,128)(2,1)S(1)}, u32[]{:S(2)}) copy-start(bf16[768,512]{1,0:T(8,128)(2,1)S(1)} %get-tuple-element.38.g_ref) | copy-start | bytes 2359300
  38.4 6.2 %copy-start.6 = (bf16[768,512]{1,0:T(8,128)(2,1)}, bf16[768,512]{1,0:T(8,128)(2,1)S(1)}, u32[]{:S(2)}) copy-start(bf16[768,512]{1,0:T(8,128)(2,1)S(1)} %get-tuple-element.37.x_ref) | copy-start | bytes 2359300
  38.4 6.2 %copy-start.17 = (bf16[512,576]{1,0:T(8,128)(2,1)}, bf16[512,576]{1,0:T(8,128)(2,1)S(1)}, u32[]{:S(2)}) copy-start(bf16[512,576]{1,0:T(8,128)(2,1)S(1)} %get-tuple-element.59.xt_first) | copy-start | bytes 1769476
  44.6 14.9 %collective-permute-start.8 = (bf16[3,96,896]{2,1,0:T(8,128)(2,1)S(1)}, bf16[3,96,896]{2,1,0:T(8,128)(2,1)S(1)}, u32[]{:S(2)}, u32[]{:S(2)}) collective-permute-start(bf16[3,96,896]{2,1,0:T(8,128)(2,1)S(1)} %get-tuple-element.44), channel_id=1, source_target_pairs={{0,4},{1,5},{2,6},{3,7},{4,0},{5,1},{6,2},{7,3},{8,12},{9,13},{10,... | collective-permute-start | bytes 1548296 | tf_op jit(solution)/shard_map/ppermute | solution.py:427
  45.9 14.4 %collective-permute-start.15 = (bf16[3,96,896]{2,1,0:T(8,128)(2,1)S(1)}, bf16[3,96,896]{2,1,0:T(8,128)(2,1)S(1)}, u32[]{:S(2)}, u32[]{:S(2)}) collective-permute-start(bf16[3,96,896]{2,1,0:T(8,128)(2,1)S(1)} %get-tuple-element.48), channel_id=1, source_target_pairs={{0,12},{1,13},{2,14},{3,15},{4,8},{5,9},{6,10},{7,11},{8,4},{9,5},... | collective-permute-start | bytes 1548296 | tf_op jit(solution)/shard_map/ppermute | solution.py:427
  47.7 13.9 %collective-permute-start.22 = (bf16[3,96,896]{2,1,0:T(8,128)(2,1)S(1)}, bf16[3,96,896]{2,1,0:T(8,128)(2,1)S(1)}, u32[]{:S(2)}, u32[]{:S(2)}) collective-permute-start(bf16[3,96,896]{2,1,0:T(8,128)(2,1)S(1)} %get-tuple-element.52), channel_id=1, source_target_pairs={{0,1},{1,0},{2,3},{3,2},{4,5},{5,4},{6,7},{7,6},{8,9},{9,8},{10,11... | collective-permute-start | bytes 1548296 | tf_op jit(solution)/shard_map/ppermute | solution.py:427
  49.0 14.1 %collective-permute-start.29 = (bf16[3,96,896]{2,1,0:T(8,128)(2,1)S(1)}, bf16[3,96,896]{2,1,0:T(8,128)(2,1)S(1)}, u32[]{:S(2)}, u32[]{:S(2)}) collective-permute-start(bf16[3,96,896]{2,1,0:T(8,128)(2,1)S(1)} %get-tuple-element.56), channel_id=1, source_target_pairs={{0,3},{1,2},{2,1},{3,0},{4,7},{5,6},{6,5},{7,4},{8,11},{9,10},{10,... | collective-permute-start | bytes 1548296 | tf_op jit(solution)/shard_map/ppermute | solution.py:427
  59.1 11.7 %collective-permute-start.7 = (bf16[3,96,896]{2,1,0:T(8,128)(2,1)S(1)}, bf16[3,96,896]{2,1,0:T(8,128)(2,1)S(1)}, u32[]{:S(2)}, u32[]{:S(2)}) collective-permute-start(bf16[3,96,896]{2,1,0:T(8,128)(2,1)S(1)} %get-tuple-element.42), channel_id=1, source_target_pairs={{0,4},{1,5},{2,6},{3,7},{4,0},{5,1},{6,2},{7,3},{8,12},{9,13},{10,... | collective-permute-start | bytes 1548296 | tf_op jit(solution)/shard_map/ppermute | solution.py:427
  59.5 24.6 %collective-permute-start.14 = (bf16[3,96,896]{2,1,0:T(8,128)(2,1)S(1)}, bf16[3,96,896]{2,1,0:T(8,128)(2,1)S(1)}, u32[]{:S(2)}, u32[]{:S(2)}) collective-permute-start(bf16[3,96,896]{2,1,0:T(8,128)(2,1)S(1)} %get-tuple-element.46), channel_id=1, source_target_pairs={{0,12},{1,13},{2,14},{3,15},{4,8},{5,9},{6,10},{7,11},{8,4},{9,5},... | collective-permute-start | bytes 1548296 | tf_op jit(solution)/shard_map/ppermute | solution.py:427
  60.3 25.6 %collective-permute-start.21 = (bf16[3,96,896]{2,1,0:T(8,128)(2,1)S(1)}, bf16[3,96,896]{2,1,0:T(8,128)(2,1)S(1)}, u32[]{:S(2)}, u32[]{:S(2)}) collective-permute-start(bf16[3,96,896]{2,1,0:T(8,128)(2,1)S(1)} %get-tuple-element.50), channel_id=1, source_target_pairs={{0,1},{1,0},{2,3},{3,2},{4,5},{5,4},{6,7},{7,6},{8,9},{9,8},{10,11... | collective-permute-start | bytes 1548296 | tf_op jit(solution)/shard_map/ppermute | solution.py:427
  61.6 21.5 %collective-permute-start.9 = (bf16[3,96,896]{2,1,0:T(8,128)(2,1)S(1)}, bf16[3,96,896]{2,1,0:T(8,128)(2,1)S(1)}, u32[]{:S(2)}, u32[]{:S(2)}) collective-permute-start(bf16[3,96,896]{2,1,0:T(8,128)(2,1)S(1)} %add_convert_fusion.4), channel_id=1, source_target_pairs={{0,12},{1,13},{2,14},{3,15},{4,8},{5,9},{6,10},{7,11},{8,4},{9,5},... | collective-permute-start | bytes 1548296 | tf_op jit(solution)/shard_map/ppermute | solution.py:427
  63.1 21.3 %collective-permute-start.16 = (bf16[3,96,896]{2,1,0:T(8,128)(2,1)S(1)}, bf16[3,96,896]{2,1,0:T(8,128)(2,1)S(1)}, u32[]{:S(2)}, u32[]{:S(2)}) collective-permute-start(bf16[3,96,896]{2,1,0:T(8,128)(2,1)S(1)} %add_convert_fusion.3), channel_id=1, source_target_pairs={{0,4},{1,5},{2,6},{3,7},{4,0},{5,1},{6,2},{7,3},{8,12},{9,13},{10,... | collective-permute-start | bytes 1548296 | tf_op jit(solution)/shard_map/ppermute | solution.py:427
  70.8 24.4 %collective-permute-start.28 = (bf16[3,96,896]{2,1,0:T(8,128)(2,1)S(1)}, bf16[3,96,896]{2,1,0:T(8,128)(2,1)S(1)}, u32[]{:S(2)}, u32[]{:S(2)}) collective-permute-start(bf16[3,96,896]{2,1,0:T(8,128)(2,1)S(1)} %get-tuple-element.54), channel_id=1, source_target_pairs={{0,3},{1,2},{2,1},{3,0},{4,7},{5,6},{6,5},{7,4},{8,11},{9,10},{10,... | collective-permute-start | bytes 1548296 | tf_op jit(solution)/shard_map/ppermute | solution.py:427
  83.1 11.6 %collective-permute-start.23 = (bf16[3,96,896]{2,1,0:T(8,128)(2,1)S(1)}, bf16[3,96,896]{2,1,0:T(8,128)(2,1)S(1)}, u32[]{:S(2)}, u32[]{:S(2)}) collective-permute-start(bf16[3,96,896]{2,1,0:T(8,128)(2,1)S(1)} %add_convert_fusion.2), channel_id=1, source_target_pairs={{0,3},{1,2},{2,1},{3,0},{4,7},{5,6},{6,5},{7,4},{8,11},{9,10},{10,... | collective-permute-start | bytes 1548296 | tf_op jit(solution)/shard_map/ppermute | solution.py:427
  84.1 11.2 %collective-permute-start.30 = (bf16[3,96,896]{2,1,0:T(8,128)(2,1)S(1)}, bf16[3,96,896]{2,1,0:T(8,128)(2,1)S(1)}, u32[]{:S(2)}, u32[]{:S(2)}) collective-permute-start(bf16[3,96,896]{2,1,0:T(8,128)(2,1)S(1)} %add_convert_fusion.1), channel_id=1, source_target_pairs={{0,1},{1,0},{2,3},{3,2},{4,5},{5,4},{6,7},{7,6},{8,9},{9,8},{10,11... | collective-permute-start | bytes 1548296 | tf_op jit(solution)/shard_map/ppermute | solution.py:427
  84.5 15.3 %collective-permute-start.10 = (bf16[3,1,2,24,896]{4,3,2,1,0:T(8,128)(2,1)S(1)}, bf16[3,1,2,24,896]{4,3,2,1,0:T(8,128)(2,1)S(1)}, u32[]{:S(2)}, u32[]{:S(2)}) collective-permute-start(bf16[3,1,2,24,896]{4,3,2,1,0:T(8,128)(2,1)S(1)} %slice.245), channel_id=1, source_target_pairs={{0,1},{1,0},{2,3},{3,2},{4,5},{5,4},{6,7},{7,6},{8,9},{9,8},{10,11... | collective-permute-start | bytes 774152 | tf_op jit(solution)/shard_map/ppermute | solution.py:427
  85.8 16.1 %collective-permute-start.17 = (bf16[3,2,1,24,896]{4,3,2,1,0:T(8,128)(2,1)S(1)}, bf16[3,2,1,24,896]{4,3,2,1,0:T(8,128)(2,1)S(1)}, u32[]{:S(2)}, u32[]{:S(2)}) collective-permute-start(bf16[3,2,1,24,896]{4,3,2,1,0:T(8,128)(2,1)S(1)} %slice.244), channel_id=1, source_target_pairs={{0,3},{1,2},{2,1},{3,0},{4,7},{5,6},{6,5},{7,4},{8,11},{9,10},{10,... | collective-permute-start | bytes 774152 | tf_op jit(solution)/shard_map/ppermute | solution.py:427
  94.9 7.2 %collective-permute-start.24 = (bf16[3,1,2,24,896]{4,3,2,1,0:T(8,128)(2,1)S(1)}, bf16[3,1,2,24,896]{4,3,2,1,0:T(8,128)(2,1)S(1)}, u32[]{:S(2)}, u32[]{:S(2)}) collective-permute-start(bf16[3,1,2,24,896]{4,3,2,1,0:T(8,128)(2,1)S(1)} %slice.243), channel_id=1, source_target_pairs={{0,4},{1,5},{2,6},{3,7},{4,0},{5,1},{6,2},{7,3},{8,12},{9,13},{10,... | collective-permute-start | bytes 774152 | tf_op jit(solution)/shard_map/ppermute | solution.py:427
  95.4 8.4 %collective-permute-start.31 = (bf16[3,2,1,24,896]{4,3,2,1,0:T(8,128)(2,1)S(1)}, bf16[3,2,1,24,896]{4,3,2,1,0:T(8,128)(2,1)S(1)}, u32[]{:S(2)}, u32[]{:S(2)}) collective-permute-start(bf16[3,2,1,24,896]{4,3,2,1,0:T(8,128)(2,1)S(1)} %slice.242), channel_id=1, source_target_pairs={{0,12},{1,13},{2,14},{3,15},{4,8},{5,9},{6,10},{7,11},{8,4},{9,5},... | collective-permute-start | bytes 774152 | tf_op jit(solution)/shard_map/ppermute | solution.py:427
  99.9 5.1 %collective-permute-start.11 = (bf16[3,1,1,24,896]{4,3,2,1,0:T(8,128)(2,1)S(1)}, bf16[3,1,1,24,896]{4,3,2,1,0:T(8,128)(2,1)S(1)}, u32[]{:S(2)}, u32[]{:S(2)}) collective-permute-start(bf16[3,1,1,24,896]{4,3,2,1,0:T(8,128)(2,1)S(1)} %slice.249), channel_id=1, source_target_pairs={{0,3},{1,2},{2,1},{3,0},{4,7},{5,6},{6,5},{7,4},{8,11},{9,10},{10,... | collective-permute-start | bytes 387080 | tf_op jit(solution)/shard_map/ppermute | solution.py:427
  102.0 5.1 %collective-permute-start.18 = (bf16[3,1,1,24,896]{4,3,2,1,0:T(8,128)(2,1)S(1)}, bf16[3,1,1,24,896]{4,3,2,1,0:T(8,128)(2,1)S(1)}, u32[]{:S(2)}, u32[]{:S(2)}) collective-permute-start(bf16[3,1,1,24,896]{4,3,2,1,0:T(8,128)(2,1)S(1)} %slice.248), channel_id=1, source_target_pairs={{0,1},{1,0},{2,3},{3,2},{4,5},{5,4},{6,7},{7,6},{8,9},{9,8},{10,11... | collective-permute-start | bytes 387080 | tf_op jit(solution)/shard_map/ppermute | solution.py:427
  102.2 6.4 %collective-permute-start.25 = (bf16[3,1,1,24,896]{4,3,2,1,0:T(8,128)(2,1)S(1)}, bf16[3,1,1,24,896]{4,3,2,1,0:T(8,128)(2,1)S(1)}, u32[]{:S(2)}, u32[]{:S(2)}) collective-permute-start(bf16[3,1,1,24,896]{4,3,2,1,0:T(8,128)(2,1)S(1)} %slice.247), channel_id=1, source_target_pairs={{0,12},{1,13},{2,14},{3,15},{4,8},{5,9},{6,10},{7,11},{8,4},{9,5},... | collective-permute-start | bytes 387080 | tf_op jit(solution)/shard_map/ppermute | solution.py:427
  104.0 6.0 %collective-permute-start.32 = (bf16[3,1,1,24,896]{4,3,2,1,0:T(8,128)(2,1)S(1)}, bf16[3,1,1,24,896]{4,3,2,1,0:T(8,128)(2,1)S(1)}, u32[]{:S(2)}, u32[]{:S(2)}) collective-permute-start(bf16[3,1,1,24,896]{4,3,2,1,0:T(8,128)(2,1)S(1)} %slice.246), channel_id=1, source_target_pairs={{0,4},{1,5},{2,6},{3,7},{4,0},{5,1},{6,2},{7,3},{8,12},{9,13},{10,... | collective-permute-start | bytes 387080 | tf_op jit(solution)/shard_map/ppermute | solution.py:427
  105.1 6.7 %collective-permute-start.12 = (bf16[3,1,1,24,896]{4,3,2,1,0:T(8,128)(2,1)S(1)}, bf16[3,1,1,24,896]{4,3,2,1,0:T(8,128)(2,1)S(1)}, u32[]{:S(2)}, u32[]{:S(2)}) collective-permute-start(bf16[3,1,1,24,896]{4,3,2,1,0:T(8,128)(2,1)S(1)} %pad_maximum_fusion.8), channel_id=1, source_target_pairs={{0,3},{1,2},{2,1},{3,0},{4,7},{5,6},{6,5},{7,4},{8,11},{9,10},{10,... | collective-permute-start | bytes 387080 | tf_op jit(solution)/shard_map/ppermute | solution.py:427
  107.2 5.1 %collective-permute-start.19 = (bf16[3,1,1,24,896]{4,3,2,1,0:T(8,128)(2,1)S(1)}, bf16[3,1,1,24,896]{4,3,2,1,0:T(8,128)(2,1)S(1)}, u32[]{:S(2)}, u32[]{:S(2)}) collective-permute-start(bf16[3,1,1,24,896]{4,3,2,1,0:T(8,128)(2,1)S(1)} %pad_maximum_fusion.9), channel_id=1, source_target_pairs={{0,1},{1,0},{2,3},{3,2},{4,5},{5,4},{6,7},{7,6},{8,9},{9,8},{10,11... | collective-permute-start | bytes 387080 | tf_op jit(solution)/shard_map/ppermute | solution.py:427
  108.7 11.6 %collective-permute-start.26 = (bf16[3,1,1,24,896]{4,3,2,1,0:T(8,128)(2,1)S(1)}, bf16[3,1,1,24,896]{4,3,2,1,0:T(8,128)(2,1)S(1)}, u32[]{:S(2)}, u32[]{:S(2)}) collective-permute-start(bf16[3,1,1,24,896]{4,3,2,1,0:T(8,128)(2,1)S(1)} %pad_maximum_fusion.10), channel_id=1, source_target_pairs={{0,12},{1,13},{2,14},{3,15},{4,8},{5,9},{6,10},{7,11},{8,4},{9,5},... | collective-permute-start | bytes 387080 | tf_op jit(solution)/shard_map/ppermute | solution.py:427
  111.9 5.6 %collective-permute-start.13 = (bf16[3,1,2,24,896]{4,3,2,1,0:T(8,128)(2,1)S(1)}, bf16[3,1,2,24,896]{4,3,2,1,0:T(8,128)(2,1)S(1)}, u32[]{:S(2)}, u32[]{:S(2)}) collective-permute-start(bf16[3,1,2,24,896]{4,3,2,1,0:T(8,128)(2,1)S(1)} %pad_maximum_fusion.4), channel_id=1, source_target_pairs={{0,1},{1,0},{2,3},{3,2},{4,5},{5,4},{6,7},{7,6},{8,9},{9,8},{10,11... | collective-permute-start | bytes 774152 | tf_op jit(solution)/shard_map/ppermute | solution.py:427
  112.3 9.0 %collective-permute-start.33 = (bf16[3,1,1,24,896]{4,3,2,1,0:T(8,128)(2,1)S(1)}, bf16[3,1,1,24,896]{4,3,2,1,0:T(8,128)(2,1)S(1)}, u32[]{:S(2)}, u32[]{:S(2)}) collective-permute-start(bf16[3,1,1,24,896]{4,3,2,1,0:T(8,128)(2,1)S(1)} %pad_maximum_fusion.11), channel_id=1, source_target_pairs={{0,4},{1,5},{2,6},{3,7},{4,0},{5,1},{6,2},{7,3},{8,12},{9,13},{10,... | collective-permute-start | bytes 387080 | tf_op jit(solution)/shard_map/ppermute | solution.py:427
  112.4 9.6 %collective-permute-start.20 = (bf16[3,2,1,24,896]{4,3,2,1,0:T(8,128)(2,1)S(1)}, bf16[3,2,1,24,896]{4,3,2,1,0:T(8,128)(2,1)S(1)}, u32[]{:S(2)}, u32[]{:S(2)}) collective-permute-start(bf16[3,2,1,24,896]{4,3,2,1,0:T(8,128)(2,1)S(1)} %pad_maximum_fusion.5), channel_id=1, source_target_pairs={{0,3},{1,2},{2,1},{3,0},{4,7},{5,6},{6,5},{7,4},{8,11},{9,10},{10,... | collective-permute-start | bytes 774152 | tf_op jit(solution)/shard_map/ppermute | solution.py:427
  117.5 18.2 %collective-permute-start.39 = (bf16[3,96,896]{2,1,0:T(8,128)(2,1)S(1)}, bf16[3,96,896]{2,1,0:T(8,128)(2,1)S(1)}, u32[]{:S(2)}, u32[]{:S(2)}) collective-permute-start(bf16[3,96,896]{2,1,0:T(8,128)(2,1)S(1)} %bitcast.23), channel_id=1, source_target_pairs={{0,4},{1,5},{2,6},{3,7},{4,0},{5,1},{6,2},{7,3},{8,12},{9,13},{10,... | collective-permute-start | bytes 1548296 | tf_op jit(solution)/shard_map/ppermute | solution.py:427
  117.6 18.2 %collective-permute-start.35 = (bf16[3,96,896]{2,1,0:T(8,128)(2,1)S(1)}, bf16[3,96,896]{2,1,0:T(8,128)(2,1)S(1)}, u32[]{:S(2)}, u32[]{:S(2)}) collective-permute-start(bf16[3,96,896]{2,1,0:T(8,128)(2,1)S(1)} %bitcast.24), channel_id=1, source_target_pairs={{0,12},{1,13},{2,14},{3,15},{4,8},{5,9},{6,10},{7,11},{8,4},{9,5},... | collective-permute-start | bytes 1548296 | tf_op jit(solution)/shard_map/ppermute | solution.py:427
  120.4 9.8 %collective-permute-start.27 = (bf16[3,1,2,24,896]{4,3,2,1,0:T(8,128)(2,1)S(1)}, bf16[3,1,2,24,896]{4,3,2,1,0:T(8,128)(2,1)S(1)}, u32[]{:S(2)}, u32[]{:S(2)}) collective-permute-start(bf16[3,1,2,24,896]{4,3,2,1,0:T(8,128)(2,1)S(1)} %pad_maximum_fusion.6), channel_id=1, source_target_pairs={{0,4},{1,5},{2,6},{3,7},{4,0},{5,1},{6,2},{7,3},{8,12},{9,13},{10,... | collective-permute-start | bytes 774152 | tf_op jit(solution)/shard_map/ppermute | solution.py:427
  121.3 13.4 %collective-permute-start.34 = (bf16[3,2,1,24,896]{4,3,2,1,0:T(8,128)(2,1)S(1)}, bf16[3,2,1,24,896]{4,3,2,1,0:T(8,128)(2,1)S(1)}, u32[]{:S(2)}, u32[]{:S(2)}) collective-permute-start(bf16[3,2,1,24,896]{4,3,2,1,0:T(8,128)(2,1)S(1)} %pad_maximum_fusion.7), channel_id=1, source_target_pairs={{0,12},{1,13},{2,14},{3,15},{4,8},{5,9},{6,10},{7,11},{8,4},{9,5},... | collective-permute-start | bytes 774152 | tf_op jit(solution)/shard_map/ppermute | solution.py:427
  122.0 19.2 %collective-permute-start.40 = (bf16[3,96,896]{2,1,0:T(8,128)(2,1)S(1)}, bf16[3,96,896]{2,1,0:T(8,128)(2,1)S(1)}, u32[]{:S(2)}, u32[]{:S(2)}) collective-permute-start(bf16[3,96,896]{2,1,0:T(8,128)(2,1)S(1)} %bitcast.27), channel_id=1, source_target_pairs={{0,4},{1,5},{2,6},{3,7},{4,0},{5,1},{6,2},{7,3},{8,12},{9,13},{10,... | collective-permute-start | bytes 1548296 | tf_op jit(solution)/shard_map/ppermute | solution.py:427
  130.2 14.4 %collective-permute-start.36 = (bf16[3,96,896]{2,1,0:T(8,128)(2,1)S(1)}, bf16[3,96,896]{2,1,0:T(8,128)(2,1)S(1)}, u32[]{:S(2)}, u32[]{:S(2)}) collective-permute-start(bf16[3,96,896]{2,1,0:T(8,128)(2,1)S(1)} %bitcast.28), channel_id=1, source_target_pairs={{0,12},{1,13},{2,14},{3,15},{4,8},{5,9},{6,10},{7,11},{8,4},{9,5},... | collective-permute-start | bytes 1548296 | tf_op jit(solution)/shard_map/ppermute | solution.py:427
  134.7 10.6 %collective-permute-start.41 = (bf16[3,96,896]{2,1,0:T(8,128)(2,1)S(1)}, bf16[3,96,896]{2,1,0:T(8,128)(2,1)S(1)}, u32[]{:S(2)}, u32[]{:S(2)}) collective-permute-start(bf16[3,96,896]{2,1,0:T(8,128)(2,1)S(1)} %bitcast.31), channel_id=1, source_target_pairs={{0,1},{1,0},{2,3},{3,2},{4,5},{5,4},{6,7},{7,6},{8,9},{9,8},{10,11... | collective-permute-start | bytes 1548296 | tf_op jit(solution)/shard_map/ppermute | solution.py:427
  135.7 10.9 %collective-permute-start.37 = (bf16[3,96,896]{2,1,0:T(8,128)(2,1)S(1)}, bf16[3,96,896]{2,1,0:T(8,128)(2,1)S(1)}, u32[]{:S(2)}, u32[]{:S(2)}) collective-permute-start(bf16[3,96,896]{2,1,0:T(8,128)(2,1)S(1)} %bitcast.32), channel_id=1, source_target_pairs={{0,3},{1,2},{2,1},{3,0},{4,7},{5,6},{6,5},{7,4},{8,11},{9,10},{10,... | collective-permute-start | bytes 1548296 | tf_op jit(solution)/shard_map/ppermute | solution.py:427
  135.8 12.7 %collective-permute-start.42 = (bf16[3,96,896]{2,1,0:T(8,128)(2,1)S(1)}, bf16[3,96,896]{2,1,0:T(8,128)(2,1)S(1)}, u32[]{:S(2)}, u32[]{:S(2)}) collective-permute-start(bf16[3,96,896]{2,1,0:T(8,128)(2,1)S(1)} %bitcast.35), channel_id=1, source_target_pairs={{0,1},{1,0},{2,3},{3,2},{4,5},{5,4},{6,7},{7,6},{8,9},{9,8},{10,11... | collective-permute-start | bytes 1548296 | tf_op jit(solution)/shard_map/ppermute | solution.py:427
  141.2 9.5 %collective-permute-start.38 = (bf16[3,96,896]{2,1,0:T(8,128)(2,1)S(1)}, bf16[3,96,896]{2,1,0:T(8,128)(2,1)S(1)}, u32[]{:S(2)}, u32[]{:S(2)}) collective-permute-start(bf16[3,96,896]{2,1,0:T(8,128)(2,1)S(1)} %bitcast.36), channel_id=1, source_target_pairs={{0,3},{1,2},{2,1},{3,0},{4,7},{5,6},{6,5},{7,4},{8,11},{9,10},{10,... | collective-permute-start | bytes 1548296 | tf_op jit(solution)/shard_map/ppermute | solution.py:427
  144.5 13.9 %collective-permute-start.43 = (bf16[3,96,896]{2,1,0:T(8,128)(2,1)S(1)}, bf16[3,96,896]{2,1,0:T(8,128)(2,1)S(1)}, u32[]{:S(2)}, u32[]{:S(2)}) collective-permute-start(bf16[3,96,896]{2,1,0:T(8,128)(2,1)S(1)} %collective-permute-done.35.refs_4_), channel_id=1, source_target_pairs={{0,4},{1,5},{2,6},{3,7},{4,0},{5,1},{6,2},{7,3},{8,12},{9,13},{10,... | collective-permute-start | bytes 1548296 | tf_op jit(solution)/shard_map/ppermute | solution.py:427
  145.3 14.4 %collective-permute-start.44 = (bf16[3,96,896]{2,1,0:T(8,128)(2,1)S(1)}, bf16[3,96,896]{2,1,0:T(8,128)(2,1)S(1)}, u32[]{:S(2)}, u32[]{:S(2)}) collective-permute-start(bf16[3,96,896]{2,1,0:T(8,128)(2,1)S(1)} %collective-permute-done.40.refs_9_), channel_id=1, source_target_pairs={{0,12},{1,13},{2,14},{3,15},{4,8},{5,9},{6,10},{7,11},{8,4},{9,5},... | collective-permute-start | bytes 1548296 | tf_op jit(solution)/shard_map/ppermute | solution.py:427
  146.6 13.1 %collective-permute-start.45 = (bf16[3,96,896]{2,1,0:T(8,128)(2,1)S(1)}, bf16[3,96,896]{2,1,0:T(8,128)(2,1)S(1)}, u32[]{:S(2)}, u32[]{:S(2)}) collective-permute-start(bf16[3,96,896]{2,1,0:T(8,128)(2,1)S(1)} %collective-permute-done.37.refs_6_), channel_id=1, source_target_pairs={{0,1},{1,0},{2,3},{3,2},{4,5},{5,4},{6,7},{7,6},{8,9},{9,8},{10,11... | collective-permute-start | bytes 1548296 | tf_op jit(solution)/shard_map/ppermute | solution.py:427
  148.5 2.2 %copy-start.18 = (bf16[3,96,896]{2,1,0:T(8,128)(2,1)}, bf16[3,96,896]{2,1,0:T(8,128)(2,1)S(1)}, u32[]{:S(2)}) copy-start(bf16[3,96,896]{2,1,0:T(8,128)(2,1)S(1)} %collective-permute-done.42.refs_11_) | copy-start | bytes 1548292
  148.5 15.0 %collective-permute-start.46 = (bf16[3,96,896]{2,1,0:T(8,128)(2,1)S(1)}, bf16[3,96,896]{2,1,0:T(8,128)(2,1)S(1)}, u32[]{:S(2)}, u32[]{:S(2)}) collective-permute-start(bf16[3,96,896]{2,1,0:T(8,128)(2,1)S(1)} %collective-permute-done.42.refs_11_), channel_id=1, source_target_pairs={{0,3},{1,2},{2,1},{3,0},{4,7},{5,6},{6,5},{7,4},{8,11},{9,10},{10,... | collective-permute-start | bytes 1548296 | tf_op jit(solution)/shard_map/ppermute | solution.py:427
  150.7 12.8 %copy-start.1 = (bf16[1792,512]{1,0:T(8,128)(2,1)S(1)}, bf16[1792,512]{1,0:T(8,128)(2,1)}, u32[]{:S(2)}) copy-start(bf16[1792,512]{1,0:T(8,128)(2,1)} %copy-done) | copy-start | bytes 5505028
  158.5 7.4 %copy-start.7 = (bf16[3,96,896]{2,1,0:T(8,128)(2,1)}, bf16[3,96,896]{2,1,0:T(8,128)(2,1)S(1)}, u32[]{:S(2)}) copy-start(bf16[3,96,896]{2,1,0:T(8,128)(2,1)S(1)} %collective-permute-done.43.refs_0_.refs_12_) | copy-start | bytes 1548292
  159.6 6.3 %copy-start.8 = (bf16[3,96,896]{2,1,0:T(8,128)(2,1)}, bf16[3,96,896]{2,1,0:T(8,128)(2,1)S(1)}, u32[]{:S(2)}) copy-start(bf16[3,96,896]{2,1,0:T(8,128)(2,1)S(1)} %collective-permute-done.44.refs_1_.refs_13_) | copy-start | bytes 1548292
  159.6 6.3 %copy-start.9 = (bf16[3,96,896]{2,1,0:T(8,128)(2,1)}, bf16[3,96,896]{2,1,0:T(8,128)(2,1)S(1)}, u32[]{:S(2)}) copy-start(bf16[3,96,896]{2,1,0:T(8,128)(2,1)S(1)} %collective-permute-done.45.refs_2_.refs_14_) | copy-start | bytes 1548292
  163.5 2.4 %copy-start.10 = (bf16[3,96,896]{2,1,0:T(8,128)(2,1)}, bf16[3,96,896]{2,1,0:T(8,128)(2,1)S(1)}, u32[]{:S(2)}) copy-start(bf16[3,96,896]{2,1,0:T(8,128)(2,1)S(1)} %collective-permute-done.46.refs_3_.refs_15_) | copy-start | bytes 1548292
  166.0 23.3 %copy-start.14 = (s32[4,14]{1,0:T(4,128)S(1)}, s32[4,14]{1,0:T(4,128)}, u32[]{:S(2)}) copy-start(s32[4,14]{1,0:T(4,128)} %gm.3) | copy-start | bytes 676
  166.0 23.3 %copy-start.16 = (s32[4,14]{1,0:T(4,128)S(1)}, s32[4,14]{1,0:T(4,128)}, u32[]{:S(2)}) copy-start(s32[4,14]{1,0:T(4,128)} %um.3) | copy-start | bytes 676
  166.0 15.8 %collective-permute-start.47 = (bf16[4,128,512]{2,1,0:T(8,128)(2,1)S(1)}, bf16[4,128,512]{2,1,0:T(8,128)(2,1)S(1)}, u32[]{:S(2)}, u32[]{:S(2)}) collective-permute-start(bf16[4,128,512]{2,1,0:T(8,128)(2,1)S(1)} %get-tuple-element.58), channel_id=1, source_target_pairs={{0,16},{16,0},{32,48},{48,32},{64,80},{80,64},{96,112},{112,96},{1... | collective-permute-start | bytes 1572872 | tf_op jit(solution)/shard_map/ppermute | solution.py:492
  182.0 17.9 %collective-permute-start.48 = (bf16[128,512]{1,0:T(8,128)(2,1)S(1)}, bf16[128,512]{1,0:T(8,128)(2,1)S(1)}, u32[]{:S(2)}, u32[]{:S(2)}) collective-permute-start(bf16[128,512]{1,0:T(8,128)(2,1)S(1)} %get-tuple-element.64), channel_id=1, source_target_pairs={{0,32},{16,48},{32,64},{48,80},{64,96},{80,112},{96,0},{112,16},{1... | collective-permute-start | bytes 393224 | tf_op jit(solution)/shard_map/ppermute | solution.py:496
  186.8 13.0 %collective-permute-start.50 = (bf16[128,512]{1,0:T(8,128)(2,1)S(1)}, bf16[128,512]{1,0:T(8,128)(2,1)S(1)}, u32[]{:S(2)}, u32[]{:S(2)}) collective-permute-start(bf16[128,512]{1,0:T(8,128)(2,1)S(1)} %get-tuple-element.65), channel_id=1, source_target_pairs={{0,96},{16,112},{32,0},{48,16},{64,32},{80,48},{96,64},{112,80},{1... | collective-permute-start | bytes 393224 | tf_op jit(solution)/shard_map/ppermute | solution.py:496
  187.8 12.0 %collective-permute-start.49 = (bf16[128,512]{1,0:T(8,128)(2,1)S(1)}, bf16[128,512]{1,0:T(8,128)(2,1)S(1)}, u32[]{:S(2)}, u32[]{:S(2)}) collective-permute-start(bf16[128,512]{1,0:T(8,128)(2,1)S(1)} %get-tuple-element.66), channel_id=1, source_target_pairs={{0,64},{16,80},{32,96},{48,112},{64,0},{80,16},{96,32},{112,48},{1... | collective-permute-start | bytes 393224 | tf_op jit(solution)/shard_map/ppermute | solution.py:496
  (6 other events, 5.8 us)

commit v3 on v2

v3 whole, which is shorter than its diff:
```python
import functools

import jax
import jax.numpy as jnp
from jax import lax
from jax.experimental import pallas as pl
from jax.experimental.pallas import tpu as pltpu
from jax.sharding import PartitionSpec as P

BF = jnp.bfloat16
F32 = jnp.float32
LIVE = 768
PAD = 144
SIDE = 4
BLK = 128
PAIR = 2 * BLK
UNITS = 1792
HALF = UNITS // 2
STEPS = UNITS // PAIR
FEAT = 512
SLOTS = 1024
CUT = 96
VMEM = 48 << 20

MASKS = {"xA": (1, 0), "xB": (3, 0), "yA": (0, 1), "yB": (0, 3)}
ROUNDS = {
    (0, 0): (("xA", 0), ("xB", 1), ("yA", 2), ("yB", 3)),
    (0, 1): (("xB", 1), ("xA", 0), ("yB", 3), ("yA", 2)),
    (1, 0): (("yA", 0), ("yB", 1), ("xA", 2), ("xB", 3)),
    (1, 1): (("yB", 1), ("yA", 0), ("xB", 3), ("xA", 2)),
}
GROUPS = tuple(ROUNDS)


def partners(name):
    dx, dy = MASKS[name]
    return [
        (x * SIDE + y, (x ^ dx) * SIDE + (y ^ dy)) for x in range(SIDE) for y in range(SIDE)
    ]


def shift(dz, dc):
    return [
        (z * 2 + c, ((z + dz) % SIDE) * 2 + (c + dc) % 2) for z in range(SIDE) for c in range(2)
    ]


def logical_rows():
    place = lax.axis_index("dp")
    x, y = place // SIDE, place % SIDE

    def sides(v):
        high = v // 2
        return (v % 2) ^ high, high

    xa, xb = sides(x)
    ya, yb = sides(y)
    first = xa * 8 + xb * 4 + ya * 2 + yb
    second = ya * 8 + yb * 4 + xa * 2 + xb
    row = lax.iota(jnp.int32, LIVE)
    half, block, rest = row // 384, (row % 384) // 24, row % 24
    return half * 384 + (block ^ jnp.where(half > 0, second, first)) * 24 + rest


def kept(mask_ref, row, col, value):
    return jnp.where(mask_ref[row, col] > 0, value, jnp.zeros_like(value))


def smem():
    return pl.BlockSpec(memory_space=pltpu.SMEM)


def whole(shape):
    return pl.BlockSpec(shape, lambda j: (0,) * len(shape))


def call(kernel, name, flops, moved, **rest):
    return pl.pallas_call(
        kernel,
        compiler_params=pltpu.CompilerParams(vmem_limit_bytes=VMEM),
        cost_estimate=pl.CostEstimate(flops=flops, bytes_accessed=moved, transcendentals=0),
        name=name,
        **rest,
    )


def pack_kernel(tok_ref, cot_ref, count_ref, out_ref):
    out_ref[:BLK, :FEAT] = tok_ref[...]
    out_ref[:BLK, FEAT:] = cot_ref[...]
    count = jnp.full((PAD - BLK, 2 * FEAT), count_ref[0], jnp.int32)
    out_ref[BLK:, :] = count.astype(F32).astype(BF)


def pack(tokens, cotangent, counts):
    vmem = pl.BlockSpec(memory_space=pltpu.VMEM)
    return call(
        pack_kernel,
        "pack",
        0,
        1 << 19,
        out_shape=jax.ShapeDtypeStruct((PAD, 2 * FEAT), BF),
        in_specs=[vmem, vmem, smem()],
        out_specs=vmem,
    )(tokens, cotangent, counts)


def prepare_kernel(gm, um, dm, wg, wu, wd, wx_ref, wdt_ref, wd_ref):
    j = pl.program_id(0)
    for which, (mask, ref) in enumerate(((gm, wg), (um, wu))):
        for r in range(4):
            for b in range(2):
                at = slice(r * BLK, (r + 1) * BLK)
                to = b * PAIR + which * BLK
                wx_ref[0, at, to : to + BLK] = kept(
                    mask, r, 2 * j + b, ref[at, b * BLK : (b + 1) * BLK]
                )
    down = jnp.concatenate(
        [
            jnp.concatenate(
                [
                    kept(dm, 2 * j + b, c, wd[b * BLK : (b + 1) * BLK, c * BLK : (c + 1) * BLK])
                    for c in range(4)
                ],
                axis=1,
            )
            for b in range(2)
        ],
        axis=0,
    )
    wd_ref[...] = down
    wdt_ref[0] = down.T


def prepare(gm, um, dm, wg, wu, wd):
    return call(
        prepare_kernel,
        "prepare",
        0,
        13 << 20,
        grid=(STEPS,),
        out_shape=(
            jax.ShapeDtypeStruct((STEPS, FEAT, 2 * PAIR), BF),
            jax.ShapeDtypeStruct((STEPS, FEAT, PAIR), BF),
            jax.ShapeDtypeStruct((UNITS, FEAT), BF),
        ),
        in_specs=[
            smem(),
            smem(),
            smem(),
            pl.BlockSpec((FEAT, PAIR), lambda j: (0, j)),
            pl.BlockSpec((FEAT, PAIR), lambda j: (0, j)),
            pl.BlockSpec((PAIR, FEAT), lambda j: (j, 0)),
        ],
        out_specs=(
            pl.BlockSpec((1, FEAT, 2 * PAIR), lambda j: (j, 0, 0)),
            pl.BlockSpec((1, FEAT, PAIR), lambda j: (j, 0, 0)),
            pl.BlockSpec((PAIR, FEAT), lambda j: (j, 0)),
        ),
    )(gm, um, dm, wg, wu, wd)


def compact_kernel(shard, rows_ref, *refs):
    sources, (x_ref, g_ref, xt_ref, offs_ref, cnts_ref) = refs[:8], refs[8:]
    rows = rows_ref[...]
    slot = lax.broadcasted_iota(jnp.int32, (LIVE, BLK), 1)
    cnts = [ref[BLK : BLK + 1, 0:1].astype(F32).astype(jnp.int32) for ref in sources]
    total = None
    for pair in range(4):
        picks = []
        for k in (2 * pair, 2 * pair + 1):
            offset = jnp.zeros((1, 1), jnp.int32)
            for other in range(8):
                if other != k:
                    offset += jnp.where(shard[other] < shard[k], cnts[other], 0)
            offs_ref[k] = jnp.broadcast_to(offset, (8, BLK))
            cnts_ref[k] = jnp.broadcast_to(cnts[k], (8, BLK))
            hit = (rows - offset == slot) & (slot < cnts[k])
            picks.append(jnp.where(hit, 1.0, 0.0).astype(BF))
        source = jnp.concatenate(
            [sources[2 * pair][:BLK, :], sources[2 * pair + 1][:BLK, :]], axis=0
        )
        part = jnp.dot(jnp.concatenate(picks, axis=1), source, preferred_element_type=F32)
        total = part if total is None else total + part
    x_ref[...] = total[:, :FEAT].astype(BF)
    g_ref[...] = total[:, FEAT:].astype(BF)
    xt_ref[...] = total[:, :FEAT].T.astype(BF)


def compact(shard, rows, sources):
    vmem = pl.BlockSpec(memory_space=pltpu.VMEM)
    return call(
        compact_kernel,
        "compact",
        2 * LIVE * SLOTS * SLOTS,
        5 << 20,
        out_shape=(
            jax.ShapeDtypeStruct((LIVE, FEAT), BF),
            jax.ShapeDtypeStruct((LIVE, FEAT), BF),
            jax.ShapeDtypeStruct((FEAT, LIVE), BF),
            jax.ShapeDtypeStruct((8, 8, BLK), jnp.int32),
            jax.ShapeDtypeStruct((8, 8, BLK), jnp.int32),
        ),
        in_specs=[smem(), vmem] + [vmem] * 8,
        out_specs=(vmem,) * 5,
    )(shard, rows, *sources)


SENT = {0: (2, 3), 1: (1, 3)}
KEPT = {0: (0, 1), 1: (0, 2)}


def partial_kernel(pieces, x_ref, g_ref, wx_ref, wdt_ref, *refs):
    outs, (xs, gs) = refs[:4], refs[4:]

    @pl.when(pl.program_id(0) == 0)
    def _():
        for q in range(2):
            for h in range(2):
                for i, piece in enumerate(pieces[q]):
                    to, at = (h * 2 + i) * CUT, (h * 4 + piece) * CUT
                    xs[q, to : to + CUT, :] = x_ref[at : at + CUT, :]
                    gs[q, to : to + CUT, :] = g_ref[at : at + CUT, :]

    for q in range(2):
        both = jnp.dot(
            xs[q], wx_ref[0, :, q * PAIR : (q + 1) * PAIR], preferred_element_type=F32
        )
        back = jnp.dot(
            gs[q], wdt_ref[0, :, q * BLK : (q + 1) * BLK], preferred_element_type=F32
        )
        for which, result in enumerate((both[:, :BLK], both[:, BLK:], back)):
            for h in range(2):
                outs[h * 2 + q][which] = result[h * 2 * CUT : (h + 1) * 2 * CUT].astype(BF)


def partials(pieces, x, g, wx, wdt):
    count = 4 * CUT
    return call(
        functools.partial(partial_kernel, pieces),
        "partials",
        2 * count * FEAT * 3 * UNITS,
        7 << 20,
        grid=(STEPS,),
        out_shape=(jax.ShapeDtypeStruct((3, 2 * CUT, HALF), BF),) * 4,
        in_specs=[
            whole((LIVE, FEAT)),
            whole((LIVE, FEAT)),
            pl.BlockSpec((1, FEAT, 2 * PAIR), lambda j: (j, 0, 0)),
            pl.BlockSpec((1, FEAT, PAIR), lambda j: (j, 0, 0)),
        ],
        out_specs=(pl.BlockSpec((3, 2 * CUT, BLK), lambda j: (0, 0, j)),) * 4,
        scratch_shapes=[pltpu.VMEM((2, count, FEAT), BF)] * 2,
    )(x, g, wx, wdt)


def picked(rows, offs, cnts, k, slot):
    hit = (rows - offs[k, 0:1, 0:1] == slot) & (slot < cnts[k, 0:1, 0:1])
    return jnp.where(hit, 1.0, 0.0).astype(BF)


def products(sides, spare, w_down):
    shared = jnp.concatenate(
        [jnp.concatenate([sides[q][h][spare] for q in range(2)], axis=1) for h in range(2)],
        axis=0,
    )
    result = [jnp.dot(shared, w_down, preferred_element_type=F32)]
    for q in range(2):
        single = jnp.concatenate([sides[q][h][1 - spare] for h in range(2)], axis=0)
        result.append(
            jnp.dot(single, w_down[q * BLK : (q + 1) * BLK, :], preferred_element_type=F32)
        )
    return result


def cut(refs, columns):
    return [
        [[refs[h * 2 + q][0, i * CUT : (i + 1) * CUT, columns] for i in range(2)] for h in range(2)]
        for q in range(2)
    ]


def first_output_kernel(wd_ref, *refs):
    parts, total = refs[:4], refs[4]
    j = pl.program_id(0)
    results = products(cut(parts, slice(None)), 0, wd_ref[...])

    @pl.when(j == 0)
    def _():
        for i in range(3):
            total[i] = results[i]

    @pl.when(j > 0)
    def _():
        for i in range(3):
            total[i] += results[i]


def first_output(wd, parts):
    return call(
        first_output_kernel,
        "first_output",
        2 * 4 * CUT * FEAT * UNITS,
        5 << 20,
        grid=(STEPS,),
        out_shape=jax.ShapeDtypeStruct((3, 2 * CUT, FEAT), F32),
        in_specs=[pl.BlockSpec((PAIR, FEAT), lambda j: (j, 0))]
        + [pl.BlockSpec((1, 2 * CUT, BLK), lambda j: (2, 0, j))] * 4,
        out_specs=whole((3, 2 * CUT, FEAT)),
    )(wd, *parts)


def last_output_kernel(rows_ref, offs, cnts, early_ref, wd_ref, *refs):
    parts, (near_ref, away_ref) = refs[:4], refs[4:]
    totals = None
    for j in range(STEPS):
        results = products(
            cut(parts, slice(j * BLK, (j + 1) * BLK)), 1, wd_ref[j * PAIR : (j + 1) * PAIR, :]
        )
        totals = results if j == 0 else [a + b for a, b in zip(totals, results)]
    pieces = (early_ref[0], early_ref[1] + totals[2], early_ref[2] + totals[1], totals[0])
    mixed = jnp.concatenate([piece.astype(BF) for piece in pieces], axis=0)
    rows = rows_ref[0:1, :]
    slot = lax.broadcasted_iota(jnp.int32, (BLK, LIVE), 0)
    for k in range(8):
        pick = picked(rows, offs, cnts, k, slot)
        target = near_ref if k < 4 else away_ref
        target[k % 4] = jnp.dot(pick, mixed, preferred_element_type=F32).astype(BF)


def last_output(rows, offs, cnts, early, wd, parts):
    return call(
        last_output_kernel,
        "last_output",
        2 * LIVE * FEAT * (HALF + SLOTS),
        5 << 20,
        grid=(1,),
        out_shape=(jax.ShapeDtypeStruct((4, BLK, FEAT), BF),) * 2,
        in_specs=[
            whole((1, LIVE)),
            whole((8, 8, BLK)),
            whole((8, 8, BLK)),
            whole((3, 2 * CUT, FEAT)),
            whole((UNITS, FEAT)),
        ]
        + [pl.BlockSpec((1, 2 * CUT, HALF), lambda j: (2, 0, 0))] * 4,
        out_specs=(whole((4, BLK, FEAT)),) * 2,
    )(rows, offs, cnts, early, wd, *parts)


def all_rows(owns, comes, which):
    columns = []
    for q in range(2):
        pieces = []
        for h in range(2):
            own, come = owns[h * 2 + q], comes[h * 2 + q]
            if q == 0:
                pieces += [own[which], come[which]]
            else:
                pieces += [ref[which, i : i + CUT] for i in (0, CUT) for ref in (own, come)]
        columns.append(jnp.concatenate(pieces, axis=0))
    return jnp.concatenate(columns, axis=1)


def down_kernel(dm, g_ref, *refs):
    owns, comes, down_out = refs[:4], refs[4:8], refs[8]
    j = pl.program_id(0)
    down = lax.dot_general(
        all_rows(owns, comes, 0),
        g_ref[...],
        (((0,), (0,)), ((), ())),
        preferred_element_type=F32,
    )
    for r in range(4):
        for b in range(2):
            at, by = slice(r * BLK, (r + 1) * BLK), slice(b * BLK, (b + 1) * BLK)
            down_out[by, at] = kept(dm, 2 * j + b, r, down[by, at])


def down_gradient(dm, g, parts):
    return call(
        down_kernel,
        "down_gradient",
        2 * LIVE * FEAT * UNITS,
        8 << 20,
        grid=(STEPS,),
        out_shape=jax.ShapeDtypeStruct((UNITS, FEAT), F32),
        in_specs=[smem(), whole((LIVE, FEAT))]
        + [pl.BlockSpec((1, 2 * CUT, BLK), lambda j: (2, 0, j))] * 8,
        out_specs=pl.BlockSpec((PAIR, FEAT), lambda j: (j, 0)),
    )(dm, g, *parts)


def grad_kernel(gm, um, xt_ref, *refs):
    owns, comes, (gate_out, up_out) = refs[:4], refs[4:8], refs[8:]
    j = pl.program_id(0)
    xt = xt_ref[...]
    for which, mask, target in ((0, gm, gate_out), (1, um, up_out)):
        grad = jnp.dot(xt, all_rows(owns, comes, which), preferred_element_type=F32)
        for r in range(4):
            for b in range(2):
                at, by = slice(r * BLK, (r + 1) * BLK), slice(b * BLK, (b + 1) * BLK)
                target[at, by] = kept(mask, r, 2 * j + b, grad[at, by])


def gradients(gm, um, xt, parts):
    return call(
        grad_kernel,
        "gradients",
        2 * LIVE * FEAT * 2 * UNITS,
        13 << 20,
        grid=(STEPS,),
        out_shape=(jax.ShapeDtypeStruct((FEAT, UNITS), F32),) * 2,
        in_specs=[smem(), smem(), whole((FEAT, LIVE))]
        + [pl.BlockSpec((2, 2 * CUT, BLK), lambda j: (0, 0, j))] * 8,
        out_specs=(pl.BlockSpec((FEAT, PAIR), lambda j: (0, j)),) * 2,
    )(gm, um, xt, *parts)


def split(value, axis):
    lower = lax.slice_in_dim(value, 0, 1, axis=axis)
    upper = lax.slice_in_dim(value, 1, 2, axis=axis)
    return lower, upper


def activate(total):
    gate, upward, back = total[0], total[1], total[2]
    sigma = jax.nn.sigmoid(gate)
    active = gate * sigma
    hidden = (active * upward).astype(BF)
    d_gate = (back * upward * sigma * (1.0 + gate * (1.0 - sigma))).astype(BF)
    d_up = (back * active).astype(BF)
    return jnp.stack([d_gate, d_up, hidden])


def exchange(values, number):
    return {
        s: lax.ppermute(values[s], "dp", partners(ROUNDS[s][number][0])) for s in GROUPS
    }


def on_device(
    tokens, cotangent, gate_weight, up_weight, down_weight, gate_mask, up_mask, down_mask, counts
):
    live = (lax.iota(jnp.int32, tokens.shape[0]) < counts[0])[:, None]
    place = lax.axis_index("col")
    order = jnp.arange(8)
    shard = ((place // 2 + order % 4) % SIDE) * 2 + ((place % 2) ^ (order // 4))
    own = pack(tokens, cotangent, counts)
    column = [own] + [lax.ppermute(own, "col", shift(-dz, 0)) for dz in (1, 2, 3)]
    beside = [lax.ppermute(own, "col", shift(0, 1))]
    wx, wdt, wd = prepare(gate_mask, up_mask, down_mask, gate_weight, up_weight, down_weight)
    rows = logical_rows()
    place_rows = rows.reshape(2, 4, CUT).transpose(1, 0, 2).reshape(1, LIVE)
    *column, wx, wdt, wd, rows, place_rows, shard = lax.optimization_barrier(
        (*column, wx, wdt, wd, rows[:, None], place_rows, shard)
    )
    beside += [lax.ppermute(value, "col", shift(0, 1)) for value in column[1:]]
    x, g, xt, offs, cnts = compact(shard, rows, column + beside)

    sent = dict(zip(GROUPS, partials(SENT, x, g, wx, wdt)))
    come = exchange(sent, 0)
    x_rest, g_rest, *_ = lax.optimization_barrier((x, g, *sent.values()))
    keep = dict(zip(GROUPS, partials(KEPT, x_rest, g_rest, wx, wdt)))
    send = {}
    for s in GROUPS:
        total = (keep[s].astype(F32) + come[s].astype(F32)).reshape(3, 2, CUT, HALF)
        keep[s], upper = split(total, 1)
        send[s] = upper.astype(BF)
    come = exchange(send, 1)
    for s in GROUPS:
        total = (keep[s] + come[s].astype(F32)).reshape(3, 2, 2, 24, HALF)
        keep[s], upper = split(total, ROUNDS[s][2][1] - 1)
        send[s] = upper.astype(BF)
    come = exchange(send, 2)
    keep = {s: (keep[s] + come[s].astype(F32)).astype(BF) for s in GROUPS}
    come = exchange(keep, 3)
    held = {}
    for s in GROUPS:
        axis = ROUNDS[s][3][1] - 1
        lower, upper = split(come[s], axis)
        arrived = jnp.concatenate([upper, lower], axis=axis)
        held[s] = activate(keep[s].astype(F32) + arrived.astype(F32))
    come = exchange(held, 2)
    held = {
        s: jnp.concatenate([held[s], come[s]], axis=ROUNDS[s][2][1] - 1).reshape(3, CUT, HALF)
        for s in GROUPS
    }
    come = exchange(held, 1)
    held = {s: jnp.concatenate([held[s], come[s]], axis=1) for s in GROUPS}
    come = exchange(held, 0)
    owns, comes = [held[s] for s in GROUPS], [come[s] for s in GROUPS]

    begun = first_output(wd, owns)
    mine, away = last_output(place_rows, offs, cnts, begun, wd, comes)
    other = lax.ppermute(away, "col", shift(0, 1))
    down_grad = down_gradient(down_mask, g, owns + comes)
    other, down_grad = lax.optimization_barrier((other, down_grad))
    summed = mine.astype(F32) + other.astype(F32)
    terms = [summed[k].astype(BF) for k in range(4)]
    mixed = terms[0].astype(F32)
    for dz in (1, 2, 3):
        mixed += lax.ppermute(terms[dz], "col", shift(dz, 0)).astype(F32)
    output = jnp.where(live, mixed, jnp.zeros_like(mixed)).astype(BF)
    gate_grad, up_grad = gradients(gate_mask, up_mask, xt, owns + comes)
    return (output, gate_grad, up_grad, down_grad)


def solution(mesh):
    in_specs = (
        P("col", "dp"),
        P("col", "dp"),
        P("dp", "col"),
        P("dp", "col"),
        P("col", "dp"),
        P("dp", "col"),
        P("dp", "col"),
        P("col", "dp"),
        P("col"),
    )
    out_specs = (P("col", "dp"), P("dp", "col"), P("dp", "col"), P("col", "dp"))
    return jax.shard_map(
        on_device, mesh=mesh, in_specs=in_specs, out_specs=out_specs, check_vma=False
    )
```

time: 202 us -> 179 us (0.89)
  starting transfers between devices: 75.6 us -> 56 us
  waiting for transfers between devices: 67.7 us -> 56.5 us
  Pallas kernels: 42.8 us -> 48.9 us
    ppermute x3, waiting for transfers between devices: 9.26 us -> 0.15 us  [on_device(): lax.ppermute(own, 'col', shift(-dz, 0))]
    ppermute x40 -> x28, starting transfers between devices: 43.2 us -> 34.1 us  [exchange(): lax.ppermute(values[s], 'dp', partners(ROUNDS[s][number][0]))]
    pallas_call x5 -> x6, Pallas kernels: 33.6 us -> 39.7 us  [the longest x2 14.5 us: partials(): call(functools.partial(partial_kernel, pieces), 'partials', 2 * count * F...]
    ppermute x5, starting transfers between devices: 18.6 us -> 12.5 us  [the longest x1 9.67 us: on_device(): other = lax.ppermute(away, 'col', shift(0, 1))]
    ppermute x3, starting transfers between devices: 7.29 us -> 4.06 us  [on_device(): mixed += lax.ppermute(terms[dz], 'col', shift(dz, 0)).astype(F32)]
    ppermute x40 -> x28, waiting for transfers between devices: 56.9 us -> 54.8 us  [exchange(): lax.ppermute(values[s], 'dp', partners(ROUNDS[s][number][0]))]
    unnamed x39 -> x27, local copies, waits for them, and re-layouts: 8.12 us -> 8.91 us
  transfers between devices with their start and end apart: 51 -> 39, of which waited for: 18 -> 16; matrix products, arithmetic and copies ran while one was open for 2% -> 3% of each run, Pallas kernels for 16% -> 19%
where the time goes in v3:
time: 179 us; the launch traced here: 177 us
  waiting for transfers between devices  56.5 us (32%)
  starting transfers between devices  56 us (31%)
  Pallas kernels  48.9 us (27%)
  local copies, waits for them, and re-layouts  9.71 us (5%)
  other arithmetic  4.45 us (2%)
  between operations  1.85 us (1%)
    ppermute x28, waiting for transfers between devices, exchange(): lax.ppermute(values[s], 'dp', partners(ROUNDS[s][number][0]))  54.8 us
    ppermute x28, starting transfers between devices, exchange(): lax.ppermute(values[s], 'dp', partners(ROUNDS[s][number][0]))  34.1 us
    pallas_call x2, Pallas kernels, partials(): call(functools.partial(partial_kernel, pieces), 'partials', 2 * count * F...  14.5 us
    ppermute x1, starting transfers between devices, on_device(): other = lax.ppermute(away, 'col', shift(0, 1))  9.67 us
    unnamed x27, local copies, waits for them, and re-layouts  8.91 us
    pallas_call x1, Pallas kernels, gradients(): call(grad_kernel, 'gradients', 2 * LIVE * FEAT * 2 * UNITS, 13 << 20, gri...  8.59 us
    pallas_call x1, Pallas kernels, down_gradient(): call(down_kernel, 'down_gradient', 2 * LIVE * FEAT * UNITS, 8 << 20, grid...  6.59 us
    pallas_call x1, Pallas kernels, prepare(): call(prepare_kernel, 'prepare', 0, 13 << 20, grid=(STEPS,), out_shape=(ja...  6.55 us
  transfers between devices with their start and end apart: 39, of which 16 were waited for; matrix products, arithmetic and copies ran while one was open for 3% of the time, Pallas kernels for 19%

profile of v3, /device:TPU:1, one launch (start us, length us, event | category | flops | bytes accessed | tf_op | source)
XLA Modules:
  0.0 177.4 jit_solution(321263940757322483)
XLA Ops:
  1.3 0.9 copy-done.6
  2.2 0.9 copy-done.7
  3.1 4.7 %collective-permute-start = (bf16[144,1024]{1,0:T(8,128)(2,1)S(1)}, bf16[144,1024]{1,0:T(8,128)(2,1)S(1)}, u32[]{:S(2)}, u32[]{:S(2)}) collective-permute-start(bf16[144,1024]{1,0:T(8,128)(2,1)S(1)} %pack.1.refs_0_), channel_id=1, source_target_pairs={{0,96},{16,112},{32,0},{48,16},{64,32},{80,48},{96,64},{112,80},{1... | collective-permute-start | bytes 884744 | tf_op jit(solution)/shard_map/ppermute | solution.py:449
  7.8 0.7 collective-permute-start.2
  8.5 1.5 collective-permute-start.3
  10.1 0.8 copy.15.dm
  11.2 0.6 fusion.13.rows_ref
  11.8 1.5 copy-done.5
  13.3 0.7 copy-done.8
  14.0 0.7 copy-done.10
  14.6 6.6 %prepare.1 = (bf16[7,512,512]{2,1,0:T(8,128)(2,1)}, bf16[7,512,256]{2,1,0:T(8,128)(2,1)S(1)}, bf16[1792,512]{1,0:T(8,128)(2,1)S(1)}) custom-call(s32[4,14]{1,0:T(4,128)S(1)} %copy-done.8, s32[4,14]{1,0:T(4,128)S(1)} %copy-done.10, s32[14,4]{1,0:T(8,128)S(1)} %copy.15.dm, bf16[512,1792]{1,0:T(8,128)(2,1)S(1)} %copy-done.5, bf16[512,1792]{1,0:T(8,128)(2,1)} %wu.1, ...), custom_call_target="tpu_custom_call" | custom-call | bytes 13631488 | tf_op jit(solution)/shard_map/prepare/pallas_call | solution.py:135
  21.2 1.2 copy-done
  22.4 1.2 copy-done.12
  23.7 0.1 collective-permute-done.2.refs_3_
  23.9 0.8 collective-permute-start.4
  24.7 0.5 collective-permute-start.6
  25.2 0.7 collective-permute-done.4.refs_5_
  25.9 0.4 collective-permute-done.5.refs_6_
  26.4 0.4 collective-permute-done.6.refs_7_
  26.8 2.6 %compact.1 = (bf16[768,512]{1,0:T(8,128)(2,1)S(1)}, bf16[768,512]{1,0:T(8,128)(2,1)S(1)}, bf16[512,768]{1,0:T(8,128)(2,1)S(1)}, s32[8,8,128]{2,1,0:T(8,128)S(1)}, s32[8,8,128]{2,1,0:T(8,128)S(1)}) custom-call(s32[8]{0:T(128)S(1)} %fusion.36.shard, s32[768,1]{1,0:T(8,128)S(1)} %fusion.13.rows_ref, bf16[144,1024]{1,0:T(8,128)(2,1)S(1)} %pack.1.refs_0_, ...), custom_call_target="tpu_custom_call" | custom-call | flops 1610612736 | bytes 5242880 | tf_op jit(solution)/shard_map/compact/pallas_call | solution.py:191
  29.4 7.3 %partials.2 = (bf16[3,192,896]{2,1,0:T(8,128)(2,1)S(1)}, bf16[3,192,896]{2,1,0:T(8,128)(2,1)S(1)}, bf16[3,192,896]{2,1,0:T(8,128)(2,1)S(1)}, bf16[3,192,896]{2,1,0:T(8,128)(2,1)S(1)}) custom-call(bf16[768,512]{1,0:T(8,128)(2,1)S(1)} %get-tuple-element.59.x_ref, bf16[768,512]{1,0:T(8,128)(2,1)S(1)} %get-tuple-element.60.g_ref, ...), custom_call_target="tpu_custom_call" | custom-call | flops 2113929216 | bytes 7340032 | tf_op jit(solution)/shard_map/partials/pallas_call | solution.py:238
  36.6 2.6 %collective-permute-start.13 = (bf16[3,192,896]{2,1,0:T(8,128)(2,1)S(1)}, bf16[3,192,896]{2,1,0:T(8,128)(2,1)S(1)}, u32[]{:S(2)}, u32[]{:S(2)}) collective-permute-start(bf16[3,192,896]{2,1,0:T(8,128)(2,1)S(1)} %get-tuple-element.56), channel_id=1, source_target_pairs={{0,12},{1,13},{2,14},{3,15},{4,8},{5,9},{6,10},{7,11},{8,4},{9,5},... | collective-permute-start | bytes 3096584 | tf_op jit(solution)/shard_map/ppermute | solution.py:437
  39.2 2.7 %collective-permute-start.25 = (bf16[3,192,896]{2,1,0:T(8,128)(2,1)S(1)}, bf16[3,192,896]{2,1,0:T(8,128)(2,1)S(1)}, u32[]{:S(2)}, u32[]{:S(2)}) collective-permute-start(bf16[3,192,896]{2,1,0:T(8,128)(2,1)S(1)} %get-tuple-element.58), channel_id=1, source_target_pairs={{0,3},{1,2},{2,1},{3,0},{4,7},{5,6},{6,5},{7,4},{8,11},{9,10},{10,... | collective-permute-start | bytes 3096584 | tf_op jit(solution)/shard_map/ppermute | solution.py:437
  41.9 7.3 %partials.3 = (bf16[3,192,896]{2,1,0:T(8,128)(2,1)S(1)}, bf16[3,192,896]{2,1,0:T(8,128)(2,1)S(1)}, bf16[3,192,896]{2,1,0:T(8,128)(2,1)S(1)}, bf16[3,192,896]{2,1,0:T(8,128)(2,1)S(1)}) custom-call(bf16[768,512]{1,0:T(8,128)(2,1)S(1)} %get-tuple-element.59.x_ref, bf16[768,512]{1,0:T(8,128)(2,1)S(1)} %get-tuple-element.60.g_ref, ...), custom_call_target="tpu_custom_call" | custom-call | flops 2113929216 | bytes 7340032 | tf_op jit(solution)/shard_map/partials/pallas_call | solution.py:238
  49.2 12.7 %collective-permute-done.13 = bf16[3,192,896]{2,1,0:T(8,128)(2,1)S(1)} collective-permute-done((bf16[3,192,896]{2,1,0:T(8,128)(2,1)S(1)}, bf16[3,192,896]{2,1,0:T(8,128)(2,1)S(1)}, u32[]{:S(2)}, u32[]{:S(2)}) %collective-permute-start.13) | collective-permute-done | bytes 1032224 | tf_op jit(solution)/shard_map/ppermute | solution.py:437
  61.9 1.0 collective-permute-done.7
  62.9 0.4 convert_add_fusion.2
  63.4 1.6 collective-permute-start.8
  65.2 0.4 convert_add_fusion
  65.6 2.8 %collective-permute-start.20 = (bf16[3,1,96,896]{3,2,1,0:T(8,128)(2,1)S(1)}, bf16[3,1,96,896]{3,2,1,0:T(8,128)(2,1)S(1)}, u32[]{:S(2)}, u32[]{:S(2)}) collective-permute-start(bf16[3,1,96,896]{3,2,1,0:T(8,128)(2,1)S(1)} %slice.283), channel_id=1, source_target_pairs={{0,3},{1,2},{2,1},{3,0},{4,7},{5,6},{6,5},{7,4},{8,11},{9,10},{10,... | collective-permute-start | bytes 1548296 | tf_op jit(solution)/shard_map/ppermute | solution.py:437
  68.6 7.8 %collective-permute-done.8 = bf16[3,1,96,896]{3,2,1,0:T(8,128)(2,1)S(1)} collective-permute-done((bf16[3,1,96,896]{3,2,1,0:T(8,128)(2,1)S(1)}, bf16[3,1,96,896]{3,2,1,0:T(8,128)(2,1)S(1)}, u32[]{:S(2)}, u32[]{:S(2)}) %collective-permute-start.8) | collective-permute-done | bytes 516128 | tf_op jit(solution)/shard_map/ppermute | solution.py:437
  76.5 1.4 collective-permute-start.9
  78.0 2.0 %collective-permute-start.15 = (bf16[3,2,1,24,896]{4,3,2,1,0:T(8,128)(2,1)S(1)}, bf16[3,2,1,24,896]{4,3,2,1,0:T(8,128)(2,1)S(1)}, u32[]{:S(2)}, u32[]{:S(2)}) collective-permute-start(bf16[3,2,1,24,896]{4,3,2,1,0:T(8,128)(2,1)S(1)} %slice.288), channel_id=1, source_target_pairs={{0,3},{1,2},{2,1},{3,0},{4,7},{5,6},{6,5},{7,4},{8,11},{9,10},{10,... | collective-permute-start | bytes 774152 | tf_op jit(solution)/shard_map/ppermute | solution.py:437
  80.1 0.2 collective-permute-start.21
  80.5 1.9 %collective-permute-start.27 = (bf16[3,2,1,24,896]{4,3,2,1,0:T(8,128)(2,1)S(1)}, bf16[3,2,1,24,896]{4,3,2,1,0:T(8,128)(2,1)S(1)}, u32[]{:S(2)}, u32[]{:S(2)}) collective-permute-start(bf16[3,2,1,24,896]{4,3,2,1,0:T(8,128)(2,1)S(1)} %slice.286), channel_id=1, source_target_pairs={{0,12},{1,13},{2,14},{3,15},{4,8},{5,9},{6,10},{7,11},{8,4},{9,5},... | collective-permute-start | bytes 774152 | tf_op jit(solution)/shard_map/ppermute | solution.py:437
  82.3 3.3 %collective-permute-done.9 = bf16[3,1,2,24,896]{4,3,2,1,0:T(8,128)(2,1)S(1)} collective-permute-done((bf16[3,1,2,24,896]{4,3,2,1,0:T(8,128)(2,1)S(1)}, bf16[3,1,2,24,896]{4,3,2,1,0:T(8,128)(2,1)S(1)}, u32[]{:S(2)}, u32[]{:S(2)}) %collective-permute-start.9) | collective-permute-done | bytes 258080 | tf_op jit(solution)/shard_map/ppermute | solution.py:437
  85.8 0.9 collective-permute-start.16
  86.7 1.3 collective-permute-start.22
  88.2 4.2 %collective-permute-done.10 = bf16[3,1,2,24,896]{4,3,2,1,0:T(8,128)(2,1)S(1)} collective-permute-done((bf16[3,1,2,24,896]{4,3,2,1,0:T(8,128)(2,1)S(1)}, bf16[3,1,2,24,896]{4,3,2,1,0:T(8,128)(2,1)S(1)}, u32[]{:S(2)}, u32[]{:S(2)}) %collective-permute-start.10) | collective-permute-done | bytes 258080 | tf_op jit(solution)/shard_map/ppermute | solution.py:437
  93.0 1.5 collective-permute-start.17
  94.5 1.6 collective-permute-done.22
  96.7 1.5 collective-permute-done.11
  98.3 1.3 collective-permute-start.12
  99.6 1.6 collective-permute-start.29
  101.3 1.9 %collective-permute-done.23 = bf16[3,1,2,24,896]{4,3,2,1,0:T(8,128)(2,1)S(1)} collective-permute-done((bf16[3,1,2,24,896]{4,3,2,1,0:T(8,128)(2,1)S(1)}, bf16[3,1,2,24,896]{4,3,2,1,0:T(8,128)(2,1)S(1)}, u32[]{:S(2)}, u32[]{:S(2)}) %collective-permute-start.23) | collective-permute-done | bytes 258080 | tf_op jit(solution)/shard_map/ppermute | solution.py:437
  103.3 1.0 collective-permute-start.24
  104.3 8.6 %collective-permute-done.29 = bf16[3,2,1,24,896]{4,3,2,1,0:T(8,128)(2,1)S(1)} collective-permute-done((bf16[3,2,1,24,896]{4,3,2,1,0:T(8,128)(2,1)S(1)}, bf16[3,2,1,24,896]{4,3,2,1,0:T(8,128)(2,1)S(1)}, u32[]{:S(2)}, u32[]{:S(2)}) %collective-permute-start.29) | collective-permute-done | bytes 258080 | tf_op jit(solution)/shard_map/ppermute | solution.py:437
  113.0 1.0 collective-permute-start.30
  114.3 1.4 collective-permute-start.32
  115.8 0.7 collective-permute-start.33
  116.5 4.5 %collective-permute-done.30 = bf16[3,96,896]{2,1,0:T(8,128)(2,1)S(1)} collective-permute-done((bf16[3,96,896]{2,1,0:T(8,128)(2,1)S(1)}, bf16[3,96,896]{2,1,0:T(8,128)(2,1)S(1)}, u32[]{:S(2)}, u32[]{:S(2)}) %collective-permute-start.30) | collective-permute-done | bytes 516128 | tf_op jit(solution)/shard_map/ppermute | solution.py:437
  121.1 7.7 %collective-permute-start.34 = (bf16[3,192,896]{2,1,0:T(8,128)(2,1)S(1)}, bf16[3,192,896]{2,1,0:T(8,128)(2,1)S(1)}, u32[]{:S(2)}, u32[]{:S(2)}) collective-permute-start(bf16[3,192,896]{2,1,0:T(8,128)(2,1)S(1)} %pad_maximum_fusion.3.refs_3_), channel_id=1, source_target_pairs={{0,3},{1,2},{2,1},{3,0},{4,7},{5,6},{6,5},{7,4},{8,11},{9,10},{10,... | collective-permute-start | bytes 3096584 | tf_op jit(solution)/shard_map/ppermute | solution.py:437
  128.8 5.5 %first_output.1.early_ref = f32[3,192,512]{2,1,0:T(8,128)S(1)} custom-call(bf16[1792,512]{1,0:T(8,128)(2,1)} %copy-done, bf16[3,192,896]{2,1,0:T(8,128)(2,1)S(1)} %pad_maximum_fusion.refs_0_, bf16[3,192,896]{2,1,0:T(8,128)(2,1)S(1)} %pad_maximum_fusion.1.refs_1_, bf16[3,192,896]{2,1,0:T(8,128)(2,1)S(1)} %pad_maximum_fusion.2.refs_2_, ...), custom_call_target="tpu_custom_call" | custom-call | flops 704643072 | bytes 5242880 | tf_op jit(solution)/shard_map/first_output/pallas_call | solution.py:299
  134.4 1.0 copy-done.1
  135.4 6.2 %collective-permute-done.33.refs_2_.refs_6_ = bf16[3,192,896]{2,1,0:T(8,128)(2,1)S(1)} collective-permute-done((bf16[3,192,896]{2,1,0:T(8,128)(2,1)S(1)}, bf16[3,192,896]{2,1,0:T(8,128)(2,1)S(1)}, u32[]{:S(2)}, u32[]{:S(2)}) %collective-permute-start.33) | collective-permute-done | bytes 1032224 | tf_op jit(solution)/shard_map/ppermute | solution.py:437
  141.6 1.5 collective-permute-done.34.refs_3_.refs_7_
  143.0 4.5 %last_output.1 = (bf16[4,128,512]{2,1,0:T(8,128)(2,1)S(1)}, bf16[4,128,512]{2,1,0:T(8,128)(2,1)S(1)}) custom-call(s32[1,768]{1,0:T(1,128)S(1)} %fusion.32.rows_ref, s32[8,8,128]{2,1,0:T(8,128)S(1)} %get-tuple-element.48.offs, s32[8,8,128]{2,1,0:T(8,128)S(1)} %get-tuple-element.49.cnts, f32[3,192,512]{2,1,0:T(8,128)} %copy-done.1, bf16[1792,512]{1,0:T(8,128)(2,1)} %copy-done, ...), custom_call_target="tpu_custom_call" | custom-call | flops 1509949440 | bytes 5242880 | tf_op jit(solution)/shard_map/last_output/pallas_call | solution.py:331
  147.6 9.7 %collective-permute-start.35 = (bf16[4,128,512]{2,1,0:T(8,128)(2,1)S(1)}, bf16[4,128,512]{2,1,0:T(8,128)(2,1)S(1)}, u32[]{:S(2)}, u32[]{:S(2)}) collective-permute-start(bf16[4,128,512]{2,1,0:T(8,128)(2,1)S(1)} %get-tuple-element.66), channel_id=1, source_target_pairs={{0,16},{16,0},{32,48},{48,32},{64,80},{80,64},{96,112},{112,96},{1... | collective-permute-start | bytes 1572872 | tf_op jit(solution)/shard_map/ppermute | solution.py:495
  157.2 6.6 %down_gradient.1 = f32[1792,512]{1,0:T(8,128)} custom-call(s32[14,4]{1,0:T(8,128)S(1)} %copy.15.dm, bf16[768,512]{1,0:T(8,128)(2,1)S(1)} %get-tuple-element.60.g_ref, bf16[3,192,896]{2,1,0:T(8,128)(2,1)S(1)} %pad_maximum_fusion.refs_0_, bf16[3,192,896]{2,1,0:T(8,128)(2,1)S(1)} %pad_maximum_fusion.1.refs_1_, ...), custom_call_target="tpu_custom_call" | custom-call | flops 1409286144 | bytes 8388608 | tf_op jit(solution)/shard_map/down_gradient/pallas_call | solution.py:380
  163.8 0.1 add_convert_fusion
  164.0 2.0 %collective-permute-start.38 = (bf16[128,512]{1,0:T(8,128)(2,1)S(1)}, bf16[128,512]{1,0:T(8,128)(2,1)S(1)}, u32[]{:S(2)}, u32[]{:S(2)}) collective-permute-start(bf16[128,512]{1,0:T(8,128)(2,1)S(1)} %get-tuple-element.73), channel_id=1, source_target_pairs={{0,96},{16,112},{32,0},{48,16},{64,32},{80,48},{96,64},{112,80},{1... | collective-permute-start | bytes 393224 | tf_op jit(solution)/shard_map/ppermute | solution.py:502
  166.0 2.0 %collective-permute-start.37 = (bf16[128,512]{1,0:T(8,128)(2,1)S(1)}, bf16[128,512]{1,0:T(8,128)(2,1)S(1)}, u32[]{:S(2)}, u32[]{:S(2)}) collective-permute-start(bf16[128,512]{1,0:T(8,128)(2,1)S(1)} %get-tuple-element.74), channel_id=1, source_target_pairs={{0,64},{16,80},{32,96},{48,112},{64,0},{80,16},{96,32},{112,48},{1... | collective-permute-start | bytes 393224 | tf_op jit(solution)/shard_map/ppermute | solution.py:502
  168.1 8.6 %gradients.1 = (f32[512,1792]{1,0:T(8,128)}, f32[512,1792]{1,0:T(8,128)}) custom-call(s32[4,14]{1,0:T(4,128)S(1)} %copy-done.9, s32[4,14]{1,0:T(4,128)S(1)} %copy-done.11, bf16[512,768]{1,0:T(8,128)(2,1)S(1)} %get-tuple-element.68.xt_ref, bf16[3,192,896]{2,1,0:T(8,128)(2,1)S(1)} %pad_maximum_fusion.refs_0_, ...), custom_call_target="tpu_custom_call" | custom-call | flops 2818572288 | bytes 13631488 | tf_op jit(solution)/shard_map/gradients/pallas_call | solution.py:406
  176.7 0.7 fusion.27
  (107 shorter events, 3.8 us)
Async XLA Ops:
  1.3 0.9 copy-start.6
  2.2 0.9 copy-start.7
  3.1 20.6 %collective-permute-start = (bf16[144,1024]{1,0:T(8,128)(2,1)S(1)}, bf16[144,1024]{1,0:T(8,128)(2,1)S(1)}, u32[]{:S(2)}, u32[]{:S(2)}) collective-permute-start(bf16[144,1024]{1,0:T(8,128)(2,1)S(1)} %pack.1.refs_0_), channel_id=1, source_target_pairs={{0,96},{16,112},{32,0},{48,16},{64,32},{80,48},{96,64},{112,80},{1... | collective-permute-start | bytes 884744 | tf_op jit(solution)/shard_map/ppermute | solution.py:449
  7.8 16.0 %collective-permute-start.1 = (bf16[144,1024]{1,0:T(8,128)(2,1)S(1)}, bf16[144,1024]{1,0:T(8,128)(2,1)S(1)}, u32[]{:S(2)}, u32[]{:S(2)}) collective-permute-start(bf16[144,1024]{1,0:T(8,128)(2,1)S(1)} %pack.1.refs_0_), channel_id=1, source_target_pairs={{0,64},{16,80},{32,96},{48,112},{64,0},{80,16},{96,32},{112,48},{1... | collective-permute-start | bytes 884744 | tf_op jit(solution)/shard_map/ppermute | solution.py:449
  7.8 16.1 %collective-permute-start.2 = (bf16[144,1024]{1,0:T(8,128)(2,1)S(1)}, bf16[144,1024]{1,0:T(8,128)(2,1)S(1)}, u32[]{:S(2)}, u32[]{:S(2)}) collective-permute-start(bf16[144,1024]{1,0:T(8,128)(2,1)S(1)} %pack.1.refs_0_), channel_id=1, source_target_pairs={{0,32},{16,48},{32,64},{48,80},{64,96},{80,112},{96,0},{112,16},{1... | collective-permute-start | bytes 884744 | tf_op jit(solution)/shard_map/ppermute | solution.py:449
  8.5 16.8 %collective-permute-start.3 = (bf16[144,1024]{1,0:T(8,128)(2,1)S(1)}, bf16[144,1024]{1,0:T(8,128)(2,1)S(1)}, u32[]{:S(2)}, u32[]{:S(2)}) collective-permute-start(bf16[144,1024]{1,0:T(8,128)(2,1)S(1)} %pack.1.refs_0_), channel_id=1, source_target_pairs={{0,16},{16,0},{32,48},{48,32},{64,80},{80,64},{96,112},{112,96},{1... | collective-permute-start | bytes 884744 | tf_op jit(solution)/shard_map/ppermute | solution.py:450
  11.8 1.5 copy-start.5
  13.3 0.7 copy-start.8
  14.0 0.7 copy-start.10
  21.2 1.2 copy-start
  22.4 1.2 copy-start.12
  23.9 2.0 %collective-permute-start.4 = (bf16[144,1024]{1,0:T(8,128)(2,1)S(1)}, bf16[144,1024]{1,0:T(8,128)(2,1)S(1)}, u32[]{:S(2)}, u32[]{:S(2)}) collective-permute-start(bf16[144,1024]{1,0:T(8,128)(2,1)S(1)} %collective-permute-done.refs_1_), channel_id=1, source_target_pairs={{0,16},{16,0},{32,48},{48,32},{64,80},{80,64},{96,112},{112,96},{1... | collective-permute-start | bytes 884744 | tf_op jit(solution)/shard_map/ppermute | solution.py:457
  24.7 1.6 collective-permute-start.5
  24.7 2.0 %collective-permute-start.6 = (bf16[144,1024]{1,0:T(8,128)(2,1)S(1)}, bf16[144,1024]{1,0:T(8,128)(2,1)S(1)}, u32[]{:S(2)}, u32[]{:S(2)}) collective-permute-start(bf16[144,1024]{1,0:T(8,128)(2,1)S(1)} %collective-permute-done.2.refs_3_), channel_id=1, source_target_pairs={{0,16},{16,0},{32,48},{48,32},{64,80},{80,64},{96,112},{112,96},{1... | collective-permute-start | bytes 884744 | tf_op jit(solution)/shard_map/ppermute | solution.py:457
  36.6 25.3 %collective-permute-start.13 = (bf16[3,192,896]{2,1,0:T(8,128)(2,1)S(1)}, bf16[3,192,896]{2,1,0:T(8,128)(2,1)S(1)}, u32[]{:S(2)}, u32[]{:S(2)}) collective-permute-start(bf16[3,192,896]{2,1,0:T(8,128)(2,1)S(1)} %get-tuple-element.56), channel_id=1, source_target_pairs={{0,12},{1,13},{2,14},{3,15},{4,8},{5,9},{6,10},{7,11},{8,4},{9,5},... | collective-permute-start | bytes 3096584 | tf_op jit(solution)/shard_map/ppermute | solution.py:437
  39.2 23.7 %collective-permute-start.7 = (bf16[3,192,896]{2,1,0:T(8,128)(2,1)S(1)}, bf16[3,192,896]{2,1,0:T(8,128)(2,1)S(1)}, u32[]{:S(2)}, u32[]{:S(2)}) collective-permute-start(bf16[3,192,896]{2,1,0:T(8,128)(2,1)S(1)} %get-tuple-element.55), channel_id=1, source_target_pairs={{0,4},{1,5},{2,6},{3,7},{4,0},{5,1},{6,2},{7,3},{8,12},{9,13},{10,... | collective-permute-start | bytes 3096584 | tf_op jit(solution)/shard_map/ppermute | solution.py:437
  39.2 25.9 %collective-permute-start.25 = (bf16[3,192,896]{2,1,0:T(8,128)(2,1)S(1)}, bf16[3,192,896]{2,1,0:T(8,128)(2,1)S(1)}, u32[]{:S(2)}, u32[]{:S(2)}) collective-permute-start(bf16[3,192,896]{2,1,0:T(8,128)(2,1)S(1)} %get-tuple-element.58), channel_id=1, source_target_pairs={{0,3},{1,2},{2,1},{3,0},{4,7},{5,6},{6,5},{7,4},{8,11},{9,10},{10,... | collective-permute-start | bytes 3096584 | tf_op jit(solution)/shard_map/ppermute | solution.py:437
  41.9 23.2 %collective-permute-start.19 = (bf16[3,192,896]{2,1,0:T(8,128)(2,1)S(1)}, bf16[3,192,896]{2,1,0:T(8,128)(2,1)S(1)}, u32[]{:S(2)}, u32[]{:S(2)}) collective-permute-start(bf16[3,192,896]{2,1,0:T(8,128)(2,1)S(1)} %get-tuple-element.57), channel_id=1, source_target_pairs={{0,1},{1,0},{2,3},{3,2},{4,5},{5,4},{6,7},{7,6},{8,9},{9,8},{10,11... | collective-permute-start | bytes 3096584 | tf_op jit(solution)/shard_map/ppermute | solution.py:437
  63.4 13.0 %collective-permute-start.8 = (bf16[3,1,96,896]{3,2,1,0:T(8,128)(2,1)S(1)}, bf16[3,1,96,896]{3,2,1,0:T(8,128)(2,1)S(1)}, u32[]{:S(2)}, u32[]{:S(2)}) collective-permute-start(bf16[3,1,96,896]{3,2,1,0:T(8,128)(2,1)S(1)} %slice.285), channel_id=1, source_target_pairs={{0,12},{1,13},{2,14},{3,15},{4,8},{5,9},{6,10},{7,11},{8,4},{9,5},... | collective-permute-start | bytes 1548296 | tf_op jit(solution)/shard_map/ppermute | solution.py:437
  65.0 12.9 %collective-permute-start.14 = (bf16[3,1,96,896]{3,2,1,0:T(8,128)(2,1)S(1)}, bf16[3,1,96,896]{3,2,1,0:T(8,128)(2,1)S(1)}, u32[]{:S(2)}, u32[]{:S(2)}) collective-permute-start(bf16[3,1,96,896]{3,2,1,0:T(8,128)(2,1)S(1)} %slice.284), channel_id=1, source_target_pairs={{0,4},{1,5},{2,6},{3,7},{4,0},{5,1},{6,2},{7,3},{8,12},{9,13},{10,... | collective-permute-start | bytes 1548296 | tf_op jit(solution)/shard_map/ppermute | solution.py:437
  65.6 14.4 %collective-permute-start.20 = (bf16[3,1,96,896]{3,2,1,0:T(8,128)(2,1)S(1)}, bf16[3,1,96,896]{3,2,1,0:T(8,128)(2,1)S(1)}, u32[]{:S(2)}, u32[]{:S(2)}) collective-permute-start(bf16[3,1,96,896]{3,2,1,0:T(8,128)(2,1)S(1)} %slice.283), channel_id=1, source_target_pairs={{0,3},{1,2},{2,1},{3,0},{4,7},{5,6},{6,5},{7,4},{8,11},{9,10},{10,... | collective-permute-start | bytes 1548296 | tf_op jit(solution)/shard_map/ppermute | solution.py:437
  68.5 11.8 %collective-permute-start.26 = (bf16[3,1,96,896]{3,2,1,0:T(8,128)(2,1)S(1)}, bf16[3,1,96,896]{3,2,1,0:T(8,128)(2,1)S(1)}, u32[]{:S(2)}, u32[]{:S(2)}) collective-permute-start(bf16[3,1,96,896]{3,2,1,0:T(8,128)(2,1)S(1)} %slice.282), channel_id=1, source_target_pairs={{0,1},{1,0},{2,3},{3,2},{4,5},{5,4},{6,7},{7,6},{8,9},{9,8},{10,11... | collective-permute-start | bytes 1548296 | tf_op jit(solution)/shard_map/ppermute | solution.py:437
  76.5 9.1 %collective-permute-start.9 = (bf16[3,1,2,24,896]{4,3,2,1,0:T(8,128)(2,1)S(1)}, bf16[3,1,2,24,896]{4,3,2,1,0:T(8,128)(2,1)S(1)}, u32[]{:S(2)}, u32[]{:S(2)}) collective-permute-start(bf16[3,1,2,24,896]{4,3,2,1,0:T(8,128)(2,1)S(1)} %slice.289), channel_id=1, source_target_pairs={{0,1},{1,0},{2,3},{3,2},{4,5},{5,4},{6,7},{7,6},{8,9},{9,8},{10,11... | collective-permute-start | bytes 774152 | tf_op jit(solution)/shard_map/ppermute | solution.py:437
  78.0 7.7 %collective-permute-start.15 = (bf16[3,2,1,24,896]{4,3,2,1,0:T(8,128)(2,1)S(1)}, bf16[3,2,1,24,896]{4,3,2,1,0:T(8,128)(2,1)S(1)}, u32[]{:S(2)}, u32[]{:S(2)}) collective-permute-start(bf16[3,2,1,24,896]{4,3,2,1,0:T(8,128)(2,1)S(1)} %slice.288), channel_id=1, source_target_pairs={{0,3},{1,2},{2,1},{3,0},{4,7},{5,6},{6,5},{7,4},{8,11},{9,10},{10,... | collective-permute-start | bytes 774152 | tf_op jit(solution)/shard_map/ppermute | solution.py:437
  80.1 6.5 %collective-permute-start.21 = (bf16[3,1,2,24,896]{4,3,2,1,0:T(8,128)(2,1)S(1)}, bf16[3,1,2,24,896]{4,3,2,1,0:T(8,128)(2,1)S(1)}, u32[]{:S(2)}, u32[]{:S(2)}) collective-permute-start(bf16[3,1,2,24,896]{4,3,2,1,0:T(8,128)(2,1)S(1)} %slice.287), channel_id=1, source_target_pairs={{0,4},{1,5},{2,6},{3,7},{4,0},{5,1},{6,2},{7,3},{8,12},{9,13},{10,... | collective-permute-start | bytes 774152 | tf_op jit(solution)/shard_map/ppermute | solution.py:437
  80.5 7.6 %collective-permute-start.27 = (bf16[3,2,1,24,896]{4,3,2,1,0:T(8,128)(2,1)S(1)}, bf16[3,2,1,24,896]{4,3,2,1,0:T(8,128)(2,1)S(1)}, u32[]{:S(2)}, u32[]{:S(2)}) collective-permute-start(bf16[3,2,1,24,896]{4,3,2,1,0:T(8,128)(2,1)S(1)} %slice.286), channel_id=1, source_target_pairs={{0,12},{1,13},{2,14},{3,15},{4,8},{5,9},{6,10},{7,11},{8,4},{9,5},... | collective-permute-start | bytes 774152 | tf_op jit(solution)/shard_map/ppermute | solution.py:437
  85.7 6.8 %collective-permute-start.10 = (bf16[3,1,2,24,896]{4,3,2,1,0:T(8,128)(2,1)S(1)}, bf16[3,1,2,24,896]{4,3,2,1,0:T(8,128)(2,1)S(1)}, u32[]{:S(2)}, u32[]{:S(2)}) collective-permute-start(bf16[3,1,2,24,896]{4,3,2,1,0:T(8,128)(2,1)S(1)} %fusion.7), channel_id=1, source_target_pairs={{0,3},{1,2},{2,1},{3,0},{4,7},{5,6},{6,5},{7,4},{8,11},{9,10},{10,... | collective-permute-start | bytes 774152 | tf_op jit(solution)/shard_map/ppermute | solution.py:437
  85.8 6.9 %collective-permute-start.16 = (bf16[3,2,1,24,896]{4,3,2,1,0:T(8,128)(2,1)S(1)}, bf16[3,2,1,24,896]{4,3,2,1,0:T(8,128)(2,1)S(1)}, u32[]{:S(2)}, u32[]{:S(2)}) collective-permute-start(bf16[3,2,1,24,896]{4,3,2,1,0:T(8,128)(2,1)S(1)} %fusion.6), channel_id=1, source_target_pairs={{0,1},{1,0},{2,3},{3,2},{4,5},{5,4},{6,7},{7,6},{8,9},{9,8},{10,11... | collective-permute-start | bytes 774152 | tf_op jit(solution)/shard_map/ppermute | solution.py:437
  86.7 9.4 %collective-permute-start.22 = (bf16[3,1,2,24,896]{4,3,2,1,0:T(8,128)(2,1)S(1)}, bf16[3,1,2,24,896]{4,3,2,1,0:T(8,128)(2,1)S(1)}, u32[]{:S(2)}, u32[]{:S(2)}) collective-permute-start(bf16[3,1,2,24,896]{4,3,2,1,0:T(8,128)(2,1)S(1)} %fusion.5), channel_id=1, source_target_pairs={{0,12},{1,13},{2,14},{3,15},{4,8},{5,9},{6,10},{7,11},{8,4},{9,5},... | collective-permute-start | bytes 774152 | tf_op jit(solution)/shard_map/ppermute | solution.py:437
  88.1 8.4 %collective-permute-start.28 = (bf16[3,2,1,24,896]{4,3,2,1,0:T(8,128)(2,1)S(1)}, bf16[3,2,1,24,896]{4,3,2,1,0:T(8,128)(2,1)S(1)}, u32[]{:S(2)}, u32[]{:S(2)}) collective-permute-start(bf16[3,2,1,24,896]{4,3,2,1,0:T(8,128)(2,1)S(1)} %fusion.4), channel_id=1, source_target_pairs={{0,4},{1,5},{2,6},{3,7},{4,0},{5,1},{6,2},{7,3},{8,12},{9,13},{10,... | collective-permute-start | bytes 774152 | tf_op jit(solution)/shard_map/ppermute | solution.py:437
  92.7 5.6 %collective-permute-start.11 = (bf16[3,1,2,24,896]{4,3,2,1,0:T(8,128)(2,1)S(1)}, bf16[3,1,2,24,896]{4,3,2,1,0:T(8,128)(2,1)S(1)}, u32[]{:S(2)}, u32[]{:S(2)}) collective-permute-start(bf16[3,1,2,24,896]{4,3,2,1,0:T(8,128)(2,1)S(1)} %pad_maximum_fusion.8), channel_id=1, source_target_pairs={{0,1},{1,0},{2,3},{3,2},{4,5},{5,4},{6,7},{7,6},{8,9},{9,8},{10,11... | collective-permute-start | bytes 774152 | tf_op jit(solution)/shard_map/ppermute | solution.py:437
  93.0 8.2 %collective-permute-start.17 = (bf16[3,2,1,24,896]{4,3,2,1,0:T(8,128)(2,1)S(1)}, bf16[3,2,1,24,896]{4,3,2,1,0:T(8,128)(2,1)S(1)}, u32[]{:S(2)}, u32[]{:S(2)}) collective-permute-start(bf16[3,2,1,24,896]{4,3,2,1,0:T(8,128)(2,1)S(1)} %pad_maximum_fusion.9), channel_id=1, source_target_pairs={{0,3},{1,2},{2,1},{3,0},{4,7},{5,6},{6,5},{7,4},{8,11},{9,10},{10,... | collective-permute-start | bytes 774152 | tf_op jit(solution)/shard_map/ppermute | solution.py:437
  96.4 6.8 %collective-permute-start.23 = (bf16[3,1,2,24,896]{4,3,2,1,0:T(8,128)(2,1)S(1)}, bf16[3,1,2,24,896]{4,3,2,1,0:T(8,128)(2,1)S(1)}, u32[]{:S(2)}, u32[]{:S(2)}) collective-permute-start(bf16[3,1,2,24,896]{4,3,2,1,0:T(8,128)(2,1)S(1)} %pad_maximum_fusion.10), channel_id=1, source_target_pairs={{0,4},{1,5},{2,6},{3,7},{4,0},{5,1},{6,2},{7,3},{8,12},{9,13},{10,... | collective-permute-start | bytes 774152 | tf_op jit(solution)/shard_map/ppermute | solution.py:437
  98.3 15.7 %collective-permute-start.12 = (bf16[3,96,896]{2,1,0:T(8,128)(2,1)S(1)}, bf16[3,96,896]{2,1,0:T(8,128)(2,1)S(1)}, u32[]{:S(2)}, u32[]{:S(2)}) collective-permute-start(bf16[3,96,896]{2,1,0:T(8,128)(2,1)S(1)} %bitcast.41), channel_id=1, source_target_pairs={{0,12},{1,13},{2,14},{3,15},{4,8},{5,9},{6,10},{7,11},{8,4},{9,5},... | collective-permute-start | bytes 1548296 | tf_op jit(solution)/shard_map/ppermute | solution.py:437
  99.6 13.3 %collective-permute-start.29 = (bf16[3,2,1,24,896]{4,3,2,1,0:T(8,128)(2,1)S(1)}, bf16[3,2,1,24,896]{4,3,2,1,0:T(8,128)(2,1)S(1)}, u32[]{:S(2)}, u32[]{:S(2)}) collective-permute-start(bf16[3,2,1,24,896]{4,3,2,1,0:T(8,128)(2,1)S(1)} %pad_maximum_fusion.11), channel_id=1, source_target_pairs={{0,12},{1,13},{2,14},{3,15},{4,8},{5,9},{6,10},{7,11},{8,4},{9,5},... | collective-permute-start | bytes 774152 | tf_op jit(solution)/shard_map/ppermute | solution.py:437
  101.2 12.9 %collective-permute-start.18 = (bf16[3,96,896]{2,1,0:T(8,128)(2,1)S(1)}, bf16[3,96,896]{2,1,0:T(8,128)(2,1)S(1)}, u32[]{:S(2)}, u32[]{:S(2)}) collective-permute-start(bf16[3,96,896]{2,1,0:T(8,128)(2,1)S(1)} %bitcast.43), channel_id=1, source_target_pairs={{0,4},{1,5},{2,6},{3,7},{4,0},{5,1},{6,2},{7,3},{8,12},{9,13},{10,... | collective-permute-start | bytes 1548296 | tf_op jit(solution)/shard_map/ppermute | solution.py:437
  103.3 12.4 %collective-permute-start.24 = (bf16[3,96,896]{2,1,0:T(8,128)(2,1)S(1)}, bf16[3,96,896]{2,1,0:T(8,128)(2,1)S(1)}, u32[]{:S(2)}, u32[]{:S(2)}) collective-permute-start(bf16[3,96,896]{2,1,0:T(8,128)(2,1)S(1)} %bitcast.45), channel_id=1, source_target_pairs={{0,3},{1,2},{2,1},{3,0},{4,7},{5,6},{6,5},{7,4},{8,11},{9,10},{10,... | collective-permute-start | bytes 1548296 | tf_op jit(solution)/shard_map/ppermute | solution.py:437
  113.0 8.0 %collective-permute-start.30 = (bf16[3,96,896]{2,1,0:T(8,128)(2,1)S(1)}, bf16[3,96,896]{2,1,0:T(8,128)(2,1)S(1)}, u32[]{:S(2)}, u32[]{:S(2)}) collective-permute-start(bf16[3,96,896]{2,1,0:T(8,128)(2,1)S(1)} %bitcast.47), channel_id=1, source_target_pairs={{0,1},{1,0},{2,3},{3,2},{4,5},{5,4},{6,7},{7,6},{8,9},{9,8},{10,11... | collective-permute-start | bytes 1548296 | tf_op jit(solution)/shard_map/ppermute | solution.py:437
  114.1 21.3 %collective-permute-start.31 = (bf16[3,192,896]{2,1,0:T(8,128)(2,1)S(1)}, bf16[3,192,896]{2,1,0:T(8,128)(2,1)S(1)}, u32[]{:S(2)}, u32[]{:S(2)}) collective-permute-start(bf16[3,192,896]{2,1,0:T(8,128)(2,1)S(1)} %pad_maximum_fusion.refs_0_), channel_id=1, source_target_pairs={{0,4},{1,5},{2,6},{3,7},{4,0},{5,1},{6,2},{7,3},{8,12},{9,13},{10,... | collective-permute-start | bytes 3096584 | tf_op jit(solution)/shard_map/ppermute | solution.py:437
  114.3 21.1 %collective-permute-start.32 = (bf16[3,192,896]{2,1,0:T(8,128)(2,1)S(1)}, bf16[3,192,896]{2,1,0:T(8,128)(2,1)S(1)}, u32[]{:S(2)}, u32[]{:S(2)}) collective-permute-start(bf16[3,192,896]{2,1,0:T(8,128)(2,1)S(1)} %pad_maximum_fusion.1.refs_1_), channel_id=1, source_target_pairs={{0,12},{1,13},{2,14},{3,15},{4,8},{5,9},{6,10},{7,11},{8,4},{9,5},... | collective-permute-start | bytes 3096584 | tf_op jit(solution)/shard_map/ppermute | solution.py:437
  115.8 25.8 %collective-permute-start.33 = (bf16[3,192,896]{2,1,0:T(8,128)(2,1)S(1)}, bf16[3,192,896]{2,1,0:T(8,128)(2,1)S(1)}, u32[]{:S(2)}, u32[]{:S(2)}) collective-permute-start(bf16[3,192,896]{2,1,0:T(8,128)(2,1)S(1)} %pad_maximum_fusion.2.refs_2_), channel_id=1, source_target_pairs={{0,1},{1,0},{2,3},{3,2},{4,5},{5,4},{6,7},{7,6},{8,9},{9,8},{10,11... | collective-permute-start | bytes 3096584 | tf_op jit(solution)/shard_map/ppermute | solution.py:437
  121.1 21.9 %collective-permute-start.34 = (bf16[3,192,896]{2,1,0:T(8,128)(2,1)S(1)}, bf16[3,192,896]{2,1,0:T(8,128)(2,1)S(1)}, u32[]{:S(2)}, u32[]{:S(2)}) collective-permute-start(bf16[3,192,896]{2,1,0:T(8,128)(2,1)S(1)} %pad_maximum_fusion.3.refs_3_), channel_id=1, source_target_pairs={{0,3},{1,2},{2,1},{3,0},{4,7},{5,6},{6,5},{7,4},{8,11},{9,10},{10,... | collective-permute-start | bytes 3096584 | tf_op jit(solution)/shard_map/ppermute | solution.py:437
  134.4 1.0 copy-start.1
  135.4 12.1 %copy-start.2 = (bf16[3,192,896]{2,1,0:T(8,128)(2,1)}, bf16[3,192,896]{2,1,0:T(8,128)(2,1)S(1)}, u32[]{:S(2)}) copy-start(bf16[3,192,896]{2,1,0:T(8,128)(2,1)S(1)} %collective-permute-done.32.refs_1_.refs_5_) | copy-start | bytes 3096580
  141.6 6.0 %copy-start.3 = (bf16[3,192,896]{2,1,0:T(8,128)(2,1)}, bf16[3,192,896]{2,1,0:T(8,128)(2,1)S(1)}, u32[]{:S(2)}) copy-start(bf16[3,192,896]{2,1,0:T(8,128)(2,1)S(1)} %collective-permute-done.33.refs_2_.refs_6_) | copy-start | bytes 3096580
  143.0 4.5 %copy-start.4 = (bf16[3,192,896]{2,1,0:T(8,128)(2,1)}, bf16[3,192,896]{2,1,0:T(8,128)(2,1)S(1)}, u32[]{:S(2)}) copy-start(bf16[3,192,896]{2,1,0:T(8,128)(2,1)S(1)} %collective-permute-done.34.refs_3_.refs_7_) | copy-start | bytes 3096580
  147.6 16.3 %collective-permute-start.35 = (bf16[4,128,512]{2,1,0:T(8,128)(2,1)S(1)}, bf16[4,128,512]{2,1,0:T(8,128)(2,1)S(1)}, u32[]{:S(2)}, u32[]{:S(2)}) collective-permute-start(bf16[4,128,512]{2,1,0:T(8,128)(2,1)S(1)} %get-tuple-element.66), channel_id=1, source_target_pairs={{0,16},{16,0},{32,48},{48,32},{64,80},{80,64},{96,112},{112,96},{1... | collective-permute-start | bytes 1572872 | tf_op jit(solution)/shard_map/ppermute | solution.py:495
  163.8 4.3 %copy-start.9 = (s32[4,14]{1,0:T(4,128)S(1)}, s32[4,14]{1,0:T(4,128)}, u32[]{:S(2)}) copy-start(s32[4,14]{1,0:T(4,128)} %gm.3) | copy-start | bytes 676
  163.8 4.3 %copy-start.11 = (s32[4,14]{1,0:T(4,128)S(1)}, s32[4,14]{1,0:T(4,128)}, u32[]{:S(2)}) copy-start(s32[4,14]{1,0:T(4,128)} %um.3) | copy-start | bytes 676
  164.0 12.7 %collective-permute-start.38 = (bf16[128,512]{1,0:T(8,128)(2,1)S(1)}, bf16[128,512]{1,0:T(8,128)(2,1)S(1)}, u32[]{:S(2)}, u32[]{:S(2)}) collective-permute-start(bf16[128,512]{1,0:T(8,128)(2,1)S(1)} %get-tuple-element.73), channel_id=1, source_target_pairs={{0,96},{16,112},{32,0},{48,16},{64,32},{80,48},{96,64},{112,80},{1... | collective-permute-start | bytes 393224 | tf_op jit(solution)/shard_map/ppermute | solution.py:502
  166.0 10.6 %collective-permute-start.37 = (bf16[128,512]{1,0:T(8,128)(2,1)S(1)}, bf16[128,512]{1,0:T(8,128)(2,1)S(1)}, u32[]{:S(2)}, u32[]{:S(2)}) collective-permute-start(bf16[128,512]{1,0:T(8,128)(2,1)S(1)} %get-tuple-element.74), channel_id=1, source_target_pairs={{0,64},{16,80},{32,96},{48,112},{64,0},{80,16},{96,32},{112,48},{1... | collective-permute-start | bytes 393224 | tf_op jit(solution)/shard_map/ppermute | solution.py:502
  168.1 8.6 %collective-permute-start.36 = (bf16[128,512]{1,0:T(8,128)(2,1)S(1)}, bf16[128,512]{1,0:T(8,128)(2,1)S(1)}, u32[]{:S(2)}, u32[]{:S(2)}) collective-permute-start(bf16[128,512]{1,0:T(8,128)(2,1)S(1)} %get-tuple-element.72), channel_id=1, source_target_pairs={{0,32},{16,48},{32,64},{48,80},{64,96},{80,112},{96,0},{112,16},{1... | collective-permute-start | bytes 393224 | tf_op jit(solution)/shard_map/ppermute | solution.py:502

commit v4 on v2

v4 whole, which is shorter than its diff:
```python
import functools

import jax
import jax.numpy as jnp
from jax import lax
from jax.experimental import pallas as pl
from jax.experimental.pallas import tpu as pltpu
from jax.sharding import PartitionSpec as P

BF = jnp.bfloat16
F32 = jnp.float32
LIVE = 768
PAD = 144
SIDE = 4
BLK = 128
PAIR = 2 * BLK
UNITS = 1792
HALF = UNITS // 2
STEPS = UNITS // PAIR
FEAT = 512
SLOTS = 1024
CUT = 192
FIRST = 576
LAST = LIVE - FIRST
VMEM = 32 << 20

MASKS = {"xA": (1, 0), "xB": (3, 0), "yA": (0, 1), "yB": (0, 3)}
ROUNDS = (
    ((0, ("xA", "yA")), (1, ("xB", "yB")), (2, ("yA", "xA")), (3, ("yB", "xB"))),
    ((1, ("xB", "yB")), (0, ("xA", "yA")), (3, ("yB", "xB")), (2, ("yA", "xA"))),
)
SIDES = (0, 1)


def partners(names):
    pairs = []
    for col in range(2 * SIDE):
        dx, dy = MASKS[names[col % 2]]
        for x in range(SIDE):
            for y in range(SIDE):
                start = (col * SIDE + x) * SIDE + y
                pairs.append((start, (col * SIDE + (x ^ dx)) * SIDE + (y ^ dy)))
    return pairs


def shift(dz, dc):
    return [
        (z * 2 + c, ((z + dz) % SIDE) * 2 + (c + dc) % 2) for z in range(SIDE) for c in range(2)
    ]


def logical_rows():
    place = lax.axis_index("dp")
    x, y = place // SIDE, place % SIDE

    def sides(v):
        high = v // 2
        return (v % 2) ^ high, high

    xa, xb = sides(x)
    ya, yb = sides(y)
    first = xa * 8 + xb * 4 + ya * 2 + yb
    second = ya * 8 + yb * 4 + xa * 2 + xb
    mask = jnp.where(lax.axis_index("col") % 2 > 0, second, first)
    row = lax.iota(jnp.int32, LIVE)
    return ((row // 48) ^ mask) * 48 + row % 48


def kept(mask_ref, row, col, value):
    return jnp.where(mask_ref[row, col] > 0, value, jnp.zeros_like(value))


def smem():
    return pl.BlockSpec(memory_space=pltpu.SMEM)


def whole(shape):
    return pl.BlockSpec(shape, lambda j: (0,) * len(shape))


def call(kernel, name, flops, moved, **rest):
    return pl.pallas_call(
        kernel,
        compiler_params=pltpu.CompilerParams(vmem_limit_bytes=VMEM),
        cost_estimate=pl.CostEstimate(flops=flops, bytes_accessed=moved, transcendentals=0),
        name=name,
        **rest,
    )


def pack_kernel(tok_ref, cot_ref, count_ref, out_ref):
    out_ref[:BLK, :FEAT] = tok_ref[...]
    out_ref[:BLK, FEAT:] = cot_ref[...]
    count = jnp.full((PAD - BLK, 2 * FEAT), count_ref[0], jnp.int32)
    out_ref[BLK:, :] = count.astype(F32).astype(BF)


def pack(tokens, cotangent, counts):
    return call(
        pack_kernel,
        "pack",
        0,
        1 << 19,
        out_shape=jax.ShapeDtypeStruct((PAD, 2 * FEAT), BF),
        grid=(1,),
        in_specs=[whole((BLK, FEAT)), whole((BLK, FEAT)), smem()],
        out_specs=whole((PAD, 2 * FEAT)),
    )(tokens, cotangent, counts)


def prepare_kernel(gm, um, dm, wg, wu, wd, wx_ref, wdt_ref, wd_ref):
    j = pl.program_id(0)
    for which, (mask, ref) in enumerate(((gm, wg), (um, wu))):
        for r in range(4):
            for b in range(2):
                at = slice(r * BLK, (r + 1) * BLK)
                wx_ref[0, at, which * PAIR + b * BLK : which * PAIR + (b + 1) * BLK] = kept(
                    mask, r, 2 * j + b, ref[at, b * BLK : (b + 1) * BLK]
                )
    down = jnp.concatenate(
        [
            jnp.concatenate(
                [
                    kept(dm, 2 * j + b, c, wd[b * BLK : (b + 1) * BLK, c * BLK : (c + 1) * BLK])
                    for c in range(4)
                ],
                axis=1,
            )
            for b in range(2)
        ],
        axis=0,
    )
    wd_ref[...] = down
    wdt_ref[0] = down.T


def prepare(gm, um, dm, wg, wu, wd):
    return call(
        prepare_kernel,
        "prepare",
        0,
        13 << 20,
        grid=(STEPS,),
        out_shape=(
            jax.ShapeDtypeStruct((STEPS, FEAT, 2 * PAIR), BF),
            jax.ShapeDtypeStruct((STEPS, FEAT, PAIR), BF),
            jax.ShapeDtypeStruct((UNITS, FEAT), BF),
        ),
        in_specs=[
            smem(),
            smem(),
            smem(),
            pl.BlockSpec((FEAT, PAIR), lambda j: (0, j)),
            pl.BlockSpec((FEAT, PAIR), lambda j: (0, j)),
            pl.BlockSpec((PAIR, FEAT), lambda j: (j, 0)),
        ],
        out_specs=(
            pl.BlockSpec((1, FEAT, 2 * PAIR), lambda j: (j, 0, 0)),
            pl.BlockSpec((1, FEAT, PAIR), lambda j: (j, 0, 0)),
            pl.BlockSpec((PAIR, FEAT), lambda j: (j, 0)),
        ),
    )(gm, um, dm, wg, wu, wd)


def compact_kernel(shard, rows_ref, *refs):
    sources, (x_ref, g_ref, xt_ref, offs_ref, cnts_ref) = refs[:8], refs[8:]
    rows = rows_ref[...]
    slot = lax.broadcasted_iota(jnp.int32, (LIVE, BLK), 1)
    cnts = [ref[BLK : BLK + 1, 0:1].astype(F32).astype(jnp.int32) for ref in sources]
    total = None
    for pair in range(4):
        picks = []
        for k in (2 * pair, 2 * pair + 1):
            offset = jnp.zeros((1, 1), jnp.int32)
            for other in range(8):
                if other != k:
                    offset += jnp.where(shard[other] < shard[k], cnts[other], 0)
            offs_ref[k] = jnp.broadcast_to(offset, (8, BLK))
            cnts_ref[k] = jnp.broadcast_to(cnts[k], (8, BLK))
            hit = (rows - offset == slot) & (slot < cnts[k])
            picks.append(jnp.where(hit, 1.0, 0.0).astype(BF))
        source = jnp.concatenate(
            [sources[2 * pair][:BLK, :], sources[2 * pair + 1][:BLK, :]], axis=0
        )
        part = jnp.dot(jnp.concatenate(picks, axis=1), source, preferred_element_type=F32)
        total = part if total is None else total + part
    x_ref[...] = total[:, :FEAT].astype(BF)
    g_ref[...] = total[:, FEAT:].astype(BF)
    xt_ref[...] = total[:, :FEAT].T.astype(BF)


def compact(shard, rows, sources):
    vmem = pl.BlockSpec(memory_space=pltpu.VMEM)
    return call(
        compact_kernel,
        "compact",
        2 * LIVE * SLOTS * SLOTS,
        5 << 20,
        out_shape=(
            jax.ShapeDtypeStruct((LIVE, FEAT), BF),
            jax.ShapeDtypeStruct((LIVE, FEAT), BF),
            jax.ShapeDtypeStruct((FEAT, LIVE), BF),
            jax.ShapeDtypeStruct((8, 8, BLK), jnp.int32),
            jax.ShapeDtypeStruct((8, 8, BLK), jnp.int32),
        ),
        in_specs=[smem(), vmem] + [vmem] * 8,
        out_specs=(vmem,) * 5,
    )(shard, rows, *sources)


def partial_kernel(start, pieces, x_ref, g_ref, wx_ref, wdt_ref, *outs):
    count = pieces * CUT
    x, g = x_ref[start : start + count, :], g_ref[start : start + count, :]
    both = jnp.dot(x, wx_ref[0], preferred_element_type=F32)
    back = jnp.dot(g, wdt_ref[0], preferred_element_type=F32)
    for which, result in enumerate((both[:, :PAIR], both[:, PAIR:], back)):
        for piece in range(pieces):
            for q in SIDES:
                outs[piece * 2 + q][which] = result[
                    piece * CUT : (piece + 1) * CUT, q * BLK : (q + 1) * BLK
                ].astype(BF)


def partials(start, pieces, x, g, wx, wdt):
    count = pieces * CUT
    return call(
        functools.partial(partial_kernel, start, pieces),
        "partials",
        2 * count * FEAT * 3 * UNITS,
        7 << 20,
        grid=(STEPS,),
        out_shape=(jax.ShapeDtypeStruct((3, CUT, HALF), BF),) * (2 * pieces),
        in_specs=[
            whole((LIVE, FEAT)),
            whole((LIVE, FEAT)),
            pl.BlockSpec((1, FEAT, 2 * PAIR), lambda j: (j, 0, 0)),
            pl.BlockSpec((1, FEAT, PAIR), lambda j: (j, 0, 0)),
        ],
        out_specs=(pl.BlockSpec((3, CUT, BLK), lambda j: (0, 0, j)),) * (2 * pieces),
    )(x, g, wx, wdt)


def stacked(refs, which, pieces):
    return jnp.concatenate(
        [jnp.concatenate([refs[p * 2 + q][which] for q in SIDES], axis=1) for p in pieces],
        axis=0,
    )


def picked(rows, offs, cnts, k, slot):
    hit = (rows - offs[k, 0:1, 0:1] == slot) & (slot < cnts[k, 0:1, 0:1])
    return jnp.where(hit, 1.0, 0.0).astype(BF)


def first_output_kernel(rows_ref, offs, cnts, wd_ref, *refs):
    parts, (out_ref, total) = refs[:6], refs[6:]
    j = pl.program_id(0)
    part = jnp.dot(stacked(parts, 0, range(3)), wd_ref[...], preferred_element_type=F32)

    @pl.when(j == 0)
    def _():
        total[...] = part

    @pl.when(j > 0)
    def _():
        total[...] += part

    @pl.when(j == STEPS - 1)
    def _():
        mixed = total[...].astype(BF)
        rows = rows_ref[0:1, :]
        slot = lax.broadcasted_iota(jnp.int32, (BLK, FIRST), 0)
        for k in range(8):
            pick = picked(rows, offs, cnts, k, slot)
            out_ref[k] = jnp.dot(pick, mixed, preferred_element_type=F32).astype(BF)


def first_output(rows, offs, cnts, wd, parts):
    return call(
        first_output_kernel,
        "first_output",
        1,
        1 << 12,
        grid=(STEPS,),
        out_shape=jax.ShapeDtypeStruct((8, BLK, FEAT), BF),
        in_specs=[whole((1, FIRST)), whole((8, 8, BLK)), whole((8, 8, BLK))]
        + [pl.BlockSpec((PAIR, FEAT), lambda j: (j, 0))]
        + [pl.BlockSpec((1, CUT, BLK), lambda j: (2, 0, j))] * 6,
        out_specs=whole((8, BLK, FEAT)),
        scratch_shapes=[pltpu.VMEM((FIRST, FEAT), F32)],
    )(rows, offs, cnts, wd, *parts)


def last_output_kernel(rows_ref, offs, cnts, early_ref, wd_ref, *refs):
    parts, (near_ref, away_ref) = refs[:2], refs[2:]
    mixed = None
    for j in range(STEPS):
        hidden = jnp.concatenate(
            [parts[q][0, :, j * BLK : (j + 1) * BLK] for q in SIDES], axis=1
        )
        part = jnp.dot(
            hidden, wd_ref[j * PAIR : (j + 1) * PAIR, :], preferred_element_type=F32
        )
        mixed = part if mixed is None else mixed + part
    mixed = mixed.astype(BF)
    rows = rows_ref[0:1, :]
    slot = lax.broadcasted_iota(jnp.int32, (BLK, LAST), 0)
    for k in range(8):
        pick = picked(rows, offs, cnts, k, slot)
        late = jnp.dot(pick, mixed, preferred_element_type=F32)
        target = near_ref if k < 4 else away_ref
        target[k % 4] = (early_ref[k].astype(F32) + late).astype(BF)


def last_output(rows, offs, cnts, early, wd, parts):
    return call(
        last_output_kernel,
        "last_output",
        1,
        1 << 12,
        grid=(1,),
        out_shape=(jax.ShapeDtypeStruct((4, BLK, FEAT), BF),) * 2,
        in_specs=[
            whole((1, LAST)),
            whole((8, 8, BLK)),
            whole((8, 8, BLK)),
            whole((8, BLK, FEAT)),
            whole((UNITS, FEAT)),
        ]
        + [whole((1, CUT, HALF))] * 2,
        out_specs=(whole((4, BLK, FEAT)),) * 2,
    )(rows, offs, cnts, early, wd, *parts)


def grad_kernel(gm, um, dm, xt_ref, g_ref, *refs):
    parts, lasts, last_hidden = refs[:6], refs[6:8], refs[8:10]
    gate_out, up_out, down_out = refs[10:]
    j = pl.program_id(0)

    def rows(which):
        late = stacked(lasts, which, (0,)) if which < 2 else stacked(last_hidden, 0, (0,))
        return jnp.concatenate([stacked(parts, which, range(3)), late], axis=0)

    xt = xt_ref[...]
    gate = jnp.dot(xt, rows(0), preferred_element_type=F32)
    up = jnp.dot(xt, rows(1), preferred_element_type=F32)
    down = lax.dot_general(
        rows(2), g_ref[...], (((0,), (0,)), ((), ())), preferred_element_type=F32
    )
    for r in range(4):
        for b in range(2):
            at, by = slice(r * BLK, (r + 1) * BLK), slice(b * BLK, (b + 1) * BLK)
            gate_out[at, by] = kept(gm, r, 2 * j + b, gate[at, by])
            up_out[at, by] = kept(um, r, 2 * j + b, up[at, by])
            down_out[by, at] = kept(dm, 2 * j + b, r, down[by, at])


def gradients(gm, um, dm, xt, g, parts, lasts, last_hidden):
    return call(
        grad_kernel,
        "gradients",
        2 * LIVE * FEAT * 3 * UNITS,
        20 << 20,
        grid=(STEPS,),
        out_shape=(
            jax.ShapeDtypeStruct((FEAT, UNITS), F32),
            jax.ShapeDtypeStruct((FEAT, UNITS), F32),
            jax.ShapeDtypeStruct((UNITS, FEAT), F32),
        ),
        in_specs=[smem(), smem(), smem(), whole((FEAT, LIVE)), whole((LIVE, FEAT))]
        + [pl.BlockSpec((3, CUT, BLK), lambda j: (0, 0, j))] * 6
        + [pl.BlockSpec((2, CUT, BLK), lambda j: (0, 0, j))] * 2
        + [pl.BlockSpec((1, CUT, BLK), lambda j: (0, 0, j))] * 2,
        out_specs=(
            pl.BlockSpec((FEAT, PAIR), lambda j: (0, j)),
            pl.BlockSpec((FEAT, PAIR), lambda j: (0, j)),
            pl.BlockSpec((PAIR, FEAT), lambda j: (j, 0)),
        ),
    )(gm, um, dm, xt, g, *parts, *lasts, *last_hidden)


def split(value, axis):
    lower = lax.slice_in_dim(value, 0, 1, axis=axis)
    upper = lax.slice_in_dim(value, 1, 2, axis=axis)
    return lower, upper


def activate(total):
    gate, upward, back = total[0], total[1], total[2]
    sigma = jax.nn.sigmoid(gate)
    active = gate * sigma
    hidden = (active * upward).astype(BF)
    d_gate = (back * upward * sigma * (1.0 + gate * (1.0 - sigma))).astype(BF)
    d_up = (back * active).astype(BF)
    return jnp.stack([d_gate, d_up, hidden])


def exchange(values, number):
    return [
        lax.ppermute(values[q], ("col", "dp"), partners(ROUNDS[q][number][1])) for q in SIDES
    ]


def on_device(
    tokens, cotangent, gate_weight, up_weight, down_weight, gate_mask, up_mask, down_mask, counts
):
    live = (lax.iota(jnp.int32, tokens.shape[0]) < counts[0])[:, None]
    place = lax.axis_index("col")
    order = jnp.arange(8)
    shard = ((place // 2 + order % 4) % SIDE) * 2 + ((place % 2) ^ (order // 4))
    own = pack(tokens, cotangent, counts)
    column = [own] + [lax.ppermute(own, "col", shift(-dz, 0)) for dz in (1, 2, 3)]
    beside = [lax.ppermute(own, "col", shift(0, 1))]
    wx, wdt, wd = prepare(gate_mask, up_mask, down_mask, gate_weight, up_weight, down_weight)
    rows = logical_rows()
    *column, wx, wdt, wd, rows_down, rows_along, shard = lax.optimization_barrier(
        (*column, wx, wdt, wd, rows[:, None], rows[None, :], shard)
    )
    beside += [lax.ppermute(value, "col", shift(0, 1)) for value in column[1:]]
    x, g, xt, offs, cnts = compact(shard, rows_down, column + beside)

    early = partials(FIRST, 1, x, g, wx, wdt)
    come_early = exchange(early, 0)
    x_rest, g_rest, *_ = lax.optimization_barrier((x, g, *early))
    late = partials(0, 3, x_rest, g_rest, wx, wdt)
    zero = [late[q] for q in SIDES]
    side = [[late[2 * (2 - ROUNDS[q][n][0]) + q] for q in SIDES] for n in range(2)]
    come_rest = exchange(side[0], 0)
    second = [
        (side[1][q].astype(F32) + come_early[q].astype(F32)).astype(BF) for q in SIDES
    ]
    come_second = exchange(second, 1)
    keep, send = [None] * 2, [None] * 2
    for q in SIDES:
        total = (
            zero[q].astype(F32) + come_rest[q].astype(F32) + come_second[q].astype(F32)
        ).reshape(3, 2, 2, 48, HALF)
        keep[q], upper = split(total, ROUNDS[q][2][0] - 1)
        send[q] = upper.astype(BF)
    come = exchange(send, 2)
    keep = [(keep[q] + come[q].astype(F32)).astype(BF) for q in SIDES]
    come = exchange(keep, 3)
    held = []
    for q in SIDES:
        axis = ROUNDS[q][3][0] - 1
        lower, upper = split(come[q], axis)
        arrived = jnp.concatenate([upper, lower], axis=axis)
        held.append(activate(keep[q].astype(F32) + arrived.astype(F32)))
    come = exchange(held, 2)
    held = [
        jnp.concatenate([held[q], come[q]], axis=ROUNDS[q][2][0] - 1).reshape(3, CUT, HALF)
        for q in SIDES
    ]
    near = exchange(held, 1)
    far = exchange(held, 0)
    last_hidden = exchange([near[q][2:] for q in SIDES], 0)
    lasts = exchange([near[q][:2] for q in SIDES], 0)
    parts = list(held)
    for piece in (1, 2):
        for q in SIDES:
            parts.append(near[q] if 2 - ROUNDS[q][1][0] == piece else far[q])

    begun = first_output(rows_along[:, :FIRST], offs, cnts, wd, parts)
    mine, away = last_output(rows_along[:, FIRST:], offs, cnts, begun, wd, last_hidden)
    other = lax.ppermute(away, "col", shift(0, 1))
    summed = mine.astype(F32) + other.astype(F32)
    terms = [summed[k].astype(BF) for k in range(4)]
    mixed = terms[0].astype(F32)
    for dz in (1, 2, 3):
        mixed += lax.ppermute(terms[dz], "col", shift(dz, 0)).astype(F32)
    output = jnp.where(live, mixed, jnp.zeros_like(mixed)).astype(BF)
    gate_grad, up_grad, down_grad = gradients(
        gate_mask, up_mask, down_mask, xt, g, parts, lasts, last_hidden
    )
    return (output, gate_grad, up_grad, down_grad)


def solution(mesh):
    in_specs = (
        P("col", "dp"),
        P("col", "dp"),
        P("dp", "col"),
        P("dp", "col"),
        P("col", "dp"),
        P("dp", "col"),
        P("dp", "col"),
        P("col", "dp"),
        P("col"),
    )
    out_specs = (P("col", "dp"), P("dp", "col"), P("dp", "col"), P("col", "dp"))
    return jax.shard_map(
        on_device, mesh=mesh, in_specs=in_specs, out_specs=out_specs, check_vma=False
    )
```

time: 202 us -> 163 us (0.81)
  starting transfers between devices: 75.6 us -> 47.7 us
  Pallas kernels: 42.8 us -> 27.5 us
  waiting for transfers between devices: 67.7 us -> 72.3 us
    ppermute x45 -> x25, starting transfers between devices: 61.7 us -> 38.4 us  [the longest x20 27.4 us: exchange(): lax.ppermute(values[q], ('col', 'dp'), partners(ROUNDS[q][number][1]))]
    ppermute x45 -> x25, waiting for transfers between devices: 58.4 us -> 68.9 us  [the longest x20 67.3 us: exchange(): lax.ppermute(values[q], ('col', 'dp'), partners(ROUNDS[q][number][1]))]
    pallas_call x2, Pallas kernels: 14.3 us -> 8.14 us  [partials(): call(functools.partial(partial_kernel, start, pieces), 'partials', 2 * co...]
    ppermute x3, waiting for transfers between devices: 9.26 us -> 3.4 us  [on_device(): lax.ppermute(own, 'col', shift(-dz, 0))]
    pallas_call x1, Pallas kernels: 6.56 us -> 2.4 us  [prepare(): call(prepare_kernel, 'prepare', 0, 13 << 20, grid=(STEPS,), out_shape=(ja...]
    ppermute x3, starting transfers between devices: 7.29 us -> 3.5 us  [on_device(): mixed += lax.ppermute(terms[dz], 'col', shift(dz, 0)).astype(F32)]
    pallas_call x2, Pallas kernels: 8.71 us -> 5.51 us  [the longest x1 4.51 us: first_output(): call(first_output_kernel, 'first_output', 1, 1 << 12, grid=(STEPS,), out_...]
    unnamed x39 -> x19, local copies, waits for them, and re-layouts: 8.12 us -> 8.44 us
  transfers between devices with their start and end apart: 51 -> 31, of which waited for: 18 -> 18; matrix products, arithmetic and copies ran while one was open for 2% -> 2% of each run, Pallas kernels for 16% -> 13%
where the time goes in v4:
time: 163 us; the launch traced here: 161 us
  waiting for transfers between devices  72.3 us (44%)
  starting transfers between devices  47.7 us (29%)
  Pallas kernels  27.5 us (17%)
  local copies, waits for them, and re-layouts  8.91 us (5%)
  other arithmetic  3.5 us (2%)
    ppermute x20, waiting for transfers between devices, exchange(): lax.ppermute(values[q], ('col', 'dp'), partners(ROUNDS[q][number][1]))  67.3 us
    ppermute x20, starting transfers between devices, exchange(): lax.ppermute(values[q], ('col', 'dp'), partners(ROUNDS[q][number][1]))  27.4 us
    pallas_call x1, Pallas kernels, gradients(): call(grad_kernel, 'gradients', 2 * LIVE * FEAT * 3 * UNITS, 20 << 20, gri...  8.84 us
    unnamed x19, local copies, waits for them, and re-layouts  8.44 us
    ppermute x1, starting transfers between devices, on_device(): other = lax.ppermute(away, 'col', shift(0, 1))  8.17 us
    pallas_call x2, Pallas kernels, partials(): call(functools.partial(partial_kernel, start, pieces), 'partials', 2 * co...  8.14 us
    ppermute x3, starting transfers between devices, on_device(): lax.ppermute(own, 'col', shift(-dz, 0))  5.77 us
    pallas_call x1, Pallas kernels, first_output(): call(first_output_kernel, 'first_output', 1, 1 << 12, grid=(STEPS,), out_...  4.51 us
  transfers between devices with their start and end apart: 31, of which 18 were waited for; matrix products, arithmetic and copies ran while one was open for 2% of the time, Pallas kernels for 13%

profile of v4, /device:TPU:1, one launch (start us, length us, event | category | flops | bytes accessed | tf_op | source)
XLA Modules:
  0.0 161.5 jit_solution(9653508683082360186)
XLA Ops:
  1.3 0.9 copy-done.3
  2.2 0.9 copy-done.4
  3.1 1.5 collective-permute-start.3
  4.6 1.7 %collective-permute-start.2 = (bf16[144,1024]{1,0:T(8,128)(2,1)S(1)}, bf16[144,1024]{1,0:T(8,128)(2,1)S(1)}, u32[]{:S(2)}, u32[]{:S(2)}) collective-permute-start(bf16[144,1024]{1,0:T(8,128)(2,1)S(1)} %pack.1.refs_0_), channel_id=1, source_target_pairs={{0,32},{16,48},{32,64},{48,80},{64,96},{80,112},{96,0},{112,16},{1... | collective-permute-start | bytes 884744 | tf_op jit(solution)/shard_map/ppermute | solution.py:412
  6.3 3.3 %collective-permute-start.1 = (bf16[144,1024]{1,0:T(8,128)(2,1)S(1)}, bf16[144,1024]{1,0:T(8,128)(2,1)S(1)}, u32[]{:S(2)}, u32[]{:S(2)}) collective-permute-start(bf16[144,1024]{1,0:T(8,128)(2,1)S(1)} %pack.1.refs_0_), channel_id=1, source_target_pairs={{0,64},{16,80},{32,96},{48,112},{64,0},{80,16},{96,32},{112,48},{1... | collective-permute-start | bytes 884744 | tf_op jit(solution)/shard_map/ppermute | solution.py:412
  9.7 0.7 collective-permute-start
  10.4 0.8 copy.13.dm
  11.2 1.5 copy-done
  12.7 1.5 copy-done.1
  14.2 1.5 copy-done.2
  15.7 0.7 copy-done.5
  16.3 0.7 copy-done.7
  17.0 2.4 %prepare.1 = (bf16[7,512,512]{2,1,0:T(8,128)(2,1)S(1)}, bf16[7,512,256]{2,1,0:T(8,128)(2,1)S(1)}, bf16[1792,512]{1,0:T(8,128)(2,1)S(1)}) custom-call(s32[4,14]{1,0:T(4,128)S(1)} %copy-done.5, s32[4,14]{1,0:T(4,128)S(1)} %copy-done.7, s32[14,4]{1,0:T(8,128)S(1)} %copy.13.dm, bf16[512,1792]{1,0:T(8,128)(2,1)S(1)} %copy-done, bf16[512,1792]{1,0:T(8,128)(2,1)S(1)} %copy-done.1, ...), custom_call_target="tpu_custom_call" | custom-call | bytes 13631488 | tf_op jit(solution)/shard_map/prepare/pallas_call | solution.py:138
  19.7 3.4 %collective-permute-done.1.refs_2_ = bf16[144,1024]{1,0:T(8,128)(2,1)S(1)} collective-permute-done((bf16[144,1024]{1,0:T(8,128)(2,1)S(1)}, bf16[144,1024]{1,0:T(8,128)(2,1)S(1)}, u32[]{:S(2)}, u32[]{:S(2)}) %collective-permute-start.1) | collective-permute-done | bytes 294944 | tf_op jit(solution)/shard_map/ppermute | solution.py:412
  23.1 0.9 collective-permute-start.4
  23.9 0.5 collective-permute-start.6
  24.4 0.7 collective-permute-done.4.refs_5_
  25.1 0.4 collective-permute-done.5.refs_6_
  25.6 0.4 collective-permute-done.6.refs_7_
  26.0 2.6 %compact.1 = (bf16[768,512]{1,0:T(8,128)(2,1)S(1)}, bf16[768,512]{1,0:T(8,128)(2,1)S(1)}, bf16[512,768]{1,0:T(8,128)(2,1)S(1)}, s32[8,8,128]{2,1,0:T(8,128)S(1)}, s32[8,8,128]{2,1,0:T(8,128)S(1)}) custom-call(s32[8]{0:T(128)S(1)} %fusion.23.shard, s32[768,1]{1,0:T(8,128)S(1)} %fusion.10.rows_ref, bf16[144,1024]{1,0:T(8,128)(2,1)S(1)} %pack.1.refs_0_, ...), custom_call_target="tpu_custom_call" | custom-call | flops 1610612736 | bytes 5242880 | tf_op jit(solution)/shard_map/compact/pallas_call | solution.py:194
  28.6 2.7 %partials.2 = (bf16[3,192,896]{2,1,0:T(8,128)(2,1)S(1)}, bf16[3,192,896]{2,1,0:T(8,128)(2,1)S(1)}) custom-call(bf16[768,512]{1,0:T(8,128)(2,1)S(1)} %get-tuple-element.56.x_ref, bf16[768,512]{1,0:T(8,128)(2,1)S(1)} %get-tuple-element.57.g_ref, bf16[7,512,512]{2,1,0:T(8,128)(2,1)S(1)} %get-tuple-element.52.wx_ref, ...), custom_call_target="tpu_custom_call" | custom-call | flops 1056964608 | bytes 7340032 | tf_op jit(solution)/shard_map/partials/pallas_call | solution.py:226
  31.2 1.4 collective-permute-start.8
  32.6 1.9 %collective-permute-start.14 = (bf16[3,192,896]{2,1,0:T(8,128)(2,1)S(1)}, bf16[3,192,896]{2,1,0:T(8,128)(2,1)S(1)}, u32[]{:S(2)}, u32[]{:S(2)}) collective-permute-start(bf16[3,192,896]{2,1,0:T(8,128)(2,1)S(1)} %get-tuple-element.55), channel_id=1, source_target_pairs={{0,12},{1,13},{2,14},{3,15},{4,8},{5,9},{6,10},{7,11},{8,4},{9,5},... | collective-permute-start | bytes 3096584 | tf_op jit(solution)/shard_map/ppermute | solution.py:400
  34.5 5.5 %partials.3 = (bf16[3,192,896]{2,1,0:T(8,128)(2,1)S(1)}, bf16[3,192,896]{2,1,0:T(8,128)(2,1)S(1)}, bf16[3,192,896]{2,1,0:T(8,128)(2,1)S(1)}, bf16[3,192,896]{2,1...) custom-call(bf16[768,512]{1,0:T(8,128)(2,1)S(1)} %get-tuple-element.56.x_ref, ...), custom_call_target="tpu_custom_call" | custom-call | flops 3170893824 | bytes 7340032 | tf_op jit(solution)/shard_map/partials/pallas_call | solution.py:226
  40.0 0.5 collective-permute-start.7
  40.5 4.6 %collective-permute-done.8 = bf16[3,192,896]{2,1,0:T(8,128)(2,1)S(1)} collective-permute-done((bf16[3,192,896]{2,1,0:T(8,128)(2,1)S(1)}, bf16[3,192,896]{2,1,0:T(8,128)(2,1)S(1)}, u32[]{:S(2)}, u32[]{:S(2)}) %collective-permute-start.8) | collective-permute-done | bytes 1032224 | tf_op jit(solution)/shard_map/ppermute | solution.py:400
  45.1 0.2 add_convert_fusion.1
  45.3 2.8 %collective-permute-start.9 = (bf16[3,192,896]{2,1,0:T(8,128)(2,1)S(1)}, bf16[3,192,896]{2,1,0:T(8,128)(2,1)S(1)}, u32[]{:S(2)}, u32[]{:S(2)}) collective-permute-start(bf16[3,192,896]{2,1,0:T(8,128)(2,1)S(1)} %add_convert_fusion.1), channel_id=1, source_target_pairs={{0,12},{1,13},{2,14},{3,15},{4,8},{5,9},{6,10},{7,11},{8,4},{9,5},... | collective-permute-start | bytes 3096584 | tf_op jit(solution)/shard_map/ppermute | solution.py:400
  48.2 0.2 add_convert_fusion
  48.6 7.6 %collective-permute-done.7 = bf16[3,192,896]{2,1,0:T(8,128)(2,1)S(1)} collective-permute-done((bf16[3,192,896]{2,1,0:T(8,128)(2,1)S(1)}, bf16[3,192,896]{2,1,0:T(8,128)(2,1)S(1)}, u32[]{:S(2)}, u32[]{:S(2)}) %collective-permute-start.7) | collective-permute-done | bytes 1032224 | tf_op jit(solution)/shard_map/ppermute | solution.py:400
  56.1 4.3 %collective-permute-done.9 = bf16[3,192,896]{2,1,0:T(8,128)(2,1)S(1)} collective-permute-done((bf16[3,192,896]{2,1,0:T(8,128)(2,1)S(1)}, bf16[3,192,896]{2,1,0:T(8,128)(2,1)S(1)}, u32[]{:S(2)}, u32[]{:S(2)}) %collective-permute-start.9) | collective-permute-done | bytes 1032224 | tf_op jit(solution)/shard_map/ppermute | solution.py:400
  60.5 0.3 convert_add_fusion.1
  60.9 1.0 collective-permute-start.10
  61.8 9.7 %collective-permute-done.13 = bf16[3,192,896]{2,1,0:T(8,128)(2,1)S(1)} collective-permute-done((bf16[3,192,896]{2,1,0:T(8,128)(2,1)S(1)}, bf16[3,192,896]{2,1,0:T(8,128)(2,1)S(1)}, u32[]{:S(2)}, u32[]{:S(2)}) %collective-permute-start.13) | collective-permute-done | bytes 1032224 | tf_op jit(solution)/shard_map/ppermute | solution.py:400
  71.5 0.3 convert_add_fusion
  71.9 2.6 %collective-permute-start.16 = (bf16[3,2,1,48,896]{4,3,2,1,0:T(8,128)(2,1)S(1)}, bf16[3,2,1,48,896]{4,3,2,1,0:T(8,128)(2,1)S(1)}, u32[]{:S(2)}, u32[]{:S(2)}) collective-permute-start(bf16[3,2,1,48,896]{4,3,2,1,0:T(8,128)(2,1)S(1)} %slice.158), channel_id=1, source_target_pairs={{0,3},{1,2},{2,1},{3,0},{4,7},{5,6},{6,5},{7,4},{8,11},{9,10},{10,... | collective-permute-start | bytes 1548296 | tf_op jit(solution)/shard_map/ppermute | solution.py:400
  74.6 1.3 collective-permute-start.11
  75.9 5.5 %collective-permute-done.16 = bf16[3,2,1,48,896]{4,3,2,1,0:T(8,128)(2,1)S(1)} collective-permute-done((bf16[3,2,1,48,896]{4,3,2,1,0:T(8,128)(2,1)S(1)}, bf16[3,2,1,48,896]{4,3,2,1,0:T(8,128)(2,1)S(1)}, u32[]{:S(2)}, u32[]{:S(2)}) %collective-permute-start.16) | collective-permute-done | bytes 516128 | tf_op jit(solution)/shard_map/ppermute | solution.py:400
  81.7 5.3 %collective-permute-done.11 = bf16[3,1,2,48,896]{4,3,2,1,0:T(8,128)(2,1)S(1)} collective-permute-done((bf16[3,1,2,48,896]{4,3,2,1,0:T(8,128)(2,1)S(1)}, bf16[3,1,2,48,896]{4,3,2,1,0:T(8,128)(2,1)S(1)}, u32[]{:S(2)}, u32[]{:S(2)}) %collective-permute-start.11) | collective-permute-done | bytes 516128 | tf_op jit(solution)/shard_map/ppermute | solution.py:400
  87.1 0.2 multiply_convert_fusion.5
  87.5 2.4 %collective-permute-done.17 = bf16[3,2,1,48,896]{4,3,2,1,0:T(8,128)(2,1)S(1)} collective-permute-done((bf16[3,2,1,48,896]{4,3,2,1,0:T(8,128)(2,1)S(1)}, bf16[3,2,1,48,896]{4,3,2,1,0:T(8,128)(2,1)S(1)}, u32[]{:S(2)}, u32[]{:S(2)}) %collective-permute-start.17) | collective-permute-done | bytes 516128 | tf_op jit(solution)/shard_map/ppermute | solution.py:400
  90.1 0.2 multiply_convert_fusion.2
  90.3 2.6 %collective-permute-start.18 = (bf16[3,2,1,48,896]{4,3,2,1,0:T(8,128)(2,1)S(1)}, bf16[3,2,1,48,896]{4,3,2,1,0:T(8,128)(2,1)S(1)}, u32[]{:S(2)}, u32[]{:S(2)}) collective-permute-start(bf16[3,2,1,48,896]{4,3,2,1,0:T(8,128)(2,1)S(1)} %pad_maximum_fusion.3), channel_id=1, source_target_pairs={{0,3},{1,2},{2,1},{3,0},{4,7},{5,6},{6,5},{7,4},{8,11},{9,10},{10,... | collective-permute-start | bytes 1548296 | tf_op jit(solution)/shard_map/ppermute | solution.py:400
  92.9 2.9 %collective-permute-done.12 = bf16[3,1,2,48,896]{4,3,2,1,0:T(8,128)(2,1)S(1)} collective-permute-done((bf16[3,1,2,48,896]{4,3,2,1,0:T(8,128)(2,1)S(1)}, bf16[3,1,2,48,896]{4,3,2,1,0:T(8,128)(2,1)S(1)}, u32[]{:S(2)}, u32[]{:S(2)}) %collective-permute-start.12) | collective-permute-done | bytes 516128 | tf_op jit(solution)/shard_map/ppermute | solution.py:400
  95.9 2.9 %collective-permute-start.19 = (bf16[3,192,896]{2,1,0:T(8,128)(2,1)S(1)}, bf16[3,192,896]{2,1,0:T(8,128)(2,1)S(1)}, u32[]{:S(2)}, u32[]{:S(2)}) collective-permute-start(bf16[3,192,896]{2,1,0:T(8,128)(2,1)S(1)} %bitcast.17), channel_id=1, source_target_pairs={{0,12},{1,13},{2,14},{3,15},{4,8},{5,9},{6,10},{7,11},{8,4},{9,5},... | collective-permute-start | bytes 3096584 | tf_op jit(solution)/shard_map/ppermute | solution.py:400
  98.8 1.1 collective-permute-done.18
  100.1 1.5 collective-permute-start.21
  101.5 2.7 %collective-permute-start.20 = (bf16[3,192,896]{2,1,0:T(8,128)(2,1)S(1)}, bf16[3,192,896]{2,1,0:T(8,128)(2,1)S(1)}, u32[]{:S(2)}, u32[]{:S(2)}) collective-permute-start(bf16[3,192,896]{2,1,0:T(8,128)(2,1)S(1)} %bitcast.22), channel_id=1, source_target_pairs={{0,12},{1,13},{2,14},{3,15},{4,8},{5,9},{6,10},{7,11},{8,4},{9,5},... | collective-permute-start | bytes 3096584 | tf_op jit(solution)/shard_map/ppermute | solution.py:400
  104.2 10.9 %collective-permute-done.19.refs_2_ = bf16[3,192,896]{2,1,0:T(8,128)(2,1)S(1)} collective-permute-done((bf16[3,192,896]{2,1,0:T(8,128)(2,1)S(1)}, bf16[3,192,896]{2,1,0:T(8,128)(2,1)S(1)}, u32[]{:S(2)}, u32[]{:S(2)}) %collective-permute-start.19) | collective-permute-done | bytes 1032224 | tf_op jit(solution)/shard_map/ppermute | solution.py:400
  115.3 2.8 %collective-permute-start.24 = (bf16[1,192,896]{2,1,0:T(8,128)(2,1)S(1)}, bf16[1,192,896]{2,1,0:T(8,128)(2,1)S(1)}, u32[]{:S(2)}, u32[]{:S(2)}) collective-permute-start(bf16[1,192,896]{2,1,0:T(8,128)(2,1)S(1)} %slice.117), channel_id=1, source_target_pairs={{0,12},{1,13},{2,14},{3,15},{4,8},{5,9},{6,10},{7,11},{8,4},{9,5},... | collective-permute-start | bytes 1032200 | tf_op jit(solution)/shard_map/ppermute | solution.py:400
  118.2 6.7 %collective-permute-done.21.refs_4_ = bf16[3,192,896]{2,1,0:T(8,128)(2,1)S(1)} collective-permute-done((bf16[3,192,896]{2,1,0:T(8,128)(2,1)S(1)}, bf16[3,192,896]{2,1,0:T(8,128)(2,1)S(1)}, u32[]{:S(2)}, u32[]{:S(2)}) %collective-permute-start.21) | collective-permute-done | bytes 1032224 | tf_op jit(solution)/shard_map/ppermute | solution.py:400
  124.9 1.3 collective-permute-done.20.refs_3_
  126.2 4.5 %first_output.1.early_ref = bf16[8,128,512]{2,1,0:T(8,128)(2,1)S(1)} custom-call(s32[1,576]{1,0:T(1,128)S(1)} %slice.79.rows_ref, s32[8,8,128]{2,1,0:T(8,128)S(1)} %get-tuple-element.47.offs, s32[8,8,128]{2,1,0:T(8,128)S(1)} %get-tuple-element.48.cnts, bf16[1792,512]{1,0:T(8,128)(2,1)S(1)} %get-tuple-element.49.wd_ref, bf16[3,192,896]{2,1,0:T(8,128)(2,1)S(1)} %bitcast.19, ...), custom_call_target="tpu_custom_call" | custom-call | flops 1 | bytes 4096 | tf_op jit(solution)/shard_map/first_output/pallas_call | solution.py:279
  130.7 1.0 last_output.1
  131.7 8.2 %collective-permute-start.25 = (bf16[4,128,512]{2,1,0:T(8,128)(2,1)S(1)}, bf16[4,128,512]{2,1,0:T(8,128)(2,1)S(1)}, u32[]{:S(2)}, u32[]{:S(2)}) collective-permute-start(bf16[4,128,512]{2,1,0:T(8,128)(2,1)S(1)} %get-tuple-element.65), channel_id=1, source_target_pairs={{0,16},{16,0},{32,48},{48,32},{64,80},{80,64},{96,112},{112,96},{1... | collective-permute-start | bytes 1572872 | tf_op jit(solution)/shard_map/ppermute | solution.py:465
  140.0 0.5 collective-permute-start.29
  140.5 2.5 %collective-permute-start.30 = (bf16[2,192,896]{2,1,0:T(8,128)(2,1)S(1)}, bf16[2,192,896]{2,1,0:T(8,128)(2,1)S(1)}, u32[]{:S(2)}, u32[]{:S(2)}) collective-permute-start(bf16[2,192,896]{2,1,0:T(8,128)(2,1)S(1)} %slice.123), channel_id=1, source_target_pairs={{0,12},{1,13},{2,14},{3,15},{4,8},{5,9},{6,10},{7,11},{8,4},{9,5},... | collective-permute-start | bytes 2064392 | tf_op jit(solution)/shard_map/ppermute | solution.py:400
  143.2 0.9 collective-permute-start.26
  144.1 1.8 %collective-permute-start.28 = (bf16[128,512]{1,0:T(8,128)(2,1)S(1)}, bf16[128,512]{1,0:T(8,128)(2,1)S(1)}, u32[]{:S(2)}, u32[]{:S(2)}) collective-permute-start(bf16[128,512]{1,0:T(8,128)(2,1)S(1)} %get-tuple-element.77), channel_id=1, source_target_pairs={{0,96},{16,112},{32,0},{48,16},{64,32},{80,48},{96,64},{112,80},{1... | collective-permute-start | bytes 393224 | tf_op jit(solution)/shard_map/ppermute | solution.py:470
  146.0 0.8 collective-permute-start.27
  146.7 3.4 %collective-permute-done.29.refs_6_ = bf16[2,192,896]{2,1,0:T(8,128)(2,1)S(1)} collective-permute-done((bf16[2,192,896]{2,1,0:T(8,128)(2,1)S(1)}, bf16[2,192,896]{2,1,0:T(8,128)(2,1)S(1)}, u32[]{:S(2)}, u32[]{:S(2)}) %collective-permute-start.29) | collective-permute-done | bytes 688160 | tf_op jit(solution)/shard_map/ppermute | solution.py:400
  150.1 1.7 %collective-permute-done.30.refs_7_ = bf16[2,192,896]{2,1,0:T(8,128)(2,1)S(1)} collective-permute-done((bf16[2,192,896]{2,1,0:T(8,128)(2,1)S(1)}, bf16[2,192,896]{2,1,0:T(8,128)(2,1)S(1)}, u32[]{:S(2)}, u32[]{:S(2)}) %collective-permute-start.30) | collective-permute-done | bytes 688160 | tf_op jit(solution)/shard_map/ppermute | solution.py:400
  151.9 8.8 %gradients.1 = (f32[512,1792]{1,0:T(8,128)}, f32[512,1792]{1,0:T(8,128)}, f32[1792,512]{1,0:T(8,128)}) custom-call(s32[4,14]{1,0:T(4,128)S(1)} %copy-done.6, s32[4,14]{1,0:T(4,128)S(1)} %copy-done.8, s32[14,4]{1,0:T(8,128)S(1)} %copy.13.dm, bf16[512,768]{1,0:T(8,128)(2,1)S(1)} %get-tuple-element.66.xt_ref, bf16[768,512]{1,0:T(8,128)(2,1)S(1)} %get-tuple-element.57.g_ref, ...), custom_call_target="tpu_custom_call" | custom-call | flops 4227858432 | bytes 20971520 | tf_op jit(solution)/shard_map/gradients/pallas_call | solution.py:359
  160.7 0.7 fusion.17
  (56 shorter events, 2.3 us)
Async XLA Ops:
  1.3 0.9 copy-start.3
  2.2 0.9 copy-start.4
  3.1 21.3 %collective-permute-start.3 = (bf16[144,1024]{1,0:T(8,128)(2,1)S(1)}, bf16[144,1024]{1,0:T(8,128)(2,1)S(1)}, u32[]{:S(2)}, u32[]{:S(2)}) collective-permute-start(bf16[144,1024]{1,0:T(8,128)(2,1)S(1)} %pack.1.refs_0_), channel_id=1, source_target_pairs={{0,16},{16,0},{32,48},{48,32},{64,80},{80,64},{96,112},{112,96},{1... | collective-permute-start | bytes 884744 | tf_op jit(solution)/shard_map/ppermute | solution.py:413
  4.6 15.0 %collective-permute-start.2 = (bf16[144,1024]{1,0:T(8,128)(2,1)S(1)}, bf16[144,1024]{1,0:T(8,128)(2,1)S(1)}, u32[]{:S(2)}, u32[]{:S(2)}) collective-permute-start(bf16[144,1024]{1,0:T(8,128)(2,1)S(1)} %pack.1.refs_0_), channel_id=1, source_target_pairs={{0,32},{16,48},{32,64},{48,80},{64,96},{80,112},{96,0},{112,16},{1... | collective-permute-start | bytes 884744 | tf_op jit(solution)/shard_map/ppermute | solution.py:412
  6.3 16.7 %collective-permute-start.1 = (bf16[144,1024]{1,0:T(8,128)(2,1)S(1)}, bf16[144,1024]{1,0:T(8,128)(2,1)S(1)}, u32[]{:S(2)}, u32[]{:S(2)}) collective-permute-start(bf16[144,1024]{1,0:T(8,128)(2,1)S(1)} %pack.1.refs_0_), channel_id=1, source_target_pairs={{0,64},{16,80},{32,96},{48,112},{64,0},{80,16},{96,32},{112,48},{1... | collective-permute-start | bytes 884744 | tf_op jit(solution)/shard_map/ppermute | solution.py:412
  9.7 13.4 %collective-permute-start = (bf16[144,1024]{1,0:T(8,128)(2,1)S(1)}, bf16[144,1024]{1,0:T(8,128)(2,1)S(1)}, u32[]{:S(2)}, u32[]{:S(2)}) collective-permute-start(bf16[144,1024]{1,0:T(8,128)(2,1)S(1)} %pack.1.refs_0_), channel_id=1, source_target_pairs={{0,96},{16,112},{32,0},{48,16},{64,32},{80,48},{96,64},{112,80},{1... | collective-permute-start | bytes 884744 | tf_op jit(solution)/shard_map/ppermute | solution.py:412
  11.1 1.5 copy-start
  12.6 1.5 copy-start.1
  14.1 1.5 copy-start.2
  15.6 0.7 copy-start.5
  16.3 0.7 copy-start.7
  23.1 2.1 %collective-permute-start.4 = (bf16[144,1024]{1,0:T(8,128)(2,1)S(1)}, bf16[144,1024]{1,0:T(8,128)(2,1)S(1)}, u32[]{:S(2)}, u32[]{:S(2)}) collective-permute-start(bf16[144,1024]{1,0:T(8,128)(2,1)S(1)} %collective-permute-done.refs_1_), channel_id=1, source_target_pairs={{0,16},{16,0},{32,48},{48,32},{64,80},{80,64},{96,112},{112,96},{1... | collective-permute-start | bytes 884744 | tf_op jit(solution)/shard_map/ppermute | solution.py:419
  23.9 1.6 %collective-permute-start.5 = (bf16[144,1024]{1,0:T(8,128)(2,1)S(1)}, bf16[144,1024]{1,0:T(8,128)(2,1)S(1)}, u32[]{:S(2)}, u32[]{:S(2)}) collective-permute-start(bf16[144,1024]{1,0:T(8,128)(2,1)S(1)} %collective-permute-done.1.refs_2_), channel_id=1, source_target_pairs={{0,16},{16,0},{32,48},{48,32},{64,80},{80,64},{96,112},{112,96},{1... | collective-permute-start | bytes 884744 | tf_op jit(solution)/shard_map/ppermute | solution.py:419
  23.9 2.0 %collective-permute-start.6 = (bf16[144,1024]{1,0:T(8,128)(2,1)S(1)}, bf16[144,1024]{1,0:T(8,128)(2,1)S(1)}, u32[]{:S(2)}, u32[]{:S(2)}) collective-permute-start(bf16[144,1024]{1,0:T(8,128)(2,1)S(1)} %collective-permute-done.2.refs_3_), channel_id=1, source_target_pairs={{0,16},{16,0},{32,48},{48,32},{64,80},{80,64},{96,112},{112,96},{1... | collective-permute-start | bytes 884744 | tf_op jit(solution)/shard_map/ppermute | solution.py:419
  31.2 13.8 %collective-permute-start.8 = (bf16[3,192,896]{2,1,0:T(8,128)(2,1)S(1)}, bf16[3,192,896]{2,1,0:T(8,128)(2,1)S(1)}, u32[]{:S(2)}, u32[]{:S(2)}) collective-permute-start(bf16[3,192,896]{2,1,0:T(8,128)(2,1)S(1)} %get-tuple-element.54), channel_id=1, source_target_pairs={{0,4},{1,5},{2,6},{3,7},{4,0},{5,1},{6,2},{7,3},{8,12},{9,13},{10,... | collective-permute-start | bytes 3096584 | tf_op jit(solution)/shard_map/ppermute | solution.py:400
  32.6 15.6 %collective-permute-start.14 = (bf16[3,192,896]{2,1,0:T(8,128)(2,1)S(1)}, bf16[3,192,896]{2,1,0:T(8,128)(2,1)S(1)}, u32[]{:S(2)}, u32[]{:S(2)}) collective-permute-start(bf16[3,192,896]{2,1,0:T(8,128)(2,1)S(1)} %get-tuple-element.55), channel_id=1, source_target_pairs={{0,12},{1,13},{2,14},{3,15},{4,8},{5,9},{6,10},{7,11},{8,4},{9,5},... | collective-permute-start | bytes 3096584 | tf_op jit(solution)/shard_map/ppermute | solution.py:400
  40.0 16.1 %collective-permute-start.7 = (bf16[3,192,896]{2,1,0:T(8,128)(2,1)S(1)}, bf16[3,192,896]{2,1,0:T(8,128)(2,1)S(1)}, u32[]{:S(2)}, u32[]{:S(2)}) collective-permute-start(bf16[3,192,896]{2,1,0:T(8,128)(2,1)S(1)} %get-tuple-element.59), channel_id=1, source_target_pairs={{0,4},{1,5},{2,6},{3,7},{4,0},{5,1},{6,2},{7,3},{8,12},{9,13},{10,... | collective-permute-start | bytes 3096584 | tf_op jit(solution)/shard_map/ppermute | solution.py:400
  45.3 15.1 %collective-permute-start.9 = (bf16[3,192,896]{2,1,0:T(8,128)(2,1)S(1)}, bf16[3,192,896]{2,1,0:T(8,128)(2,1)S(1)}, u32[]{:S(2)}, u32[]{:S(2)}) collective-permute-start(bf16[3,192,896]{2,1,0:T(8,128)(2,1)S(1)} %add_convert_fusion.1), channel_id=1, source_target_pairs={{0,12},{1,13},{2,14},{3,15},{4,8},{5,9},{6,10},{7,11},{8,4},{9,5},... | collective-permute-start | bytes 3096584 | tf_op jit(solution)/shard_map/ppermute | solution.py:400
  48.1 23.4 %collective-permute-start.13 = (bf16[3,192,896]{2,1,0:T(8,128)(2,1)S(1)}, bf16[3,192,896]{2,1,0:T(8,128)(2,1)S(1)}, u32[]{:S(2)}, u32[]{:S(2)}) collective-permute-start(bf16[3,192,896]{2,1,0:T(8,128)(2,1)S(1)} %get-tuple-element.62), channel_id=1, source_target_pairs={{0,12},{1,13},{2,14},{3,15},{4,8},{5,9},{6,10},{7,11},{8,4},{9,5},... | collective-permute-start | bytes 3096584 | tf_op jit(solution)/shard_map/ppermute | solution.py:400
  48.5 23.0 %collective-permute-start.15 = (bf16[3,192,896]{2,1,0:T(8,128)(2,1)S(1)}, bf16[3,192,896]{2,1,0:T(8,128)(2,1)S(1)}, u32[]{:S(2)}, u32[]{:S(2)}) collective-permute-start(bf16[3,192,896]{2,1,0:T(8,128)(2,1)S(1)} %add_convert_fusion), channel_id=1, source_target_pairs={{0,4},{1,5},{2,6},{3,7},{4,0},{5,1},{6,2},{7,3},{8,12},{9,13},{10,... | collective-permute-start | bytes 3096584 | tf_op jit(solution)/shard_map/ppermute | solution.py:400
  60.9 13.6 %collective-permute-start.10 = (bf16[3,1,2,48,896]{4,3,2,1,0:T(8,128)(2,1)S(1)}, bf16[3,1,2,48,896]{4,3,2,1,0:T(8,128)(2,1)S(1)}, u32[]{:S(2)}, u32[]{:S(2)}) collective-permute-start(bf16[3,1,2,48,896]{4,3,2,1,0:T(8,128)(2,1)S(1)} %slice.159), channel_id=1, source_target_pairs={{0,1},{1,0},{2,3},{3,2},{4,5},{5,4},{6,7},{7,6},{8,9},{9,8},{10,11... | collective-permute-start | bytes 1548296 | tf_op jit(solution)/shard_map/ppermute | solution.py:400
  71.9 9.5 %collective-permute-start.16 = (bf16[3,2,1,48,896]{4,3,2,1,0:T(8,128)(2,1)S(1)}, bf16[3,2,1,48,896]{4,3,2,1,0:T(8,128)(2,1)S(1)}, u32[]{:S(2)}, u32[]{:S(2)}) collective-permute-start(bf16[3,2,1,48,896]{4,3,2,1,0:T(8,128)(2,1)S(1)} %slice.158), channel_id=1, source_target_pairs={{0,3},{1,2},{2,1},{3,0},{4,7},{5,6},{6,5},{7,4},{8,11},{9,10},{10,... | collective-permute-start | bytes 1548296 | tf_op jit(solution)/shard_map/ppermute | solution.py:400
  74.6 12.4 %collective-permute-start.11 = (bf16[3,1,2,48,896]{4,3,2,1,0:T(8,128)(2,1)S(1)}, bf16[3,1,2,48,896]{4,3,2,1,0:T(8,128)(2,1)S(1)}, u32[]{:S(2)}, u32[]{:S(2)}) collective-permute-start(bf16[3,1,2,48,896]{4,3,2,1,0:T(8,128)(2,1)S(1)} %fusion.1), channel_id=1, source_target_pairs={{0,3},{1,2},{2,1},{3,0},{4,7},{5,6},{6,5},{7,4},{8,11},{9,10},{10,... | collective-permute-start | bytes 1548296 | tf_op jit(solution)/shard_map/ppermute | solution.py:400
  81.6 8.3 %collective-permute-start.17 = (bf16[3,2,1,48,896]{4,3,2,1,0:T(8,128)(2,1)S(1)}, bf16[3,2,1,48,896]{4,3,2,1,0:T(8,128)(2,1)S(1)}, u32[]{:S(2)}, u32[]{:S(2)}) collective-permute-start(bf16[3,2,1,48,896]{4,3,2,1,0:T(8,128)(2,1)S(1)} %fusion), channel_id=1, source_target_pairs={{0,1},{1,0},{2,3},{3,2},{4,5},{5,4},{6,7},{7,6},{8,9},{9,8},{10,11... | collective-permute-start | bytes 1548296 | tf_op jit(solution)/shard_map/ppermute | solution.py:400
  87.4 8.3 %collective-permute-start.12 = (bf16[3,1,2,48,896]{4,3,2,1,0:T(8,128)(2,1)S(1)}, bf16[3,1,2,48,896]{4,3,2,1,0:T(8,128)(2,1)S(1)}, u32[]{:S(2)}, u32[]{:S(2)}) collective-permute-start(bf16[3,1,2,48,896]{4,3,2,1,0:T(8,128)(2,1)S(1)} %pad_maximum_fusion.2), channel_id=1, source_target_pairs={{0,1},{1,0},{2,3},{3,2},{4,5},{5,4},{6,7},{7,6},{8,9},{9,8},{10,11... | collective-permute-start | bytes 1548296 | tf_op jit(solution)/shard_map/ppermute | solution.py:400
  90.3 9.5 %collective-permute-start.18 = (bf16[3,2,1,48,896]{4,3,2,1,0:T(8,128)(2,1)S(1)}, bf16[3,2,1,48,896]{4,3,2,1,0:T(8,128)(2,1)S(1)}, u32[]{:S(2)}, u32[]{:S(2)}) collective-permute-start(bf16[3,2,1,48,896]{4,3,2,1,0:T(8,128)(2,1)S(1)} %pad_maximum_fusion.3), channel_id=1, source_target_pairs={{0,3},{1,2},{2,1},{3,0},{4,7},{5,6},{6,5},{7,4},{8,11},{9,10},{10,... | collective-permute-start | bytes 1548296 | tf_op jit(solution)/shard_map/ppermute | solution.py:400
  95.9 19.2 %collective-permute-start.19 = (bf16[3,192,896]{2,1,0:T(8,128)(2,1)S(1)}, bf16[3,192,896]{2,1,0:T(8,128)(2,1)S(1)}, u32[]{:S(2)}, u32[]{:S(2)}) collective-permute-start(bf16[3,192,896]{2,1,0:T(8,128)(2,1)S(1)} %bitcast.17), channel_id=1, source_target_pairs={{0,12},{1,13},{2,14},{3,15},{4,8},{5,9},{6,10},{7,11},{8,4},{9,5},... | collective-permute-start | bytes 3096584 | tf_op jit(solution)/shard_map/ppermute | solution.py:400
  100.0 15.2 %collective-permute-start.22 = (bf16[3,192,896]{2,1,0:T(8,128)(2,1)S(1)}, bf16[3,192,896]{2,1,0:T(8,128)(2,1)S(1)}, u32[]{:S(2)}, u32[]{:S(2)}) collective-permute-start(bf16[3,192,896]{2,1,0:T(8,128)(2,1)S(1)} %bitcast.21), channel_id=1, source_target_pairs={{0,4},{1,5},{2,6},{3,7},{4,0},{5,1},{6,2},{7,3},{8,12},{9,13},{10,... | collective-permute-start | bytes 3096584 | tf_op jit(solution)/shard_map/ppermute | solution.py:400
  100.1 24.8 %collective-permute-start.21 = (bf16[3,192,896]{2,1,0:T(8,128)(2,1)S(1)}, bf16[3,192,896]{2,1,0:T(8,128)(2,1)S(1)}, u32[]{:S(2)}, u32[]{:S(2)}) collective-permute-start(bf16[3,192,896]{2,1,0:T(8,128)(2,1)S(1)} %bitcast.18), channel_id=1, source_target_pairs={{0,4},{1,5},{2,6},{3,7},{4,0},{5,1},{6,2},{7,3},{8,12},{9,13},{10,... | collective-permute-start | bytes 3096584 | tf_op jit(solution)/shard_map/ppermute | solution.py:400
  101.5 24.6 %collective-permute-start.20 = (bf16[3,192,896]{2,1,0:T(8,128)(2,1)S(1)}, bf16[3,192,896]{2,1,0:T(8,128)(2,1)S(1)}, u32[]{:S(2)}, u32[]{:S(2)}) collective-permute-start(bf16[3,192,896]{2,1,0:T(8,128)(2,1)S(1)} %bitcast.22), channel_id=1, source_target_pairs={{0,12},{1,13},{2,14},{3,15},{4,8},{5,9},{6,10},{7,11},{8,4},{9,5},... | collective-permute-start | bytes 3096584 | tf_op jit(solution)/shard_map/ppermute | solution.py:400
  115.1 15.5 %collective-permute-start.23 = (bf16[1,192,896]{2,1,0:T(8,128)(2,1)S(1)}, bf16[1,192,896]{2,1,0:T(8,128)(2,1)S(1)}, u32[]{:S(2)}, u32[]{:S(2)}) collective-permute-start(bf16[1,192,896]{2,1,0:T(8,128)(2,1)S(1)} %slice.116), channel_id=1, source_target_pairs={{0,4},{1,5},{2,6},{3,7},{4,0},{5,1},{6,2},{7,3},{8,12},{9,13},{10,... | collective-permute-start | bytes 1032200 | tf_op jit(solution)/shard_map/ppermute | solution.py:400
  115.3 15.4 %collective-permute-start.24 = (bf16[1,192,896]{2,1,0:T(8,128)(2,1)S(1)}, bf16[1,192,896]{2,1,0:T(8,128)(2,1)S(1)}, u32[]{:S(2)}, u32[]{:S(2)}) collective-permute-start(bf16[1,192,896]{2,1,0:T(8,128)(2,1)S(1)} %slice.117), channel_id=1, source_target_pairs={{0,12},{1,13},{2,14},{3,15},{4,8},{5,9},{6,10},{7,11},{8,4},{9,5},... | collective-permute-start | bytes 1032200 | tf_op jit(solution)/shard_map/ppermute | solution.py:400
  131.7 11.3 %collective-permute-start.25 = (bf16[4,128,512]{2,1,0:T(8,128)(2,1)S(1)}, bf16[4,128,512]{2,1,0:T(8,128)(2,1)S(1)}, u32[]{:S(2)}, u32[]{:S(2)}) collective-permute-start(bf16[4,128,512]{2,1,0:T(8,128)(2,1)S(1)} %get-tuple-element.65), channel_id=1, source_target_pairs={{0,16},{16,0},{32,48},{48,32},{64,80},{80,64},{96,112},{112,96},{1... | collective-permute-start | bytes 1572872 | tf_op jit(solution)/shard_map/ppermute | solution.py:465
  139.9 11.9 %copy-start.6 = (s32[4,14]{1,0:T(4,128)S(1)}, s32[4,14]{1,0:T(4,128)}, u32[]{:S(2)}) copy-start(s32[4,14]{1,0:T(4,128)} %gm.3) | copy-start | bytes 676
  140.0 11.9 %copy-start.8 = (s32[4,14]{1,0:T(4,128)S(1)}, s32[4,14]{1,0:T(4,128)}, u32[]{:S(2)}) copy-start(s32[4,14]{1,0:T(4,128)} %um.3) | copy-start | bytes 676
  140.0 10.2 %collective-permute-start.29 = (bf16[2,192,896]{2,1,0:T(8,128)(2,1)S(1)}, bf16[2,192,896]{2,1,0:T(8,128)(2,1)S(1)}, u32[]{:S(2)}, u32[]{:S(2)}) collective-permute-start(bf16[2,192,896]{2,1,0:T(8,128)(2,1)S(1)} %slice.122), channel_id=1, source_target_pairs={{0,4},{1,5},{2,6},{3,7},{4,0},{5,1},{6,2},{7,3},{8,12},{9,13},{10,... | collective-permute-start | bytes 2064392 | tf_op jit(solution)/shard_map/ppermute | solution.py:400
  140.5 11.4 %collective-permute-start.30 = (bf16[2,192,896]{2,1,0:T(8,128)(2,1)S(1)}, bf16[2,192,896]{2,1,0:T(8,128)(2,1)S(1)}, u32[]{:S(2)}, u32[]{:S(2)}) collective-permute-start(bf16[2,192,896]{2,1,0:T(8,128)(2,1)S(1)} %slice.123), channel_id=1, source_target_pairs={{0,12},{1,13},{2,14},{3,15},{4,8},{5,9},{6,10},{7,11},{8,4},{9,5},... | collective-permute-start | bytes 2064392 | tf_op jit(solution)/shard_map/ppermute | solution.py:400
  143.2 17.5 %collective-permute-start.26 = (bf16[128,512]{1,0:T(8,128)(2,1)S(1)}, bf16[128,512]{1,0:T(8,128)(2,1)S(1)}, u32[]{:S(2)}, u32[]{:S(2)}) collective-permute-start(bf16[128,512]{1,0:T(8,128)(2,1)S(1)} %get-tuple-element.76), channel_id=1, source_target_pairs={{0,32},{16,48},{32,64},{48,80},{64,96},{80,112},{96,0},{112,16},{1... | collective-permute-start | bytes 393224 | tf_op jit(solution)/shard_map/ppermute | solution.py:470
  144.1 16.6 %collective-permute-start.28 = (bf16[128,512]{1,0:T(8,128)(2,1)S(1)}, bf16[128,512]{1,0:T(8,128)(2,1)S(1)}, u32[]{:S(2)}, u32[]{:S(2)}) collective-permute-start(bf16[128,512]{1,0:T(8,128)(2,1)S(1)} %get-tuple-element.77), channel_id=1, source_target_pairs={{0,96},{16,112},{32,0},{48,16},{64,32},{80,48},{96,64},{112,80},{1... | collective-permute-start | bytes 393224 | tf_op jit(solution)/shard_map/ppermute | solution.py:470
  146.0 14.8 %collective-permute-start.27 = (bf16[128,512]{1,0:T(8,128)(2,1)S(1)}, bf16[128,512]{1,0:T(8,128)(2,1)S(1)}, u32[]{:S(2)}, u32[]{:S(2)}) collective-permute-start(bf16[128,512]{1,0:T(8,128)(2,1)S(1)} %get-tuple-element.78), channel_id=1, source_target_pairs={{0,64},{16,80},{32,96},{48,112},{64,0},{80,16},{96,32},{112,48},{1... | collective-permute-start | bytes 393224 | tf_op jit(solution)/shard_map/ppermute | solution.py:470

commit v5 on v4

--- a/solution.py
+++ b/solution.py
@@ -240,79 +240,73 @@
     )(x, g, wx, wdt)
 
 
-def stacked(refs, which, pieces):
-    return jnp.concatenate(
-        [jnp.concatenate([refs[p * 2 + q][which] for q in SIDES], axis=1) for p in pieces],
-        axis=0,
-    )
-
-
 def picked(rows, offs, cnts, k, slot):
     hit = (rows - offs[k, 0:1, 0:1] == slot) & (slot < cnts[k, 0:1, 0:1])
     return jnp.where(hit, 1.0, 0.0).astype(BF)
 
 
-def first_output_kernel(rows_ref, offs, cnts, wd_ref, *refs):
-    parts, (out_ref, total) = refs[:6], refs[6:]
+def products(lower, upper, shared, w_down):
+    both, single = (lower, upper) if shared == 0 else (upper, lower)
+    result = [
+        jnp.dot(jnp.concatenate(both, axis=1), w_down, preferred_element_type=F32)
+    ]
+    for q in SIDES:
+        result.append(
+            jnp.dot(single[q], w_down[q * BLK : (q + 1) * BLK, :], preferred_element_type=F32)
+        )
+    return result
+
+
+def first_output_kernel(wd_ref, own0, own1, total):
     j = pl.program_id(0)
-    part = jnp.dot(stacked(parts, 0, range(3)), wd_ref[...], preferred_element_type=F32)
+    lower = [ref[0, :CUT, :] for ref in (own0, own1)]
+    upper = [ref[0, CUT:, :] for ref in (own0, own1)]
+    results = products(lower, upper, 0, wd_ref[...])
 
     @pl.when(j == 0)
     def _():
-        total[...] = part
+        for i in range(3):
+            total[i] = results[i]
 
     @pl.when(j > 0)
     def _():
-        total[...] += part
-
-    @pl.when(j == STEPS - 1)
-    def _():
-        mixed = total[...].astype(BF)
-        rows = rows_ref[0:1, :]
-        slot = lax.broadcasted_iota(jnp.int32, (BLK, FIRST), 0)
-        for k in range(8):
-            pick = picked(rows, offs, cnts, k, slot)
-            out_ref[k] = jnp.dot(pick, mixed, preferred_element_type=F32).astype(BF)
-
-
-def first_output(rows, offs, cnts, wd, parts):
+        for i in range(3):
+            total[i] += results[i]
+
+
+def first_output(wd, hidden_own):
     return call(
         first_output_kernel,
         "first_output",
         1,
         1 << 12,
         grid=(STEPS,),
-        out_shape=jax.ShapeDtypeStruct((8, BLK, FEAT), BF),
-        in_specs=[whole((1, FIRST)), whole((8, 8, BLK)), whole((8, 8, BLK))]
-        + [pl.BlockSpec((PAIR, FEAT), lambda j: (j, 0))]
-        + [pl.BlockSpec((1, CUT, BLK), lambda j: (2, 0, j))] * 6,
-        out_specs=whole((8, BLK, FEAT)),
-        scratch_shapes=[pltpu.VMEM((FIRST, FEAT), F32)],
-    )(rows, offs, cnts, wd, *parts)
-
-
-def last_output_kernel(rows_ref, offs, cnts, early_ref, wd_ref, *refs):
-    parts, (near_ref, away_ref) = refs[:2], refs[2:]
-    mixed = None
+        out_shape=jax.ShapeDtypeStruct((3, CUT, FEAT), F32),
+        in_specs=[pl.BlockSpec((PAIR, FEAT), lambda j: (j, 0))]
+        + [pl.BlockSpec((1, 2 * CUT, BLK), lambda j: (0, 0, j))] * 2,
+        out_specs=whole((3, CUT, FEAT)),
+    )(wd, *hidden_own)
+
+
+def last_output_kernel(rows_ref, offs, cnts, early_ref, wd_ref, come0, come1, near_ref, away_ref):
+    totals = None
     for j in range(STEPS):
-        hidden = jnp.concatenate(
-            [parts[q][0, :, j * BLK : (j + 1) * BLK] for q in SIDES], axis=1
-        )
-        part = jnp.dot(
-            hidden, wd_ref[j * PAIR : (j + 1) * PAIR, :], preferred_element_type=F32
-        )
-        mixed = part if mixed is None else mixed + part
-    mixed = mixed.astype(BF)
+        by = slice(j * BLK, (j + 1) * BLK)
+        lower = [ref[0, :CUT, by] for ref in (come0, come1)]
+        upper = [ref[0, CUT:, by] for ref in (come0, come1)]
+        results = products(lower, upper, 1, wd_ref[j * PAIR : (j + 1) * PAIR, :])
+        totals = results if j == 0 else [a + b for a, b in zip(totals, results)]
+    pieces = (early_ref[0], early_ref[1] + totals[2], early_ref[2] + totals[1], totals[0])
+    mixed = jnp.concatenate([piece.astype(BF) for piece in pieces], axis=0)
     rows = rows_ref[0:1, :]
-    slot = lax.broadcasted_iota(jnp.int32, (BLK, LAST), 0)
+    slot = lax.broadcasted_iota(jnp.int32, (BLK, LIVE), 0)
     for k in range(8):
         pick = picked(rows, offs, cnts, k, slot)
-        late = jnp.dot(pick, mixed, preferred_element_type=F32)
         target = near_ref if k < 4 else away_ref
-        target[k % 4] = (early_ref[k].astype(F32) + late).astype(BF)
-
-
-def last_output(rows, offs, cnts, early, wd, parts):
+        target[k % 4] = jnp.dot(pick, mixed, preferred_element_type=F32).astype(BF)
+
+
+def last_output(rows, offs, cnts, early, wd, hidden_come):
     return call(
         last_output_kernel,
         "last_output",
@@ -321,62 +315,77 @@
         grid=(1,),
         out_shape=(jax.ShapeDtypeStruct((4, BLK, FEAT), BF),) * 2,
         in_specs=[
-            whole((1, LAST)),
+            whole((1, LIVE)),
             whole((8, 8, BLK)),
             whole((8, 8, BLK)),
-            whole((8, BLK, FEAT)),
+            whole((3, CUT, FEAT)),
             whole((UNITS, FEAT)),
         ]
-        + [whole((1, CUT, HALF))] * 2,
+        + [whole((1, 2 * CUT, HALF))] * 2,
         out_specs=(whole((4, BLK, FEAT)),) * 2,
-    )(rows, offs, cnts, early, wd, *parts)
-
-
-def grad_kernel(gm, um, dm, xt_ref, g_ref, *refs):
-    parts, lasts, last_hidden = refs[:6], refs[6:8], refs[8:10]
-    gate_out, up_out, down_out = refs[10:]
+    )(rows, offs, cnts, early, wd, *hidden_come)
+
+
+def all_rows(owns, comes, which):
+    left = jnp.concatenate([owns[0][which], comes[0][which]], axis=0)
+    right = jnp.concatenate(
+        [ref[which, i : i + CUT] for i in (0, CUT) for ref in (owns[1], comes[1])], axis=0
+    )
+    return jnp.concatenate([left, right], axis=1)
+
+
+def down_kernel(dm, g_ref, own0, own1, come0, come1, down_out):
     j = pl.program_id(0)
-
-    def rows(which):
-        late = stacked(lasts, which, (0,)) if which < 2 else stacked(last_hidden, 0, (0,))
-        return jnp.concatenate([stacked(parts, which, range(3)), late], axis=0)
-
-    xt = xt_ref[...]
-    gate = jnp.dot(xt, rows(0), preferred_element_type=F32)
-    up = jnp.dot(xt, rows(1), preferred_element_type=F32)
     down = lax.dot_general(
-        rows(2), g_ref[...], (((0,), (0,)), ((), ())), preferred_element_type=F32
+        all_rows((own0, own1), (come0, come1), 0),
+        g_ref[...],
+        (((0,), (0,)), ((), ())),
+        preferred_element_type=F32,
     )
     for r in range(4):
         for b in range(2):
             at, by = slice(r * BLK, (r + 1) * BLK), slice(b * BLK, (b + 1) * BLK)
-            gate_out[at, by] = kept(gm, r, 2 * j + b, gate[at, by])
-            up_out[at, by] = kept(um, r, 2 * j + b, up[at, by])
             down_out[by, at] = kept(dm, 2 * j + b, r, down[by, at])
 
 
-def gradients(gm, um, dm, xt, g, parts, lasts, last_hidden):
+def down_gradient(dm, g, parts):
+    return call(
+        down_kernel,
+        "down_gradient",
+        1,
+        1 << 12,
+        grid=(STEPS,),
+        out_shape=jax.ShapeDtypeStruct((UNITS, FEAT), F32),
+        in_specs=[smem(), whole((LIVE, FEAT))]
+        + [pl.BlockSpec((1, 2 * CUT, BLK), lambda j: (0, 0, j))] * 4,
+        out_specs=pl.BlockSpec((PAIR, FEAT), lambda j: (j, 0)),
+    )(dm, g, *parts)
+
+
+def grad_kernel(gm, um, xt_ref, own0, own1, come0, come1, gate_out, up_out):
+    j = pl.program_id(0)
+    xt = xt_ref[...]
+    for which, mask, target in ((0, gm, gate_out), (1, um, up_out)):
+        rows = all_rows((own0, own1), (come0, come1), which)
+        grad = jnp.dot(xt, rows, preferred_element_type=F32)
+        for r in range(4):
+            for b in range(2):
+                at, by = slice(r * BLK, (r + 1) * BLK), slice(b * BLK, (b + 1) * BLK)
+                target[at, by] = kept(mask, r, 2 * j + b, grad[at, by])
+
+
+def gradients(gm, um, xt, parts):
     return call(
         grad_kernel,
         "gradients",
-        2 * LIVE * FEAT * 3 * UNITS,
-        20 << 20,
+        2 * LIVE * FEAT * 2 * UNITS,
+        13 << 20,
         grid=(STEPS,),
-        out_shape=(
-            jax.ShapeDtypeStruct((FEAT, UNITS), F32),
-            jax.ShapeDtypeStruct((FEAT, UNITS), F32),
-            jax.ShapeDtypeStruct((UNITS, FEAT), F32),
-        ),
-        in_specs=[smem(), smem(), smem(), whole((FEAT, LIVE)), whole((LIVE, FEAT))]
-        + [pl.BlockSpec((3, CUT, BLK), lambda j: (0, 0, j))] * 6
-        + [pl.BlockSpec((2, CUT, BLK), lambda j: (0, 0, j))] * 2
-        + [pl.BlockSpec((1, CUT, BLK), lambda j: (0, 0, j))] * 2,
-        out_specs=(
-            pl.BlockSpec((FEAT, PAIR), lambda j: (0, j)),
-            pl.BlockSpec((FEAT, PAIR), lambda j: (0, j)),
-            pl.BlockSpec((PAIR, FEAT), lambda j: (j, 0)),
-        ),
-    )(gm, um, dm, xt, g, *parts, *lasts, *last_hidden)
+        out_shape=(jax.ShapeDtypeStruct((FEAT, UNITS), F32),) * 2,
+        in_specs=[smem(), smem(), whole((FEAT, LIVE))]
+        + [pl.BlockSpec((2, 2 * CUT, BLK), lambda j: (0, 0, j))] * 4,
+        out_specs=(pl.BlockSpec((FEAT, PAIR), lambda j: (0, j)),) * 2,
+    )(gm, um, xt, *parts)
 
 
 def split(value, axis):
@@ -426,10 +435,13 @@
     zero = [late[q] for q in SIDES]
     side = [[late[2 * (2 - ROUNDS[q][n][0]) + q] for q in SIDES] for n in range(2)]
     come_rest = exchange(side[0], 0)
+    come_early = lax.optimization_barrier(come_early)
     second = [
         (side[1][q].astype(F32) + come_early[q].astype(F32)).astype(BF) for q in SIDES
     ]
     come_second = exchange(second, 1)
+    *come_rest, last0, last1 = lax.optimization_barrier((*come_rest, *come_second))
+    come_second = [last0, last1]
     keep, send = [None] * 2, [None] * 2
     for q in SIDES:
         total = (
@@ -452,26 +464,23 @@
         for q in SIDES
     ]
     near = exchange(held, 1)
-    far = exchange(held, 0)
-    last_hidden = exchange([near[q][2:] for q in SIDES], 0)
-    lasts = exchange([near[q][:2] for q in SIDES], 0)
-    parts = list(held)
-    for piece in (1, 2):
-        for q in SIDES:
-            parts.append(near[q] if 2 - ROUNDS[q][1][0] == piece else far[q])
-
-    begun = first_output(rows_along[:, :FIRST], offs, cnts, wd, parts)
-    mine, away = last_output(rows_along[:, FIRST:], offs, cnts, begun, wd, last_hidden)
+    hidden_own = [jnp.concatenate([held[q][2:], near[q][2:]], axis=1) for q in SIDES]
+    derived_own = [jnp.concatenate([held[q][:2], near[q][:2]], axis=1) for q in SIDES]
+    hidden_come = exchange(hidden_own, 0)
+    derived_come = exchange(derived_own, 0)
+
+    begun = first_output(wd, hidden_own)
+    mine, away = last_output(rows_along, offs, cnts, begun, wd, hidden_come)
     other = lax.ppermute(away, "col", shift(0, 1))
+    down_grad = down_gradient(down_mask, g, hidden_own + hidden_come)
+    other, down_grad = lax.optimization_barrier((other, down_grad))
     summed = mine.astype(F32) + other.astype(F32)
     terms = [summed[k].astype(BF) for k in range(4)]
-    mixed = terms[0].astype(F32)
-    for dz in (1, 2, 3):
-        mixed += lax.ppermute(terms[dz], "col", shift(dz, 0)).astype(F32)
+    arrived = [lax.ppermute(terms[dz], "col", shift(dz, 0)) for dz in (1, 2, 3)]
+    gate_grad, up_grad = gradients(gate_mask, up_mask, xt, derived_own + derived_come)
+    *arrived, gate_grad, up_grad = lax.optimization_barrier((*arrived, gate_grad, up_grad))
+    mixed = sum((term.astype(F32) for term in arrived), terms[0].astype(F32))
     output = jnp.where(live, mixed, jnp.zeros_like(mixed)).astype(BF)
-    gate_grad, up_grad, down_grad = gradients(
-        gate_mask, up_mask, down_mask, xt, g, parts, lasts, last_hidden
-    )
     return (output, gate_grad, up_grad, down_grad)
 
 

time: 163 us -> 156 us (0.957)
  starting transfers between devices: 47.7 us -> 38 us
  Pallas kernels: 27.5 us -> 31.7 us
  waiting for transfers between devices: 72.3 us -> 70.3 us
    ppermute x20 -> x18, starting transfers between devices: 27.4 us -> 19.2 us  [exchange(): lax.ppermute(values[q], ('col', 'dp'), partners(ROUNDS[q][number][1]))]
    pallas_call x1 -> x2, Pallas kernels: 8.84 us -> 12.9 us  [the longest x1 7.23 us: gradients(): call(grad_kernel, 'gradients', 2 * LIVE * FEAT * 2 * UNITS, 13 << 20, gri...]
    ppermute x20 -> x18, waiting for transfers between devices: 67.3 us -> 63.9 us  [exchange(): lax.ppermute(values[q], ('col', 'dp'), partners(ROUNDS[q][number][1]))]
  transfers between devices with their start and end apart: 31 -> 29, of which waited for: 18 -> 19; matrix products, arithmetic and copies ran while one was open for 2% -> 2% of each run, Pallas kernels for 13% -> 17%
where the time goes in v5:
time: 156 us; the launch traced here: 155 us
  waiting for transfers between devices  70.3 us (45%)
  starting transfers between devices  38 us (24%)
  Pallas kernels  31.7 us (20%)
  local copies, waits for them, and re-layouts  9 us (6%)
  other arithmetic  3.89 us (2%)
  between operations  1.63 us (1%)
    ppermute x18, waiting for transfers between devices, exchange(): lax.ppermute(values[q], ('col', 'dp'), partners(ROUNDS[q][number][1]))  63.9 us
    ppermute x18, starting transfers between devices, exchange(): lax.ppermute(values[q], ('col', 'dp'), partners(ROUNDS[q][number][1]))  19.2 us
    unnamed x19, local copies, waits for them, and re-layouts  8.44 us
    pallas_call x2, Pallas kernels, partials(): call(functools.partial(partial_kernel, start, pieces), 'partials', 2 * co...  8.1 us
    ppermute x1, starting transfers between devices, on_device(): other = lax.ppermute(away, 'col', shift(0, 1))  7.33 us
    pallas_call x1, Pallas kernels, gradients(): call(grad_kernel, 'gradients', 2 * LIVE * FEAT * 2 * UNITS, 13 << 20, gri...  7.23 us
    ppermute x3, starting transfers between devices, on_device(): lax.ppermute(own, 'col', shift(-dz, 0))  5.77 us
    pallas_call x1, Pallas kernels, down_gradient(): call(down_kernel, 'down_gradient', 1, 1 << 12, grid=(STEPS,), out_shape=j...  5.67 us
  transfers between devices with their start and end apart: 29, of which 19 were waited for; matrix products, arithmetic and copies ran while one was open for 2% of the time, Pallas kernels for 17%

profile of v5, /device:TPU:1, one launch (start us, length us, event | category | flops | bytes accessed | tf_op | source)
XLA Modules:
  0.0 154.6 jit_solution(317636918064407708)
XLA Ops:
  1.3 0.9 copy-done.3
  2.2 0.9 copy-done.4
  3.1 1.5 collective-permute-start.3
  4.6 1.7 %collective-permute-start.2 = (bf16[144,1024]{1,0:T(8,128)(2,1)S(1)}, bf16[144,1024]{1,0:T(8,128)(2,1)S(1)}, u32[]{:S(2)}, u32[]{:S(2)}) collective-permute-start(bf16[144,1024]{1,0:T(8,128)(2,1)S(1)} %pack.1.refs_0_), channel_id=1, source_target_pairs={{0,32},{16,48},{32,64},{48,80},{64,96},{80,112},{96,0},{112,16},{1... | collective-permute-start | bytes 884744 | tf_op jit(solution)/shard_map/ppermute | solution.py:421
  6.3 3.3 %collective-permute-start.1 = (bf16[144,1024]{1,0:T(8,128)(2,1)S(1)}, bf16[144,1024]{1,0:T(8,128)(2,1)S(1)}, u32[]{:S(2)}, u32[]{:S(2)}) collective-permute-start(bf16[144,1024]{1,0:T(8,128)(2,1)S(1)} %pack.1.refs_0_), channel_id=1, source_target_pairs={{0,64},{16,80},{32,96},{48,112},{64,0},{80,16},{96,32},{112,48},{1... | collective-permute-start | bytes 884744 | tf_op jit(solution)/shard_map/ppermute | solution.py:421
  9.7 0.7 collective-permute-start
  10.4 0.8 copy.13.dm
  11.2 1.5 copy-done
  12.7 1.5 copy-done.1
  14.2 1.5 copy-done.2
  15.7 0.7 copy-done.5
  16.3 0.7 copy-done.7
  17.0 2.4 %prepare.1 = (bf16[7,512,512]{2,1,0:T(8,128)(2,1)S(1)}, bf16[7,512,256]{2,1,0:T(8,128)(2,1)S(1)}, bf16[1792,512]{1,0:T(8,128)(2,1)S(1)}) custom-call(s32[4,14]{1,0:T(4,128)S(1)} %copy-done.5, s32[4,14]{1,0:T(4,128)S(1)} %copy-done.7, s32[14,4]{1,0:T(8,128)S(1)} %copy.13.dm, bf16[512,1792]{1,0:T(8,128)(2,1)S(1)} %copy-done, bf16[512,1792]{1,0:T(8,128)(2,1)S(1)} %copy-done.1, ...), custom_call_target="tpu_custom_call" | custom-call | bytes 13631488 | tf_op jit(solution)/shard_map/prepare/pallas_call | solution.py:138
  19.5 0.2 fusion.10.rows_ref
  19.7 3.4 %collective-permute-done.1.refs_2_ = bf16[144,1024]{1,0:T(8,128)(2,1)S(1)} collective-permute-done((bf16[144,1024]{1,0:T(8,128)(2,1)S(1)}, bf16[144,1024]{1,0:T(8,128)(2,1)S(1)}, u32[]{:S(2)}, u32[]{:S(2)}) %collective-permute-start.1) | collective-permute-done | bytes 294944 | tf_op jit(solution)/shard_map/ppermute | solution.py:421
  23.1 0.9 collective-permute-start.4
  23.9 0.5 collective-permute-start.6
  24.4 0.7 collective-permute-done.4.refs_5_
  25.1 0.4 collective-permute-done.5.refs_6_
  25.6 0.4 collective-permute-done.6.refs_7_
  26.0 2.6 %compact.1 = (bf16[768,512]{1,0:T(8,128)(2,1)S(1)}, bf16[768,512]{1,0:T(8,128)(2,1)S(1)}, bf16[512,768]{1,0:T(8,128)(2,1)S(1)}, s32[8,8,128]{2,1,0:T(8,128)S(1)}, s32[8,8,128]{2,1,0:T(8,128)S(1)}) custom-call(s32[8]{0:T(128)S(1)} %fusion.23.shard, s32[768,1]{1,0:T(8,128)S(1)} %fusion.10.rows_ref, bf16[144,1024]{1,0:T(8,128)(2,1)S(1)} %pack.1.refs_0_, ...), custom_call_target="tpu_custom_call" | custom-call | flops 1610612736 | bytes 5242880 | tf_op jit(solution)/shard_map/compact/pallas_call | solution.py:194
  28.6 2.7 %partials.2 = (bf16[3,192,896]{2,1,0:T(8,128)(2,1)S(1)}, bf16[3,192,896]{2,1,0:T(8,128)(2,1)S(1)}) custom-call(bf16[768,512]{1,0:T(8,128)(2,1)S(1)} %get-tuple-element.68.x_ref, bf16[768,512]{1,0:T(8,128)(2,1)S(1)} %get-tuple-element.69.g_ref, bf16[7,512,512]{2,1,0:T(8,128)(2,1)S(1)} %get-tuple-element.64.wx_ref, ...), custom_call_target="tpu_custom_call" | custom-call | flops 1056964608 | bytes 7340032 | tf_op jit(solution)/shard_map/partials/pallas_call | solution.py:226
  31.2 1.4 collective-permute-start.9
  32.6 1.9 %collective-permute-start.10 = (bf16[3,192,896]{2,1,0:T(8,128)(2,1)S(1)}, bf16[3,192,896]{2,1,0:T(8,128)(2,1)S(1)}, u32[]{:S(2)}, u32[]{:S(2)}) collective-permute-start(bf16[3,192,896]{2,1,0:T(8,128)(2,1)S(1)} %get-tuple-element.67), channel_id=1, source_target_pairs={{0,12},{1,13},{2,14},{3,15},{4,8},{5,9},{6,10},{7,11},{8,4},{9,5},... | collective-permute-start | bytes 3096584 | tf_op jit(solution)/shard_map/ppermute | solution.py:409
  34.5 5.4 %partials.3 = (bf16[3,192,896]{2,1,0:T(8,128)(2,1)S(1)}, bf16[3,192,896]{2,1,0:T(8,128)(2,1)S(1)}, bf16[3,192,896]{2,1,0:T(8,128)(2,1)S(1)}, bf16[3,192,896]{2,1...) custom-call(bf16[768,512]{1,0:T(8,128)(2,1)S(1)} %get-tuple-element.68.x_ref, ...), custom_call_target="tpu_custom_call" | custom-call | flops 3170893824 | bytes 7340032 | tf_op jit(solution)/shard_map/partials/pallas_call | solution.py:226
  40.0 0.5 collective-permute-start.7
  40.4 0.6 collective-permute-start.8
  41.0 4.0 %collective-permute-done.9 = bf16[3,192,896]{2,1,0:T(8,128)(2,1)S(1)} collective-permute-done((bf16[3,192,896]{2,1,0:T(8,128)(2,1)S(1)}, bf16[3,192,896]{2,1,0:T(8,128)(2,1)S(1)}, u32[]{:S(2)}, u32[]{:S(2)}) %collective-permute-start.9) | collective-permute-done | bytes 1032224 | tf_op jit(solution)/shard_map/ppermute | solution.py:409
  45.1 2.5 %collective-permute-done.10 = bf16[3,192,896]{2,1,0:T(8,128)(2,1)S(1)} collective-permute-done((bf16[3,192,896]{2,1,0:T(8,128)(2,1)S(1)}, bf16[3,192,896]{2,1,0:T(8,128)(2,1)S(1)}, u32[]{:S(2)}, u32[]{:S(2)}) %collective-permute-start.10) | collective-permute-done | bytes 1032224 | tf_op jit(solution)/shard_map/ppermute | solution.py:409
  47.6 0.2 add_convert_fusion
  47.9 0.3 add_convert_fusion.1
  48.2 2.0 %collective-permute-start.11 = (bf16[3,192,896]{2,1,0:T(8,128)(2,1)S(1)}, bf16[3,192,896]{2,1,0:T(8,128)(2,1)S(1)}, u32[]{:S(2)}, u32[]{:S(2)}) collective-permute-start(bf16[3,192,896]{2,1,0:T(8,128)(2,1)S(1)} %add_convert_fusion.1), channel_id=1, source_target_pairs={{0,12},{1,13},{2,14},{3,15},{4,8},{5,9},{6,10},{7,11},{8,4},{9,5},... | collective-permute-start | bytes 3096584 | tf_op jit(solution)/shard_map/ppermute | solution.py:409
  50.2 6.0 %collective-permute-done.7 = bf16[3,192,896]{2,1,0:T(8,128)(2,1)S(1)} collective-permute-done((bf16[3,192,896]{2,1,0:T(8,128)(2,1)S(1)}, bf16[3,192,896]{2,1,0:T(8,128)(2,1)S(1)}, u32[]{:S(2)}, u32[]{:S(2)}) %collective-permute-start.7) | collective-permute-done | bytes 1032224 | tf_op jit(solution)/shard_map/ppermute | solution.py:409
  56.1 2.5 %collective-permute-done.8 = bf16[3,192,896]{2,1,0:T(8,128)(2,1)S(1)} collective-permute-done((bf16[3,192,896]{2,1,0:T(8,128)(2,1)S(1)}, bf16[3,192,896]{2,1,0:T(8,128)(2,1)S(1)}, u32[]{:S(2)}, u32[]{:S(2)}) %collective-permute-start.8) | collective-permute-done | bytes 1032224 | tf_op jit(solution)/shard_map/ppermute | solution.py:409
  58.6 8.6 %collective-permute-done.12 = bf16[3,192,896]{2,1,0:T(8,128)(2,1)S(1)} collective-permute-done((bf16[3,192,896]{2,1,0:T(8,128)(2,1)S(1)}, bf16[3,192,896]{2,1,0:T(8,128)(2,1)S(1)}, u32[]{:S(2)}, u32[]{:S(2)}) %collective-permute-start.12) | collective-permute-done | bytes 1032224 | tf_op jit(solution)/shard_map/ppermute | solution.py:409
  67.2 2.5 %collective-permute-done.11 = bf16[3,192,896]{2,1,0:T(8,128)(2,1)S(1)} collective-permute-done((bf16[3,192,896]{2,1,0:T(8,128)(2,1)S(1)}, bf16[3,192,896]{2,1,0:T(8,128)(2,1)S(1)}, u32[]{:S(2)}, u32[]{:S(2)}) %collective-permute-start.11) | collective-permute-done | bytes 1032224 | tf_op jit(solution)/shard_map/ppermute | solution.py:409
  69.7 0.7 convert_add_fusion
  70.4 1.0 collective-permute-start.13
  71.5 1.9 %collective-permute-start.17 = (bf16[3,2,1,48,896]{4,3,2,1,0:T(8,128)(2,1)S(1)}, bf16[3,2,1,48,896]{4,3,2,1,0:T(8,128)(2,1)S(1)}, u32[]{:S(2)}, u32[]{:S(2)}) collective-permute-start(bf16[3,2,1,48,896]{4,3,2,1,0:T(8,128)(2,1)S(1)} %slice.186), channel_id=1, source_target_pairs={{0,3},{1,2},{2,1},{3,0},{4,7},{5,6},{6,5},{7,4},{8,11},{9,10},{10,... | collective-permute-start | bytes 1548296 | tf_op jit(solution)/shard_map/ppermute | solution.py:409
  73.4 5.4 %collective-permute-done.13 = bf16[3,1,2,48,896]{4,3,2,1,0:T(8,128)(2,1)S(1)} collective-permute-done((bf16[3,1,2,48,896]{4,3,2,1,0:T(8,128)(2,1)S(1)}, bf16[3,1,2,48,896]{4,3,2,1,0:T(8,128)(2,1)S(1)}, u32[]{:S(2)}, u32[]{:S(2)}) %collective-permute-start.13) | collective-permute-done | bytes 516128 | tf_op jit(solution)/shard_map/ppermute | solution.py:409
  78.9 2.6 %collective-permute-start.14 = (bf16[3,1,2,48,896]{4,3,2,1,0:T(8,128)(2,1)S(1)}, bf16[3,1,2,48,896]{4,3,2,1,0:T(8,128)(2,1)S(1)}, u32[]{:S(2)}, u32[]{:S(2)}) collective-permute-start(bf16[3,1,2,48,896]{4,3,2,1,0:T(8,128)(2,1)S(1)} %fusion.1), channel_id=1, source_target_pairs={{0,3},{1,2},{2,1},{3,0},{4,7},{5,6},{6,5},{7,4},{8,11},{9,10},{10,... | collective-permute-start | bytes 1548296 | tf_op jit(solution)/shard_map/ppermute | solution.py:409
  81.7 6.7 %collective-permute-done.14 = bf16[3,1,2,48,896]{4,3,2,1,0:T(8,128)(2,1)S(1)} collective-permute-done((bf16[3,1,2,48,896]{4,3,2,1,0:T(8,128)(2,1)S(1)}, bf16[3,1,2,48,896]{4,3,2,1,0:T(8,128)(2,1)S(1)}, u32[]{:S(2)}, u32[]{:S(2)}) %collective-permute-start.14) | collective-permute-done | bytes 516128 | tf_op jit(solution)/shard_map/ppermute | solution.py:409
  88.6 0.2 multiply_convert_fusion.5
  89.0 0.9 collective-permute-done.18
  90.1 0.2 multiply_convert_fusion.2
  90.3 1.6 %collective-permute-start.19 = (bf16[3,2,1,48,896]{4,3,2,1,0:T(8,128)(2,1)S(1)}, bf16[3,2,1,48,896]{4,3,2,1,0:T(8,128)(2,1)S(1)}, u32[]{:S(2)}, u32[]{:S(2)}) collective-permute-start(bf16[3,2,1,48,896]{4,3,2,1,0:T(8,128)(2,1)S(1)} %pad_maximum_fusion.7), channel_id=1, source_target_pairs={{0,3},{1,2},{2,1},{3,0},{4,7},{5,6},{6,5},{7,4},{8,11},{9,10},{10,... | collective-permute-start | bytes 1548296 | tf_op jit(solution)/shard_map/ppermute | solution.py:409
  92.0 5.2 %collective-permute-done.15 = bf16[3,1,2,48,896]{4,3,2,1,0:T(8,128)(2,1)S(1)} collective-permute-done((bf16[3,1,2,48,896]{4,3,2,1,0:T(8,128)(2,1)S(1)}, bf16[3,1,2,48,896]{4,3,2,1,0:T(8,128)(2,1)S(1)}, u32[]{:S(2)}, u32[]{:S(2)}) %collective-permute-start.15) | collective-permute-done | bytes 516128 | tf_op jit(solution)/shard_map/ppermute | solution.py:409
  97.3 2.2 %collective-permute-start.16 = (bf16[3,192,896]{2,1,0:T(8,128)(2,1)S(1)}, bf16[3,192,896]{2,1,0:T(8,128)(2,1)S(1)}, u32[]{:S(2)}, u32[]{:S(2)}) collective-permute-start(bf16[3,192,896]{2,1,0:T(8,128)(2,1)S(1)} %bitcast.25), channel_id=1, source_target_pairs={{0,12},{1,13},{2,14},{3,15},{4,8},{5,9},{6,10},{7,11},{8,4},{9,5},... | collective-permute-start | bytes 3096584 | tf_op jit(solution)/shard_map/ppermute | solution.py:409
  99.5 0.4 collective-permute-done.19
  100.2 14.9 %collective-permute-done.16 = bf16[3,192,896]{2,1,0:T(8,128)(2,1)S(1)} collective-permute-done((bf16[3,192,896]{2,1,0:T(8,128)(2,1)S(1)}, bf16[3,192,896]{2,1,0:T(8,128)(2,1)S(1)}, u32[]{:S(2)}, u32[]{:S(2)}) %collective-permute-start.16) | collective-permute-done | bytes 1032224 | tf_op jit(solution)/shard_map/ppermute | solution.py:409
  115.4 1.8 %collective-permute-start.22 = (bf16[1,384,896]{2,1,0:T(8,128)(2,1)S(1)}, bf16[1,384,896]{2,1,0:T(8,128)(2,1)S(1)}, u32[]{:S(2)}, u32[]{:S(2)}) collective-permute-start(bf16[1,384,896]{2,1,0:T(8,128)(2,1)S(1)} %pad_maximum_fusion.5.own1), channel_id=1, source_target_pairs={{0,12},{1,13},{2,14},{3,15},{4,8},{5,9},{6,10},{7,11},{8,4},{9,5},... | collective-permute-start | bytes 2064392 | tf_op jit(solution)/shard_map/ppermute | solution.py:409
  117.5 1.0 collective-permute-start.28
  118.7 0.3 collective-permute-start.27
  119.0 3.4 %first_output.1.early_ref = f32[3,192,512]{2,1,0:T(8,128)S(1)} custom-call(bf16[1792,512]{1,0:T(8,128)(2,1)S(1)} %get-tuple-element.61.wd_ref, bf16[1,384,896]{2,1,0:T(8,128)(2,1)S(1)} %pad_maximum_fusion.4.own0, bf16[1,384,896]{2,1,0:T(8,128)(2,1)S(1)} %pad_maximum_fusion.5.own1), custom_call_target="tpu_custom_call" | custom-call | flops 1 | bytes 4096 | tf_op jit(solution)/shard_map/first_output/pallas_call | solution.py:278
  122.4 2.9 %collective-permute-done.21.come0 = bf16[1,384,896]{2,1,0:T(8,128)(2,1)S(1)} collective-permute-done((bf16[1,384,896]{2,1,0:T(8,128)(2,1)S(1)}, bf16[1,384,896]{2,1,0:T(8,128)(2,1)S(1)}, u32[]{:S(2)}, u32[]{:S(2)}) %collective-permute-start.21) | collective-permute-done | bytes 688160 | tf_op jit(solution)/shard_map/ppermute | solution.py:409
  125.3 1.4 collective-permute-done.22.come1
  126.7 2.3 %last_output.1 = (bf16[4,128,512]{2,1,0:T(8,128)(2,1)S(1)}, bf16[4,128,512]{2,1,0:T(8,128)(2,1)S(1)}) custom-call(s32[1,768]{1,0:T(1,128)S(1)} %fusion.18.rows_ref, s32[8,8,128]{2,1,0:T(8,128)S(1)} %get-tuple-element.59.offs, s32[8,8,128]{2,1,0:T(8,128)S(1)} %get-tuple-element.60.cnts, f32[3,192,512]{2,1,0:T(8,128)S(1)} %first_output.1.early_ref, ...), custom_call_target="tpu_custom_call" | custom-call | flops 1 | bytes 4096 | tf_op jit(solution)/shard_map/last_output/pallas_call | solution.py:310
  129.0 7.3 %collective-permute-start.23 = (bf16[4,128,512]{2,1,0:T(8,128)(2,1)S(1)}, bf16[4,128,512]{2,1,0:T(8,128)(2,1)S(1)}, u32[]{:S(2)}, u32[]{:S(2)}) collective-permute-start(bf16[4,128,512]{2,1,0:T(8,128)(2,1)S(1)} %get-tuple-element.83), channel_id=1, source_target_pairs={{0,16},{16,0},{32,48},{48,32},{64,80},{80,64},{96,112},{112,96},{1... | collective-permute-start | bytes 1572872 | tf_op jit(solution)/shard_map/ppermute | solution.py:474
  136.4 5.7 %down_gradient.1 = f32[1792,512]{1,0:T(8,128)} custom-call(s32[14,4]{1,0:T(8,128)S(1)} %copy.13.dm, bf16[768,512]{1,0:T(8,128)(2,1)S(1)} %get-tuple-element.69.g_ref, bf16[1,384,896]{2,1,0:T(8,128)(2,1)S(1)} %pad_maximum_fusion.4.own0, bf16[1,384,896]{2,1,0:T(8,128)(2,1)S(1)} %pad_maximum_fusion.5.own1, ...), custom_call_target="tpu_custom_call" | custom-call | flops 1 | bytes 4096 | tf_op jit(solution)/shard_map/down_gradient/pallas_call | solution.py:352
  142.2 1.9 %collective-permute-start.26 = (bf16[128,512]{1,0:T(8,128)(2,1)S(1)}, bf16[128,512]{1,0:T(8,128)(2,1)S(1)}, u32[]{:S(2)}, u32[]{:S(2)}) collective-permute-start(bf16[128,512]{1,0:T(8,128)(2,1)S(1)} %get-tuple-element.100), channel_id=1, source_target_pairs={{0,96},{16,112},{32,0},{48,16},{64,32},{80,48},{96,64},{112,80},{1... | collective-permute-start | bytes 393224 | tf_op jit(solution)/shard_map/ppermute | solution.py:479
  144.1 0.9 collective-permute-start.25
  145.1 7.2 %gradients.1 = (f32[512,1792]{1,0:T(8,128)}, f32[512,1792]{1,0:T(8,128)}) custom-call(s32[4,14]{1,0:T(4,128)S(1)} %copy-done.6, s32[4,14]{1,0:T(4,128)S(1)} %copy-done.8, bf16[512,768]{1,0:T(8,128)(2,1)S(1)} %get-tuple-element.85.xt_ref, bf16[2,384,896]{2,1,0:T(8,128)(2,1)S(1)} %pad_maximum_fusion.own0, bf16[2,384,896]{2,1,0:T(8,128)(2,1)S(1)} %pad_maximum_fusion.1.own1, ...), custom_call_target="tpu_custom_call" | custom-call | flops 2818572288 | bytes 13631488 | tf_op jit(solution)/shard_map/gradients/pallas_call | solution.py:378
  152.3 1.5 collective-permute-done.24
  153.8 0.7 fusion.17
  (58 shorter events, 2.6 us)
Async XLA Ops:
  1.3 0.9 copy-start.3
  2.2 0.9 copy-start.4
  3.1 21.3 %collective-permute-start.3 = (bf16[144,1024]{1,0:T(8,128)(2,1)S(1)}, bf16[144,1024]{1,0:T(8,128)(2,1)S(1)}, u32[]{:S(2)}, u32[]{:S(2)}) collective-permute-start(bf16[144,1024]{1,0:T(8,128)(2,1)S(1)} %pack.1.refs_0_), channel_id=1, source_target_pairs={{0,16},{16,0},{32,48},{48,32},{64,80},{80,64},{96,112},{112,96},{1... | collective-permute-start | bytes 884744 | tf_op jit(solution)/shard_map/ppermute | solution.py:422
  4.6 15.0 %collective-permute-start.2 = (bf16[144,1024]{1,0:T(8,128)(2,1)S(1)}, bf16[144,1024]{1,0:T(8,128)(2,1)S(1)}, u32[]{:S(2)}, u32[]{:S(2)}) collective-permute-start(bf16[144,1024]{1,0:T(8,128)(2,1)S(1)} %pack.1.refs_0_), channel_id=1, source_target_pairs={{0,32},{16,48},{32,64},{48,80},{64,96},{80,112},{96,0},{112,16},{1... | collective-permute-start | bytes 884744 | tf_op jit(solution)/shard_map/ppermute | solution.py:421
  6.3 16.7 %collective-permute-start.1 = (bf16[144,1024]{1,0:T(8,128)(2,1)S(1)}, bf16[144,1024]{1,0:T(8,128)(2,1)S(1)}, u32[]{:S(2)}, u32[]{:S(2)}) collective-permute-start(bf16[144,1024]{1,0:T(8,128)(2,1)S(1)} %pack.1.refs_0_), channel_id=1, source_target_pairs={{0,64},{16,80},{32,96},{48,112},{64,0},{80,16},{96,32},{112,48},{1... | collective-permute-start | bytes 884744 | tf_op jit(solution)/shard_map/ppermute | solution.py:421
  9.7 13.4 %collective-permute-start = (bf16[144,1024]{1,0:T(8,128)(2,1)S(1)}, bf16[144,1024]{1,0:T(8,128)(2,1)S(1)}, u32[]{:S(2)}, u32[]{:S(2)}) collective-permute-start(bf16[144,1024]{1,0:T(8,128)(2,1)S(1)} %pack.1.refs_0_), channel_id=1, source_target_pairs={{0,96},{16,112},{32,0},{48,16},{64,32},{80,48},{96,64},{112,80},{1... | collective-permute-start | bytes 884744 | tf_op jit(solution)/shard_map/ppermute | solution.py:421
  11.1 1.5 copy-start
  12.6 1.5 copy-start.1
  14.1 1.5 copy-start.2
  15.6 0.7 copy-start.5
  16.3 0.7 copy-start.7
  23.1 2.1 %collective-permute-start.4 = (bf16[144,1024]{1,0:T(8,128)(2,1)S(1)}, bf16[144,1024]{1,0:T(8,128)(2,1)S(1)}, u32[]{:S(2)}, u32[]{:S(2)}) collective-permute-start(bf16[144,1024]{1,0:T(8,128)(2,1)S(1)} %collective-permute-done.refs_1_), channel_id=1, source_target_pairs={{0,16},{16,0},{32,48},{48,32},{64,80},{80,64},{96,112},{112,96},{1... | collective-permute-start | bytes 884744 | tf_op jit(solution)/shard_map/ppermute | solution.py:428
  23.9 1.6 %collective-permute-start.5 = (bf16[144,1024]{1,0:T(8,128)(2,1)S(1)}, bf16[144,1024]{1,0:T(8,128)(2,1)S(1)}, u32[]{:S(2)}, u32[]{:S(2)}) collective-permute-start(bf16[144,1024]{1,0:T(8,128)(2,1)S(1)} %collective-permute-done.1.refs_2_), channel_id=1, source_target_pairs={{0,16},{16,0},{32,48},{48,32},{64,80},{80,64},{96,112},{112,96},{1... | collective-permute-start | bytes 884744 | tf_op jit(solution)/shard_map/ppermute | solution.py:428
  23.9 2.0 %collective-permute-start.6 = (bf16[144,1024]{1,0:T(8,128)(2,1)S(1)}, bf16[144,1024]{1,0:T(8,128)(2,1)S(1)}, u32[]{:S(2)}, u32[]{:S(2)}) collective-permute-start(bf16[144,1024]{1,0:T(8,128)(2,1)S(1)} %collective-permute-done.2.refs_3_), channel_id=1, source_target_pairs={{0,16},{16,0},{32,48},{48,32},{64,80},{80,64},{96,112},{112,96},{1... | collective-permute-start | bytes 884744 | tf_op jit(solution)/shard_map/ppermute | solution.py:428
  31.2 13.8 %collective-permute-start.9 = (bf16[3,192,896]{2,1,0:T(8,128)(2,1)S(1)}, bf16[3,192,896]{2,1,0:T(8,128)(2,1)S(1)}, u32[]{:S(2)}, u32[]{:S(2)}) collective-permute-start(bf16[3,192,896]{2,1,0:T(8,128)(2,1)S(1)} %get-tuple-element.66), channel_id=1, source_target_pairs={{0,4},{1,5},{2,6},{3,7},{4,0},{5,1},{6,2},{7,3},{8,12},{9,13},{10,... | collective-permute-start | bytes 3096584 | tf_op jit(solution)/shard_map/ppermute | solution.py:409
  32.6 15.0 %collective-permute-start.10 = (bf16[3,192,896]{2,1,0:T(8,128)(2,1)S(1)}, bf16[3,192,896]{2,1,0:T(8,128)(2,1)S(1)}, u32[]{:S(2)}, u32[]{:S(2)}) collective-permute-start(bf16[3,192,896]{2,1,0:T(8,128)(2,1)S(1)} %get-tuple-element.67), channel_id=1, source_target_pairs={{0,12},{1,13},{2,14},{3,15},{4,8},{5,9},{6,10},{7,11},{8,4},{9,5},... | collective-permute-start | bytes 3096584 | tf_op jit(solution)/shard_map/ppermute | solution.py:409
  40.0 16.2 %collective-permute-start.7 = (bf16[3,192,896]{2,1,0:T(8,128)(2,1)S(1)}, bf16[3,192,896]{2,1,0:T(8,128)(2,1)S(1)}, u32[]{:S(2)}, u32[]{:S(2)}) collective-permute-start(bf16[3,192,896]{2,1,0:T(8,128)(2,1)S(1)} %get-tuple-element.71), channel_id=1, source_target_pairs={{0,4},{1,5},{2,6},{3,7},{4,0},{5,1},{6,2},{7,3},{8,12},{9,13},{10,... | collective-permute-start | bytes 3096584 | tf_op jit(solution)/shard_map/ppermute | solution.py:409
  40.4 18.2 %collective-permute-start.8 = (bf16[3,192,896]{2,1,0:T(8,128)(2,1)S(1)}, bf16[3,192,896]{2,1,0:T(8,128)(2,1)S(1)}, u32[]{:S(2)}, u32[]{:S(2)}) collective-permute-start(bf16[3,192,896]{2,1,0:T(8,128)(2,1)S(1)} %get-tuple-element.72), channel_id=1, source_target_pairs={{0,12},{1,13},{2,14},{3,15},{4,8},{5,9},{6,10},{7,11},{8,4},{9,5},... | collective-permute-start | bytes 3096584 | tf_op jit(solution)/shard_map/ppermute | solution.py:409
  47.8 19.4 %collective-permute-start.12 = (bf16[3,192,896]{2,1,0:T(8,128)(2,1)S(1)}, bf16[3,192,896]{2,1,0:T(8,128)(2,1)S(1)}, u32[]{:S(2)}, u32[]{:S(2)}) collective-permute-start(bf16[3,192,896]{2,1,0:T(8,128)(2,1)S(1)} %add_convert_fusion), channel_id=1, source_target_pairs={{0,4},{1,5},{2,6},{3,7},{4,0},{5,1},{6,2},{7,3},{8,12},{9,13},{10,... | collective-permute-start | bytes 3096584 | tf_op jit(solution)/shard_map/ppermute | solution.py:409
  48.2 21.5 %collective-permute-start.11 = (bf16[3,192,896]{2,1,0:T(8,128)(2,1)S(1)}, bf16[3,192,896]{2,1,0:T(8,128)(2,1)S(1)}, u32[]{:S(2)}, u32[]{:S(2)}) collective-permute-start(bf16[3,192,896]{2,1,0:T(8,128)(2,1)S(1)} %add_convert_fusion.1), channel_id=1, source_target_pairs={{0,12},{1,13},{2,14},{3,15},{4,8},{5,9},{6,10},{7,11},{8,4},{9,5},... | collective-permute-start | bytes 3096584 | tf_op jit(solution)/shard_map/ppermute | solution.py:409
  70.4 8.3 %collective-permute-start.13 = (bf16[3,1,2,48,896]{4,3,2,1,0:T(8,128)(2,1)S(1)}, bf16[3,1,2,48,896]{4,3,2,1,0:T(8,128)(2,1)S(1)}, u32[]{:S(2)}, u32[]{:S(2)}) collective-permute-start(bf16[3,1,2,48,896]{4,3,2,1,0:T(8,128)(2,1)S(1)} %slice.187), channel_id=1, source_target_pairs={{0,1},{1,0},{2,3},{3,2},{4,5},{5,4},{6,7},{7,6},{8,9},{9,8},{10,11... | collective-permute-start | bytes 1548296 | tf_op jit(solution)/shard_map/ppermute | solution.py:409
  71.5 10.0 %collective-permute-start.17 = (bf16[3,2,1,48,896]{4,3,2,1,0:T(8,128)(2,1)S(1)}, bf16[3,2,1,48,896]{4,3,2,1,0:T(8,128)(2,1)S(1)}, u32[]{:S(2)}, u32[]{:S(2)}) collective-permute-start(bf16[3,2,1,48,896]{4,3,2,1,0:T(8,128)(2,1)S(1)} %slice.186), channel_id=1, source_target_pairs={{0,3},{1,2},{2,1},{3,0},{4,7},{5,6},{6,5},{7,4},{8,11},{9,10},{10,... | collective-permute-start | bytes 1548296 | tf_op jit(solution)/shard_map/ppermute | solution.py:409
  78.9 9.5 %collective-permute-start.14 = (bf16[3,1,2,48,896]{4,3,2,1,0:T(8,128)(2,1)S(1)}, bf16[3,1,2,48,896]{4,3,2,1,0:T(8,128)(2,1)S(1)}, u32[]{:S(2)}, u32[]{:S(2)}) collective-permute-start(bf16[3,1,2,48,896]{4,3,2,1,0:T(8,128)(2,1)S(1)} %fusion.1), channel_id=1, source_target_pairs={{0,3},{1,2},{2,1},{3,0},{4,7},{5,6},{6,5},{7,4},{8,11},{9,10},{10,... | collective-permute-start | bytes 1548296 | tf_op jit(solution)/shard_map/ppermute | solution.py:409
  81.6 8.3 %collective-permute-start.18 = (bf16[3,2,1,48,896]{4,3,2,1,0:T(8,128)(2,1)S(1)}, bf16[3,2,1,48,896]{4,3,2,1,0:T(8,128)(2,1)S(1)}, u32[]{:S(2)}, u32[]{:S(2)}) collective-permute-start(bf16[3,2,1,48,896]{4,3,2,1,0:T(8,128)(2,1)S(1)} %fusion), channel_id=1, source_target_pairs={{0,1},{1,0},{2,3},{3,2},{4,5},{5,4},{6,7},{7,6},{8,9},{9,8},{10,11... | collective-permute-start | bytes 1548296 | tf_op jit(solution)/shard_map/ppermute | solution.py:409
  88.9 8.3 %collective-permute-start.15 = (bf16[3,1,2,48,896]{4,3,2,1,0:T(8,128)(2,1)S(1)}, bf16[3,1,2,48,896]{4,3,2,1,0:T(8,128)(2,1)S(1)}, u32[]{:S(2)}, u32[]{:S(2)}) collective-permute-start(bf16[3,1,2,48,896]{4,3,2,1,0:T(8,128)(2,1)S(1)} %pad_maximum_fusion.6), channel_id=1, source_target_pairs={{0,1},{1,0},{2,3},{3,2},{4,5},{5,4},{6,7},{7,6},{8,9},{9,8},{10,11... | collective-permute-start | bytes 1548296 | tf_op jit(solution)/shard_map/ppermute | solution.py:409
  90.3 9.5 %collective-permute-start.19 = (bf16[3,2,1,48,896]{4,3,2,1,0:T(8,128)(2,1)S(1)}, bf16[3,2,1,48,896]{4,3,2,1,0:T(8,128)(2,1)S(1)}, u32[]{:S(2)}, u32[]{:S(2)}) collective-permute-start(bf16[3,2,1,48,896]{4,3,2,1,0:T(8,128)(2,1)S(1)} %pad_maximum_fusion.7), channel_id=1, source_target_pairs={{0,3},{1,2},{2,1},{3,0},{4,7},{5,6},{6,5},{7,4},{8,11},{9,10},{10,... | collective-permute-start | bytes 1548296 | tf_op jit(solution)/shard_map/ppermute | solution.py:409
  97.3 17.7 %collective-permute-start.16 = (bf16[3,192,896]{2,1,0:T(8,128)(2,1)S(1)}, bf16[3,192,896]{2,1,0:T(8,128)(2,1)S(1)}, u32[]{:S(2)}, u32[]{:S(2)}) collective-permute-start(bf16[3,192,896]{2,1,0:T(8,128)(2,1)S(1)} %bitcast.25), channel_id=1, source_target_pairs={{0,12},{1,13},{2,14},{3,15},{4,8},{5,9},{6,10},{7,11},{8,4},{9,5},... | collective-permute-start | bytes 3096584 | tf_op jit(solution)/shard_map/ppermute | solution.py:409
  100.0 15.2 %collective-permute-start.20 = (bf16[3,192,896]{2,1,0:T(8,128)(2,1)S(1)}, bf16[3,192,896]{2,1,0:T(8,128)(2,1)S(1)}, u32[]{:S(2)}, u32[]{:S(2)}) collective-permute-start(bf16[3,192,896]{2,1,0:T(8,128)(2,1)S(1)} %bitcast.26), channel_id=1, source_target_pairs={{0,4},{1,5},{2,6},{3,7},{4,0},{5,1},{6,2},{7,3},{8,12},{9,13},{10,... | collective-permute-start | bytes 3096584 | tf_op jit(solution)/shard_map/ppermute | solution.py:409
  115.2 10.2 %collective-permute-start.21 = (bf16[1,384,896]{2,1,0:T(8,128)(2,1)S(1)}, bf16[1,384,896]{2,1,0:T(8,128)(2,1)S(1)}, u32[]{:S(2)}, u32[]{:S(2)}) collective-permute-start(bf16[1,384,896]{2,1,0:T(8,128)(2,1)S(1)} %pad_maximum_fusion.4.own0), channel_id=1, source_target_pairs={{0,4},{1,5},{2,6},{3,7},{4,0},{5,1},{6,2},{7,3},{8,12},{9,13},{10,... | collective-permute-start | bytes 2064392 | tf_op jit(solution)/shard_map/ppermute | solution.py:409
  115.4 11.4 %collective-permute-start.22 = (bf16[1,384,896]{2,1,0:T(8,128)(2,1)S(1)}, bf16[1,384,896]{2,1,0:T(8,128)(2,1)S(1)}, u32[]{:S(2)}, u32[]{:S(2)}) collective-permute-start(bf16[1,384,896]{2,1,0:T(8,128)(2,1)S(1)} %pad_maximum_fusion.5.own1), channel_id=1, source_target_pairs={{0,12},{1,13},{2,14},{3,15},{4,8},{5,9},{6,10},{7,11},{8,4},{9,5},... | collective-permute-start | bytes 2064392 | tf_op jit(solution)/shard_map/ppermute | solution.py:409
  117.5 27.6 %collective-permute-start.28 = (bf16[2,384,896]{2,1,0:T(8,128)(2,1)S(1)}, bf16[2,384,896]{2,1,0:T(8,128)(2,1)S(1)}, u32[]{:S(2)}, u32[]{:S(2)}) collective-permute-start(bf16[2,384,896]{2,1,0:T(8,128)(2,1)S(1)} %pad_maximum_fusion.1.own1), channel_id=1, source_target_pairs={{0,12},{1,13},{2,14},{3,15},{4,8},{5,9},{6,10},{7,11},{8,4},{9,5},... | collective-permute-start | bytes 4128776 | tf_op jit(solution)/shard_map/ppermute | solution.py:409
  118.7 26.4 %collective-permute-start.27 = (bf16[2,384,896]{2,1,0:T(8,128)(2,1)S(1)}, bf16[2,384,896]{2,1,0:T(8,128)(2,1)S(1)}, u32[]{:S(2)}, u32[]{:S(2)}) collective-permute-start(bf16[2,384,896]{2,1,0:T(8,128)(2,1)S(1)} %pad_maximum_fusion.own0), channel_id=1, source_target_pairs={{0,4},{1,5},{2,6},{3,7},{4,0},{5,1},{6,2},{7,3},{8,12},{9,13},{10,... | collective-permute-start | bytes 4128776 | tf_op jit(solution)/shard_map/ppermute | solution.py:409
  129.0 13.0 %collective-permute-start.23 = (bf16[4,128,512]{2,1,0:T(8,128)(2,1)S(1)}, bf16[4,128,512]{2,1,0:T(8,128)(2,1)S(1)}, u32[]{:S(2)}, u32[]{:S(2)}) collective-permute-start(bf16[4,128,512]{2,1,0:T(8,128)(2,1)S(1)} %get-tuple-element.83), channel_id=1, source_target_pairs={{0,16},{16,0},{32,48},{48,32},{64,80},{80,64},{96,112},{112,96},{1... | collective-permute-start | bytes 1572872 | tf_op jit(solution)/shard_map/ppermute | solution.py:474
  142.0 3.1 %copy-start.6 = (s32[4,14]{1,0:T(4,128)S(1)}, s32[4,14]{1,0:T(4,128)}, u32[]{:S(2)}) copy-start(s32[4,14]{1,0:T(4,128)} %gm.3) | copy-start | bytes 676
  142.0 3.1 %copy-start.8 = (s32[4,14]{1,0:T(4,128)S(1)}, s32[4,14]{1,0:T(4,128)}, u32[]{:S(2)}) copy-start(s32[4,14]{1,0:T(4,128)} %um.3) | copy-start | bytes 676
  142.2 10.1 %collective-permute-start.26 = (bf16[128,512]{1,0:T(8,128)(2,1)S(1)}, bf16[128,512]{1,0:T(8,128)(2,1)S(1)}, u32[]{:S(2)}, u32[]{:S(2)}) collective-permute-start(bf16[128,512]{1,0:T(8,128)(2,1)S(1)} %get-tuple-element.100), channel_id=1, source_target_pairs={{0,96},{16,112},{32,0},{48,16},{64,32},{80,48},{96,64},{112,80},{1... | collective-permute-start | bytes 393224 | tf_op jit(solution)/shard_map/ppermute | solution.py:479
  144.1 8.3 %collective-permute-start.25 = (bf16[128,512]{1,0:T(8,128)(2,1)S(1)}, bf16[128,512]{1,0:T(8,128)(2,1)S(1)}, u32[]{:S(2)}, u32[]{:S(2)}) collective-permute-start(bf16[128,512]{1,0:T(8,128)(2,1)S(1)} %get-tuple-element.101), channel_id=1, source_target_pairs={{0,64},{16,80},{32,96},{48,112},{64,0},{80,16},{96,32},{112,48},{1... | collective-permute-start | bytes 393224 | tf_op jit(solution)/shard_map/ppermute | solution.py:479
  144.9 8.9 %collective-permute-start.24 = (bf16[128,512]{1,0:T(8,128)(2,1)S(1)}, bf16[128,512]{1,0:T(8,128)(2,1)S(1)}, u32[]{:S(2)}, u32[]{:S(2)}) collective-permute-start(bf16[128,512]{1,0:T(8,128)(2,1)S(1)} %get-tuple-element.102), channel_id=1, source_target_pairs={{0,32},{16,48},{32,64},{48,80},{64,96},{80,112},{96,0},{112,16},{1... | collective-permute-start | bytes 393224 | tf_op jit(solution)/shard_map/ppermute | solution.py:479

commit v6 on v5

--- a/solution.py
+++ b/solution.py
@@ -88,35 +88,33 @@
     )
 
 
-def pack_kernel(tok_ref, cot_ref, count_ref, out_ref):
-    out_ref[:BLK, :FEAT] = tok_ref[...]
-    out_ref[:BLK, FEAT:] = cot_ref[...]
-    count = jnp.full((PAD - BLK, 2 * FEAT), count_ref[0], jnp.int32)
+def pack_kernel(tok_ref, count_ref, out_ref):
+    out_ref[:BLK, :] = tok_ref[...]
+    count = jnp.full((PAD - BLK, FEAT), count_ref[0], jnp.int32)
     out_ref[BLK:, :] = count.astype(F32).astype(BF)
 
 
-def pack(tokens, cotangent, counts):
+def pack(tokens, counts):
     return call(
         pack_kernel,
         "pack",
         0,
-        1 << 19,
-        out_shape=jax.ShapeDtypeStruct((PAD, 2 * FEAT), BF),
+        1 << 18,
+        out_shape=jax.ShapeDtypeStruct((PAD, FEAT), BF),
         grid=(1,),
-        in_specs=[whole((BLK, FEAT)), whole((BLK, FEAT)), smem()],
-        out_specs=whole((PAD, 2 * FEAT)),
-    )(tokens, cotangent, counts)
-
-
-def prepare_kernel(gm, um, dm, wg, wu, wd, wx_ref, wdt_ref, wd_ref):
+        in_specs=[whole((BLK, FEAT)), smem()],
+        out_specs=whole((PAD, FEAT)),
+    )(tokens, counts)
+
+
+def prepare_kernel(gm, um, dm, wg, wu, wd, wg_ref, wu_ref, wdt_ref, wd_ref):
     j = pl.program_id(0)
-    for which, (mask, ref) in enumerate(((gm, wg), (um, wu))):
+    for mask, ref, target in ((gm, wg, wg_ref), (um, wu, wu_ref)):
         for r in range(4):
             for b in range(2):
                 at = slice(r * BLK, (r + 1) * BLK)
-                wx_ref[0, at, which * PAIR + b * BLK : which * PAIR + (b + 1) * BLK] = kept(
-                    mask, r, 2 * j + b, ref[at, b * BLK : (b + 1) * BLK]
-                )
+                by = slice(b * BLK, (b + 1) * BLK)
+                target[0, at, by] = kept(mask, r, 2 * j + b, ref[at, by])
     down = jnp.concatenate(
         [
             jnp.concatenate(
@@ -142,7 +140,8 @@
         13 << 20,
         grid=(STEPS,),
         out_shape=(
-            jax.ShapeDtypeStruct((STEPS, FEAT, 2 * PAIR), BF),
+            jax.ShapeDtypeStruct((STEPS, FEAT, PAIR), BF),
+            jax.ShapeDtypeStruct((STEPS, FEAT, PAIR), BF),
             jax.ShapeDtypeStruct((STEPS, FEAT, PAIR), BF),
             jax.ShapeDtypeStruct((UNITS, FEAT), BF),
         ),
@@ -155,94 +154,126 @@
             pl.BlockSpec((PAIR, FEAT), lambda j: (j, 0)),
         ],
         out_specs=(
-            pl.BlockSpec((1, FEAT, 2 * PAIR), lambda j: (j, 0, 0)),
+            pl.BlockSpec((1, FEAT, PAIR), lambda j: (j, 0, 0)),
+            pl.BlockSpec((1, FEAT, PAIR), lambda j: (j, 0, 0)),
             pl.BlockSpec((1, FEAT, PAIR), lambda j: (j, 0, 0)),
             pl.BlockSpec((PAIR, FEAT), lambda j: (j, 0)),
         ),
     )(gm, um, dm, wg, wu, wd)
 
 
-def compact_kernel(shard, rows_ref, *refs):
-    sources, (x_ref, g_ref, xt_ref, offs_ref, cnts_ref) = refs[:8], refs[8:]
-    rows = rows_ref[...]
+def picked(rows, offset, count, slot):
+    hit = (rows - offset == slot) & (slot < count)
+    return jnp.where(hit, 1.0, 0.0).astype(BF)
+
+
+def gathered_rows(rows, offs, cnts, sources):
     slot = lax.broadcasted_iota(jnp.int32, (LIVE, BLK), 1)
+    total = None
+    for k in range(0, 8, 2):
+        pick = jnp.concatenate(
+            [picked(rows, offs[i], cnts[i], slot) for i in (k, k + 1)], axis=1
+        )
+        source = jnp.concatenate([sources[i][:BLK, :] for i in (k, k + 1)], axis=0)
+        part = jnp.dot(pick, source, preferred_element_type=F32)
+        total = part if total is None else total + part
+    return total
+
+
+def compact_tokens_kernel(shard, rows_ref, *refs):
+    sources, (x_ref, xt_ref, offs_ref, cnts_ref) = refs[:8], refs[8:]
     cnts = [ref[BLK : BLK + 1, 0:1].astype(F32).astype(jnp.int32) for ref in sources]
-    total = None
-    for pair in range(4):
-        picks = []
-        for k in (2 * pair, 2 * pair + 1):
-            offset = jnp.zeros((1, 1), jnp.int32)
-            for other in range(8):
-                if other != k:
-                    offset += jnp.where(shard[other] < shard[k], cnts[other], 0)
-            offs_ref[k] = jnp.broadcast_to(offset, (8, BLK))
-            cnts_ref[k] = jnp.broadcast_to(cnts[k], (8, BLK))
-            hit = (rows - offset == slot) & (slot < cnts[k])
-            picks.append(jnp.where(hit, 1.0, 0.0).astype(BF))
-        source = jnp.concatenate(
-            [sources[2 * pair][:BLK, :], sources[2 * pair + 1][:BLK, :]], axis=0
-        )
-        part = jnp.dot(jnp.concatenate(picks, axis=1), source, preferred_element_type=F32)
-        total = part if total is None else total + part
-    x_ref[...] = total[:, :FEAT].astype(BF)
-    g_ref[...] = total[:, FEAT:].astype(BF)
-    xt_ref[...] = total[:, :FEAT].T.astype(BF)
-
-
-def compact(shard, rows, sources):
+    offs = []
+    for k in range(8):
+        offset = jnp.zeros((1, 1), jnp.int32)
+        for other in range(8):
+            if other != k:
+                offset += jnp.where(shard[other] < shard[k], cnts[other], 0)
+        offs.append(offset)
+        offs_ref[k] = jnp.broadcast_to(offset, (8, BLK))
+        cnts_ref[k] = jnp.broadcast_to(cnts[k], (8, BLK))
+    total = gathered_rows(rows_ref[...], offs, cnts, sources)
+    x_ref[...] = total.astype(BF)
+    xt_ref[...] = total.T.astype(BF)
+
+
+def compact_tokens(shard, rows, sources):
     vmem = pl.BlockSpec(memory_space=pltpu.VMEM)
     return call(
-        compact_kernel,
-        "compact",
-        2 * LIVE * SLOTS * SLOTS,
-        5 << 20,
+        compact_tokens_kernel,
+        "compact_tokens",
+        2 * LIVE * SLOTS * FEAT,
+        3 << 20,
         out_shape=(
-            jax.ShapeDtypeStruct((LIVE, FEAT), BF),
             jax.ShapeDtypeStruct((LIVE, FEAT), BF),
             jax.ShapeDtypeStruct((FEAT, LIVE), BF),
             jax.ShapeDtypeStruct((8, 8, BLK), jnp.int32),
             jax.ShapeDtypeStruct((8, 8, BLK), jnp.int32),
         ),
         in_specs=[smem(), vmem] + [vmem] * 8,
-        out_specs=(vmem,) * 5,
+        out_specs=(vmem,) * 4,
     )(shard, rows, *sources)
 
 
-def partial_kernel(start, pieces, x_ref, g_ref, wx_ref, wdt_ref, *outs):
-    count = pieces * CUT
-    x, g = x_ref[start : start + count, :], g_ref[start : start + count, :]
-    both = jnp.dot(x, wx_ref[0], preferred_element_type=F32)
-    back = jnp.dot(g, wdt_ref[0], preferred_element_type=F32)
-    for which, result in enumerate((both[:, :PAIR], both[:, PAIR:], back)):
-        for piece in range(pieces):
+def compact_kernel(rows_ref, offs, cnts, *refs):
+    sources, g_ref = refs[:8], refs[8]
+    starts = [offs[k, 0:1, 0:1] for k in range(8)]
+    sizes = [cnts[k, 0:1, 0:1] for k in range(8)]
+    g_ref[...] = gathered_rows(rows_ref[...], starts, sizes, sources).astype(BF)
+
+
+def compact_cotangent(rows, offs, cnts, sources):
+    vmem = pl.BlockSpec(memory_space=pltpu.VMEM)
+    return call(
+        compact_kernel,
+        "compact_cotangent",
+        1,
+        1 << 12,
+        out_shape=jax.ShapeDtypeStruct((LIVE, FEAT), BF),
+        in_specs=[vmem] * 11,
+        out_specs=vmem,
+    )(rows, offs, cnts, *sources)
+
+
+SENT = ((2, 3), (1, 3))
+KEPT = ((0, 1), (0, 2))
+
+
+def partial_kernel(pieces, planes, *refs):
+    operands, weights = refs[:planes], refs[planes : 2 * planes]
+    outs, rows = refs[2 * planes : 2 * planes + 2], refs[2 * planes + 2]
+
+    @pl.when(pl.program_id(0) == 0)
+    def _():
+        for which, ref in enumerate(operands):
             for q in SIDES:
-                outs[piece * 2 + q][which] = result[
-                    piece * CUT : (piece + 1) * CUT, q * BLK : (q + 1) * BLK
-                ].astype(BF)
-
-
-def partials(start, pieces, x, g, wx, wdt):
-    count = pieces * CUT
-    return call(
-        functools.partial(partial_kernel, start, pieces),
+                for i, piece in enumerate(pieces[q]):
+                    to, at = slice(i * CUT, (i + 1) * CUT), slice(piece * CUT, (piece + 1) * CUT)
+                    rows[2 * which + q, to, :] = ref[at, :]
+
+    for which, w_ref in enumerate(weights):
+        for q, out in enumerate(outs):
+            out[which] = jnp.dot(
+                rows[2 * which + q],
+                w_ref[0, :, q * BLK : (q + 1) * BLK],
+                preferred_element_type=F32,
+            ).astype(BF)
+
+
+def partials(pieces, operands, weights):
+    planes = len(operands)
+    return call(
+        functools.partial(partial_kernel, pieces, planes),
         "partials",
-        2 * count * FEAT * 3 * UNITS,
-        7 << 20,
+        1,
+        1 << 12,
         grid=(STEPS,),
-        out_shape=(jax.ShapeDtypeStruct((3, CUT, HALF), BF),) * (2 * pieces),
-        in_specs=[
-            whole((LIVE, FEAT)),
-            whole((LIVE, FEAT)),
-            pl.BlockSpec((1, FEAT, 2 * PAIR), lambda j: (j, 0, 0)),
-            pl.BlockSpec((1, FEAT, PAIR), lambda j: (j, 0, 0)),
-        ],
-        out_specs=(pl.BlockSpec((3, CUT, BLK), lambda j: (0, 0, j)),) * (2 * pieces),
-    )(x, g, wx, wdt)
-
-
-def picked(rows, offs, cnts, k, slot):
-    hit = (rows - offs[k, 0:1, 0:1] == slot) & (slot < cnts[k, 0:1, 0:1])
-    return jnp.where(hit, 1.0, 0.0).astype(BF)
+        out_shape=(jax.ShapeDtypeStruct((planes, 2 * CUT, HALF), BF),) * 2,
+        in_specs=[whole((LIVE, FEAT))] * planes
+        + [pl.BlockSpec((1, FEAT, PAIR), lambda j: (j, 0, 0))] * planes,
+        out_specs=(pl.BlockSpec((planes, 2 * CUT, BLK), lambda j: (0, 0, j)),) * 2,
+        scratch_shapes=[pltpu.VMEM((2 * planes, 2 * CUT, FEAT), BF)],
+    )(*operands, *weights)
 
 
 def products(lower, upper, shared, w_down):
@@ -301,7 +332,7 @@
     rows = rows_ref[0:1, :]
     slot = lax.broadcasted_iota(jnp.int32, (BLK, LIVE), 0)
     for k in range(8):
-        pick = picked(rows, offs, cnts, k, slot)
+        pick = picked(rows, offs[k, 0:1, 0:1], cnts[k, 0:1, 0:1], slot)
         target = near_ref if k < 4 else away_ref
         target[k % 4] = jnp.dot(pick, mixed, preferred_element_type=F32).astype(BF)
 
@@ -394,20 +425,53 @@
     return lower, upper
 
 
-def activate(total):
-    gate, upward, back = total[0], total[1], total[2]
+def activate(gate, upward, back):
     sigma = jax.nn.sigmoid(gate)
     active = gate * sigma
-    hidden = (active * upward).astype(BF)
     d_gate = (back * upward * sigma * (1.0 + gate * (1.0 - sigma))).astype(BF)
     d_up = (back * active).astype(BF)
-    return jnp.stack([d_gate, d_up, hidden])
+    hidden = (active * upward).astype(BF)
+    return hidden[None], jnp.stack([d_gate, d_up])
 
 
 def exchange(values, number):
-    return [
+    come = [
         lax.ppermute(values[q], ("col", "dp"), partners(ROUNDS[q][number][1])) for q in SIDES
     ]
+    return lax.optimization_barrier(come)
+
+
+def tie(*lists):
+    flat = iter(lax.optimization_barrier([value for values in lists for value in values]))
+    return [[next(flat) for _ in values] for values in lists]
+
+
+def widened(value):
+    return value.astype(F32)
+
+
+def halve(keep, come, planes, number):
+    kept_rows, send = [], []
+    for q in SIDES:
+        total = widened(keep[q]) + widened(come[q])
+        if number == 1:
+            total, axis = total.reshape(planes, 2, CUT, HALF), 1
+        else:
+            total, axis = total.reshape(planes, 2, 2, 48, HALF), ROUNDS[q][2][0] - 1
+        lower, upper = split(total, axis)
+        kept_rows.append(lower)
+        send.append(upper.astype(BF))
+    return kept_rows, send
+
+
+def met(keep, come):
+    totals = []
+    for q in SIDES:
+        axis = ROUNDS[q][3][0] - 1
+        lower, upper = split(come[q], axis)
+        arrived = jnp.concatenate([upper, lower], axis=axis)
+        totals.append(widened(keep[q]) + widened(arrived))
+    return totals
 
 
 def on_device(
@@ -417,56 +481,63 @@
     place = lax.axis_index("col")
     order = jnp.arange(8)
     shard = ((place // 2 + order % 4) % SIDE) * 2 + ((place % 2) ^ (order // 4))
-    own = pack(tokens, cotangent, counts)
+    own = pack(tokens, counts)
     column = [own] + [lax.ppermute(own, "col", shift(-dz, 0)) for dz in (1, 2, 3)]
     beside = [lax.ppermute(own, "col", shift(0, 1))]
-    wx, wdt, wd = prepare(gate_mask, up_mask, down_mask, gate_weight, up_weight, down_weight)
+    wg, wu, wdt, wd = prepare(gate_mask, up_mask, down_mask, gate_weight, up_weight, down_weight)
     rows = logical_rows()
-    *column, wx, wdt, wd, rows_down, rows_along, shard = lax.optimization_barrier(
-        (*column, wx, wdt, wd, rows[:, None], rows[None, :], shard)
+    *column, wg, wu, wdt, wd, rows_down, rows_along, shard, cotangent = lax.optimization_barrier(
+        (*column, wg, wu, wdt, wd, rows[:, None], rows[None, :], shard, cotangent)
     )
     beside += [lax.ppermute(value, "col", shift(0, 1)) for value in column[1:]]
-    x, g, xt, offs, cnts = compact(shard, rows_down, column + beside)
-
-    early = partials(FIRST, 1, x, g, wx, wdt)
-    come_early = exchange(early, 0)
-    x_rest, g_rest, *_ = lax.optimization_barrier((x, g, *early))
-    late = partials(0, 3, x_rest, g_rest, wx, wdt)
-    zero = [late[q] for q in SIDES]
-    side = [[late[2 * (2 - ROUNDS[q][n][0]) + q] for q in SIDES] for n in range(2)]
-    come_rest = exchange(side[0], 0)
-    come_early = lax.optimization_barrier(come_early)
-    second = [
-        (side[1][q].astype(F32) + come_early[q].astype(F32)).astype(BF) for q in SIDES
-    ]
-    come_second = exchange(second, 1)
-    *come_rest, last0, last1 = lax.optimization_barrier((*come_rest, *come_second))
-    come_second = [last0, last1]
-    keep, send = [None] * 2, [None] * 2
+    cot_column = [cotangent]
+    cot_column += [lax.ppermute(cotangent, "col", shift(-dz, 0)) for dz in (1, 2, 3)]
+    x, xt, offs, cnts = compact_tokens(shard, rows_down, column + beside)
+    lead_send = partials(SENT, [x], [wg])
+    lead_come = exchange(lead_send, 0)
+    cot_column, _ = tie(cot_column, lead_send)
+    cot_beside = [lax.ppermute(value, "col", shift(0, 1)) for value in cot_column]
+    g = compact_cotangent(rows_down, offs, cnts, cot_column + cot_beside)
+    next_send = partials(SENT, [x, g], [wu, wdt])
+    next_come = exchange(next_send, 0)
+    x_rest, g_rest, *_ = lax.optimization_barrier((x, g, *lead_send, *next_send))
+    lead_keep = partials(KEPT, [x_rest], [wg])
+    next_keep = partials(KEPT, [x_rest, g_rest], [wu, wdt])
+
+    for number in (1, 2):
+        lead_keep, lead_send = halve(lead_keep, lead_come, 1, number)
+        lead_come = exchange(lead_send, number)
+        next_keep, next_send = halve(next_keep, next_come, 2, number)
+        next_come = exchange(next_send, number)
+    lead_keep = [(lead_keep[q] + widened(lead_come[q])).astype(BF) for q in SIDES]
+    lead_come = exchange(lead_keep, 3)
+    next_keep = [(next_keep[q] + widened(next_come[q])).astype(BF) for q in SIDES]
+    next_come = exchange(next_keep, 3)
+    gate = met(lead_keep, lead_come)
+    rest = met(next_keep, next_come)
+    hidden, derived = [], []
     for q in SIDES:
-        total = (
-            zero[q].astype(F32) + come_rest[q].astype(F32) + come_second[q].astype(F32)
-        ).reshape(3, 2, 2, 48, HALF)
-        keep[q], upper = split(total, ROUNDS[q][2][0] - 1)
-        send[q] = upper.astype(BF)
-    come = exchange(send, 2)
-    keep = [(keep[q] + come[q].astype(F32)).astype(BF) for q in SIDES]
-    come = exchange(keep, 3)
-    held = []
-    for q in SIDES:
-        axis = ROUNDS[q][3][0] - 1
-        lower, upper = split(come[q], axis)
-        arrived = jnp.concatenate([upper, lower], axis=axis)
-        held.append(activate(keep[q].astype(F32) + arrived.astype(F32)))
-    come = exchange(held, 2)
-    held = [
-        jnp.concatenate([held[q], come[q]], axis=ROUNDS[q][2][0] - 1).reshape(3, CUT, HALF)
-        for q in SIDES
-    ]
-    near = exchange(held, 1)
-    hidden_own = [jnp.concatenate([held[q][2:], near[q][2:]], axis=1) for q in SIDES]
-    derived_own = [jnp.concatenate([held[q][:2], near[q][:2]], axis=1) for q in SIDES]
+        first, second = activate(gate[q][0], rest[q][0], rest[q][1])
+        hidden.append(first)
+        derived.append(second)
+    hidden_come = exchange(hidden, 2)
+    derived_come = exchange(derived, 2)
+
+    def joined(own_rows, come_rows, planes):
+        return [
+            jnp.concatenate(
+                [own_rows[q], come_rows[q]], axis=ROUNDS[q][2][0] - 1
+            ).reshape(planes, CUT, HALF)
+            for q in SIDES
+        ]
+
+    hidden = joined(hidden, hidden_come, 1)
+    near = exchange(hidden, 1)
+    derived = joined(derived, derived_come, 2)
+    derived_near = exchange(derived, 1)
+    hidden_own = [jnp.concatenate([hidden[q], near[q]], axis=1) for q in SIDES]
     hidden_come = exchange(hidden_own, 0)
+    derived_own = [jnp.concatenate([derived[q], derived_near[q]], axis=1) for q in SIDES]
     derived_come = exchange(derived_own, 0)
 
     begun = first_output(wd, hidden_own)

time: 156 us -> 168 us (1.077)
  starting transfers between devices: 38 us -> 56.1 us
  waiting for transfers between devices: 70.3 us -> 56.9 us
  Pallas kernels: 31.7 us -> 39.1 us
    ppermute x18 -> x28, waiting for transfers between devices: 63.9 us -> 53.8 us  [exchange(): lax.ppermute(values[q], ('col', 'dp'), partners(ROUNDS[q][number][1]))]
    ppermute x18 -> x28, starting transfers between devices: 19.2 us -> 28.8 us  [exchange(): lax.ppermute(values[q], ('col', 'dp'), partners(ROUNDS[q][number][1]))]
    pallas_call x4 -> x7, Pallas kernels: 10.7 us -> 18.3 us  [the longest x4 14.9 us: partials(): call(functools.partial(partial_kernel, pieces, planes), 'partials', 1, 1...]
    ppermute x0 -> x7, starting transfers between devices: none -> 5.82 us  [the longest x3 3.74 us: on_device(): lax.ppermute(cotangent, 'col', shift(-dz, 0))]
    ppermute x3, waiting for transfers between devices: 3.4 us -> 0.01 us  [on_device(): lax.ppermute(own, 'col', shift(-dz, 0))]
    ppermute x0 -> x7, waiting for transfers between devices: none -> 3.12 us  [the longest x3 2.1 us: on_device(): lax.ppermute(cotangent, 'col', shift(-dz, 0))]
    ppermute x1, starting transfers between devices: 7.33 us -> 10.4 us  [on_device(): other = lax.ppermute(away, 'col', shift(0, 1))]
  transfers between devices with their start and end apart: 29 -> 46, of which waited for: 19 -> 20; matrix products, arithmetic and copies ran while one was open for 2% -> 2% of each run, Pallas kernels for 17% -> 24%
where the time goes in v6:
time: 168 us; the launch traced here: 166 us
  waiting for transfers between devices  56.9 us (34%)
  starting transfers between devices  56.1 us (33%)
  Pallas kernels  39.1 us (23%)
  local copies, waits for them, and re-layouts  8.01 us (5%)
  other arithmetic  3.72 us (2%)
  between operations  1.8 us (1%)
    ppermute x28, waiting for transfers between devices, exchange(): lax.ppermute(values[q], ('col', 'dp'), partners(ROUNDS[q][number][1]))  53.8 us
    ppermute x28, starting transfers between devices, exchange(): lax.ppermute(values[q], ('col', 'dp'), partners(ROUNDS[q][number][1]))  28.8 us
    pallas_call x4, Pallas kernels, partials(): call(functools.partial(partial_kernel, pieces, planes), 'partials', 1, 1...  14.9 us
    ppermute x1, starting transfers between devices, on_device(): other = lax.ppermute(away, 'col', shift(0, 1))  10.4 us
    unnamed x19, local copies, waits for them, and re-layouts  7.54 us
    pallas_call x1, Pallas kernels, gradients(): call(grad_kernel, 'gradients', 2 * LIVE * FEAT * 2 * UNITS, 13 << 20, gri...  7.21 us
    pallas_call x1, Pallas kernels, down_gradient(): call(down_kernel, 'down_gradient', 1, 1 << 12, grid=(STEPS,), out_shape=j...  5.67 us
    ppermute x3, starting transfers between devices, on_device(): lax.ppermute(own, 'col', shift(-dz, 0))  5.36 us
  transfers between devices with their start and end apart: 46, of which 20 were waited for; matrix products, arithmetic and copies ran while one was open for 2% of the time, Pallas kernels for 24%

profile of v6, /device:TPU:1, one launch (start us, length us, event | category | flops | bytes accessed | tf_op | source)
XLA Modules:
  0.0 165.7 jit_solution(4360564223404778258)
XLA Ops:
  1.3 0.9 copy-done.4
  2.2 4.7 %collective-permute-start = (bf16[144,512]{1,0:T(8,128)(2,1)S(1)}, bf16[144,512]{1,0:T(8,128)(2,1)S(1)}, u32[]{:S(2)}, u32[]{:S(2)}) collective-permute-start(bf16[144,512]{1,0:T(8,128)(2,1)S(1)} %pack.1.refs_0_), channel_id=1, source_target_pairs={{0,96},{16,112},{32,0},{48,16},{64,32},{80,48},{96,64},{112,80},{1... | collective-permute-start | bytes 442376 | tf_op jit(solution)/shard_map/ppermute | solution.py:485
  6.9 0.7 collective-permute-start.2
  7.6 1.5 collective-permute-start.3
  9.1 0.8 copy.13.dm
  9.9 1.5 copy-done
  11.4 1.5 copy-done.1
  12.9 1.5 copy-done.2
  14.4 0.7 copy-done.5
  15.1 0.7 copy-done.7
  15.8 2.4 %prepare.1 = (bf16[7,512,256]{2,1,0:T(8,128)(2,1)S(1)}, bf16[7,512,256]{2,1,0:T(8,128)(2,1)S(1)}, bf16[7,512,256]{2,1,0:T(8,128)(2,1)S(1)}, bf16[1792,512]{1,0:T(8,128)(2,1)S(1)}) custom-call(s32[4,14]{1,0:T(4,128)S(1)} %copy-done.5, s32[4,14]{1,0:T(4,128)S(1)} %copy-done.7, s32[14,4]{1,0:T(8,128)S(1)} %copy.13.dm, bf16[512,1792]{1,0:T(8,128)(2,1)S(1)} %copy-done, ...), custom_call_target="tpu_custom_call" | custom-call | bytes 13631488 | tf_op jit(solution)/shard_map/prepare/pallas_call | solution.py:136
  19.1 1.7 %collective-permute-start.7 = (bf16[128,512]{1,0:T(8,128)(2,1)S(1)}, bf16[128,512]{1,0:T(8,128)(2,1)S(1)}, u32[]{:S(2)}, u32[]{:S(2)}) collective-permute-start(bf16[128,512]{1,0:T(8,128)(2,1)S(1)} %copy-done.3), channel_id=1, source_target_pairs={{0,96},{16,112},{32,0},{48,16},{64,32},{80,48},{96,64},{112,80},{1... | collective-permute-start | bytes 393224 | tf_op jit(solution)/shard_map/ppermute | solution.py:494
  20.8 2.0 %collective-permute-start.8 = (bf16[128,512]{1,0:T(8,128)(2,1)S(1)}, bf16[128,512]{1,0:T(8,128)(2,1)S(1)}, u32[]{:S(2)}, u32[]{:S(2)}) collective-permute-start(bf16[128,512]{1,0:T(8,128)(2,1)S(1)} %copy-done.3), channel_id=1, source_target_pairs={{0,64},{16,80},{32,96},{48,112},{64,0},{80,16},{96,32},{112,48},{1... | collective-permute-start | bytes 393224 | tf_op jit(solution)/shard_map/ppermute | solution.py:494
  22.8 2.0 %compact_tokens.1 = (bf16[768,512]{1,0:T(8,128)(2,1)S(1)}, bf16[512,768]{1,0:T(8,128)(2,1)S(1)}, s32[8,8,128]{2,1,0:T(8,128)S(1)}, s32[8,8,128]{2,1,0:T(8,128)S(1)}) custom-call(s32[8]{0:T(128)S(1)} %fusion.25.shard, s32[768,1]{1,0:T(8,128)S(1)} %fusion.10.rows_ref, bf16[144,512]{1,0:T(8,128)(2,1)S(1)} %pack.1.refs_0_, ...), custom_call_target="tpu_custom_call" | custom-call | flops 805306368 | bytes 3145728 | tf_op jit(solution)/shard_map/compact_tokens/pallas_call | solution.py:202
  24.8 2.9 %partials.4 = (bf16[1,384,896]{2,1,0:T(8,128)(2,1)S(1)}, bf16[1,384,896]{2,1,0:T(8,128)(2,1)S(1)}) custom-call(bf16[768,512]{1,0:T(8,128)(2,1)S(1)} %get-tuple-element.104.refs_0_, bf16[7,512,256]{2,1,0:T(8,128)(2,1)S(1)} %get-tuple-element.93.refs_1_), custom_call_target="tpu_custom_call" | custom-call | flops 1 | bytes 4096 | tf_op jit(solution)/shard_map/partials/pallas_call | solution.py:265
  27.8 2.1 %collective-permute-done.9.refs_3_ = bf16[128,512]{1,0:T(8,128)(2,1)S(1)} collective-permute-done((bf16[128,512]{1,0:T(8,128)(2,1)S(1)}, bf16[128,512]{1,0:T(8,128)(2,1)S(1)}, u32[]{:S(2)}, u32[]{:S(2)}) %collective-permute-start.9) | collective-permute-done | bytes 131104 | tf_op jit(solution)/shard_map/ppermute | solution.py:494
  29.9 1.2 collective-permute-start.10
  31.1 1.3 collective-permute-start.14
  32.4 1.9 %collective-permute-start.15 = (bf16[1,384,896]{2,1,0:T(8,128)(2,1)S(1)}, bf16[1,384,896]{2,1,0:T(8,128)(2,1)S(1)}, u32[]{:S(2)}, u32[]{:S(2)}) collective-permute-start(bf16[1,384,896]{2,1,0:T(8,128)(2,1)S(1)} %get-tuple-element.95), channel_id=1, source_target_pairs={{0,12},{1,13},{2,14},{3,15},{4,8},{5,9},{6,10},{7,11},{8,4},{9,5},... | collective-permute-start | bytes 2064392 | tf_op jit(solution)/shard_map/ppermute | solution.py:439
  36.2 1.4 compact_cotangent.1.refs_1_.g_ref
  37.6 4.6 %partials.5 = (bf16[2,384,896]{2,1,0:T(8,128)(2,1)S(1)}, bf16[2,384,896]{2,1,0:T(8,128)(2,1)S(1)}) custom-call(bf16[768,512]{1,0:T(8,128)(2,1)S(1)} %get-tuple-element.104.refs_0_, bf16[768,512]{1,0:T(8,128)(2,1)S(1)} %compact_cotangent.1.refs_1_.g_ref, bf16[7,512,256]{2,1,0:T(8,128)(2,1)S(1)} %get-tuple-element.100.refs_2_, ...), custom_call_target="tpu_custom_call" | custom-call | flops 1 | bytes 4096 | tf_op jit(solution)/shard_map/partials/pallas_call | solution.py:265
  42.1 1.4 collective-permute-start.22
  43.5 1.9 %collective-permute-start.23 = (bf16[2,384,896]{2,1,0:T(8,128)(2,1)S(1)}, bf16[2,384,896]{2,1,0:T(8,128)(2,1)S(1)}, u32[]{:S(2)}, u32[]{:S(2)}) collective-permute-start(bf16[2,384,896]{2,1,0:T(8,128)(2,1)S(1)} %get-tuple-element.103), channel_id=1, source_target_pairs={{0,12},{1,13},{2,14},{3,15},{4,8},{5,9},{6,10},{7,11},{8,4},{9,5},... | collective-permute-start | bytes 4128776 | tf_op jit(solution)/shard_map/ppermute | solution.py:439
  45.4 2.9 %partials.6 = (bf16[1,384,896]{2,1,0:T(8,128)(2,1)S(1)}, bf16[1,384,896]{2,1,0:T(8,128)(2,1)S(1)}) custom-call(bf16[768,512]{1,0:T(8,128)(2,1)S(1)} %get-tuple-element.104.refs_0_, bf16[7,512,256]{2,1,0:T(8,128)(2,1)S(1)} %get-tuple-element.93.refs_1_), custom_call_target="tpu_custom_call" | custom-call | flops 1 | bytes 4096 | tf_op jit(solution)/shard_map/partials/pallas_call | solution.py:265
  49.2 0.7 collective-permute-start.16
  49.9 4.5 %partials.7 = (bf16[2,384,896]{2,1,0:T(8,128)(2,1)S(1)}, bf16[2,384,896]{2,1,0:T(8,128)(2,1)S(1)}) custom-call(bf16[768,512]{1,0:T(8,128)(2,1)S(1)} %get-tuple-element.104.refs_0_, bf16[768,512]{1,0:T(8,128)(2,1)S(1)} %compact_cotangent.1.refs_1_.g_ref, bf16[7,512,256]{2,1,0:T(8,128)(2,1)S(1)} %get-tuple-element.100.refs_2_, ...), custom_call_target="tpu_custom_call" | custom-call | flops 1 | bytes 4096 | tf_op jit(solution)/shard_map/partials/pallas_call | solution.py:265
  54.4 8.9 %collective-permute-done.17 = bf16[1,1,192,896]{3,2,1,0:T(8,128)(2,1)S(1)} collective-permute-done((bf16[1,1,192,896]{3,2,1,0:T(8,128)(2,1)S(1)}, bf16[1,1,192,896]{3,2,1,0:T(8,128)(2,1)S(1)}, u32[]{:S(2)}, u32[]{:S(2)}) %collective-permute-start.17) | collective-permute-done | bytes 344096 | tf_op jit(solution)/shard_map/ppermute | solution.py:439
  63.4 2.5 %collective-permute-done.16 = bf16[1,1,192,896]{3,2,1,0:T(8,128)(2,1)S(1)} collective-permute-done((bf16[1,1,192,896]{3,2,1,0:T(8,128)(2,1)S(1)}, bf16[1,1,192,896]{3,2,1,0:T(8,128)(2,1)S(1)}, u32[]{:S(2)}, u32[]{:S(2)}) %collective-permute-start.16) | collective-permute-done | bytes 344096 | tf_op jit(solution)/shard_map/ppermute | solution.py:439
  66.9 2.0 %collective-permute-start.24 = (bf16[2,1,192,896]{3,2,1,0:T(8,128)(2,1)S(1)}, bf16[2,1,192,896]{3,2,1,0:T(8,128)(2,1)S(1)}, u32[]{:S(2)}, u32[]{:S(2)}) collective-permute-start(bf16[2,1,192,896]{3,2,1,0:T(8,128)(2,1)S(1)} %slice.203), channel_id=1, source_target_pairs={{0,12},{1,13},{2,14},{3,15},{4,8},{5,9},{6,10},{7,11},{8,4},{9,5},... | collective-permute-start | bytes 2064392 | tf_op jit(solution)/shard_map/ppermute | solution.py:439
  68.9 0.9 collective-permute-start.19
  70.1 6.5 %collective-permute-done.19 = bf16[1,2,1,48,896]{4,3,2,1,0:T(8,128)(2,1)S(1)} collective-permute-done((bf16[1,2,1,48,896]{4,3,2,1,0:T(8,128)(2,1)S(1)}, bf16[1,2,1,48,896]{4,3,2,1,0:T(8,128)(2,1)S(1)}, u32[]{:S(2)}, u32[]{:S(2)}) %collective-permute-start.19) | collective-permute-done | bytes 172064 | tf_op jit(solution)/shard_map/ppermute | solution.py:439
  76.5 1.2 collective-permute-done.25
  77.8 2.3 %collective-permute-done.24 = bf16[2,1,192,896]{3,2,1,0:T(8,128)(2,1)S(1)} collective-permute-done((bf16[2,1,192,896]{3,2,1,0:T(8,128)(2,1)S(1)}, bf16[2,1,192,896]{3,2,1,0:T(8,128)(2,1)S(1)}, u32[]{:S(2)}, u32[]{:S(2)}) %collective-permute-start.24) | collective-permute-done | bytes 688160 | tf_op jit(solution)/shard_map/ppermute | solution.py:439
  80.2 1.6 collective-permute-start.27
  82.1 1.5 collective-permute-start.21
  83.7 1.2 collective-permute-start.20
  84.9 3.0 %collective-permute-done.27 = bf16[2,2,1,48,896]{4,3,2,1,0:T(8,128)(2,1)S(1)} collective-permute-done((bf16[2,2,1,48,896]{4,3,2,1,0:T(8,128)(2,1)S(1)}, bf16[2,2,1,48,896]{4,3,2,1,0:T(8,128)(2,1)S(1)}, u32[]{:S(2)}, u32[]{:S(2)}) %collective-permute-start.27) | collective-permute-done | bytes 344096 | tf_op jit(solution)/shard_map/ppermute | solution.py:439
  87.9 0.5 collective-permute-done.26
  88.7 1.2 collective-permute-start.28
  90.4 4.7 %collective-permute-done.29 = bf16[2,2,1,48,896]{4,3,2,1,0:T(8,128)(2,1)S(1)} collective-permute-done((bf16[2,2,1,48,896]{4,3,2,1,0:T(8,128)(2,1)S(1)}, bf16[2,2,1,48,896]{4,3,2,1,0:T(8,128)(2,1)S(1)}, u32[]{:S(2)}, u32[]{:S(2)}) %collective-permute-start.29) | collective-permute-done | bytes 344096 | tf_op jit(solution)/shard_map/ppermute | solution.py:439
  95.0 1.1 collective-permute-done.28
  96.5 1.2 collective-permute-start.41
  98.2 1.6 collective-permute-start.31
  99.8 0.8 collective-permute-start.30
  100.6 5.5 %collective-permute-done.31 = bf16[1,2,1,48,896]{4,3,2,1,0:T(8,128)(2,1)S(1)} collective-permute-done((bf16[1,2,1,48,896]{4,3,2,1,0:T(8,128)(2,1)S(1)}, bf16[1,2,1,48,896]{4,3,2,1,0:T(8,128)(2,1)S(1)}, u32[]{:S(2)}, u32[]{:S(2)}) %collective-permute-start.31) | collective-permute-done | bytes 172064 | tf_op jit(solution)/shard_map/ppermute | solution.py:439
  106.9 1.3 collective-permute-start.43
  108.3 2.3 %collective-permute-start.42 = (bf16[2,192,896]{2,1,0:T(8,128)(2,1)S(1)}, bf16[2,192,896]{2,1,0:T(8,128)(2,1)S(1)}, u32[]{:S(2)}, u32[]{:S(2)}) collective-permute-start(bf16[2,192,896]{2,1,0:T(8,128)(2,1)S(1)} %bitcast.39), channel_id=1, source_target_pairs={{0,12},{1,13},{2,14},{3,15},{4,8},{5,9},{6,10},{7,11},{8,4},{9,5},... | collective-permute-start | bytes 2064392 | tf_op jit(solution)/shard_map/ppermute | solution.py:439
  110.6 0.6 collective-permute-start.32
  111.1 4.2 %collective-permute-done.33 = bf16[1,192,896]{2,1,0:T(8,128)(2,1)S(1)} collective-permute-done((bf16[1,192,896]{2,1,0:T(8,128)(2,1)S(1)}, bf16[1,192,896]{2,1,0:T(8,128)(2,1)S(1)}, u32[]{:S(2)}, u32[]{:S(2)}) %collective-permute-start.33) | collective-permute-done | bytes 344096 | tf_op jit(solution)/shard_map/ppermute | solution.py:439
  115.3 8.0 %collective-permute-done.32 = bf16[1,192,896]{2,1,0:T(8,128)(2,1)S(1)} collective-permute-done((bf16[1,192,896]{2,1,0:T(8,128)(2,1)S(1)}, bf16[1,192,896]{2,1,0:T(8,128)(2,1)S(1)}, u32[]{:S(2)}, u32[]{:S(2)}) %collective-permute-start.32) | collective-permute-done | bytes 344096 | tf_op jit(solution)/shard_map/ppermute | solution.py:439
  123.4 2.3 %collective-permute-start.35 = (bf16[1,384,896]{2,1,0:T(8,128)(2,1)S(1)}, bf16[1,384,896]{2,1,0:T(8,128)(2,1)S(1)}, u32[]{:S(2)}, u32[]{:S(2)}) collective-permute-start(bf16[1,384,896]{2,1,0:T(8,128)(2,1)S(1)} %pad_maximum_fusion.3.own1), channel_id=1, source_target_pairs={{0,12},{1,13},{2,14},{3,15},{4,8},{5,9},{6,10},{7,11},{8,4},{9,5},... | collective-permute-start | bytes 2064392 | tf_op jit(solution)/shard_map/ppermute | solution.py:439
  126.0 0.6 collective-permute-start.45
  126.6 1.1 collective-permute-start.44
  127.7 3.3 %first_output.1.early_ref = f32[3,192,512]{2,1,0:T(8,128)S(1)} custom-call(bf16[1792,512]{1,0:T(8,128)(2,1)S(1)} %get-tuple-element.90.wd_ref, bf16[1,384,896]{2,1,0:T(8,128)(2,1)S(1)} %pad_maximum_fusion.2.own0, bf16[1,384,896]{2,1,0:T(8,128)(2,1)S(1)} %pad_maximum_fusion.3.own1), custom_call_target="tpu_custom_call" | custom-call | flops 1 | bytes 4096 | tf_op jit(solution)/shard_map/first_output/pallas_call | solution.py:309
  131.0 3.5 %collective-permute-done.35.come1 = bf16[1,384,896]{2,1,0:T(8,128)(2,1)S(1)} collective-permute-done((bf16[1,384,896]{2,1,0:T(8,128)(2,1)S(1)}, bf16[1,384,896]{2,1,0:T(8,128)(2,1)S(1)}, u32[]{:S(2)}, u32[]{:S(2)}) %collective-permute-start.35) | collective-permute-done | bytes 688160 | tf_op jit(solution)/shard_map/ppermute | solution.py:439
  134.5 1.1 collective-permute-done.34.come0
  135.6 2.3 %last_output.1 = (bf16[4,128,512]{2,1,0:T(8,128)(2,1)S(1)}, bf16[4,128,512]{2,1,0:T(8,128)(2,1)S(1)}) custom-call(s32[1,768]{1,0:T(1,128)S(1)} %fusion.20.rows_ref, s32[8,8,128]{2,1,0:T(8,128)S(1)} %get-tuple-element.88.offs, s32[8,8,128]{2,1,0:T(8,128)S(1)} %get-tuple-element.89.cnts, f32[3,192,512]{2,1,0:T(8,128)S(1)} %first_output.1.early_ref, ...), custom_call_target="tpu_custom_call" | custom-call | flops 1 | bytes 4096 | tf_op jit(solution)/shard_map/last_output/pallas_call | solution.py:341
  137.9 10.4 %collective-permute-start.36 = (bf16[4,128,512]{2,1,0:T(8,128)(2,1)S(1)}, bf16[4,128,512]{2,1,0:T(8,128)(2,1)S(1)}, u32[]{:S(2)}, u32[]{:S(2)}) collective-permute-start(bf16[4,128,512]{2,1,0:T(8,128)(2,1)S(1)} %get-tuple-element.133), channel_id=1, source_target_pairs={{0,16},{16,0},{32,48},{48,32},{64,80},{80,64},{96,112},{112,96},{1... | collective-permute-start | bytes 1572872 | tf_op jit(solution)/shard_map/ppermute | solution.py:545
  148.3 5.7 %down_gradient.1 = f32[1792,512]{1,0:T(8,128)} custom-call(s32[14,4]{1,0:T(8,128)S(1)} %copy.13.dm, bf16[768,512]{1,0:T(8,128)(2,1)S(1)} %compact_cotangent.1.refs_1_.g_ref, bf16[1,384,896]{2,1,0:T(8,128)(2,1)S(1)} %pad_maximum_fusion.2.own0, bf16[1,384,896]{2,1,0:T(8,128)(2,1)S(1)} %pad_maximum_fusion.3.own1, ...), custom_call_target="tpu_custom_call" | custom-call | flops 1 | bytes 4096 | tf_op jit(solution)/shard_map/down_gradient/pallas_call | solution.py:383
  154.2 0.6 collective-permute-start.37
  154.7 1.5 collective-permute-start.38
  156.3 1.4 collective-permute-start.39
  157.7 7.2 %gradients.1 = (f32[512,1792]{1,0:T(8,128)}, f32[512,1792]{1,0:T(8,128)}) custom-call(s32[4,14]{1,0:T(4,128)S(1)} %copy-done.6, s32[4,14]{1,0:T(4,128)S(1)} %copy-done.8, bf16[512,768]{1,0:T(8,128)(2,1)S(1)} %get-tuple-element.135.xt_ref, bf16[2,384,896]{2,1,0:T(8,128)(2,1)S(1)} %pad_maximum_fusion.own0, bf16[2,384,896]{2,1,0:T(8,128)(2,1)S(1)} %pad_maximum_fusion.1.own1, ...), custom_call_target="tpu_custom_call" | custom-call | flops 2818572288 | bytes 13631488 | tf_op jit(solution)/shard_map/gradients/pallas_call | solution.py:409
  164.9 0.7 fusion.19
  (102 shorter events, 8.4 us)
Async XLA Ops:
  1.3 0.9 copy-start.4
  2.2 16.2 %collective-permute-start = (bf16[144,512]{1,0:T(8,128)(2,1)S(1)}, bf16[144,512]{1,0:T(8,128)(2,1)S(1)}, u32[]{:S(2)}, u32[]{:S(2)}) collective-permute-start(bf16[144,512]{1,0:T(8,128)(2,1)S(1)} %pack.1.refs_0_), channel_id=1, source_target_pairs={{0,96},{16,112},{32,0},{48,16},{64,32},{80,48},{96,64},{112,80},{1... | collective-permute-start | bytes 442376 | tf_op jit(solution)/shard_map/ppermute | solution.py:485
  6.9 11.5 %collective-permute-start.1 = (bf16[144,512]{1,0:T(8,128)(2,1)S(1)}, bf16[144,512]{1,0:T(8,128)(2,1)S(1)}, u32[]{:S(2)}, u32[]{:S(2)}) collective-permute-start(bf16[144,512]{1,0:T(8,128)(2,1)S(1)} %pack.1.refs_0_), channel_id=1, source_target_pairs={{0,64},{16,80},{32,96},{48,112},{64,0},{80,16},{96,32},{112,48},{1... | collective-permute-start | bytes 442376 | tf_op jit(solution)/shard_map/ppermute | solution.py:485
  6.9 11.5 %collective-permute-start.2 = (bf16[144,512]{1,0:T(8,128)(2,1)S(1)}, bf16[144,512]{1,0:T(8,128)(2,1)S(1)}, u32[]{:S(2)}, u32[]{:S(2)}) collective-permute-start(bf16[144,512]{1,0:T(8,128)(2,1)S(1)} %pack.1.refs_0_), channel_id=1, source_target_pairs={{0,32},{16,48},{32,64},{48,80},{64,96},{80,112},{96,0},{112,16},{1... | collective-permute-start | bytes 442376 | tf_op jit(solution)/shard_map/ppermute | solution.py:485
  7.6 13.2 %collective-permute-start.3 = (bf16[144,512]{1,0:T(8,128)(2,1)S(1)}, bf16[144,512]{1,0:T(8,128)(2,1)S(1)}, u32[]{:S(2)}, u32[]{:S(2)}) collective-permute-start(bf16[144,512]{1,0:T(8,128)(2,1)S(1)} %pack.1.refs_0_), channel_id=1, source_target_pairs={{0,16},{16,0},{32,48},{48,32},{64,80},{80,64},{96,112},{112,96},{1... | collective-permute-start | bytes 442376 | tf_op jit(solution)/shard_map/ppermute | solution.py:486
  9.9 1.5 copy-start
  11.4 1.5 copy-start.1
  12.9 1.5 copy-start.2
  14.4 0.7 copy-start.5
  15.1 0.7 copy-start.7
  15.8 3.3 %copy-start.3 = (bf16[128,512]{1,0:T(8,128)(2,1)S(1)}, bf16[128,512]{1,0:T(8,128)(2,1)}, u32[]{:S(2)}) copy-start(bf16[128,512]{1,0:T(8,128)(2,1)} %refs_0_) | copy-start | bytes 393220
  18.4 4.4 %collective-permute-start.4 = (bf16[144,512]{1,0:T(8,128)(2,1)S(1)}, bf16[144,512]{1,0:T(8,128)(2,1)S(1)}, u32[]{:S(2)}, u32[]{:S(2)}) collective-permute-start(bf16[144,512]{1,0:T(8,128)(2,1)S(1)} %collective-permute-done.refs_1_), channel_id=1, source_target_pairs={{0,16},{16,0},{32,48},{48,32},{64,80},{80,64},{96,112},{112,96},{1... | collective-permute-start | bytes 442376 | tf_op jit(solution)/shard_map/ppermute | solution.py:492
  18.5 4.3 %collective-permute-start.5 = (bf16[144,512]{1,0:T(8,128)(2,1)S(1)}, bf16[144,512]{1,0:T(8,128)(2,1)S(1)}, u32[]{:S(2)}, u32[]{:S(2)}) collective-permute-start(bf16[144,512]{1,0:T(8,128)(2,1)S(1)} %collective-permute-done.1.refs_2_), channel_id=1, source_target_pairs={{0,16},{16,0},{32,48},{48,32},{64,80},{80,64},{96,112},{112,96},{1... | collective-permute-start | bytes 442376 | tf_op jit(solution)/shard_map/ppermute | solution.py:492
  19.0 3.9 %collective-permute-start.6 = (bf16[144,512]{1,0:T(8,128)(2,1)S(1)}, bf16[144,512]{1,0:T(8,128)(2,1)S(1)}, u32[]{:S(2)}, u32[]{:S(2)}) collective-permute-start(bf16[144,512]{1,0:T(8,128)(2,1)S(1)} %collective-permute-done.2.refs_3_), channel_id=1, source_target_pairs={{0,16},{16,0},{32,48},{48,32},{64,80},{80,64},{96,112},{112,96},{1... | collective-permute-start | bytes 442376 | tf_op jit(solution)/shard_map/ppermute | solution.py:492
  19.1 8.7 %collective-permute-start.7 = (bf16[128,512]{1,0:T(8,128)(2,1)S(1)}, bf16[128,512]{1,0:T(8,128)(2,1)S(1)}, u32[]{:S(2)}, u32[]{:S(2)}) collective-permute-start(bf16[128,512]{1,0:T(8,128)(2,1)S(1)} %copy-done.3), channel_id=1, source_target_pairs={{0,96},{16,112},{32,0},{48,16},{64,32},{80,48},{96,64},{112,80},{1... | collective-permute-start | bytes 393224 | tf_op jit(solution)/shard_map/ppermute | solution.py:494
  20.8 7.0 %collective-permute-start.8 = (bf16[128,512]{1,0:T(8,128)(2,1)S(1)}, bf16[128,512]{1,0:T(8,128)(2,1)S(1)}, u32[]{:S(2)}, u32[]{:S(2)}) collective-permute-start(bf16[128,512]{1,0:T(8,128)(2,1)S(1)} %copy-done.3), channel_id=1, source_target_pairs={{0,64},{16,80},{32,96},{48,112},{64,0},{80,16},{96,32},{112,48},{1... | collective-permute-start | bytes 393224 | tf_op jit(solution)/shard_map/ppermute | solution.py:494
  22.8 7.1 %collective-permute-start.9 = (bf16[128,512]{1,0:T(8,128)(2,1)S(1)}, bf16[128,512]{1,0:T(8,128)(2,1)S(1)}, u32[]{:S(2)}, u32[]{:S(2)}) collective-permute-start(bf16[128,512]{1,0:T(8,128)(2,1)S(1)} %copy-done.3), channel_id=1, source_target_pairs={{0,32},{16,48},{32,64},{48,80},{64,96},{80,112},{96,0},{112,16},{1... | collective-permute-start | bytes 393224 | tf_op jit(solution)/shard_map/ppermute | solution.py:494
  29.9 4.9 %collective-permute-start.10 = (bf16[128,512]{1,0:T(8,128)(2,1)S(1)}, bf16[128,512]{1,0:T(8,128)(2,1)S(1)}, u32[]{:S(2)}, u32[]{:S(2)}) collective-permute-start(bf16[128,512]{1,0:T(8,128)(2,1)S(1)} %copy-done.3), channel_id=1, source_target_pairs={{0,16},{16,0},{32,48},{48,32},{64,80},{80,64},{96,112},{112,96},{1... | collective-permute-start | bytes 393224 | tf_op jit(solution)/shard_map/ppermute | solution.py:499
  31.1 17.3 %collective-permute-start.14 = (bf16[1,384,896]{2,1,0:T(8,128)(2,1)S(1)}, bf16[1,384,896]{2,1,0:T(8,128)(2,1)S(1)}, u32[]{:S(2)}, u32[]{:S(2)}) collective-permute-start(bf16[1,384,896]{2,1,0:T(8,128)(2,1)S(1)} %get-tuple-element.94), channel_id=1, source_target_pairs={{0,4},{1,5},{2,6},{3,7},{4,0},{5,1},{6,2},{7,3},{8,12},{9,13},{10,... | collective-permute-start | bytes 2064392 | tf_op jit(solution)/shard_map/ppermute | solution.py:439
  32.4 16.0 %collective-permute-start.15 = (bf16[1,384,896]{2,1,0:T(8,128)(2,1)S(1)}, bf16[1,384,896]{2,1,0:T(8,128)(2,1)S(1)}, u32[]{:S(2)}, u32[]{:S(2)}) collective-permute-start(bf16[1,384,896]{2,1,0:T(8,128)(2,1)S(1)} %get-tuple-element.95), channel_id=1, source_target_pairs={{0,12},{1,13},{2,14},{3,15},{4,8},{5,9},{6,10},{7,11},{8,4},{9,5},... | collective-permute-start | bytes 2064392 | tf_op jit(solution)/shard_map/ppermute | solution.py:439
  34.3 1.4 collective-permute-start.11
  34.7 1.3 collective-permute-start.12
  34.8 1.4 collective-permute-start.13
  42.1 23.7 %collective-permute-start.22 = (bf16[2,384,896]{2,1,0:T(8,128)(2,1)S(1)}, bf16[2,384,896]{2,1,0:T(8,128)(2,1)S(1)}, u32[]{:S(2)}, u32[]{:S(2)}) collective-permute-start(bf16[2,384,896]{2,1,0:T(8,128)(2,1)S(1)} %get-tuple-element.102), channel_id=1, source_target_pairs={{0,4},{1,5},{2,6},{3,7},{4,0},{5,1},{6,2},{7,3},{8,12},{9,13},{10,... | collective-permute-start | bytes 4128776 | tf_op jit(solution)/shard_map/ppermute | solution.py:439
  43.5 22.4 %collective-permute-start.23 = (bf16[2,384,896]{2,1,0:T(8,128)(2,1)S(1)}, bf16[2,384,896]{2,1,0:T(8,128)(2,1)S(1)}, u32[]{:S(2)}, u32[]{:S(2)}) collective-permute-start(bf16[2,384,896]{2,1,0:T(8,128)(2,1)S(1)} %get-tuple-element.103), channel_id=1, source_target_pairs={{0,12},{1,13},{2,14},{3,15},{4,8},{5,9},{6,10},{7,11},{8,4},{9,5},... | collective-permute-start | bytes 4128776 | tf_op jit(solution)/shard_map/ppermute | solution.py:439
  48.5 14.8 %collective-permute-start.17 = (bf16[1,1,192,896]{3,2,1,0:T(8,128)(2,1)S(1)}, bf16[1,1,192,896]{3,2,1,0:T(8,128)(2,1)S(1)}, u32[]{:S(2)}, u32[]{:S(2)}) collective-permute-start(bf16[1,1,192,896]{3,2,1,0:T(8,128)(2,1)S(1)} %slice.206), channel_id=1, source_target_pairs={{0,4},{1,5},{2,6},{3,7},{4,0},{5,1},{6,2},{7,3},{8,12},{9,13},{10,... | collective-permute-start | bytes 1032200 | tf_op jit(solution)/shard_map/ppermute | solution.py:439
  49.2 16.7 %collective-permute-start.16 = (bf16[1,1,192,896]{3,2,1,0:T(8,128)(2,1)S(1)}, bf16[1,1,192,896]{3,2,1,0:T(8,128)(2,1)S(1)}, u32[]{:S(2)}, u32[]{:S(2)}) collective-permute-start(bf16[1,1,192,896]{3,2,1,0:T(8,128)(2,1)S(1)} %slice.207), channel_id=1, source_target_pairs={{0,12},{1,13},{2,14},{3,15},{4,8},{5,9},{6,10},{7,11},{8,4},{9,5},... | collective-permute-start | bytes 1032200 | tf_op jit(solution)/shard_map/ppermute | solution.py:439
  66.2 11.6 %collective-permute-start.25 = (bf16[2,1,192,896]{3,2,1,0:T(8,128)(2,1)S(1)}, bf16[2,1,192,896]{3,2,1,0:T(8,128)(2,1)S(1)}, u32[]{:S(2)}, u32[]{:S(2)}) collective-permute-start(bf16[2,1,192,896]{3,2,1,0:T(8,128)(2,1)S(1)} %slice.202), channel_id=1, source_target_pairs={{0,4},{1,5},{2,6},{3,7},{4,0},{5,1},{6,2},{7,3},{8,12},{9,13},{10,... | collective-permute-start | bytes 2064392 | tf_op jit(solution)/shard_map/ppermute | solution.py:439
  66.9 13.2 %collective-permute-start.24 = (bf16[2,1,192,896]{3,2,1,0:T(8,128)(2,1)S(1)}, bf16[2,1,192,896]{3,2,1,0:T(8,128)(2,1)S(1)}, u32[]{:S(2)}, u32[]{:S(2)}) collective-permute-start(bf16[2,1,192,896]{3,2,1,0:T(8,128)(2,1)S(1)} %slice.203), channel_id=1, source_target_pairs={{0,12},{1,13},{2,14},{3,15},{4,8},{5,9},{6,10},{7,11},{8,4},{9,5},... | collective-permute-start | bytes 2064392 | tf_op jit(solution)/shard_map/ppermute | solution.py:439
  68.9 7.6 %collective-permute-start.19 = (bf16[1,2,1,48,896]{4,3,2,1,0:T(8,128)(2,1)S(1)}, bf16[1,2,1,48,896]{4,3,2,1,0:T(8,128)(2,1)S(1)}, u32[]{:S(2)}, u32[]{:S(2)}) collective-permute-start(bf16[1,2,1,48,896]{4,3,2,1,0:T(8,128)(2,1)S(1)} %slice.208), channel_id=1, source_target_pairs={{0,3},{1,2},{2,1},{3,0},{4,7},{5,6},{6,5},{7,4},{8,11},{9,10},{10,... | collective-permute-start | bytes 516104 | tf_op jit(solution)/shard_map/ppermute | solution.py:439
  70.0 6.6 %collective-permute-start.18 = (bf16[1,1,2,48,896]{4,3,2,1,0:T(8,128)(2,1)S(1)}, bf16[1,1,2,48,896]{4,3,2,1,0:T(8,128)(2,1)S(1)}, u32[]{:S(2)}, u32[]{:S(2)}) collective-permute-start(bf16[1,1,2,48,896]{4,3,2,1,0:T(8,128)(2,1)S(1)} %slice.209), channel_id=1, source_target_pairs={{0,1},{1,0},{2,3},{3,2},{4,5},{5,4},{6,7},{7,6},{8,9},{9,8},{10,11... | collective-permute-start | bytes 516104 | tf_op jit(solution)/shard_map/ppermute | solution.py:439
  80.2 7.7 %collective-permute-start.27 = (bf16[2,2,1,48,896]{4,3,2,1,0:T(8,128)(2,1)S(1)}, bf16[2,2,1,48,896]{4,3,2,1,0:T(8,128)(2,1)S(1)}, u32[]{:S(2)}, u32[]{:S(2)}) collective-permute-start(bf16[2,2,1,48,896]{4,3,2,1,0:T(8,128)(2,1)S(1)} %slice.204), channel_id=1, source_target_pairs={{0,3},{1,2},{2,1},{3,0},{4,7},{5,6},{6,5},{7,4},{8,11},{9,10},{10,... | collective-permute-start | bytes 1032200 | tf_op jit(solution)/shard_map/ppermute | solution.py:439
  82.0 6.5 %collective-permute-start.26 = (bf16[2,1,2,48,896]{4,3,2,1,0:T(8,128)(2,1)S(1)}, bf16[2,1,2,48,896]{4,3,2,1,0:T(8,128)(2,1)S(1)}, u32[]{:S(2)}, u32[]{:S(2)}) collective-permute-start(bf16[2,1,2,48,896]{4,3,2,1,0:T(8,128)(2,1)S(1)} %slice.205), channel_id=1, source_target_pairs={{0,1},{1,0},{2,3},{3,2},{4,5},{5,4},{6,7},{7,6},{8,9},{9,8},{10,11... | collective-permute-start | bytes 1032200 | tf_op jit(solution)/shard_map/ppermute | solution.py:439
  82.1 8.2 %collective-permute-start.21 = (bf16[1,2,1,48,896]{4,3,2,1,0:T(8,128)(2,1)S(1)}, bf16[1,2,1,48,896]{4,3,2,1,0:T(8,128)(2,1)S(1)}, u32[]{:S(2)}, u32[]{:S(2)}) collective-permute-start(bf16[1,2,1,48,896]{4,3,2,1,0:T(8,128)(2,1)S(1)} %fusion.12), channel_id=1, source_target_pairs={{0,1},{1,0},{2,3},{3,2},{4,5},{5,4},{6,7},{7,6},{8,9},{9,8},{10,11... | collective-permute-start | bytes 516104 | tf_op jit(solution)/shard_map/ppermute | solution.py:439
  83.7 6.6 %collective-permute-start.20 = (bf16[1,1,2,48,896]{4,3,2,1,0:T(8,128)(2,1)S(1)}, bf16[1,1,2,48,896]{4,3,2,1,0:T(8,128)(2,1)S(1)}, u32[]{:S(2)}, u32[]{:S(2)}) collective-permute-start(bf16[1,1,2,48,896]{4,3,2,1,0:T(8,128)(2,1)S(1)} %fusion.13), channel_id=1, source_target_pairs={{0,3},{1,2},{2,1},{3,0},{4,7},{5,6},{6,5},{7,4},{8,11},{9,10},{10,... | collective-permute-start | bytes 516104 | tf_op jit(solution)/shard_map/ppermute | solution.py:439
  88.6 6.5 %collective-permute-start.29 = (bf16[2,2,1,48,896]{4,3,2,1,0:T(8,128)(2,1)S(1)}, bf16[2,2,1,48,896]{4,3,2,1,0:T(8,128)(2,1)S(1)}, u32[]{:S(2)}, u32[]{:S(2)}) collective-permute-start(bf16[2,2,1,48,896]{4,3,2,1,0:T(8,128)(2,1)S(1)} %fusion.4), channel_id=1, source_target_pairs={{0,1},{1,0},{2,3},{3,2},{4,5},{5,4},{6,7},{7,6},{8,9},{9,8},{10,11... | collective-permute-start | bytes 1032200 | tf_op jit(solution)/shard_map/ppermute | solution.py:439
  88.7 7.4 %collective-permute-start.28 = (bf16[2,1,2,48,896]{4,3,2,1,0:T(8,128)(2,1)S(1)}, bf16[2,1,2,48,896]{4,3,2,1,0:T(8,128)(2,1)S(1)}, u32[]{:S(2)}, u32[]{:S(2)}) collective-permute-start(bf16[2,1,2,48,896]{4,3,2,1,0:T(8,128)(2,1)S(1)} %fusion.5), channel_id=1, source_target_pairs={{0,3},{1,2},{2,1},{3,0},{4,7},{5,6},{6,5},{7,4},{8,11},{9,10},{10,... | collective-permute-start | bytes 1032200 | tf_op jit(solution)/shard_map/ppermute | solution.py:439
  96.5 10.3 %collective-permute-start.41 = (bf16[2,2,1,48,896]{4,3,2,1,0:T(8,128)(2,1)S(1)}, bf16[2,2,1,48,896]{4,3,2,1,0:T(8,128)(2,1)S(1)}, u32[]{:S(2)}, u32[]{:S(2)}) collective-permute-start(bf16[2,2,1,48,896]{4,3,2,1,0:T(8,128)(2,1)S(1)} %pad_maximum_fusion.9), channel_id=1, source_target_pairs={{0,3},{1,2},{2,1},{3,0},{4,7},{5,6},{6,5},{7,4},{8,11},{9,10},{10,... | collective-permute-start | bytes 1032200 | tf_op jit(solution)/shard_map/ppermute | solution.py:439
  98.1 8.7 %collective-permute-start.40 = (bf16[2,1,2,48,896]{4,3,2,1,0:T(8,128)(2,1)S(1)}, bf16[2,1,2,48,896]{4,3,2,1,0:T(8,128)(2,1)S(1)}, u32[]{:S(2)}, u32[]{:S(2)}) collective-permute-start(bf16[2,1,2,48,896]{4,3,2,1,0:T(8,128)(2,1)S(1)} %pad_maximum_fusion.8), channel_id=1, source_target_pairs={{0,1},{1,0},{2,3},{3,2},{4,5},{5,4},{6,7},{7,6},{8,9},{9,8},{10,11... | collective-permute-start | bytes 1032200 | tf_op jit(solution)/shard_map/ppermute | solution.py:439
  98.2 7.9 %collective-permute-start.31 = (bf16[1,2,1,48,896]{4,3,2,1,0:T(8,128)(2,1)S(1)}, bf16[1,2,1,48,896]{4,3,2,1,0:T(8,128)(2,1)S(1)}, u32[]{:S(2)}, u32[]{:S(2)}) collective-permute-start(bf16[1,2,1,48,896]{4,3,2,1,0:T(8,128)(2,1)S(1)} %get-tuple-element.152), channel_id=1, source_target_pairs={{0,3},{1,2},{2,1},{3,0},{4,7},{5,6},{6,5},{7,4},{8,11},{9,10},{10,... | collective-permute-start | bytes 516104 | tf_op jit(solution)/shard_map/ppermute | solution.py:439
  99.8 6.6 %collective-permute-start.30 = (bf16[1,1,2,48,896]{4,3,2,1,0:T(8,128)(2,1)S(1)}, bf16[1,1,2,48,896]{4,3,2,1,0:T(8,128)(2,1)S(1)}, u32[]{:S(2)}, u32[]{:S(2)}) collective-permute-start(bf16[1,1,2,48,896]{4,3,2,1,0:T(8,128)(2,1)S(1)} %get-tuple-element.155), channel_id=1, source_target_pairs={{0,1},{1,0},{2,3},{3,2},{4,5},{5,4},{6,7},{7,6},{8,9},{9,8},{10,11... | collective-permute-start | bytes 516104 | tf_op jit(solution)/shard_map/ppermute | solution.py:439
  106.5 8.9 %collective-permute-start.33 = (bf16[1,192,896]{2,1,0:T(8,128)(2,1)S(1)}, bf16[1,192,896]{2,1,0:T(8,128)(2,1)S(1)}, u32[]{:S(2)}, u32[]{:S(2)}) collective-permute-start(bf16[1,192,896]{2,1,0:T(8,128)(2,1)S(1)} %bitcast.45), channel_id=1, source_target_pairs={{0,4},{1,5},{2,6},{3,7},{4,0},{5,1},{6,2},{7,3},{8,12},{9,13},{10,... | collective-permute-start | bytes 1032200 | tf_op jit(solution)/shard_map/ppermute | solution.py:439
  106.9 18.9 %collective-permute-start.43 = (bf16[2,192,896]{2,1,0:T(8,128)(2,1)S(1)}, bf16[2,192,896]{2,1,0:T(8,128)(2,1)S(1)}, u32[]{:S(2)}, u32[]{:S(2)}) collective-permute-start(bf16[2,192,896]{2,1,0:T(8,128)(2,1)S(1)} %bitcast.37), channel_id=1, source_target_pairs={{0,4},{1,5},{2,6},{3,7},{4,0},{5,1},{6,2},{7,3},{8,12},{9,13},{10,... | collective-permute-start | bytes 2064392 | tf_op jit(solution)/shard_map/ppermute | solution.py:439
  108.3 17.6 %collective-permute-start.42 = (bf16[2,192,896]{2,1,0:T(8,128)(2,1)S(1)}, bf16[2,192,896]{2,1,0:T(8,128)(2,1)S(1)}, u32[]{:S(2)}, u32[]{:S(2)}) collective-permute-start(bf16[2,192,896]{2,1,0:T(8,128)(2,1)S(1)} %bitcast.39), channel_id=1, source_target_pairs={{0,12},{1,13},{2,14},{3,15},{4,8},{5,9},{6,10},{7,11},{8,4},{9,5},... | collective-permute-start | bytes 2064392 | tf_op jit(solution)/shard_map/ppermute | solution.py:439
  110.6 12.7 %collective-permute-start.32 = (bf16[1,192,896]{2,1,0:T(8,128)(2,1)S(1)}, bf16[1,192,896]{2,1,0:T(8,128)(2,1)S(1)}, u32[]{:S(2)}, u32[]{:S(2)}) collective-permute-start(bf16[1,192,896]{2,1,0:T(8,128)(2,1)S(1)} %bitcast.47), channel_id=1, source_target_pairs={{0,12},{1,13},{2,14},{3,15},{4,8},{5,9},{6,10},{7,11},{8,4},{9,5},... | collective-permute-start | bytes 1032200 | tf_op jit(solution)/shard_map/ppermute | solution.py:439
  123.4 11.1 %collective-permute-start.35 = (bf16[1,384,896]{2,1,0:T(8,128)(2,1)S(1)}, bf16[1,384,896]{2,1,0:T(8,128)(2,1)S(1)}, u32[]{:S(2)}, u32[]{:S(2)}) collective-permute-start(bf16[1,384,896]{2,1,0:T(8,128)(2,1)S(1)} %pad_maximum_fusion.3.own1), channel_id=1, source_target_pairs={{0,12},{1,13},{2,14},{3,15},{4,8},{5,9},{6,10},{7,11},{8,4},{9,5},... | collective-permute-start | bytes 2064392 | tf_op jit(solution)/shard_map/ppermute | solution.py:439
  125.7 9.9 %collective-permute-start.34 = (bf16[1,384,896]{2,1,0:T(8,128)(2,1)S(1)}, bf16[1,384,896]{2,1,0:T(8,128)(2,1)S(1)}, u32[]{:S(2)}, u32[]{:S(2)}) collective-permute-start(bf16[1,384,896]{2,1,0:T(8,128)(2,1)S(1)} %pad_maximum_fusion.2.own0), channel_id=1, source_target_pairs={{0,4},{1,5},{2,6},{3,7},{4,0},{5,1},{6,2},{7,3},{8,12},{9,13},{10,... | collective-permute-start | bytes 2064392 | tf_op jit(solution)/shard_map/ppermute | solution.py:439
  126.0 31.7 %collective-permute-start.45 = (bf16[2,384,896]{2,1,0:T(8,128)(2,1)S(1)}, bf16[2,384,896]{2,1,0:T(8,128)(2,1)S(1)}, u32[]{:S(2)}, u32[]{:S(2)}) collective-permute-start(bf16[2,384,896]{2,1,0:T(8,128)(2,1)S(1)} %pad_maximum_fusion.1.own1), channel_id=1, source_target_pairs={{0,12},{1,13},{2,14},{3,15},{4,8},{5,9},{6,10},{7,11},{8,4},{9,5},... | collective-permute-start | bytes 4128776 | tf_op jit(solution)/shard_map/ppermute | solution.py:439
  126.6 31.1 %collective-permute-start.44 = (bf16[2,384,896]{2,1,0:T(8,128)(2,1)S(1)}, bf16[2,384,896]{2,1,0:T(8,128)(2,1)S(1)}, u32[]{:S(2)}, u32[]{:S(2)}) collective-permute-start(bf16[2,384,896]{2,1,0:T(8,128)(2,1)S(1)} %pad_maximum_fusion.own0), channel_id=1, source_target_pairs={{0,4},{1,5},{2,6},{3,7},{4,0},{5,1},{6,2},{7,3},{8,12},{9,13},{10,... | collective-permute-start | bytes 4128776 | tf_op jit(solution)/shard_map/ppermute | solution.py:439
  137.9 16.1 %collective-permute-start.36 = (bf16[4,128,512]{2,1,0:T(8,128)(2,1)S(1)}, bf16[4,128,512]{2,1,0:T(8,128)(2,1)S(1)}, u32[]{:S(2)}, u32[]{:S(2)}) collective-permute-start(bf16[4,128,512]{2,1,0:T(8,128)(2,1)S(1)} %get-tuple-element.133), channel_id=1, source_target_pairs={{0,16},{16,0},{32,48},{48,32},{64,80},{80,64},{96,112},{112,96},{1... | collective-permute-start | bytes 1572872 | tf_op jit(solution)/shard_map/ppermute | solution.py:545
  154.0 3.7 %copy-start.6 = (s32[4,14]{1,0:T(4,128)S(1)}, s32[4,14]{1,0:T(4,128)}, u32[]{:S(2)}) copy-start(s32[4,14]{1,0:T(4,128)} %gm.3) | copy-start | bytes 676
  154.0 3.7 %copy-start.8 = (s32[4,14]{1,0:T(4,128)S(1)}, s32[4,14]{1,0:T(4,128)}, u32[]{:S(2)}) copy-start(s32[4,14]{1,0:T(4,128)} %um.3) | copy-start | bytes 676
  154.2 10.8 %collective-permute-start.37 = (bf16[128,512]{1,0:T(8,128)(2,1)S(1)}, bf16[128,512]{1,0:T(8,128)(2,1)S(1)}, u32[]{:S(2)}, u32[]{:S(2)}) collective-permute-start(bf16[128,512]{1,0:T(8,128)(2,1)S(1)} %get-tuple-element.158), channel_id=1, source_target_pairs={{0,32},{16,48},{32,64},{48,80},{64,96},{80,112},{96,0},{112,16},{1... | collective-permute-start | bytes 393224 | tf_op jit(solution)/shard_map/ppermute | solution.py:550
  154.7 10.2 %collective-permute-start.38 = (bf16[128,512]{1,0:T(8,128)(2,1)S(1)}, bf16[128,512]{1,0:T(8,128)(2,1)S(1)}, u32[]{:S(2)}, u32[]{:S(2)}) collective-permute-start(bf16[128,512]{1,0:T(8,128)(2,1)S(1)} %get-tuple-element.157), channel_id=1, source_target_pairs={{0,64},{16,80},{32,96},{48,112},{64,0},{80,16},{96,32},{112,48},{1... | collective-permute-start | bytes 393224 | tf_op jit(solution)/shard_map/ppermute | solution.py:550
  156.3 8.7 %collective-permute-start.39 = (bf16[128,512]{1,0:T(8,128)(2,1)S(1)}, bf16[128,512]{1,0:T(8,128)(2,1)S(1)}, u32[]{:S(2)}, u32[]{:S(2)}) collective-permute-start(bf16[128,512]{1,0:T(8,128)(2,1)S(1)} %get-tuple-element.156), channel_id=1, source_target_pairs={{0,96},{16,112},{32,0},{48,16},{64,32},{80,48},{96,64},{112,80},{1... | collective-permute-start | bytes 393224 | tf_op jit(solution)/shard_map/ppermute | solution.py:550

commit v7 on v5

--- a/solution.py
+++ b/solution.py
@@ -88,11 +88,19 @@
     )
 
 
-def pack_kernel(tok_ref, cot_ref, count_ref, out_ref):
-    out_ref[:BLK, :FEAT] = tok_ref[...]
-    out_ref[:BLK, FEAT:] = cot_ref[...]
+def pack_kernel(tok_ref, cot_ref, count_ref, out_ref, sems):
+    copies = [
+        pltpu.make_async_copy(
+            ref, out_ref.at[pl.ds(0, BLK), pl.ds(i * FEAT, FEAT)], sems.at[i]
+        )
+        for i, ref in enumerate((tok_ref, cot_ref))
+    ]
+    for copy in copies:
+        copy.start()
     count = jnp.full((PAD - BLK, 2 * FEAT), count_ref[0], jnp.int32)
     out_ref[BLK:, :] = count.astype(F32).astype(BF)
+    for copy in copies:
+        copy.wait()
 
 
 def pack(tokens, cotangent, counts):
@@ -102,9 +110,9 @@
         0,
         1 << 19,
         out_shape=jax.ShapeDtypeStruct((PAD, 2 * FEAT), BF),
-        grid=(1,),
-        in_specs=[whole((BLK, FEAT)), whole((BLK, FEAT)), smem()],
-        out_specs=whole((PAD, 2 * FEAT)),
+        in_specs=[pl.BlockSpec(memory_space=pl.ANY)] * 2 + [smem()],
+        out_specs=pl.BlockSpec(memory_space=pltpu.VMEM),
+        scratch_shapes=[pltpu.SemaphoreType.DMA((2,))],
     )(tokens, cotangent, counts)
 
 
@@ -163,7 +171,7 @@
 
 
 def compact_kernel(shard, rows_ref, *refs):
-    sources, (x_ref, g_ref, xt_ref, offs_ref, cnts_ref) = refs[:8], refs[8:]
+    sources, (x_ref, g_ref, offs_ref, cnts_ref) = refs[:8], refs[8:]
     rows = rows_ref[...]
     slot = lax.broadcasted_iota(jnp.int32, (LIVE, BLK), 1)
     cnts = [ref[BLK : BLK + 1, 0:1].astype(F32).astype(jnp.int32) for ref in sources]
@@ -186,7 +194,6 @@
         total = part if total is None else total + part
     x_ref[...] = total[:, :FEAT].astype(BF)
     g_ref[...] = total[:, FEAT:].astype(BF)
-    xt_ref[...] = total[:, :FEAT].T.astype(BF)
 
 
 def compact(shard, rows, sources):
@@ -199,13 +206,34 @@
         out_shape=(
             jax.ShapeDtypeStruct((LIVE, FEAT), BF),
             jax.ShapeDtypeStruct((LIVE, FEAT), BF),
-            jax.ShapeDtypeStruct((FEAT, LIVE), BF),
             jax.ShapeDtypeStruct((8, 8, BLK), jnp.int32),
             jax.ShapeDtypeStruct((8, 8, BLK), jnp.int32),
         ),
         in_specs=[smem(), vmem] + [vmem] * 8,
-        out_specs=(vmem,) * 5,
+        out_specs=(vmem,) * 4,
     )(shard, rows, *sources)
+
+
+ORDERS = ((0, 1, 2, 3), (0, 2, 1, 3))
+
+
+def turn_kernel(x_ref, *outs):
+    for order, out in zip(ORDERS, outs):
+        rows = [x_ref[p * CUT : (p + 1) * CUT, :] for p in order]
+        out[...] = jnp.concatenate(rows, axis=0).astype(F32).T.astype(BF)
+
+
+def turned(x):
+    vmem = pl.BlockSpec(memory_space=pltpu.VMEM)
+    return call(
+        turn_kernel,
+        "turned",
+        1,
+        1 << 12,
+        out_shape=(jax.ShapeDtypeStruct((FEAT, LIVE), BF),) * 2,
+        in_specs=[vmem],
+        out_specs=(vmem,) * 2,
+    )(x)
 
 
 def partial_kernel(start, pieces, x_ref, g_ref, wx_ref, wdt_ref, *outs):
@@ -362,30 +390,48 @@
     )(dm, g, *parts)
 
 
-def grad_kernel(gm, um, xt_ref, own0, own1, come0, come1, gate_out, up_out):
+def plane_products(turns, parts, at):
+    return [
+        jnp.dot(
+            turn[:, at : at + 2 * CUT],
+            jnp.concatenate([part[0], part[1]], axis=1),
+            preferred_element_type=F32,
+        )
+        for turn, part in zip(turns, parts)
+    ]
+
+
+def first_grad_kernel(xt0, xt1, own0, own1, gate_out, up_out):
+    for q, both in enumerate(plane_products((xt0, xt1), (own0, own1), 0)):
+        gate_out[:, q * BLK : (q + 1) * BLK] = both[:, :BLK]
+        up_out[:, q * BLK : (q + 1) * BLK] = both[:, BLK:]
+
+
+def last_grad_kernel(gm, um, xt0, xt1, gate_in, up_in, come0, come1, gate_out, up_out):
     j = pl.program_id(0)
-    xt = xt_ref[...]
-    for which, mask, target in ((0, gm, gate_out), (1, um, up_out)):
-        rows = all_rows((own0, own1), (come0, come1), which)
-        grad = jnp.dot(xt, rows, preferred_element_type=F32)
+    for q, both in enumerate(plane_products((xt0, xt1), (come0, come1), 2 * CUT)):
+        by = slice(q * BLK, (q + 1) * BLK)
         for r in range(4):
-            for b in range(2):
-                at, by = slice(r * BLK, (r + 1) * BLK), slice(b * BLK, (b + 1) * BLK)
-                target[at, by] = kept(mask, r, 2 * j + b, grad[at, by])
-
-
-def gradients(gm, um, xt, parts):
-    return call(
-        grad_kernel,
-        "gradients",
-        2 * LIVE * FEAT * 2 * UNITS,
+            at = slice(r * BLK, (r + 1) * BLK)
+            gate_out[at, by] = kept(gm, r, 2 * j + q, gate_in[at, by] + both[at, :BLK])
+            up_out[at, by] = kept(um, r, 2 * j + q, up_in[at, by] + both[at, BLK:])
+
+
+def grad_call(kernel, name, first_specs, middle_specs):
+    columns = pl.BlockSpec((FEAT, PAIR), lambda j: (0, j))
+    return call(
+        kernel,
+        name,
+        2 * LIVE * FEAT * UNITS,
         13 << 20,
         grid=(STEPS,),
         out_shape=(jax.ShapeDtypeStruct((FEAT, UNITS), F32),) * 2,
-        in_specs=[smem(), smem(), whole((FEAT, LIVE))]
-        + [pl.BlockSpec((2, 2 * CUT, BLK), lambda j: (0, 0, j))] * 4,
-        out_specs=(pl.BlockSpec((FEAT, PAIR), lambda j: (0, j)),) * 2,
-    )(gm, um, xt, *parts)
+        in_specs=[smem()] * first_specs
+        + [whole((FEAT, LIVE))] * 2
+        + [columns] * middle_specs
+        + [pl.BlockSpec((2, 2 * CUT, BLK), lambda j: (0, 0, j))] * 2,
+        out_specs=(columns,) * 2,
+    )
 
 
 def split(value, axis):
@@ -422,11 +468,11 @@
     beside = [lax.ppermute(own, "col", shift(0, 1))]
     wx, wdt, wd = prepare(gate_mask, up_mask, down_mask, gate_weight, up_weight, down_weight)
     rows = logical_rows()
-    *column, wx, wdt, wd, rows_down, rows_along, shard = lax.optimization_barrier(
-        (*column, wx, wdt, wd, rows[:, None], rows[None, :], shard)
+    column[1], column[3], wx, wdt, wd, rows_down, rows_along, shard = lax.optimization_barrier(
+        (column[1], column[3], wx, wdt, wd, rows[:, None], rows[None, :], shard)
     )
     beside += [lax.ppermute(value, "col", shift(0, 1)) for value in column[1:]]
-    x, g, xt, offs, cnts = compact(shard, rows_down, column + beside)
+    x, g, offs, cnts = compact(shard, rows_down, column + beside)
 
     early = partials(FIRST, 1, x, g, wx, wdt)
     come_early = exchange(early, 0)
@@ -435,7 +481,8 @@
     zero = [late[q] for q in SIDES]
     side = [[late[2 * (2 - ROUNDS[q][n][0]) + q] for q in SIDES] for n in range(2)]
     come_rest = exchange(side[0], 0)
-    come_early = lax.optimization_barrier(come_early)
+    turns = turned(x_rest)
+    *come_early, turn0, turn1 = lax.optimization_barrier((*come_early, *turns))
     second = [
         (side[1][q].astype(F32) + come_early[q].astype(F32)).astype(BF) for q in SIDES
     ]
@@ -470,6 +517,8 @@
     derived_come = exchange(derived_own, 0)
 
     begun = first_output(wd, hidden_own)
+    grads_begun = grad_call(first_grad_kernel, "first_grad", 0, 0)(turn0, turn1, *derived_own)
+    begun, *grads_begun = lax.optimization_barrier((begun, *grads_begun))
     mine, away = last_output(rows_along, offs, cnts, begun, wd, hidden_come)
     other = lax.ppermute(away, "col", shift(0, 1))
     down_grad = down_gradient(down_mask, g, hidden_own + hidden_come)
@@ -477,7 +526,9 @@
     summed = mine.astype(F32) + other.astype(F32)
     terms = [summed[k].astype(BF) for k in range(4)]
     arrived = [lax.ppermute(terms[dz], "col", shift(dz, 0)) for dz in (1, 2, 3)]
-    gate_grad, up_grad = gradients(gate_mask, up_mask, xt, derived_own + derived_come)
+    gate_grad, up_grad = grad_call(last_grad_kernel, "last_grad", 2, 2)(
+        gate_mask, up_mask, turn0, turn1, *grads_begun, *derived_come
+    )
     *arrived, gate_grad, up_grad = lax.optimization_barrier((*arrived, gate_grad, up_grad))
     mixed = sum((term.astype(F32) for term in arrived), terms[0].astype(F32))
     output = jnp.where(live, mixed, jnp.zeros_like(mixed)).astype(BF)

time: 156 us -> 155 us (level)
  waiting for transfers between devices: 70.3 us -> 65.5 us
  Pallas kernels: 31.7 us -> 35.5 us
    ppermute x18, waiting for transfers between devices: 63.9 us -> 59.7 us  [exchange(): lax.ppermute(values[q], ('col', 'dp'), partners(ROUNDS[q][number][1]))]
    pallas_call x1 -> x3, Pallas kernels: 7.23 us -> 11.2 us  [the longest x1 6.69 us: on_device(): grad_call(last_grad_kernel, 'last_grad', 2, 2)]
  transfers between devices with their start and end apart: 29 -> 29, of which waited for: 19 -> 18; matrix products, arithmetic and copies ran while one was open for 2% -> 2% of each run, Pallas kernels for 17% -> 20%
where the time goes in v7:
time: 155 us
  waiting for transfers between devices  65.5 us (42%)
  starting transfers between devices  39.2 us (25%)
  Pallas kernels  35.5 us (23%)
  local copies, waits for them, and re-layouts  9 us (6%)
  other arithmetic  3.89 us (3%)
  between operations  1.65 us (1%)
    ppermute x18, waiting for transfers between devices, exchange(): lax.ppermute(values[q], ('col', 'dp'), partners(ROUNDS[q][number][1]))  59.7 us
    ppermute x18, starting transfers between devices, exchange(): lax.ppermute(values[q], ('col', 'dp'), partners(ROUNDS[q][number][1]))  19.1 us
    unnamed x19, local copies, waits for them, and re-layouts  8.44 us
    pallas_call x2, Pallas kernels, partials(): call(functools.partial(partial_kernel, start, pieces), 'partials', 2 * co...  8.2 us
    ppermute x1, starting transfers between devices, on_device(): other = lax.ppermute(away, 'col', shift(0, 1))  7.69 us
    pallas_call x1, Pallas kernels, on_device(): grad_call(last_grad_kernel, 'last_grad', 2, 2)  6.69 us
    ppermute x3, starting transfers between devices, on_device(): lax.ppermute(own, 'col', shift(-dz, 0))  6.37 us
    pallas_call x1, Pallas kernels, down_gradient(): call(down_kernel, 'down_gradient', 1, 1 << 12, grid=(STEPS,), out_shape=j...  5.67 us
  transfers between devices with their start and end apart: 29, of which 18 were waited for; matrix products, arithmetic and copies ran while one was open for 2% of the time, Pallas kernels for 20%

profile of v7, /device:TPU:1, one launch (start us, length us, event | category | flops | bytes accessed | tf_op | source)
XLA Modules:
  0.0 154.8 jit_solution(2435297471487014459)
XLA Ops:
  1.3 0.9 copy-done.3
  2.2 0.9 copy-done.4
  3.2 1.5 collective-permute-start.3
  4.7 3.7 %collective-permute-start.2 = (bf16[144,1024]{1,0:T(8,128)(2,1)S(1)}, bf16[144,1024]{1,0:T(8,128)(2,1)S(1)}, u32[]{:S(2)}, u32[]{:S(2)}) collective-permute-start(bf16[144,1024]{1,0:T(8,128)(2,1)S(1)} %pack.1.refs_0_), channel_id=1, source_target_pairs={{0,64},{16,80},{32,96},{48,112},{64,0},{80,16},{96,32},{112,48},{1... | collective-permute-start | bytes 884744 | tf_op jit(solution)/shard_map/ppermute | solution.py:467
  8.3 0.7 collective-permute-start.1
  9.1 1.9 %collective-permute-start = (bf16[144,1024]{1,0:T(8,128)(2,1)S(1)}, bf16[144,1024]{1,0:T(8,128)(2,1)S(1)}, u32[]{:S(2)}, u32[]{:S(2)}) collective-permute-start(bf16[144,1024]{1,0:T(8,128)(2,1)S(1)} %pack.1.refs_0_), channel_id=1, source_target_pairs={{0,96},{16,112},{32,0},{48,16},{64,32},{80,48},{96,64},{112,80},{1... | collective-permute-start | bytes 884744 | tf_op jit(solution)/shard_map/ppermute | solution.py:467
  11.0 0.8 copy.13.dm
  11.8 1.5 copy-done
  13.3 1.5 copy-done.1
  14.8 1.5 copy-done.2
  16.3 0.7 copy-done.5
  17.0 0.7 copy-done.7
  17.7 2.4 %prepare.1 = (bf16[7,512,512]{2,1,0:T(8,128)(2,1)S(1)}, bf16[7,512,256]{2,1,0:T(8,128)(2,1)S(1)}, bf16[1792,512]{1,0:T(8,128)(2,1)S(1)}) custom-call(s32[4,14]{1,0:T(4,128)S(1)} %copy-done.5, s32[4,14]{1,0:T(4,128)S(1)} %copy-done.7, s32[14,4]{1,0:T(8,128)S(1)} %copy.13.dm, bf16[512,1792]{1,0:T(8,128)(2,1)S(1)} %copy-done, bf16[512,1792]{1,0:T(8,128)(2,1)S(1)} %copy-done.1, ...), custom_call_target="tpu_custom_call" | custom-call | bytes 13631488 | tf_op jit(solution)/shard_map/prepare/pallas_call | solution.py:146
  20.3 1.8 %collective-permute-done.1.refs_3_ = bf16[144,1024]{1,0:T(8,128)(2,1)S(1)} collective-permute-done((bf16[144,1024]{1,0:T(8,128)(2,1)S(1)}, bf16[144,1024]{1,0:T(8,128)(2,1)S(1)}, u32[]{:S(2)}, u32[]{:S(2)}) %collective-permute-start.1) | collective-permute-done | bytes 294944 | tf_op jit(solution)/shard_map/ppermute | solution.py:467
  22.1 0.4 collective-permute-done.refs_1_
  22.5 0.9 collective-permute-start.4
  23.4 0.5 collective-permute-start.6
  23.9 1.1 collective-permute-done.5.refs_6_
  25.0 0.4 collective-permute-done.6.refs_7_
  25.5 2.4 %compact.1 = (bf16[768,512]{1,0:T(8,128)(2,1)S(1)}, bf16[768,512]{1,0:T(8,128)(2,1)S(1)}, s32[8,8,128]{2,1,0:T(8,128)S(1)}, s32[8,8,128]{2,1,0:T(8,128)S(1)}) custom-call(s32[8]{0:T(128)S(1)} %fusion.23.shard, s32[768,1]{1,0:T(8,128)S(1)} %fusion.10.rows_ref, bf16[144,1024]{1,0:T(8,128)(2,1)S(1)} %pack.1.refs_0_, ...), custom_call_target="tpu_custom_call" | custom-call | flops 1610612736 | bytes 5242880 | tf_op jit(solution)/shard_map/compact/pallas_call | solution.py:201
  27.9 2.7 %partials.2 = (bf16[3,192,896]{2,1,0:T(8,128)(2,1)S(1)}, bf16[3,192,896]{2,1,0:T(8,128)(2,1)S(1)}) custom-call(bf16[768,512]{1,0:T(8,128)(2,1)S(1)} %get-tuple-element.72.x_ref, bf16[768,512]{1,0:T(8,128)(2,1)S(1)} %get-tuple-element.73.g_ref, bf16[7,512,512]{2,1,0:T(8,128)(2,1)S(1)} %get-tuple-element.68.wx_ref, ...), custom_call_target="tpu_custom_call" | custom-call | flops 1056964608 | bytes 7340032 | tf_op jit(solution)/shard_map/partials/pallas_call | solution.py:254
  30.6 1.4 collective-permute-start.9
  32.0 1.9 %collective-permute-start.10 = (bf16[3,192,896]{2,1,0:T(8,128)(2,1)S(1)}, bf16[3,192,896]{2,1,0:T(8,128)(2,1)S(1)}, u32[]{:S(2)}, u32[]{:S(2)}) collective-permute-start(bf16[3,192,896]{2,1,0:T(8,128)(2,1)S(1)} %get-tuple-element.71), channel_id=1, source_target_pairs={{0,12},{1,13},{2,14},{3,15},{4,8},{5,9},{6,10},{7,11},{8,4},{9,5},... | collective-permute-start | bytes 3096584 | tf_op jit(solution)/shard_map/ppermute | solution.py:455
  33.9 0.5 turned.1
  34.4 5.5 %partials.3 = (bf16[3,192,896]{2,1,0:T(8,128)(2,1)S(1)}, bf16[3,192,896]{2,1,0:T(8,128)(2,1)S(1)}, bf16[3,192,896]{2,1,0:T(8,128)(2,1)S(1)}, bf16[3,192,896]{2,1...) custom-call(bf16[768,512]{1,0:T(8,128)(2,1)S(1)} %get-tuple-element.72.x_ref, ...), custom_call_target="tpu_custom_call" | custom-call | flops 3170893824 | bytes 7340032 | tf_op jit(solution)/shard_map/partials/pallas_call | solution.py:254
  39.9 0.5 collective-permute-start.7
  40.3 0.6 collective-permute-start.8
  41.0 3.5 %collective-permute-done.9 = bf16[3,192,896]{2,1,0:T(8,128)(2,1)S(1)} collective-permute-done((bf16[3,192,896]{2,1,0:T(8,128)(2,1)S(1)}, bf16[3,192,896]{2,1,0:T(8,128)(2,1)S(1)}, u32[]{:S(2)}, u32[]{:S(2)}) %collective-permute-start.9) | collective-permute-done | bytes 1032224 | tf_op jit(solution)/shard_map/ppermute | solution.py:455
  44.4 2.5 %collective-permute-done.10 = bf16[3,192,896]{2,1,0:T(8,128)(2,1)S(1)} collective-permute-done((bf16[3,192,896]{2,1,0:T(8,128)(2,1)S(1)}, bf16[3,192,896]{2,1,0:T(8,128)(2,1)S(1)}, u32[]{:S(2)}, u32[]{:S(2)}) %collective-permute-start.10) | collective-permute-done | bytes 1032224 | tf_op jit(solution)/shard_map/ppermute | solution.py:455
  47.0 0.2 add_convert_fusion
  47.3 0.3 add_convert_fusion.1
  47.6 2.0 %collective-permute-start.11 = (bf16[3,192,896]{2,1,0:T(8,128)(2,1)S(1)}, bf16[3,192,896]{2,1,0:T(8,128)(2,1)S(1)}, u32[]{:S(2)}, u32[]{:S(2)}) collective-permute-start(bf16[3,192,896]{2,1,0:T(8,128)(2,1)S(1)} %add_convert_fusion.1), channel_id=1, source_target_pairs={{0,12},{1,13},{2,14},{3,15},{4,8},{5,9},{6,10},{7,11},{8,4},{9,5},... | collective-permute-start | bytes 3096584 | tf_op jit(solution)/shard_map/ppermute | solution.py:455
  49.5 6.0 %collective-permute-done.7 = bf16[3,192,896]{2,1,0:T(8,128)(2,1)S(1)} collective-permute-done((bf16[3,192,896]{2,1,0:T(8,128)(2,1)S(1)}, bf16[3,192,896]{2,1,0:T(8,128)(2,1)S(1)}, u32[]{:S(2)}, u32[]{:S(2)}) %collective-permute-start.7) | collective-permute-done | bytes 1032224 | tf_op jit(solution)/shard_map/ppermute | solution.py:455
  55.5 2.5 %collective-permute-done.8 = bf16[3,192,896]{2,1,0:T(8,128)(2,1)S(1)} collective-permute-done((bf16[3,192,896]{2,1,0:T(8,128)(2,1)S(1)}, bf16[3,192,896]{2,1,0:T(8,128)(2,1)S(1)}, u32[]{:S(2)}, u32[]{:S(2)}) %collective-permute-start.8) | collective-permute-done | bytes 1032224 | tf_op jit(solution)/shard_map/ppermute | solution.py:455
  58.0 8.6 %collective-permute-done.12 = bf16[3,192,896]{2,1,0:T(8,128)(2,1)S(1)} collective-permute-done((bf16[3,192,896]{2,1,0:T(8,128)(2,1)S(1)}, bf16[3,192,896]{2,1,0:T(8,128)(2,1)S(1)}, u32[]{:S(2)}, u32[]{:S(2)}) %collective-permute-start.12) | collective-permute-done | bytes 1032224 | tf_op jit(solution)/shard_map/ppermute | solution.py:455
  66.6 2.5 %collective-permute-done.11 = bf16[3,192,896]{2,1,0:T(8,128)(2,1)S(1)} collective-permute-done((bf16[3,192,896]{2,1,0:T(8,128)(2,1)S(1)}, bf16[3,192,896]{2,1,0:T(8,128)(2,1)S(1)}, u32[]{:S(2)}, u32[]{:S(2)}) %collective-permute-start.11) | collective-permute-done | bytes 1032224 | tf_op jit(solution)/shard_map/ppermute | solution.py:455
  69.1 0.7 convert_add_fusion
  69.8 1.0 collective-permute-start.13
  70.9 1.9 %collective-permute-start.17 = (bf16[3,2,1,48,896]{4,3,2,1,0:T(8,128)(2,1)S(1)}, bf16[3,2,1,48,896]{4,3,2,1,0:T(8,128)(2,1)S(1)}, u32[]{:S(2)}, u32[]{:S(2)}) collective-permute-start(bf16[3,2,1,48,896]{4,3,2,1,0:T(8,128)(2,1)S(1)} %slice.186), channel_id=1, source_target_pairs={{0,3},{1,2},{2,1},{3,0},{4,7},{5,6},{6,5},{7,4},{8,11},{9,10},{10,... | collective-permute-start | bytes 1548296 | tf_op jit(solution)/shard_map/ppermute | solution.py:455
  72.8 5.4 %collective-permute-done.13 = bf16[3,1,2,48,896]{4,3,2,1,0:T(8,128)(2,1)S(1)} collective-permute-done((bf16[3,1,2,48,896]{4,3,2,1,0:T(8,128)(2,1)S(1)}, bf16[3,1,2,48,896]{4,3,2,1,0:T(8,128)(2,1)S(1)}, u32[]{:S(2)}, u32[]{:S(2)}) %collective-permute-start.13) | collective-permute-done | bytes 516128 | tf_op jit(solution)/shard_map/ppermute | solution.py:455
  78.3 2.6 %collective-permute-start.14 = (bf16[3,1,2,48,896]{4,3,2,1,0:T(8,128)(2,1)S(1)}, bf16[3,1,2,48,896]{4,3,2,1,0:T(8,128)(2,1)S(1)}, u32[]{:S(2)}, u32[]{:S(2)}) collective-permute-start(bf16[3,1,2,48,896]{4,3,2,1,0:T(8,128)(2,1)S(1)} %fusion.1), channel_id=1, source_target_pairs={{0,3},{1,2},{2,1},{3,0},{4,7},{5,6},{6,5},{7,4},{8,11},{9,10},{10,... | collective-permute-start | bytes 1548296 | tf_op jit(solution)/shard_map/ppermute | solution.py:455
  81.0 6.8 %collective-permute-done.14 = bf16[3,1,2,48,896]{4,3,2,1,0:T(8,128)(2,1)S(1)} collective-permute-done((bf16[3,1,2,48,896]{4,3,2,1,0:T(8,128)(2,1)S(1)}, bf16[3,1,2,48,896]{4,3,2,1,0:T(8,128)(2,1)S(1)}, u32[]{:S(2)}, u32[]{:S(2)}) %collective-permute-start.14) | collective-permute-done | bytes 516128 | tf_op jit(solution)/shard_map/ppermute | solution.py:455
  87.9 0.2 multiply_convert_fusion.5
  88.3 0.9 collective-permute-done.18
  89.4 0.2 multiply_convert_fusion.2
  89.7 1.8 %collective-permute-start.19 = (bf16[3,2,1,48,896]{4,3,2,1,0:T(8,128)(2,1)S(1)}, bf16[3,2,1,48,896]{4,3,2,1,0:T(8,128)(2,1)S(1)}, u32[]{:S(2)}, u32[]{:S(2)}) collective-permute-start(bf16[3,2,1,48,896]{4,3,2,1,0:T(8,128)(2,1)S(1)} %pad_maximum_fusion.7), channel_id=1, source_target_pairs={{0,3},{1,2},{2,1},{3,0},{4,7},{5,6},{6,5},{7,4},{8,11},{9,10},{10,... | collective-permute-start | bytes 1548296 | tf_op jit(solution)/shard_map/ppermute | solution.py:455
  91.5 5.0 %collective-permute-done.15 = bf16[3,1,2,48,896]{4,3,2,1,0:T(8,128)(2,1)S(1)} collective-permute-done((bf16[3,1,2,48,896]{4,3,2,1,0:T(8,128)(2,1)S(1)}, bf16[3,1,2,48,896]{4,3,2,1,0:T(8,128)(2,1)S(1)}, u32[]{:S(2)}, u32[]{:S(2)}) %collective-permute-start.15) | collective-permute-done | bytes 516128 | tf_op jit(solution)/shard_map/ppermute | solution.py:455
  96.7 2.0 %collective-permute-start.16 = (bf16[3,192,896]{2,1,0:T(8,128)(2,1)S(1)}, bf16[3,192,896]{2,1,0:T(8,128)(2,1)S(1)}, u32[]{:S(2)}, u32[]{:S(2)}) collective-permute-start(bf16[3,192,896]{2,1,0:T(8,128)(2,1)S(1)} %bitcast.25), channel_id=1, source_target_pairs={{0,12},{1,13},{2,14},{3,15},{4,8},{5,9},{6,10},{7,11},{8,4},{9,5},... | collective-permute-start | bytes 3096584 | tf_op jit(solution)/shard_map/ppermute | solution.py:455
  98.7 0.7 collective-permute-done.19
  99.7 14.9 %collective-permute-done.16 = bf16[3,192,896]{2,1,0:T(8,128)(2,1)S(1)} collective-permute-done((bf16[3,192,896]{2,1,0:T(8,128)(2,1)S(1)}, bf16[3,192,896]{2,1,0:T(8,128)(2,1)S(1)}, u32[]{:S(2)}, u32[]{:S(2)}) %collective-permute-start.16) | collective-permute-done | bytes 1032224 | tf_op jit(solution)/shard_map/ppermute | solution.py:455
  114.9 1.8 %collective-permute-start.22 = (bf16[1,384,896]{2,1,0:T(8,128)(2,1)S(1)}, bf16[1,384,896]{2,1,0:T(8,128)(2,1)S(1)}, u32[]{:S(2)}, u32[]{:S(2)}) collective-permute-start(bf16[1,384,896]{2,1,0:T(8,128)(2,1)S(1)} %pad_maximum_fusion.5.own1), channel_id=1, source_target_pairs={{0,12},{1,13},{2,14},{3,15},{4,8},{5,9},{6,10},{7,11},{8,4},{9,5},... | collective-permute-start | bytes 2064392 | tf_op jit(solution)/shard_map/ppermute | solution.py:455
  117.0 1.0 collective-permute-start.28
  118.2 0.3 collective-permute-start.27
  118.5 3.3 %first_output.1.early_ref = f32[3,192,512]{2,1,0:T(8,128)S(1)} custom-call(bf16[1792,512]{1,0:T(8,128)(2,1)S(1)} %get-tuple-element.65.wd_ref, bf16[1,384,896]{2,1,0:T(8,128)(2,1)S(1)} %pad_maximum_fusion.4.own0, bf16[1,384,896]{2,1,0:T(8,128)(2,1)S(1)} %pad_maximum_fusion.5.own1), custom_call_target="tpu_custom_call" | custom-call | flops 1 | bytes 4096 | tf_op jit(solution)/shard_map/first_output/pallas_call | solution.py:306
  121.8 4.1 %first_grad.1 = (f32[512,1792]{1,0:T(8,128)S(1)}, f32[512,1792]{1,0:T(8,128)S(1)}) custom-call(bf16[512,768]{1,0:T(8,128)(2,1)S(1)} %get-tuple-element.88.xt0, bf16[512,768]{1,0:T(8,128)(2,1)S(1)} %get-tuple-element.89.xt1, bf16[2,384,896]{2,1,0:T(8,128)(2,1)S(1)} %pad_maximum_fusion.own0, bf16[2,384,896]{2,1,0:T(8,128)(2,1)S(1)} %pad_maximum_fusion.1.own1), custom_call_target="tpu_custom_call" | custom-call | flops 1409286144 | bytes 13631488 | tf_op jit(solution)/shard_map/first_grad/pallas_call | solution.py:520
  125.9 0.4 collective-permute-done.22.come1
  126.3 2.3 %last_output.1 = (bf16[4,128,512]{2,1,0:T(8,128)(2,1)S(1)}, bf16[4,128,512]{2,1,0:T(8,128)(2,1)S(1)}) custom-call(s32[1,768]{1,0:T(1,128)S(1)} %fusion.18.rows_ref, s32[8,8,128]{2,1,0:T(8,128)S(1)} %get-tuple-element.63.offs, s32[8,8,128]{2,1,0:T(8,128)S(1)} %get-tuple-element.64.cnts, f32[3,192,512]{2,1,0:T(8,128)S(1)} %first_output.1.early_ref, ...), custom_call_target="tpu_custom_call" | custom-call | flops 1 | bytes 4096 | tf_op jit(solution)/shard_map/last_output/pallas_call | solution.py:338
  128.6 7.7 %collective-permute-start.23 = (bf16[4,128,512]{2,1,0:T(8,128)(2,1)S(1)}, bf16[4,128,512]{2,1,0:T(8,128)(2,1)S(1)}, u32[]{:S(2)}, u32[]{:S(2)}) collective-permute-start(bf16[4,128,512]{2,1,0:T(8,128)(2,1)S(1)} %get-tuple-element.94), channel_id=1, source_target_pairs={{0,16},{16,0},{32,48},{48,32},{64,80},{80,64},{96,112},{112,96},{1... | collective-permute-start | bytes 1572872 | tf_op jit(solution)/shard_map/ppermute | solution.py:523
  136.3 5.7 %down_gradient.1 = f32[1792,512]{1,0:T(8,128)} custom-call(s32[14,4]{1,0:T(8,128)S(1)} %copy.13.dm, bf16[768,512]{1,0:T(8,128)(2,1)S(1)} %get-tuple-element.73.g_ref, bf16[1,384,896]{2,1,0:T(8,128)(2,1)S(1)} %pad_maximum_fusion.4.own0, bf16[1,384,896]{2,1,0:T(8,128)(2,1)S(1)} %pad_maximum_fusion.5.own1, ...), custom_call_target="tpu_custom_call" | custom-call | flops 1 | bytes 4096 | tf_op jit(solution)/shard_map/down_gradient/pallas_call | solution.py:380
  142.1 2.4 %collective-permute-start.26 = (bf16[128,512]{1,0:T(8,128)(2,1)S(1)}, bf16[128,512]{1,0:T(8,128)(2,1)S(1)}, u32[]{:S(2)}, u32[]{:S(2)}) collective-permute-start(bf16[128,512]{1,0:T(8,128)(2,1)S(1)} %get-tuple-element.112), channel_id=1, source_target_pairs={{0,96},{16,112},{32,0},{48,16},{64,32},{80,48},{96,64},{112,80},{1... | collective-permute-start | bytes 393224 | tf_op jit(solution)/shard_map/ppermute | solution.py:528
  144.7 0.5 collective-permute-start.24
  145.2 6.7 %last_grad.1 = (f32[512,1792]{1,0:T(8,128)}, f32[512,1792]{1,0:T(8,128)}) custom-call(s32[4,14]{1,0:T(4,128)S(1)} %copy-done.6, s32[4,14]{1,0:T(4,128)S(1)} %copy-done.8, bf16[512,768]{1,0:T(8,128)(2,1)S(1)} %get-tuple-element.88.xt0, bf16[512,768]{1,0:T(8,128)(2,1)S(1)} %get-tuple-element.89.xt1, f32[512,1792]{1,0:T(8,128)S(1)} %get-tuple-element.96.gate_in, ...), custom_call_target="tpu_custom_call" | custom-call | flops 1409286144 | bytes 13631488 | tf_op jit(solution)/shard_map/last_grad/pallas_call | solution.py:529
  151.9 2.1 %collective-permute-done.24 = bf16[128,512]{1,0:T(8,128)(2,1)S(1)} collective-permute-done((bf16[128,512]{1,0:T(8,128)(2,1)S(1)}, bf16[128,512]{1,0:T(8,128)(2,1)S(1)}, u32[]{:S(2)}, u32[]{:S(2)}) %collective-permute-start.24) | collective-permute-done | bytes 131104 | tf_op jit(solution)/shard_map/ppermute | solution.py:528
  154.0 0.7 fusion.17
  (60 shorter events, 2.9 us)
Async XLA Ops:
  1.3 0.9 copy-start.3
  2.2 0.9 copy-start.4
  3.2 20.8 %collective-permute-start.3 = (bf16[144,1024]{1,0:T(8,128)(2,1)S(1)}, bf16[144,1024]{1,0:T(8,128)(2,1)S(1)}, u32[]{:S(2)}, u32[]{:S(2)}) collective-permute-start(bf16[144,1024]{1,0:T(8,128)(2,1)S(1)} %pack.1.refs_0_), channel_id=1, source_target_pairs={{0,16},{16,0},{32,48},{48,32},{64,80},{80,64},{96,112},{112,96},{1... | collective-permute-start | bytes 884744 | tf_op jit(solution)/shard_map/ppermute | solution.py:468
  4.7 18.8 %collective-permute-start.2 = (bf16[144,1024]{1,0:T(8,128)(2,1)S(1)}, bf16[144,1024]{1,0:T(8,128)(2,1)S(1)}, u32[]{:S(2)}, u32[]{:S(2)}) collective-permute-start(bf16[144,1024]{1,0:T(8,128)(2,1)S(1)} %pack.1.refs_0_), channel_id=1, source_target_pairs={{0,64},{16,80},{32,96},{48,112},{64,0},{80,16},{96,32},{112,48},{1... | collective-permute-start | bytes 884744 | tf_op jit(solution)/shard_map/ppermute | solution.py:467
  8.3 13.8 %collective-permute-start.1 = (bf16[144,1024]{1,0:T(8,128)(2,1)S(1)}, bf16[144,1024]{1,0:T(8,128)(2,1)S(1)}, u32[]{:S(2)}, u32[]{:S(2)}) collective-permute-start(bf16[144,1024]{1,0:T(8,128)(2,1)S(1)} %pack.1.refs_0_), channel_id=1, source_target_pairs={{0,32},{16,48},{32,64},{48,80},{64,96},{80,112},{96,0},{112,16},{1... | collective-permute-start | bytes 884744 | tf_op jit(solution)/shard_map/ppermute | solution.py:467
  9.1 13.4 %collective-permute-start = (bf16[144,1024]{1,0:T(8,128)(2,1)S(1)}, bf16[144,1024]{1,0:T(8,128)(2,1)S(1)}, u32[]{:S(2)}, u32[]{:S(2)}) collective-permute-start(bf16[144,1024]{1,0:T(8,128)(2,1)S(1)} %pack.1.refs_0_), channel_id=1, source_target_pairs={{0,96},{16,112},{32,0},{48,16},{64,32},{80,48},{96,64},{112,80},{1... | collective-permute-start | bytes 884744 | tf_op jit(solution)/shard_map/ppermute | solution.py:467
  11.8 1.5 copy-start
  13.3 1.5 copy-start.1
  14.8 1.5 copy-start.2
  16.3 0.7 copy-start.5
  17.0 0.7 copy-start.7
  22.5 2.5 %collective-permute-start.4 = (bf16[144,1024]{1,0:T(8,128)(2,1)S(1)}, bf16[144,1024]{1,0:T(8,128)(2,1)S(1)}, u32[]{:S(2)}, u32[]{:S(2)}) collective-permute-start(bf16[144,1024]{1,0:T(8,128)(2,1)S(1)} %collective-permute-done.refs_1_), channel_id=1, source_target_pairs={{0,16},{16,0},{32,48},{48,32},{64,80},{80,64},{96,112},{112,96},{1... | collective-permute-start | bytes 884744 | tf_op jit(solution)/shard_map/ppermute | solution.py:474
  23.4 1.6 %collective-permute-start.5 = (bf16[144,1024]{1,0:T(8,128)(2,1)S(1)}, bf16[144,1024]{1,0:T(8,128)(2,1)S(1)}, u32[]{:S(2)}, u32[]{:S(2)}) collective-permute-start(bf16[144,1024]{1,0:T(8,128)(2,1)S(1)} %collective-permute-done.2.refs_2_), channel_id=1, source_target_pairs={{0,16},{16,0},{32,48},{48,32},{64,80},{80,64},{96,112},{112,96},{1... | collective-permute-start | bytes 884744 | tf_op jit(solution)/shard_map/ppermute | solution.py:474
  23.4 2.0 %collective-permute-start.6 = (bf16[144,1024]{1,0:T(8,128)(2,1)S(1)}, bf16[144,1024]{1,0:T(8,128)(2,1)S(1)}, u32[]{:S(2)}, u32[]{:S(2)}) collective-permute-start(bf16[144,1024]{1,0:T(8,128)(2,1)S(1)} %collective-permute-done.1.refs_3_), channel_id=1, source_target_pairs={{0,16},{16,0},{32,48},{48,32},{64,80},{80,64},{96,112},{112,96},{1... | collective-permute-start | bytes 884744 | tf_op jit(solution)/shard_map/ppermute | solution.py:474
  30.6 13.8 %collective-permute-start.9 = (bf16[3,192,896]{2,1,0:T(8,128)(2,1)S(1)}, bf16[3,192,896]{2,1,0:T(8,128)(2,1)S(1)}, u32[]{:S(2)}, u32[]{:S(2)}) collective-permute-start(bf16[3,192,896]{2,1,0:T(8,128)(2,1)S(1)} %get-tuple-element.70), channel_id=1, source_target_pairs={{0,4},{1,5},{2,6},{3,7},{4,0},{5,1},{6,2},{7,3},{8,12},{9,13},{10,... | collective-permute-start | bytes 3096584 | tf_op jit(solution)/shard_map/ppermute | solution.py:455
  32.0 15.0 %collective-permute-start.10 = (bf16[3,192,896]{2,1,0:T(8,128)(2,1)S(1)}, bf16[3,192,896]{2,1,0:T(8,128)(2,1)S(1)}, u32[]{:S(2)}, u32[]{:S(2)}) collective-permute-start(bf16[3,192,896]{2,1,0:T(8,128)(2,1)S(1)} %get-tuple-element.71), channel_id=1, source_target_pairs={{0,12},{1,13},{2,14},{3,15},{4,8},{5,9},{6,10},{7,11},{8,4},{9,5},... | collective-permute-start | bytes 3096584 | tf_op jit(solution)/shard_map/ppermute | solution.py:455
  39.9 15.6 %collective-permute-start.7 = (bf16[3,192,896]{2,1,0:T(8,128)(2,1)S(1)}, bf16[3,192,896]{2,1,0:T(8,128)(2,1)S(1)}, u32[]{:S(2)}, u32[]{:S(2)}) collective-permute-start(bf16[3,192,896]{2,1,0:T(8,128)(2,1)S(1)} %get-tuple-element.75), channel_id=1, source_target_pairs={{0,4},{1,5},{2,6},{3,7},{4,0},{5,1},{6,2},{7,3},{8,12},{9,13},{10,... | collective-permute-start | bytes 3096584 | tf_op jit(solution)/shard_map/ppermute | solution.py:455
  40.3 17.7 %collective-permute-start.8 = (bf16[3,192,896]{2,1,0:T(8,128)(2,1)S(1)}, bf16[3,192,896]{2,1,0:T(8,128)(2,1)S(1)}, u32[]{:S(2)}, u32[]{:S(2)}) collective-permute-start(bf16[3,192,896]{2,1,0:T(8,128)(2,1)S(1)} %get-tuple-element.76), channel_id=1, source_target_pairs={{0,12},{1,13},{2,14},{3,15},{4,8},{5,9},{6,10},{7,11},{8,4},{9,5},... | collective-permute-start | bytes 3096584 | tf_op jit(solution)/shard_map/ppermute | solution.py:455
  47.2 19.4 %collective-permute-start.12 = (bf16[3,192,896]{2,1,0:T(8,128)(2,1)S(1)}, bf16[3,192,896]{2,1,0:T(8,128)(2,1)S(1)}, u32[]{:S(2)}, u32[]{:S(2)}) collective-permute-start(bf16[3,192,896]{2,1,0:T(8,128)(2,1)S(1)} %add_convert_fusion), channel_id=1, source_target_pairs={{0,4},{1,5},{2,6},{3,7},{4,0},{5,1},{6,2},{7,3},{8,12},{9,13},{10,... | collective-permute-start | bytes 3096584 | tf_op jit(solution)/shard_map/ppermute | solution.py:455
  47.6 21.5 %collective-permute-start.11 = (bf16[3,192,896]{2,1,0:T(8,128)(2,1)S(1)}, bf16[3,192,896]{2,1,0:T(8,128)(2,1)S(1)}, u32[]{:S(2)}, u32[]{:S(2)}) collective-permute-start(bf16[3,192,896]{2,1,0:T(8,128)(2,1)S(1)} %add_convert_fusion.1), channel_id=1, source_target_pairs={{0,12},{1,13},{2,14},{3,15},{4,8},{5,9},{6,10},{7,11},{8,4},{9,5},... | collective-permute-start | bytes 3096584 | tf_op jit(solution)/shard_map/ppermute | solution.py:455
  69.8 8.3 %collective-permute-start.13 = (bf16[3,1,2,48,896]{4,3,2,1,0:T(8,128)(2,1)S(1)}, bf16[3,1,2,48,896]{4,3,2,1,0:T(8,128)(2,1)S(1)}, u32[]{:S(2)}, u32[]{:S(2)}) collective-permute-start(bf16[3,1,2,48,896]{4,3,2,1,0:T(8,128)(2,1)S(1)} %slice.187), channel_id=1, source_target_pairs={{0,1},{1,0},{2,3},{3,2},{4,5},{5,4},{6,7},{7,6},{8,9},{9,8},{10,11... | collective-permute-start | bytes 1548296 | tf_op jit(solution)/shard_map/ppermute | solution.py:455
  70.9 9.9 %collective-permute-start.17 = (bf16[3,2,1,48,896]{4,3,2,1,0:T(8,128)(2,1)S(1)}, bf16[3,2,1,48,896]{4,3,2,1,0:T(8,128)(2,1)S(1)}, u32[]{:S(2)}, u32[]{:S(2)}) collective-permute-start(bf16[3,2,1,48,896]{4,3,2,1,0:T(8,128)(2,1)S(1)} %slice.186), channel_id=1, source_target_pairs={{0,3},{1,2},{2,1},{3,0},{4,7},{5,6},{6,5},{7,4},{8,11},{9,10},{10,... | collective-permute-start | bytes 1548296 | tf_op jit(solution)/shard_map/ppermute | solution.py:455
  78.3 9.5 %collective-permute-start.14 = (bf16[3,1,2,48,896]{4,3,2,1,0:T(8,128)(2,1)S(1)}, bf16[3,1,2,48,896]{4,3,2,1,0:T(8,128)(2,1)S(1)}, u32[]{:S(2)}, u32[]{:S(2)}) collective-permute-start(bf16[3,1,2,48,896]{4,3,2,1,0:T(8,128)(2,1)S(1)} %fusion.1), channel_id=1, source_target_pairs={{0,3},{1,2},{2,1},{3,0},{4,7},{5,6},{6,5},{7,4},{8,11},{9,10},{10,... | collective-permute-start | bytes 1548296 | tf_op jit(solution)/shard_map/ppermute | solution.py:455
  80.9 8.3 %collective-permute-start.18 = (bf16[3,2,1,48,896]{4,3,2,1,0:T(8,128)(2,1)S(1)}, bf16[3,2,1,48,896]{4,3,2,1,0:T(8,128)(2,1)S(1)}, u32[]{:S(2)}, u32[]{:S(2)}) collective-permute-start(bf16[3,2,1,48,896]{4,3,2,1,0:T(8,128)(2,1)S(1)} %fusion), channel_id=1, source_target_pairs={{0,1},{1,0},{2,3},{3,2},{4,5},{5,4},{6,7},{7,6},{8,9},{9,8},{10,11... | collective-permute-start | bytes 1548296 | tf_op jit(solution)/shard_map/ppermute | solution.py:455
  88.2 8.3 %collective-permute-start.15 = (bf16[3,1,2,48,896]{4,3,2,1,0:T(8,128)(2,1)S(1)}, bf16[3,1,2,48,896]{4,3,2,1,0:T(8,128)(2,1)S(1)}, u32[]{:S(2)}, u32[]{:S(2)}) collective-permute-start(bf16[3,1,2,48,896]{4,3,2,1,0:T(8,128)(2,1)S(1)} %pad_maximum_fusion.6), channel_id=1, source_target_pairs={{0,1},{1,0},{2,3},{3,2},{4,5},{5,4},{6,7},{7,6},{8,9},{9,8},{10,11... | collective-permute-start | bytes 1548296 | tf_op jit(solution)/shard_map/ppermute | solution.py:455
  89.7 9.7 %collective-permute-start.19 = (bf16[3,2,1,48,896]{4,3,2,1,0:T(8,128)(2,1)S(1)}, bf16[3,2,1,48,896]{4,3,2,1,0:T(8,128)(2,1)S(1)}, u32[]{:S(2)}, u32[]{:S(2)}) collective-permute-start(bf16[3,2,1,48,896]{4,3,2,1,0:T(8,128)(2,1)S(1)} %pad_maximum_fusion.7), channel_id=1, source_target_pairs={{0,3},{1,2},{2,1},{3,0},{4,7},{5,6},{6,5},{7,4},{8,11},{9,10},{10,... | collective-permute-start | bytes 1548296 | tf_op jit(solution)/shard_map/ppermute | solution.py:455
  96.7 17.9 %collective-permute-start.16 = (bf16[3,192,896]{2,1,0:T(8,128)(2,1)S(1)}, bf16[3,192,896]{2,1,0:T(8,128)(2,1)S(1)}, u32[]{:S(2)}, u32[]{:S(2)}) collective-permute-start(bf16[3,192,896]{2,1,0:T(8,128)(2,1)S(1)} %bitcast.25), channel_id=1, source_target_pairs={{0,12},{1,13},{2,14},{3,15},{4,8},{5,9},{6,10},{7,11},{8,4},{9,5},... | collective-permute-start | bytes 3096584 | tf_op jit(solution)/shard_map/ppermute | solution.py:455
  99.5 15.2 %collective-permute-start.20 = (bf16[3,192,896]{2,1,0:T(8,128)(2,1)S(1)}, bf16[3,192,896]{2,1,0:T(8,128)(2,1)S(1)}, u32[]{:S(2)}, u32[]{:S(2)}) collective-permute-start(bf16[3,192,896]{2,1,0:T(8,128)(2,1)S(1)} %bitcast.26), channel_id=1, source_target_pairs={{0,4},{1,5},{2,6},{3,7},{4,0},{5,1},{6,2},{7,3},{8,12},{9,13},{10,... | collective-permute-start | bytes 3096584 | tf_op jit(solution)/shard_map/ppermute | solution.py:455
  114.7 11.2 %collective-permute-start.21 = (bf16[1,384,896]{2,1,0:T(8,128)(2,1)S(1)}, bf16[1,384,896]{2,1,0:T(8,128)(2,1)S(1)}, u32[]{:S(2)}, u32[]{:S(2)}) collective-permute-start(bf16[1,384,896]{2,1,0:T(8,128)(2,1)S(1)} %pad_maximum_fusion.4.own0), channel_id=1, source_target_pairs={{0,4},{1,5},{2,6},{3,7},{4,0},{5,1},{6,2},{7,3},{8,12},{9,13},{10,... | collective-permute-start | bytes 2064392 | tf_op jit(solution)/shard_map/ppermute | solution.py:455
  114.9 11.4 %collective-permute-start.22 = (bf16[1,384,896]{2,1,0:T(8,128)(2,1)S(1)}, bf16[1,384,896]{2,1,0:T(8,128)(2,1)S(1)}, u32[]{:S(2)}, u32[]{:S(2)}) collective-permute-start(bf16[1,384,896]{2,1,0:T(8,128)(2,1)S(1)} %pad_maximum_fusion.5.own1), channel_id=1, source_target_pairs={{0,12},{1,13},{2,14},{3,15},{4,8},{5,9},{6,10},{7,11},{8,4},{9,5},... | collective-permute-start | bytes 2064392 | tf_op jit(solution)/shard_map/ppermute | solution.py:455
  117.0 28.2 %collective-permute-start.28 = (bf16[2,384,896]{2,1,0:T(8,128)(2,1)S(1)}, bf16[2,384,896]{2,1,0:T(8,128)(2,1)S(1)}, u32[]{:S(2)}, u32[]{:S(2)}) collective-permute-start(bf16[2,384,896]{2,1,0:T(8,128)(2,1)S(1)} %pad_maximum_fusion.1.own1), channel_id=1, source_target_pairs={{0,12},{1,13},{2,14},{3,15},{4,8},{5,9},{6,10},{7,11},{8,4},{9,5},... | collective-permute-start | bytes 4128776 | tf_op jit(solution)/shard_map/ppermute | solution.py:455
  118.2 27.0 %collective-permute-start.27 = (bf16[2,384,896]{2,1,0:T(8,128)(2,1)S(1)}, bf16[2,384,896]{2,1,0:T(8,128)(2,1)S(1)}, u32[]{:S(2)}, u32[]{:S(2)}) collective-permute-start(bf16[2,384,896]{2,1,0:T(8,128)(2,1)S(1)} %pad_maximum_fusion.own0), channel_id=1, source_target_pairs={{0,4},{1,5},{2,6},{3,7},{4,0},{5,1},{6,2},{7,3},{8,12},{9,13},{10,... | collective-permute-start | bytes 4128776 | tf_op jit(solution)/shard_map/ppermute | solution.py:455
  128.6 13.4 %collective-permute-start.23 = (bf16[4,128,512]{2,1,0:T(8,128)(2,1)S(1)}, bf16[4,128,512]{2,1,0:T(8,128)(2,1)S(1)}, u32[]{:S(2)}, u32[]{:S(2)}) collective-permute-start(bf16[4,128,512]{2,1,0:T(8,128)(2,1)S(1)} %get-tuple-element.94), channel_id=1, source_target_pairs={{0,16},{16,0},{32,48},{48,32},{64,80},{80,64},{96,112},{112,96},{1... | collective-permute-start | bytes 1572872 | tf_op jit(solution)/shard_map/ppermute | solution.py:523
  141.9 3.3 %copy-start.6 = (s32[4,14]{1,0:T(4,128)S(1)}, s32[4,14]{1,0:T(4,128)}, u32[]{:S(2)}) copy-start(s32[4,14]{1,0:T(4,128)} %gm.3) | copy-start | bytes 676
  141.9 3.3 %copy-start.8 = (s32[4,14]{1,0:T(4,128)S(1)}, s32[4,14]{1,0:T(4,128)}, u32[]{:S(2)}) copy-start(s32[4,14]{1,0:T(4,128)} %um.3) | copy-start | bytes 676
  142.1 9.8 %collective-permute-start.26 = (bf16[128,512]{1,0:T(8,128)(2,1)S(1)}, bf16[128,512]{1,0:T(8,128)(2,1)S(1)}, u32[]{:S(2)}, u32[]{:S(2)}) collective-permute-start(bf16[128,512]{1,0:T(8,128)(2,1)S(1)} %get-tuple-element.112), channel_id=1, source_target_pairs={{0,96},{16,112},{32,0},{48,16},{64,32},{80,48},{96,64},{112,80},{1... | collective-permute-start | bytes 393224 | tf_op jit(solution)/shard_map/ppermute | solution.py:528
  144.5 7.4 %collective-permute-start.25 = (bf16[128,512]{1,0:T(8,128)(2,1)S(1)}, bf16[128,512]{1,0:T(8,128)(2,1)S(1)}, u32[]{:S(2)}, u32[]{:S(2)}) collective-permute-start(bf16[128,512]{1,0:T(8,128)(2,1)S(1)} %get-tuple-element.113), channel_id=1, source_target_pairs={{0,64},{16,80},{32,96},{48,112},{64,0},{80,16},{96,32},{112,48},{1... | collective-permute-start | bytes 393224 | tf_op jit(solution)/shard_map/ppermute | solution.py:528
  144.7 9.3 %collective-permute-start.24 = (bf16[128,512]{1,0:T(8,128)(2,1)S(1)}, bf16[128,512]{1,0:T(8,128)(2,1)S(1)}, u32[]{:S(2)}, u32[]{:S(2)}) collective-permute-start(bf16[128,512]{1,0:T(8,128)(2,1)S(1)} %get-tuple-element.114), channel_id=1, source_target_pairs={{0,32},{16,48},{32,64},{48,80},{64,96},{80,112},{96,0},{112,16},{1... | collective-permute-start | bytes 393224 | tf_op jit(solution)/shard_map/ppermute | solution.py:528

commit v8 on v7

--- a/solution.py
+++ b/solution.py
@@ -407,31 +407,53 @@
         up_out[:, q * BLK : (q + 1) * BLK] = both[:, BLK:]
 
 
-def last_grad_kernel(gm, um, xt0, xt1, gate_in, up_in, come0, come1, gate_out, up_out):
+def last_grad_kernel(mask, xt0, xt1, early, low0, high0, low1, high1, out):
     j = pl.program_id(0)
-    for q, both in enumerate(plane_products((xt0, xt1), (come0, come1), 2 * CUT)):
+    for q, (turn, low, high) in enumerate(((xt0, low0, high0), (xt1, low1, high1))):
         by = slice(q * BLK, (q + 1) * BLK)
+        grad = jnp.dot(
+            turn[:, 2 * CUT :],
+            jnp.concatenate([low[0], high[0]], axis=0),
+            preferred_element_type=F32,
+        )
         for r in range(4):
             at = slice(r * BLK, (r + 1) * BLK)
-            gate_out[at, by] = kept(gm, r, 2 * j + q, gate_in[at, by] + both[at, :BLK])
-            up_out[at, by] = kept(um, r, 2 * j + q, up_in[at, by] + both[at, BLK:])
-
-
-def grad_call(kernel, name, first_specs, middle_specs):
-    columns = pl.BlockSpec((FEAT, PAIR), lambda j: (0, j))
-    return call(
-        kernel,
-        name,
+            out[at, by] = kept(mask, r, 2 * j + q, early[at, by] + grad[at, :])
+
+
+COLUMNS = pl.BlockSpec((FEAT, PAIR), lambda j: (0, j))
+
+
+def first_grad(turns, derived_own):
+    return call(
+        first_grad_kernel,
+        "first_grad",
         2 * LIVE * FEAT * UNITS,
         13 << 20,
         grid=(STEPS,),
         out_shape=(jax.ShapeDtypeStruct((FEAT, UNITS), F32),) * 2,
-        in_specs=[smem()] * first_specs
-        + [whole((FEAT, LIVE))] * 2
-        + [columns] * middle_specs
+        in_specs=[whole((FEAT, LIVE))] * 2
         + [pl.BlockSpec((2, 2 * CUT, BLK), lambda j: (0, 0, j))] * 2,
-        out_specs=(columns,) * 2,
-    )
+        out_specs=(COLUMNS,) * 2,
+    )(*turns, *derived_own)
+
+
+def last_grad(mask, turns, early, low, high):
+    specs, arrays = [], []
+    for q in SIDES:
+        for values, plane in (low, high):
+            arrays.append(values[q])
+            specs.append(pl.BlockSpec((1, CUT, BLK), lambda j, plane=plane: (plane, 0, j)))
+    return call(
+        last_grad_kernel,
+        "last_grad",
+        LIVE * FEAT * UNITS,
+        6 << 20,
+        grid=(STEPS,),
+        out_shape=jax.ShapeDtypeStruct((FEAT, UNITS), F32),
+        in_specs=[smem()] + [whole((FEAT, LIVE))] * 2 + [COLUMNS] + specs,
+        out_specs=COLUMNS,
+    )(mask, *turns, early, *arrays)
 
 
 def split(value, axis):
@@ -514,11 +536,17 @@
     hidden_own = [jnp.concatenate([held[q][2:], near[q][2:]], axis=1) for q in SIDES]
     derived_own = [jnp.concatenate([held[q][:2], near[q][:2]], axis=1) for q in SIDES]
     hidden_come = exchange(hidden_own, 0)
-    derived_come = exchange(derived_own, 0)
+    quarters = [value.reshape(4, CUT, HALF) for value in derived_own]
+    most_come = exchange([value[:3] for value in quarters], 0)
 
     begun = first_output(wd, hidden_own)
-    grads_begun = grad_call(first_grad_kernel, "first_grad", 0, 0)(turn0, turn1, *derived_own)
-    begun, *grads_begun = lax.optimization_barrier((begun, *grads_begun))
+    turns = (turn0, turn1)
+    gate_begun, up_begun = first_grad(turns, derived_own)
+    ends = [value[3:] for value in quarters]
+    *ends, begun, gate_begun, up_begun = lax.optimization_barrier(
+        (*ends, begun, gate_begun, up_begun)
+    )
+    end_come = exchange(ends, 0)
     mine, away = last_output(rows_along, offs, cnts, begun, wd, hidden_come)
     other = lax.ppermute(away, "col", shift(0, 1))
     down_grad = down_gradient(down_mask, g, hidden_own + hidden_come)
@@ -526,9 +554,9 @@
     summed = mine.astype(F32) + other.astype(F32)
     terms = [summed[k].astype(BF) for k in range(4)]
     arrived = [lax.ppermute(terms[dz], "col", shift(dz, 0)) for dz in (1, 2, 3)]
-    gate_grad, up_grad = grad_call(last_grad_kernel, "last_grad", 2, 2)(
-        gate_mask, up_mask, turn0, turn1, *grads_begun, *derived_come
-    )
+    gate_grad = last_grad(gate_mask, turns, gate_begun, (most_come, 0), (most_come, 1))
+    *end_come, gate_grad = lax.optimization_barrier((*end_come, gate_grad))
+    up_grad = last_grad(up_mask, turns, up_begun, (most_come, 2), (end_come, 0))
     *arrived, gate_grad, up_grad = lax.optimization_barrier((*arrived, gate_grad, up_grad))
     mixed = sum((term.astype(F32) for term in arrived), terms[0].astype(F32))
     output = jnp.where(live, mixed, jnp.zeros_like(mixed)).astype(BF)

time: 155 us -> 161 us (1.039)
  Pallas kernels: 35.5 us -> 39.7 us
  starting transfers between devices: 39.2 us -> 41.8 us
  waiting for transfers between devices: 65.5 us -> 63.3 us
    pallas_call x2 -> x3, Pallas kernels: 10.8 us -> 14.9 us  [the longest x2 10.9 us: last_grad(): call(last_grad_kernel, 'last_grad', LIVE * FEAT * UNITS, 6 << 20, grid=(S...]
    ppermute x3, starting transfers between devices: 1.38 us -> 5.34 us  [on_device(): beside += [lax.ppermute(value, 'col', shift(0, 1)) for value in column[1:]]]
    ppermute x3, waiting for transfers between devices: 2.23 us -> 0.01 us  [on_device(): lax.ppermute(own, 'col', shift(-dz, 0))]
    ppermute x18 -> x20, waiting for transfers between devices: 59.7 us -> 61.7 us  [exchange(): lax.ppermute(values[q], ('col', 'dp'), partners(ROUNDS[q][number][1]))]
    ppermute x3, waiting for transfers between devices: 2.08 us -> 0.01 us  [on_device(): arrived = [lax.ppermute(terms[dz], 'col', shift(dz, 0)) for dz in (1, 2, 3)]]
    ppermute x18 -> x20, starting transfers between devices: 19.1 us -> 18.8 us  [exchange(): lax.ppermute(values[q], ('col', 'dp'), partners(ROUNDS[q][number][1]))]
  transfers between devices with their start and end apart: 29 -> 31, of which waited for: 18 -> 13; matrix products, arithmetic and copies ran while one was open for 2% -> 2% of each run, Pallas kernels for 20% -> 22%
where the time goes in v8:
time: 161 us; the launch traced here: 160 us
  waiting for transfers between devices  63.3 us (39%)
  starting transfers between devices  41.8 us (26%)
  Pallas kernels  39.7 us (25%)
  local copies, waits for them, and re-layouts  9.23 us (6%)
  other arithmetic  3.9 us (2%)
  between operations  1.72 us (1%)
    ppermute x20, waiting for transfers between devices, exchange(): lax.ppermute(values[q], ('col', 'dp'), partners(ROUNDS[q][number][1]))  61.7 us
    ppermute x20, starting transfers between devices, exchange(): lax.ppermute(values[q], ('col', 'dp'), partners(ROUNDS[q][number][1]))  18.8 us
    pallas_call x2, Pallas kernels, last_grad(): call(last_grad_kernel, 'last_grad', LIVE * FEAT * UNITS, 6 << 20, grid=(S...  10.9 us
    unnamed x19, local copies, waits for them, and re-layouts  8.44 us
    pallas_call x2, Pallas kernels, partials(): call(functools.partial(partial_kernel, start, pieces), 'partials', 2 * co...  8.2 us
    ppermute x1, starting transfers between devices, on_device(): other = lax.ppermute(away, 'col', shift(0, 1))  7.37 us
    ppermute x3, starting transfers between devices, on_device(): lax.ppermute(own, 'col', shift(-dz, 0))  5.96 us
    pallas_call x1, Pallas kernels, down_gradient(): call(down_kernel, 'down_gradient', 1, 1 << 12, grid=(STEPS,), out_shape=j...  5.67 us
  transfers between devices with their start and end apart: 31, of which 13 were waited for; matrix products, arithmetic and copies ran while one was open for 2% of the time, Pallas kernels for 22%

profile of v8, /device:TPU:1, one launch (start us, length us, event | category | flops | bytes accessed | tf_op | source)
XLA Modules:
  0.0 159.6 jit_solution(12413407765511830947)
XLA Ops:
  1.3 0.9 copy-done.3
  2.2 0.9 copy-done.4
  3.2 4.7 %collective-permute-start = (bf16[144,1024]{1,0:T(8,128)(2,1)S(1)}, bf16[144,1024]{1,0:T(8,128)(2,1)S(1)}, u32[]{:S(2)}, u32[]{:S(2)}) collective-permute-start(bf16[144,1024]{1,0:T(8,128)(2,1)S(1)} %pack.1.refs_0_), channel_id=1, source_target_pairs={{0,96},{16,112},{32,0},{48,16},{64,32},{80,48},{96,64},{112,80},{1... | collective-permute-start | bytes 884744 | tf_op jit(solution)/shard_map/ppermute | solution.py:489
  7.8 1.3 collective-permute-start.2
  9.1 1.5 collective-permute-start.3
  10.6 0.8 copy.13.dm
  11.4 1.5 copy-done
  12.9 1.5 copy-done.1
  14.4 1.5 copy-done.2
  15.9 0.7 copy-done.5
  16.6 0.7 copy-done.7
  17.3 2.4 %prepare.1 = (bf16[7,512,512]{2,1,0:T(8,128)(2,1)S(1)}, bf16[7,512,256]{2,1,0:T(8,128)(2,1)S(1)}, bf16[1792,512]{1,0:T(8,128)(2,1)S(1)}) custom-call(s32[4,14]{1,0:T(4,128)S(1)} %copy-done.7, s32[4,14]{1,0:T(4,128)S(1)} %copy-done.5, s32[14,4]{1,0:T(8,128)S(1)} %copy.13.dm, bf16[512,1792]{1,0:T(8,128)(2,1)S(1)} %copy-done, bf16[512,1792]{1,0:T(8,128)(2,1)S(1)} %copy-done.1, ...), custom_call_target="tpu_custom_call" | custom-call | bytes 13631488 | tf_op jit(solution)/shard_map/prepare/pallas_call | solution.py:146
  19.7 0.2 fusion.10.rows_ref
  19.9 4.8 %collective-permute-start.4 = (bf16[144,1024]{1,0:T(8,128)(2,1)S(1)}, bf16[144,1024]{1,0:T(8,128)(2,1)S(1)}, u32[]{:S(2)}, u32[]{:S(2)}) collective-permute-start(bf16[144,1024]{1,0:T(8,128)(2,1)S(1)} %collective-permute-done.refs_1_), channel_id=1, source_target_pairs={{0,16},{16,0},{32,48},{48,32},{64,80},{80,64},{96,112},{112,96},{1... | collective-permute-start | bytes 884744 | tf_op jit(solution)/shard_map/ppermute | solution.py:496
  24.8 0.5 collective-permute-start.5
  25.3 0.7 collective-permute-done.4.refs_5_
  26.0 0.4 collective-permute-done.6.refs_7_
  26.4 0.4 collective-permute-done.5.refs_6_
  26.8 2.4 %compact.1 = (bf16[768,512]{1,0:T(8,128)(2,1)S(1)}, bf16[768,512]{1,0:T(8,128)(2,1)S(1)}, s32[8,8,128]{2,1,0:T(8,128)S(1)}, s32[8,8,128]{2,1,0:T(8,128)S(1)}) custom-call(s32[8]{0:T(128)S(1)} %fusion.23.shard, s32[768,1]{1,0:T(8,128)S(1)} %fusion.10.rows_ref, bf16[144,1024]{1,0:T(8,128)(2,1)S(1)} %pack.1.refs_0_, ...), custom_call_target="tpu_custom_call" | custom-call | flops 1610612736 | bytes 5242880 | tf_op jit(solution)/shard_map/compact/pallas_call | solution.py:201
  29.3 2.7 %partials.2 = (bf16[3,192,896]{2,1,0:T(8,128)(2,1)S(1)}, bf16[3,192,896]{2,1,0:T(8,128)(2,1)S(1)}) custom-call(bf16[768,512]{1,0:T(8,128)(2,1)S(1)} %get-tuple-element.74.x_ref, bf16[768,512]{1,0:T(8,128)(2,1)S(1)} %get-tuple-element.75.g_ref, bf16[7,512,512]{2,1,0:T(8,128)(2,1)S(1)} %get-tuple-element.70.wx_ref, ...), custom_call_target="tpu_custom_call" | custom-call | flops 1056964608 | bytes 7340032 | tf_op jit(solution)/shard_map/partials/pallas_call | solution.py:254
  32.0 2.8 %collective-permute-start.10 = (bf16[3,192,896]{2,1,0:T(8,128)(2,1)S(1)}, bf16[3,192,896]{2,1,0:T(8,128)(2,1)S(1)}, u32[]{:S(2)}, u32[]{:S(2)}) collective-permute-start(bf16[3,192,896]{2,1,0:T(8,128)(2,1)S(1)} %get-tuple-element.73), channel_id=1, source_target_pairs={{0,12},{1,13},{2,14},{3,15},{4,8},{5,9},{6,10},{7,11},{8,4},{9,5},... | collective-permute-start | bytes 3096584 | tf_op jit(solution)/shard_map/ppermute | solution.py:477
  34.8 0.5 turned.1
  35.2 5.5 %partials.3 = (bf16[3,192,896]{2,1,0:T(8,128)(2,1)S(1)}, bf16[3,192,896]{2,1,0:T(8,128)(2,1)S(1)}, bf16[3,192,896]{2,1,0:T(8,128)(2,1)S(1)}, bf16[3,192,896]{2,1...) custom-call(bf16[768,512]{1,0:T(8,128)(2,1)S(1)} %get-tuple-element.74.x_ref, ...), custom_call_target="tpu_custom_call" | custom-call | flops 3170893824 | bytes 7340032 | tf_op jit(solution)/shard_map/partials/pallas_call | solution.py:254
  40.8 1.5 collective-permute-start.7
  42.4 4.7 %collective-permute-done.10 = bf16[3,192,896]{2,1,0:T(8,128)(2,1)S(1)} collective-permute-done((bf16[3,192,896]{2,1,0:T(8,128)(2,1)S(1)}, bf16[3,192,896]{2,1,0:T(8,128)(2,1)S(1)}, u32[]{:S(2)}, u32[]{:S(2)}) %collective-permute-start.10) | collective-permute-done | bytes 1032224 | tf_op jit(solution)/shard_map/ppermute | solution.py:477
  47.1 1.5 collective-permute-done.9
  48.5 0.2 add_convert_fusion
  48.9 0.2 add_convert_fusion.1
  49.1 1.3 collective-permute-start.11
  50.4 9.2 %collective-permute-done.7 = bf16[3,192,896]{2,1,0:T(8,128)(2,1)S(1)} collective-permute-done((bf16[3,192,896]{2,1,0:T(8,128)(2,1)S(1)}, bf16[3,192,896]{2,1,0:T(8,128)(2,1)S(1)}, u32[]{:S(2)}, u32[]{:S(2)}) %collective-permute-start.7) | collective-permute-done | bytes 1032224 | tf_op jit(solution)/shard_map/ppermute | solution.py:477
  59.6 11.1 %collective-permute-done.12 = bf16[3,192,896]{2,1,0:T(8,128)(2,1)S(1)} collective-permute-done((bf16[3,192,896]{2,1,0:T(8,128)(2,1)S(1)}, bf16[3,192,896]{2,1,0:T(8,128)(2,1)S(1)}, u32[]{:S(2)}, u32[]{:S(2)}) %collective-permute-start.12) | collective-permute-done | bytes 1032224 | tf_op jit(solution)/shard_map/ppermute | solution.py:477
  70.7 0.7 convert_add_fusion
  71.4 2.3 %collective-permute-start.17 = (bf16[3,2,1,48,896]{4,3,2,1,0:T(8,128)(2,1)S(1)}, bf16[3,2,1,48,896]{4,3,2,1,0:T(8,128)(2,1)S(1)}, u32[]{:S(2)}, u32[]{:S(2)}) collective-permute-start(bf16[3,2,1,48,896]{4,3,2,1,0:T(8,128)(2,1)S(1)} %slice.206), channel_id=1, source_target_pairs={{0,3},{1,2},{2,1},{3,0},{4,7},{5,6},{6,5},{7,4},{8,11},{9,10},{10,... | collective-permute-start | bytes 1548296 | tf_op jit(solution)/shard_map/ppermute | solution.py:477
  73.8 7.1 %collective-permute-done.17 = bf16[3,2,1,48,896]{4,3,2,1,0:T(8,128)(2,1)S(1)} collective-permute-done((bf16[3,2,1,48,896]{4,3,2,1,0:T(8,128)(2,1)S(1)}, bf16[3,2,1,48,896]{4,3,2,1,0:T(8,128)(2,1)S(1)}, u32[]{:S(2)}, u32[]{:S(2)}) %collective-permute-start.17) | collective-permute-done | bytes 516128 | tf_op jit(solution)/shard_map/ppermute | solution.py:477
  81.0 0.1 fusion
  81.2 0.9 collective-permute-done.13
  82.1 0.1 fusion.1
  82.2 1.4 collective-permute-start.14
  83.6 5.8 %collective-permute-done.18 = bf16[3,2,1,48,896]{4,3,2,1,0:T(8,128)(2,1)S(1)} collective-permute-done((bf16[3,2,1,48,896]{4,3,2,1,0:T(8,128)(2,1)S(1)}, bf16[3,2,1,48,896]{4,3,2,1,0:T(8,128)(2,1)S(1)}, u32[]{:S(2)}, u32[]{:S(2)}) %collective-permute-start.18) | collective-permute-done | bytes 516128 | tf_op jit(solution)/shard_map/ppermute | solution.py:477
  89.6 0.2 multiply_convert_fusion.2
  89.8 2.3 %collective-permute-start.19 = (bf16[3,2,1,48,896]{4,3,2,1,0:T(8,128)(2,1)S(1)}, bf16[3,2,1,48,896]{4,3,2,1,0:T(8,128)(2,1)S(1)}, u32[]{:S(2)}, u32[]{:S(2)}) collective-permute-start(bf16[3,2,1,48,896]{4,3,2,1,0:T(8,128)(2,1)S(1)} %pad_maximum_fusion.7), channel_id=1, source_target_pairs={{0,3},{1,2},{2,1},{3,0},{4,7},{5,6},{6,5},{7,4},{8,11},{9,10},{10,... | collective-permute-start | bytes 1548296 | tf_op jit(solution)/shard_map/ppermute | solution.py:477
  92.3 0.2 multiply_convert_fusion.5
  92.6 0.3 collective-permute-start.15
  92.8 6.5 %collective-permute-done.19 = bf16[3,2,1,48,896]{4,3,2,1,0:T(8,128)(2,1)S(1)} collective-permute-done((bf16[3,2,1,48,896]{4,3,2,1,0:T(8,128)(2,1)S(1)}, bf16[3,2,1,48,896]{4,3,2,1,0:T(8,128)(2,1)S(1)}, u32[]{:S(2)}, u32[]{:S(2)}) %collective-permute-start.19) | collective-permute-done | bytes 516128 | tf_op jit(solution)/shard_map/ppermute | solution.py:477
  99.4 0.1 pad_maximum_fusion.3
  99.6 1.4 collective-permute-done.15
  101.0 0.1 pad_maximum_fusion.2
  101.2 1.6 collective-permute-start.16
  102.8 13.5 %collective-permute-done.20 = bf16[3,192,896]{2,1,0:T(8,128)(2,1)S(1)} collective-permute-done((bf16[3,192,896]{2,1,0:T(8,128)(2,1)S(1)}, bf16[3,192,896]{2,1,0:T(8,128)(2,1)S(1)}, u32[]{:S(2)}, u32[]{:S(2)}) %collective-permute-start.20) | collective-permute-done | bytes 1032224 | tf_op jit(solution)/shard_map/ppermute | solution.py:477
  116.5 0.7 collective-permute-start.22
  117.8 2.1 %collective-permute-start.30 = (bf16[3,192,896]{2,1,0:T(8,128)(2,1)S(1)}, bf16[3,192,896]{2,1,0:T(8,128)(2,1)S(1)}, u32[]{:S(2)}, u32[]{:S(2)}) collective-permute-start(bf16[3,192,896]{2,1,0:T(8,128)(2,1)S(1)} %slice.171), channel_id=1, source_target_pairs={{0,12},{1,13},{2,14},{3,15},{4,8},{5,9},{6,10},{7,11},{8,4},{9,5},... | collective-permute-start | bytes 3096584 | tf_op jit(solution)/shard_map/ppermute | solution.py:477
  120.2 0.9 collective-permute-start.29
  121.1 4.0 %first_grad.1 = (f32[512,1792]{1,0:T(8,128)S(1)}, f32[512,1792]{1,0:T(8,128)S(1)}) custom-call(bf16[512,768]{1,0:T(8,128)(2,1)S(1)} %get-tuple-element.91.xt0, bf16[512,768]{1,0:T(8,128)(2,1)S(1)} %get-tuple-element.92.xt1, bf16[2,384,896]{2,1,0:T(8,128)(2,1)S(1)} %pad_maximum_fusion.own0, bf16[2,384,896]{2,1,0:T(8,128)(2,1)S(1)} %pad_maximum_fusion.1.own1), custom_call_target="tpu_custom_call" | custom-call | flops 1409286144 | bytes 13631488 | tf_op jit(solution)/shard_map/first_grad/pallas_call | solution.py:428
  125.1 3.3 %first_output.1.early_ref = f32[3,192,512]{2,1,0:T(8,128)S(1)} custom-call(bf16[1792,512]{1,0:T(8,128)(2,1)S(1)} %get-tuple-element.90.wd_ref, bf16[1,384,896]{2,1,0:T(8,128)(2,1)S(1)} %pad_maximum_fusion.4.own0, bf16[1,384,896]{2,1,0:T(8,128)(2,1)S(1)} %pad_maximum_fusion.5.own1), custom_call_target="tpu_custom_call" | custom-call | flops 1 | bytes 4096 | tf_op jit(solution)/shard_map/first_output/pallas_call | solution.py:306
  128.5 2.3 %last_output.1 = (bf16[4,128,512]{2,1,0:T(8,128)(2,1)S(1)}, bf16[4,128,512]{2,1,0:T(8,128)(2,1)S(1)}) custom-call(s32[1,768]{1,0:T(1,128)S(1)} %fusion.18.rows_ref, s32[8,8,128]{2,1,0:T(8,128)S(1)} %get-tuple-element.66.offs, s32[8,8,128]{2,1,0:T(8,128)S(1)} %get-tuple-element.67.cnts, f32[3,192,512]{2,1,0:T(8,128)S(1)} %first_output.1.early_ref, ...), custom_call_target="tpu_custom_call" | custom-call | flops 1 | bytes 4096 | tf_op jit(solution)/shard_map/last_output/pallas_call | solution.py:338
  130.8 7.4 %collective-permute-start.23 = (bf16[4,128,512]{2,1,0:T(8,128)(2,1)S(1)}, bf16[4,128,512]{2,1,0:T(8,128)(2,1)S(1)}, u32[]{:S(2)}, u32[]{:S(2)}) collective-permute-start(bf16[4,128,512]{2,1,0:T(8,128)(2,1)S(1)} %get-tuple-element.97), channel_id=1, source_target_pairs={{0,16},{16,0},{32,48},{48,32},{64,80},{80,64},{96,112},{112,96},{1... | collective-permute-start | bytes 1572872 | tf_op jit(solution)/shard_map/ppermute | solution.py:551
  138.2 1.1 collective-permute-start.28
  139.3 5.7 %down_gradient.1 = f32[1792,512]{1,0:T(8,128)} custom-call(s32[14,4]{1,0:T(8,128)S(1)} %copy.13.dm, bf16[768,512]{1,0:T(8,128)(2,1)S(1)} %get-tuple-element.75.g_ref, bf16[1,384,896]{2,1,0:T(8,128)(2,1)S(1)} %pad_maximum_fusion.4.own0, bf16[1,384,896]{2,1,0:T(8,128)(2,1)S(1)} %pad_maximum_fusion.5.own1, ...), custom_call_target="tpu_custom_call" | custom-call | flops 1 | bytes 4096 | tf_op jit(solution)/shard_map/down_gradient/pallas_call | solution.py:380
  144.9 0.1 add_convert_fusion.2
  145.2 1.1 collective-permute-start.25
  146.4 1.6 %collective-permute-start.26 = (bf16[128,512]{1,0:T(8,128)(2,1)S(1)}, bf16[128,512]{1,0:T(8,128)(2,1)S(1)}, u32[]{:S(2)}, u32[]{:S(2)}) collective-permute-start(bf16[128,512]{1,0:T(8,128)(2,1)S(1)} %get-tuple-element.118), channel_id=1, source_target_pairs={{0,96},{16,112},{32,0},{48,16},{64,32},{80,48},{96,64},{112,80},{1... | collective-permute-start | bytes 393224 | tf_op jit(solution)/shard_map/ppermute | solution.py:556
  148.0 5.4 %last_grad.2 = f32[512,1792]{1,0:T(8,128)} custom-call(s32[4,14]{1,0:T(4,128)S(1)} %copy-done.8, bf16[512,768]{1,0:T(8,128)(2,1)S(1)} %get-tuple-element.91.xt0, bf16[512,768]{1,0:T(8,128)(2,1)S(1)} %get-tuple-element.92.xt1, f32[512,1792]{1,0:T(8,128)S(1)} %get-tuple-element.101.early, bf16[3,192,896]{2,1,0:T(8,128)(2,1)S(1)} %collective-permute-done.29.low0.high0, ...), custom_call_target="tpu_custom_call" | custom-call | flops 704643072 | bytes 6291456 | tf_op jit(solution)/shard_map/last_grad/pallas_call | solution.py:447
  153.4 5.4 %last_grad.3 = f32[512,1792]{1,0:T(8,128)} custom-call(s32[4,14]{1,0:T(4,128)S(1)} %copy-done.6, bf16[512,768]{1,0:T(8,128)(2,1)S(1)} %get-tuple-element.91.xt0, bf16[512,768]{1,0:T(8,128)(2,1)S(1)} %get-tuple-element.92.xt1, f32[512,1792]{1,0:T(8,128)S(1)} %get-tuple-element.103.early, bf16[3,192,896]{2,1,0:T(8,128)(2,1)S(1)} %collective-permute-done.29.low0.high0, ...), custom_call_target="tpu_custom_call" | custom-call | flops 704643072 | bytes 6291456 | tf_op jit(solution)/shard_map/last_grad/pallas_call | solution.py:447
  158.8 0.8 fusion.17
  (69 shorter events, 2.3 us)
Async XLA Ops:
  1.3 0.9 copy-start.3
  2.2 0.9 copy-start.4
  3.2 16.8 %collective-permute-start = (bf16[144,1024]{1,0:T(8,128)(2,1)S(1)}, bf16[144,1024]{1,0:T(8,128)(2,1)S(1)}, u32[]{:S(2)}, u32[]{:S(2)}) collective-permute-start(bf16[144,1024]{1,0:T(8,128)(2,1)S(1)} %pack.1.refs_0_), channel_id=1, source_target_pairs={{0,96},{16,112},{32,0},{48,16},{64,32},{80,48},{96,64},{112,80},{1... | collective-permute-start | bytes 884744 | tf_op jit(solution)/shard_map/ppermute | solution.py:489
  7.8 12.1 %collective-permute-start.1 = (bf16[144,1024]{1,0:T(8,128)(2,1)S(1)}, bf16[144,1024]{1,0:T(8,128)(2,1)S(1)}, u32[]{:S(2)}, u32[]{:S(2)}) collective-permute-start(bf16[144,1024]{1,0:T(8,128)(2,1)S(1)} %pack.1.refs_0_), channel_id=1, source_target_pairs={{0,32},{16,48},{32,64},{48,80},{64,96},{80,112},{96,0},{112,16},{1... | collective-permute-start | bytes 884744 | tf_op jit(solution)/shard_map/ppermute | solution.py:489
  7.8 17.0 %collective-permute-start.2 = (bf16[144,1024]{1,0:T(8,128)(2,1)S(1)}, bf16[144,1024]{1,0:T(8,128)(2,1)S(1)}, u32[]{:S(2)}, u32[]{:S(2)}) collective-permute-start(bf16[144,1024]{1,0:T(8,128)(2,1)S(1)} %pack.1.refs_0_), channel_id=1, source_target_pairs={{0,64},{16,80},{32,96},{48,112},{64,0},{80,16},{96,32},{112,48},{1... | collective-permute-start | bytes 884744 | tf_op jit(solution)/shard_map/ppermute | solution.py:489
  9.1 16.2 %collective-permute-start.3 = (bf16[144,1024]{1,0:T(8,128)(2,1)S(1)}, bf16[144,1024]{1,0:T(8,128)(2,1)S(1)}, u32[]{:S(2)}, u32[]{:S(2)}) collective-permute-start(bf16[144,1024]{1,0:T(8,128)(2,1)S(1)} %pack.1.refs_0_), channel_id=1, source_target_pairs={{0,16},{16,0},{32,48},{48,32},{64,80},{80,64},{96,112},{112,96},{1... | collective-permute-start | bytes 884744 | tf_op jit(solution)/shard_map/ppermute | solution.py:490
  11.4 1.5 copy-start
  12.9 1.5 copy-start.1
  14.4 1.5 copy-start.2
  15.9 0.7 copy-start.5
  16.6 0.7 copy-start.7
  19.9 6.0 %collective-permute-start.4 = (bf16[144,1024]{1,0:T(8,128)(2,1)S(1)}, bf16[144,1024]{1,0:T(8,128)(2,1)S(1)}, u32[]{:S(2)}, u32[]{:S(2)}) collective-permute-start(bf16[144,1024]{1,0:T(8,128)(2,1)S(1)} %collective-permute-done.refs_1_), channel_id=1, source_target_pairs={{0,16},{16,0},{32,48},{48,32},{64,80},{80,64},{96,112},{112,96},{1... | collective-permute-start | bytes 884744 | tf_op jit(solution)/shard_map/ppermute | solution.py:496
  24.8 1.6 %collective-permute-start.6 = (bf16[144,1024]{1,0:T(8,128)(2,1)S(1)}, bf16[144,1024]{1,0:T(8,128)(2,1)S(1)}, u32[]{:S(2)}, u32[]{:S(2)}) collective-permute-start(bf16[144,1024]{1,0:T(8,128)(2,1)S(1)} %collective-permute-done.1.refs_3_), channel_id=1, source_target_pairs={{0,16},{16,0},{32,48},{48,32},{64,80},{80,64},{96,112},{112,96},{1... | collective-permute-start | bytes 884744 | tf_op jit(solution)/shard_map/ppermute | solution.py:496
  24.8 2.0 %collective-permute-start.5 = (bf16[144,1024]{1,0:T(8,128)(2,1)S(1)}, bf16[144,1024]{1,0:T(8,128)(2,1)S(1)}, u32[]{:S(2)}, u32[]{:S(2)}) collective-permute-start(bf16[144,1024]{1,0:T(8,128)(2,1)S(1)} %collective-permute-done.2.refs_2_), channel_id=1, source_target_pairs={{0,16},{16,0},{32,48},{48,32},{64,80},{80,64},{96,112},{112,96},{1... | collective-permute-start | bytes 884744 | tf_op jit(solution)/shard_map/ppermute | solution.py:496
  32.0 15.1 %collective-permute-start.10 = (bf16[3,192,896]{2,1,0:T(8,128)(2,1)S(1)}, bf16[3,192,896]{2,1,0:T(8,128)(2,1)S(1)}, u32[]{:S(2)}, u32[]{:S(2)}) collective-permute-start(bf16[3,192,896]{2,1,0:T(8,128)(2,1)S(1)} %get-tuple-element.73), channel_id=1, source_target_pairs={{0,12},{1,13},{2,14},{3,15},{4,8},{5,9},{6,10},{7,11},{8,4},{9,5},... | collective-permute-start | bytes 3096584 | tf_op jit(solution)/shard_map/ppermute | solution.py:477
  34.8 13.8 %collective-permute-start.9 = (bf16[3,192,896]{2,1,0:T(8,128)(2,1)S(1)}, bf16[3,192,896]{2,1,0:T(8,128)(2,1)S(1)}, u32[]{:S(2)}, u32[]{:S(2)}) collective-permute-start(bf16[3,192,896]{2,1,0:T(8,128)(2,1)S(1)} %get-tuple-element.72), channel_id=1, source_target_pairs={{0,4},{1,5},{2,6},{3,7},{4,0},{5,1},{6,2},{7,3},{8,12},{9,13},{10,... | collective-permute-start | bytes 3096584 | tf_op jit(solution)/shard_map/ppermute | solution.py:477
  40.8 18.8 %collective-permute-start.7 = (bf16[3,192,896]{2,1,0:T(8,128)(2,1)S(1)}, bf16[3,192,896]{2,1,0:T(8,128)(2,1)S(1)}, u32[]{:S(2)}, u32[]{:S(2)}) collective-permute-start(bf16[3,192,896]{2,1,0:T(8,128)(2,1)S(1)} %get-tuple-element.77), channel_id=1, source_target_pairs={{0,4},{1,5},{2,6},{3,7},{4,0},{5,1},{6,2},{7,3},{8,12},{9,13},{10,... | collective-permute-start | bytes 3096584 | tf_op jit(solution)/shard_map/ppermute | solution.py:477
  42.3 17.3 %collective-permute-start.8 = (bf16[3,192,896]{2,1,0:T(8,128)(2,1)S(1)}, bf16[3,192,896]{2,1,0:T(8,128)(2,1)S(1)}, u32[]{:S(2)}, u32[]{:S(2)}) collective-permute-start(bf16[3,192,896]{2,1,0:T(8,128)(2,1)S(1)} %get-tuple-element.78), channel_id=1, source_target_pairs={{0,12},{1,13},{2,14},{3,15},{4,8},{5,9},{6,10},{7,11},{8,4},{9,5},... | collective-permute-start | bytes 3096584 | tf_op jit(solution)/shard_map/ppermute | solution.py:477
  48.8 21.9 %collective-permute-start.12 = (bf16[3,192,896]{2,1,0:T(8,128)(2,1)S(1)}, bf16[3,192,896]{2,1,0:T(8,128)(2,1)S(1)}, u32[]{:S(2)}, u32[]{:S(2)}) collective-permute-start(bf16[3,192,896]{2,1,0:T(8,128)(2,1)S(1)} %add_convert_fusion), channel_id=1, source_target_pairs={{0,4},{1,5},{2,6},{3,7},{4,0},{5,1},{6,2},{7,3},{8,12},{9,13},{10,... | collective-permute-start | bytes 3096584 | tf_op jit(solution)/shard_map/ppermute | solution.py:477
  49.1 21.5 %collective-permute-start.11 = (bf16[3,192,896]{2,1,0:T(8,128)(2,1)S(1)}, bf16[3,192,896]{2,1,0:T(8,128)(2,1)S(1)}, u32[]{:S(2)}, u32[]{:S(2)}) collective-permute-start(bf16[3,192,896]{2,1,0:T(8,128)(2,1)S(1)} %add_convert_fusion.1), channel_id=1, source_target_pairs={{0,12},{1,13},{2,14},{3,15},{4,8},{5,9},{6,10},{7,11},{8,4},{9,5},... | collective-permute-start | bytes 3096584 | tf_op jit(solution)/shard_map/ppermute | solution.py:477
  71.4 9.5 %collective-permute-start.17 = (bf16[3,2,1,48,896]{4,3,2,1,0:T(8,128)(2,1)S(1)}, bf16[3,2,1,48,896]{4,3,2,1,0:T(8,128)(2,1)S(1)}, u32[]{:S(2)}, u32[]{:S(2)}) collective-permute-start(bf16[3,2,1,48,896]{4,3,2,1,0:T(8,128)(2,1)S(1)} %slice.206), channel_id=1, source_target_pairs={{0,3},{1,2},{2,1},{3,0},{4,7},{5,6},{6,5},{7,4},{8,11},{9,10},{10,... | collective-permute-start | bytes 1548296 | tf_op jit(solution)/shard_map/ppermute | solution.py:477
  73.8 8.3 %collective-permute-start.13 = (bf16[3,1,2,48,896]{4,3,2,1,0:T(8,128)(2,1)S(1)}, bf16[3,1,2,48,896]{4,3,2,1,0:T(8,128)(2,1)S(1)}, u32[]{:S(2)}, u32[]{:S(2)}) collective-permute-start(bf16[3,1,2,48,896]{4,3,2,1,0:T(8,128)(2,1)S(1)} %slice.207), channel_id=1, source_target_pairs={{0,1},{1,0},{2,3},{3,2},{4,5},{5,4},{6,7},{7,6},{8,9},{9,8},{10,11... | collective-permute-start | bytes 1548296 | tf_op jit(solution)/shard_map/ppermute | solution.py:477
  81.1 8.3 %collective-permute-start.18 = (bf16[3,2,1,48,896]{4,3,2,1,0:T(8,128)(2,1)S(1)}, bf16[3,2,1,48,896]{4,3,2,1,0:T(8,128)(2,1)S(1)}, u32[]{:S(2)}, u32[]{:S(2)}) collective-permute-start(bf16[3,2,1,48,896]{4,3,2,1,0:T(8,128)(2,1)S(1)} %fusion), channel_id=1, source_target_pairs={{0,1},{1,0},{2,3},{3,2},{4,5},{5,4},{6,7},{7,6},{8,9},{9,8},{10,11... | collective-permute-start | bytes 1548296 | tf_op jit(solution)/shard_map/ppermute | solution.py:477
  82.2 9.9 %collective-permute-start.14 = (bf16[3,1,2,48,896]{4,3,2,1,0:T(8,128)(2,1)S(1)}, bf16[3,1,2,48,896]{4,3,2,1,0:T(8,128)(2,1)S(1)}, u32[]{:S(2)}, u32[]{:S(2)}) collective-permute-start(bf16[3,1,2,48,896]{4,3,2,1,0:T(8,128)(2,1)S(1)} %fusion.1), channel_id=1, source_target_pairs={{0,3},{1,2},{2,1},{3,0},{4,7},{5,6},{6,5},{7,4},{8,11},{9,10},{10,... | collective-permute-start | bytes 1548296 | tf_op jit(solution)/shard_map/ppermute | solution.py:477
  89.8 9.5 %collective-permute-start.19 = (bf16[3,2,1,48,896]{4,3,2,1,0:T(8,128)(2,1)S(1)}, bf16[3,2,1,48,896]{4,3,2,1,0:T(8,128)(2,1)S(1)}, u32[]{:S(2)}, u32[]{:S(2)}) collective-permute-start(bf16[3,2,1,48,896]{4,3,2,1,0:T(8,128)(2,1)S(1)} %pad_maximum_fusion.7), channel_id=1, source_target_pairs={{0,3},{1,2},{2,1},{3,0},{4,7},{5,6},{6,5},{7,4},{8,11},{9,10},{10,... | collective-permute-start | bytes 1548296 | tf_op jit(solution)/shard_map/ppermute | solution.py:477
  92.6 8.5 %collective-permute-start.15 = (bf16[3,1,2,48,896]{4,3,2,1,0:T(8,128)(2,1)S(1)}, bf16[3,1,2,48,896]{4,3,2,1,0:T(8,128)(2,1)S(1)}, u32[]{:S(2)}, u32[]{:S(2)}) collective-permute-start(bf16[3,1,2,48,896]{4,3,2,1,0:T(8,128)(2,1)S(1)} %pad_maximum_fusion.6), channel_id=1, source_target_pairs={{0,1},{1,0},{2,3},{3,2},{4,5},{5,4},{6,7},{7,6},{8,9},{9,8},{10,11... | collective-permute-start | bytes 1548296 | tf_op jit(solution)/shard_map/ppermute | solution.py:477
  99.5 16.9 %collective-permute-start.20 = (bf16[3,192,896]{2,1,0:T(8,128)(2,1)S(1)}, bf16[3,192,896]{2,1,0:T(8,128)(2,1)S(1)}, u32[]{:S(2)}, u32[]{:S(2)}) collective-permute-start(bf16[3,192,896]{2,1,0:T(8,128)(2,1)S(1)} %bitcast.31), channel_id=1, source_target_pairs={{0,4},{1,5},{2,6},{3,7},{4,0},{5,1},{6,2},{7,3},{8,12},{9,13},{10,... | collective-permute-start | bytes 3096584 | tf_op jit(solution)/shard_map/ppermute | solution.py:477
  101.2 16.0 %collective-permute-start.16 = (bf16[3,192,896]{2,1,0:T(8,128)(2,1)S(1)}, bf16[3,192,896]{2,1,0:T(8,128)(2,1)S(1)}, u32[]{:S(2)}, u32[]{:S(2)}) collective-permute-start(bf16[3,192,896]{2,1,0:T(8,128)(2,1)S(1)} %bitcast.32), channel_id=1, source_target_pairs={{0,12},{1,13},{2,14},{3,15},{4,8},{5,9},{6,10},{7,11},{8,4},{9,5},... | collective-permute-start | bytes 3096584 | tf_op jit(solution)/shard_map/ppermute | solution.py:477
  116.5 12.0 %collective-permute-start.22 = (bf16[1,384,896]{2,1,0:T(8,128)(2,1)S(1)}, bf16[1,384,896]{2,1,0:T(8,128)(2,1)S(1)}, u32[]{:S(2)}, u32[]{:S(2)}) collective-permute-start(bf16[1,384,896]{2,1,0:T(8,128)(2,1)S(1)} %pad_maximum_fusion.5.own1), channel_id=1, source_target_pairs={{0,12},{1,13},{2,14},{3,15},{4,8},{5,9},{6,10},{7,11},{8,4},{9,5},... | collective-permute-start | bytes 2064392 | tf_op jit(solution)/shard_map/ppermute | solution.py:477
  117.3 11.2 %collective-permute-start.21 = (bf16[1,384,896]{2,1,0:T(8,128)(2,1)S(1)}, bf16[1,384,896]{2,1,0:T(8,128)(2,1)S(1)}, u32[]{:S(2)}, u32[]{:S(2)}) collective-permute-start(bf16[1,384,896]{2,1,0:T(8,128)(2,1)S(1)} %pad_maximum_fusion.4.own0), channel_id=1, source_target_pairs={{0,4},{1,5},{2,6},{3,7},{4,0},{5,1},{6,2},{7,3},{8,12},{9,13},{10,... | collective-permute-start | bytes 2064392 | tf_op jit(solution)/shard_map/ppermute | solution.py:477
  117.8 27.4 %collective-permute-start.30 = (bf16[3,192,896]{2,1,0:T(8,128)(2,1)S(1)}, bf16[3,192,896]{2,1,0:T(8,128)(2,1)S(1)}, u32[]{:S(2)}, u32[]{:S(2)}) collective-permute-start(bf16[3,192,896]{2,1,0:T(8,128)(2,1)S(1)} %slice.171), channel_id=1, source_target_pairs={{0,12},{1,13},{2,14},{3,15},{4,8},{5,9},{6,10},{7,11},{8,4},{9,5},... | collective-permute-start | bytes 3096584 | tf_op jit(solution)/shard_map/ppermute | solution.py:477
  120.2 26.2 %collective-permute-start.29 = (bf16[3,192,896]{2,1,0:T(8,128)(2,1)S(1)}, bf16[3,192,896]{2,1,0:T(8,128)(2,1)S(1)}, u32[]{:S(2)}, u32[]{:S(2)}) collective-permute-start(bf16[3,192,896]{2,1,0:T(8,128)(2,1)S(1)} %slice.170), channel_id=1, source_target_pairs={{0,4},{1,5},{2,6},{3,7},{4,0},{5,1},{6,2},{7,3},{8,12},{9,13},{10,... | collective-permute-start | bytes 3096584 | tf_op jit(solution)/shard_map/ppermute | solution.py:477
  130.8 14.1 %collective-permute-start.23 = (bf16[4,128,512]{2,1,0:T(8,128)(2,1)S(1)}, bf16[4,128,512]{2,1,0:T(8,128)(2,1)S(1)}, u32[]{:S(2)}, u32[]{:S(2)}) collective-permute-start(bf16[4,128,512]{2,1,0:T(8,128)(2,1)S(1)} %get-tuple-element.97), channel_id=1, source_target_pairs={{0,16},{16,0},{32,48},{48,32},{64,80},{80,64},{96,112},{112,96},{1... | collective-permute-start | bytes 1572872 | tf_op jit(solution)/shard_map/ppermute | solution.py:551
  138.2 15.2 %collective-permute-start.27 = (bf16[1,192,896]{2,1,0:T(8,128)(2,1)S(1)}, bf16[1,192,896]{2,1,0:T(8,128)(2,1)S(1)}, u32[]{:S(2)}, u32[]{:S(2)}) collective-permute-start(bf16[1,192,896]{2,1,0:T(8,128)(2,1)S(1)} %slice.151), channel_id=1, source_target_pairs={{0,4},{1,5},{2,6},{3,7},{4,0},{5,1},{6,2},{7,3},{8,12},{9,13},{10,... | collective-permute-start | bytes 1032200 | tf_op jit(solution)/shard_map/ppermute | solution.py:477
  138.2 15.2 %collective-permute-start.28 = (bf16[1,192,896]{2,1,0:T(8,128)(2,1)S(1)}, bf16[1,192,896]{2,1,0:T(8,128)(2,1)S(1)}, u32[]{:S(2)}, u32[]{:S(2)}) collective-permute-start(bf16[1,192,896]{2,1,0:T(8,128)(2,1)S(1)} %slice.161), channel_id=1, source_target_pairs={{0,12},{1,13},{2,14},{3,15},{4,8},{5,9},{6,10},{7,11},{8,4},{9,5},... | collective-permute-start | bytes 1032200 | tf_op jit(solution)/shard_map/ppermute | solution.py:477
  144.9 3.0 %copy-start.8 = (s32[4,14]{1,0:T(4,128)S(1)}, s32[4,14]{1,0:T(4,128)}, u32[]{:S(2)}) copy-start(s32[4,14]{1,0:T(4,128)} %mask.2) | copy-start | bytes 676
  145.1 13.7 %collective-permute-start.24 = (bf16[128,512]{1,0:T(8,128)(2,1)S(1)}, bf16[128,512]{1,0:T(8,128)(2,1)S(1)}, u32[]{:S(2)}, u32[]{:S(2)}) collective-permute-start(bf16[128,512]{1,0:T(8,128)(2,1)S(1)} %get-tuple-element.120), channel_id=1, source_target_pairs={{0,32},{16,48},{32,64},{48,80},{64,96},{80,112},{96,0},{112,16},{1... | collective-permute-start | bytes 393224 | tf_op jit(solution)/shard_map/ppermute | solution.py:556
  145.2 13.6 %collective-permute-start.25 = (bf16[128,512]{1,0:T(8,128)(2,1)S(1)}, bf16[128,512]{1,0:T(8,128)(2,1)S(1)}, u32[]{:S(2)}, u32[]{:S(2)}) collective-permute-start(bf16[128,512]{1,0:T(8,128)(2,1)S(1)} %get-tuple-element.119), channel_id=1, source_target_pairs={{0,64},{16,80},{32,96},{48,112},{64,0},{80,16},{96,32},{112,48},{1... | collective-permute-start | bytes 393224 | tf_op jit(solution)/shard_map/ppermute | solution.py:556
  146.3 7.0 %copy-start.6 = (s32[4,14]{1,0:T(4,128)S(1)}, s32[4,14]{1,0:T(4,128)}, u32[]{:S(2)}) copy-start(s32[4,14]{1,0:T(4,128)} %mask.3) | copy-start | bytes 676
  146.4 12.5 %collective-permute-start.26 = (bf16[128,512]{1,0:T(8,128)(2,1)S(1)}, bf16[128,512]{1,0:T(8,128)(2,1)S(1)}, u32[]{:S(2)}, u32[]{:S(2)}) collective-permute-start(bf16[128,512]{1,0:T(8,128)(2,1)S(1)} %get-tuple-element.118), channel_id=1, source_target_pairs={{0,96},{16,112},{32,0},{48,16},{64,32},{80,48},{96,64},{112,80},{1... | collective-permute-start | bytes 393224 | tf_op jit(solution)/shard_map/ppermute | solution.py:556

commit v9 on v7

--- a/solution.py
+++ b/solution.py
@@ -76,6 +76,14 @@
 
 def whole(shape):
     return pl.BlockSpec(shape, lambda j: (0,) * len(shape))
+
+
+def vmem():
+    return pl.BlockSpec(memory_space=pltpu.VMEM)
+
+
+def block(j, size):
+    return slice(j * size, (j + 1) * size)
 
 
 def call(kernel, name, flops, moved, **rest):
@@ -224,29 +232,29 @@
 
 
 def turned(x):
-    vmem = pl.BlockSpec(memory_space=pltpu.VMEM)
     return call(
         turn_kernel,
         "turned",
         1,
         1 << 12,
         out_shape=(jax.ShapeDtypeStruct((FEAT, LIVE), BF),) * 2,
-        in_specs=[vmem],
-        out_specs=(vmem,) * 2,
+        in_specs=[vmem()],
+        out_specs=(vmem(),) * 2,
     )(x)
 
 
 def partial_kernel(start, pieces, x_ref, g_ref, wx_ref, wdt_ref, *outs):
     count = pieces * CUT
     x, g = x_ref[start : start + count, :], g_ref[start : start + count, :]
-    both = jnp.dot(x, wx_ref[0], preferred_element_type=F32)
-    back = jnp.dot(g, wdt_ref[0], preferred_element_type=F32)
-    for which, result in enumerate((both[:, :PAIR], both[:, PAIR:], back)):
-        for piece in range(pieces):
-            for q in SIDES:
-                outs[piece * 2 + q][which] = result[
-                    piece * CUT : (piece + 1) * CUT, q * BLK : (q + 1) * BLK
-                ].astype(BF)
+    for j in range(STEPS):
+        both = jnp.dot(x, wx_ref[j], preferred_element_type=F32)
+        back = jnp.dot(g, wdt_ref[j], preferred_element_type=F32)
+        for which, result in enumerate((both[:, :PAIR], both[:, PAIR:], back)):
+            for piece in range(pieces):
+                for q in SIDES:
+                    outs[piece * 2 + q][which, :, block(j, BLK)] = result[
+                        block(piece, CUT), block(q, BLK)
+                    ].astype(BF)
 
 
 def partials(start, pieces, x, g, wx, wdt):
@@ -256,15 +264,9 @@
         "partials",
         2 * count * FEAT * 3 * UNITS,
         7 << 20,
-        grid=(STEPS,),
         out_shape=(jax.ShapeDtypeStruct((3, CUT, HALF), BF),) * (2 * pieces),
-        in_specs=[
-            whole((LIVE, FEAT)),
-            whole((LIVE, FEAT)),
-            pl.BlockSpec((1, FEAT, 2 * PAIR), lambda j: (j, 0, 0)),
-            pl.BlockSpec((1, FEAT, PAIR), lambda j: (j, 0, 0)),
-        ],
-        out_specs=(pl.BlockSpec((3, CUT, BLK), lambda j: (0, 0, j)),) * (2 * pieces),
+        in_specs=[vmem()] * 4,
+        out_specs=(vmem(),) * (2 * pieces),
     )(x, g, wx, wdt)
 
 
@@ -286,20 +288,16 @@
 
 
 def first_output_kernel(wd_ref, own0, own1, total):
-    j = pl.program_id(0)
-    lower = [ref[0, :CUT, :] for ref in (own0, own1)]
-    upper = [ref[0, CUT:, :] for ref in (own0, own1)]
-    results = products(lower, upper, 0, wd_ref[...])
-
-    @pl.when(j == 0)
-    def _():
+    for j in range(STEPS):
+        by = block(j, BLK)
+        lower = [ref[0, :CUT, by] for ref in (own0, own1)]
+        upper = [ref[0, CUT:, by] for ref in (own0, own1)]
+        results = products(lower, upper, 0, wd_ref[block(j, PAIR), :])
         for i in range(3):
-            total[i] = results[i]
-
-    @pl.when(j > 0)
-    def _():
-        for i in range(3):
-            total[i] += results[i]
+            if j == 0:
+                total[i] = results[i]
+            else:
+                total[i] += results[i]
 
 
 def first_output(wd, hidden_own):
@@ -308,11 +306,9 @@
         "first_output",
         1,
         1 << 12,
-        grid=(STEPS,),
         out_shape=jax.ShapeDtypeStruct((3, CUT, FEAT), F32),
-        in_specs=[pl.BlockSpec((PAIR, FEAT), lambda j: (j, 0))]
-        + [pl.BlockSpec((1, 2 * CUT, BLK), lambda j: (0, 0, j))] * 2,
-        out_specs=whole((3, CUT, FEAT)),
+        in_specs=[vmem()] * 3,
+        out_specs=vmem(),
     )(wd, *hidden_own)
 
 
@@ -354,26 +350,45 @@
     )(rows, offs, cnts, early, wd, *hidden_come)
 
 
-def all_rows(owns, comes, which):
-    left = jnp.concatenate([owns[0][which], comes[0][which]], axis=0)
-    right = jnp.concatenate(
-        [ref[which, i : i + CUT] for i in (0, CUT) for ref in (owns[1], comes[1])], axis=0
-    )
-    return jnp.concatenate([left, right], axis=1)
-
-
-def down_kernel(dm, g_ref, own0, own1, come0, come1, down_out):
-    j = pl.program_id(0)
-    down = lax.dot_general(
-        all_rows((own0, own1), (come0, come1), 0),
-        g_ref[...],
-        (((0,), (0,)), ((), ())),
-        preferred_element_type=F32,
-    )
-    for r in range(4):
-        for b in range(2):
-            at, by = slice(r * BLK, (r + 1) * BLK), slice(b * BLK, (b + 1) * BLK)
-            down_out[by, at] = kept(dm, 2 * j + b, r, down[by, at])
+def store(block_of, scratch, outs, sems):
+    copies = [None, None]
+    for j in range(STEPS):
+        slot = j % 2
+        if copies[slot] is not None:
+            for copy in copies[slot]:
+                copy.wait()
+        places = block_of(j, [ref.at[slot] for ref in scratch])
+        copies[slot] = [
+            pltpu.make_async_copy(ref.at[slot], out.at[place], sems.at[i, slot])
+            for i, (ref, out, place) in enumerate(zip(scratch, outs, places))
+        ]
+        for copy in copies[slot]:
+            copy.start()
+    for pair in copies:
+        for copy in pair:
+            copy.wait()
+
+
+def down_kernel(dm, g_ref, own0, own1, come0, come1, out, scratch, sems):
+    def block_of(j, targets):
+        by = block(j, BLK)
+        left = jnp.concatenate([own0[0, :, by], come0[0, :, by]], axis=0)
+        right = jnp.concatenate(
+            [ref[0, block(i, CUT), by] for i in range(2) for ref in (own1, come1)], axis=0
+        )
+        down = lax.dot_general(
+            jnp.concatenate([left, right], axis=1),
+            g_ref[...],
+            (((0,), (0,)), ((), ())),
+            preferred_element_type=F32,
+        )
+        for r in range(4):
+            for b in range(2):
+                at, to = block(r, BLK), block(b, BLK)
+                targets[0][to, at] = kept(dm, 2 * j + b, r, down[to, at])
+        return [(pl.ds(j * PAIR, PAIR), pl.ds(0, FEAT))]
+
+    store(block_of, [scratch], [out], sems)
 
 
 def down_gradient(dm, g, parts):
@@ -382,19 +397,21 @@
         "down_gradient",
         1,
         1 << 12,
-        grid=(STEPS,),
         out_shape=jax.ShapeDtypeStruct((UNITS, FEAT), F32),
-        in_specs=[smem(), whole((LIVE, FEAT))]
-        + [pl.BlockSpec((1, 2 * CUT, BLK), lambda j: (0, 0, j))] * 4,
-        out_specs=pl.BlockSpec((PAIR, FEAT), lambda j: (j, 0)),
+        in_specs=[smem()] + [vmem()] * 5,
+        out_specs=pl.BlockSpec(memory_space=pl.ANY),
+        scratch_shapes=[
+            pltpu.VMEM((2, PAIR, FEAT), F32),
+            pltpu.SemaphoreType.DMA((1, 2)),
+        ],
     )(dm, g, *parts)
 
 
-def plane_products(turns, parts, at):
+def plane_products(turns, parts, at, by):
     return [
         jnp.dot(
             turn[:, at : at + 2 * CUT],
-            jnp.concatenate([part[0], part[1]], axis=1),
+            jnp.concatenate([part[0, :, by], part[1, :, by]], axis=1),
             preferred_element_type=F32,
         )
         for turn, part in zip(turns, parts)
@@ -402,36 +419,54 @@
 
 
 def first_grad_kernel(xt0, xt1, own0, own1, gate_out, up_out):
-    for q, both in enumerate(plane_products((xt0, xt1), (own0, own1), 0)):
-        gate_out[:, q * BLK : (q + 1) * BLK] = both[:, :BLK]
-        up_out[:, q * BLK : (q + 1) * BLK] = both[:, BLK:]
-
-
-def last_grad_kernel(gm, um, xt0, xt1, gate_in, up_in, come0, come1, gate_out, up_out):
-    j = pl.program_id(0)
-    for q, both in enumerate(plane_products((xt0, xt1), (come0, come1), 2 * CUT)):
-        by = slice(q * BLK, (q + 1) * BLK)
-        for r in range(4):
-            at = slice(r * BLK, (r + 1) * BLK)
-            gate_out[at, by] = kept(gm, r, 2 * j + q, gate_in[at, by] + both[at, :BLK])
-            up_out[at, by] = kept(um, r, 2 * j + q, up_in[at, by] + both[at, BLK:])
-
-
-def grad_call(kernel, name, first_specs, middle_specs):
-    columns = pl.BlockSpec((FEAT, PAIR), lambda j: (0, j))
-    return call(
-        kernel,
-        name,
+    for j in range(STEPS):
+        sums = plane_products((xt0, xt1), (own0, own1), 0, block(j, BLK))
+        for q, both in enumerate(sums):
+            to = block(2 * j + q, BLK)
+            gate_out[:, to] = both[:, :BLK]
+            up_out[:, to] = both[:, BLK:]
+
+
+def first_grad(turns, derived_own):
+    return call(
+        first_grad_kernel,
+        "first_grad",
         2 * LIVE * FEAT * UNITS,
         13 << 20,
-        grid=(STEPS,),
         out_shape=(jax.ShapeDtypeStruct((FEAT, UNITS), F32),) * 2,
-        in_specs=[smem()] * first_specs
-        + [whole((FEAT, LIVE))] * 2
-        + [columns] * middle_specs
-        + [pl.BlockSpec((2, 2 * CUT, BLK), lambda j: (0, 0, j))] * 2,
-        out_specs=(columns,) * 2,
-    )
+        in_specs=[vmem()] * 4,
+        out_specs=(vmem(),) * 2,
+    )(*turns, *derived_own)
+
+
+def last_grad_kernel(
+    gm, um, xt0, xt1, gate_in, up_in, come0, come1, gate_out, up_out, gate_part, up_part, sems
+):
+    def block_of(j, targets):
+        sums = plane_products((xt0, xt1), (come0, come1), 2 * CUT, block(j, BLK))
+        for q, both in enumerate(sums):
+            of, to = block(2 * j + q, BLK), block(q, BLK)
+            for r in range(4):
+                at = block(r, BLK)
+                targets[0][at, to] = kept(gm, r, 2 * j + q, gate_in[at, of] + both[at, :BLK])
+                targets[1][at, to] = kept(um, r, 2 * j + q, up_in[at, of] + both[at, BLK:])
+        return [(pl.ds(0, FEAT), pl.ds(j * PAIR, PAIR))] * 2
+
+    store(block_of, [gate_part, up_part], [gate_out, up_out], sems)
+
+
+def last_grad(gm, um, turns, begun, derived_come):
+    return call(
+        last_grad_kernel,
+        "last_grad",
+        2 * LIVE * FEAT * UNITS,
+        13 << 20,
+        out_shape=(jax.ShapeDtypeStruct((FEAT, UNITS), F32),) * 2,
+        in_specs=[smem()] * 2 + [vmem()] * 6,
+        out_specs=(pl.BlockSpec(memory_space=pl.ANY),) * 2,
+        scratch_shapes=[pltpu.VMEM((2, FEAT, PAIR), F32)] * 2
+        + [pltpu.SemaphoreType.DMA((2, 2))],
+    )(gm, um, *turns, *begun, *derived_come)
 
 
 def split(value, axis):
@@ -517,7 +552,7 @@
     derived_come = exchange(derived_own, 0)
 
     begun = first_output(wd, hidden_own)
-    grads_begun = grad_call(first_grad_kernel, "first_grad", 0, 0)(turn0, turn1, *derived_own)
+    grads_begun = first_grad((turn0, turn1), derived_own)
     begun, *grads_begun = lax.optimization_barrier((begun, *grads_begun))
     mine, away = last_output(rows_along, offs, cnts, begun, wd, hidden_come)
     other = lax.ppermute(away, "col", shift(0, 1))
@@ -526,8 +561,8 @@
     summed = mine.astype(F32) + other.astype(F32)
     terms = [summed[k].astype(BF) for k in range(4)]
     arrived = [lax.ppermute(terms[dz], "col", shift(dz, 0)) for dz in (1, 2, 3)]
-    gate_grad, up_grad = grad_call(last_grad_kernel, "last_grad", 2, 2)(
-        gate_mask, up_mask, turn0, turn1, *grads_begun, *derived_come
+    gate_grad, up_grad = last_grad(
+        gate_mask, up_mask, (turn0, turn1), grads_begun, derived_come
     )
     *arrived, gate_grad, up_grad = lax.optimization_barrier((*arrived, gate_grad, up_grad))
     mixed = sum((term.astype(F32) for term in arrived), terms[0].astype(F32))

time: 155 us -> 153 us (0.987)
  Pallas kernels: 35.5 us -> 27.4 us
  waiting for transfers between devices: 65.5 us -> 72.1 us
    ppermute x18, waiting for transfers between devices: 59.7 us -> 65.8 us  [exchange(): lax.ppermute(values[q], ('col', 'dp'), partners(ROUNDS[q][number][1]))]
    pallas_call x4, Pallas kernels: 19.7 us -> 15 us  [the longest x1 6.28 us: last_grad(): call(last_grad_kernel, 'last_grad', 2 * LIVE * FEAT * UNITS, 13 << 20, ou...]
    pallas_call x2, Pallas kernels: 8.2 us -> 4.7 us  [partials(): call(functools.partial(partial_kernel, start, pieces), 'partials', 2 * co...]
  transfers between devices with their start and end apart: 29 -> 29, of which waited for: 18 -> 19; matrix products, arithmetic and copies ran while one was open for 2% -> 2% of each run, Pallas kernels for 20% -> 15%
where the time goes in v9:
time: 153 us
  waiting for transfers between devices  72.1 us (47%)
  starting transfers between devices  39 us (25%)
  Pallas kernels  27.4 us (18%)
  local copies, waits for them, and re-layouts  9.01 us (6%)
  other arithmetic  3.89 us (3%)
  between operations  1.68 us (1%)
    ppermute x18, waiting for transfers between devices, exchange(): lax.ppermute(values[q], ('col', 'dp'), partners(ROUNDS[q][number][1]))  65.8 us
    ppermute x18, starting transfers between devices, exchange(): lax.ppermute(values[q], ('col', 'dp'), partners(ROUNDS[q][number][1]))  19.2 us
    unnamed x19, local copies, waits for them, and re-layouts  8.44 us
    ppermute x1, starting transfers between devices, on_device(): other = lax.ppermute(away, 'col', shift(0, 1))  7.51 us
    ppermute x3, starting transfers between devices, on_device(): lax.ppermute(own, 'col', shift(-dz, 0))  6.37 us
    pallas_call x1, Pallas kernels, last_grad(): call(last_grad_kernel, 'last_grad', 2 * LIVE * FEAT * UNITS, 13 << 20, ou...  6.28 us
    pallas_call x1, Pallas kernels, down_gradient(): call(down_kernel, 'down_gradient', 1, 1 << 12, out_shape=jax.ShapeDtypeSt...  5.45 us
    pallas_call x2, Pallas kernels, partials(): call(functools.partial(partial_kernel, start, pieces), 'partials', 2 * co...  4.7 us
  transfers between devices with their start and end apart: 29, of which 19 were waited for; matrix products, arithmetic and copies ran while one was open for 2% of the time, Pallas kernels for 15%

profile of v9, /device:TPU:1, one launch (start us, length us, event | category | flops | bytes accessed | tf_op | source)
XLA Modules:
  0.0 153.0 jit_solution(8891743047194283987)
XLA Ops:
  1.3 0.9 copy-done.3
  2.2 0.9 copy-done.4
  3.2 1.5 collective-permute-start.3
  4.7 3.7 %collective-permute-start.2 = (bf16[144,1024]{1,0:T(8,128)(2,1)S(1)}, bf16[144,1024]{1,0:T(8,128)(2,1)S(1)}, u32[]{:S(2)}, u32[]{:S(2)}) collective-permute-start(bf16[144,1024]{1,0:T(8,128)(2,1)S(1)} %pack.1.refs_0_), channel_id=1, source_target_pairs={{0,64},{16,80},{32,96},{48,112},{64,0},{80,16},{96,32},{112,48},{1... | collective-permute-start | bytes 884744 | tf_op jit(solution)/shard_map/ppermute | solution.py:502
  8.3 0.7 collective-permute-start.1
  9.1 1.9 %collective-permute-start = (bf16[144,1024]{1,0:T(8,128)(2,1)S(1)}, bf16[144,1024]{1,0:T(8,128)(2,1)S(1)}, u32[]{:S(2)}, u32[]{:S(2)}) collective-permute-start(bf16[144,1024]{1,0:T(8,128)(2,1)S(1)} %pack.1.refs_0_), channel_id=1, source_target_pairs={{0,96},{16,112},{32,0},{48,16},{64,32},{80,48},{96,64},{112,80},{1... | collective-permute-start | bytes 884744 | tf_op jit(solution)/shard_map/ppermute | solution.py:502
  11.0 0.8 copy.13.dm
  11.8 1.5 copy-done
  13.3 1.5 copy-done.1
  14.8 1.5 copy-done.2
  16.3 0.7 copy-done.5
  17.0 0.7 copy-done.7
  17.7 2.4 %prepare.1 = (bf16[7,512,512]{2,1,0:T(8,128)(2,1)S(1)}, bf16[7,512,256]{2,1,0:T(8,128)(2,1)S(1)}, bf16[1792,512]{1,0:T(8,128)(2,1)S(1)}) custom-call(s32[4,14]{1,0:T(4,128)S(1)} %copy-done.5, s32[4,14]{1,0:T(4,128)S(1)} %copy-done.7, s32[14,4]{1,0:T(8,128)S(1)} %copy.13.dm, bf16[512,1792]{1,0:T(8,128)(2,1)S(1)} %copy-done, bf16[512,1792]{1,0:T(8,128)(2,1)S(1)} %copy-done.1, ...), custom_call_target="tpu_custom_call" | custom-call | bytes 13631488 | tf_op jit(solution)/shard_map/prepare/pallas_call | solution.py:154
  20.3 1.8 %collective-permute-done.1.refs_3_ = bf16[144,1024]{1,0:T(8,128)(2,1)S(1)} collective-permute-done((bf16[144,1024]{1,0:T(8,128)(2,1)S(1)}, bf16[144,1024]{1,0:T(8,128)(2,1)S(1)}, u32[]{:S(2)}, u32[]{:S(2)}) %collective-permute-start.1) | collective-permute-done | bytes 294944 | tf_op jit(solution)/shard_map/ppermute | solution.py:502
  22.1 0.4 collective-permute-done.refs_1_
  22.5 0.9 collective-permute-start.4
  23.4 0.5 collective-permute-start.6
  23.9 1.1 collective-permute-done.5.refs_6_
  25.0 0.4 collective-permute-done.6.refs_7_
  25.5 2.4 %compact.1 = (bf16[768,512]{1,0:T(8,128)(2,1)S(1)}, bf16[768,512]{1,0:T(8,128)(2,1)S(1)}, s32[8,8,128]{2,1,0:T(8,128)S(1)}, s32[8,8,128]{2,1,0:T(8,128)S(1)}) custom-call(s32[8]{0:T(128)S(1)} %fusion.23.shard, s32[768,1]{1,0:T(8,128)S(1)} %fusion.10.rows_ref, bf16[144,1024]{1,0:T(8,128)(2,1)S(1)} %pack.1.refs_0_, ...), custom_call_target="tpu_custom_call" | custom-call | flops 1610612736 | bytes 5242880 | tf_op jit(solution)/shard_map/compact/pallas_call | solution.py:209
  27.9 1.3 partials.2
  29.2 1.4 collective-permute-start.9
  30.6 1.9 %collective-permute-start.10 = (bf16[3,192,896]{2,1,0:T(8,128)(2,1)S(1)}, bf16[3,192,896]{2,1,0:T(8,128)(2,1)S(1)}, u32[]{:S(2)}, u32[]{:S(2)}) collective-permute-start(bf16[3,192,896]{2,1,0:T(8,128)(2,1)S(1)} %get-tuple-element.71), channel_id=1, source_target_pairs={{0,12},{1,13},{2,14},{3,15},{4,8},{5,9},{6,10},{7,11},{8,4},{9,5},... | collective-permute-start | bytes 3096584 | tf_op jit(solution)/shard_map/ppermute | solution.py:490
  32.5 0.5 turned.1
  33.0 3.4 %partials.3 = (bf16[3,192,896]{2,1,0:T(8,128)(2,1)S(1)}, bf16[3,192,896]{2,1,0:T(8,128)(2,1)S(1)}, bf16[3,192,896]{2,1,0:T(8,128)(2,1)S(1)}, bf16[3,192,896]{2,1...) custom-call(bf16[768,512]{1,0:T(8,128)(2,1)S(1)} %get-tuple-element.72.x_ref, ...), custom_call_target="tpu_custom_call" | custom-call | flops 3170893824 | bytes 7340032 | tf_op jit(solution)/shard_map/partials/pallas_call | solution.py:262
  36.4 0.5 collective-permute-start.7
  36.9 0.6 collective-permute-start.8
  37.5 5.6 %collective-permute-done.9 = bf16[3,192,896]{2,1,0:T(8,128)(2,1)S(1)} collective-permute-done((bf16[3,192,896]{2,1,0:T(8,128)(2,1)S(1)}, bf16[3,192,896]{2,1,0:T(8,128)(2,1)S(1)}, u32[]{:S(2)}, u32[]{:S(2)}) %collective-permute-start.9) | collective-permute-done | bytes 1032224 | tf_op jit(solution)/shard_map/ppermute | solution.py:490
  43.0 2.5 %collective-permute-done.10 = bf16[3,192,896]{2,1,0:T(8,128)(2,1)S(1)} collective-permute-done((bf16[3,192,896]{2,1,0:T(8,128)(2,1)S(1)}, bf16[3,192,896]{2,1,0:T(8,128)(2,1)S(1)}, u32[]{:S(2)}, u32[]{:S(2)}) %collective-permute-start.10) | collective-permute-done | bytes 1032224 | tf_op jit(solution)/shard_map/ppermute | solution.py:490
  45.6 0.2 add_convert_fusion
  45.9 0.3 add_convert_fusion.1
  46.2 2.0 %collective-permute-start.11 = (bf16[3,192,896]{2,1,0:T(8,128)(2,1)S(1)}, bf16[3,192,896]{2,1,0:T(8,128)(2,1)S(1)}, u32[]{:S(2)}, u32[]{:S(2)}) collective-permute-start(bf16[3,192,896]{2,1,0:T(8,128)(2,1)S(1)} %add_convert_fusion.1), channel_id=1, source_target_pairs={{0,12},{1,13},{2,14},{3,15},{4,8},{5,9},{6,10},{7,11},{8,4},{9,5},... | collective-permute-start | bytes 3096584 | tf_op jit(solution)/shard_map/ppermute | solution.py:490
  48.1 6.0 %collective-permute-done.7 = bf16[3,192,896]{2,1,0:T(8,128)(2,1)S(1)} collective-permute-done((bf16[3,192,896]{2,1,0:T(8,128)(2,1)S(1)}, bf16[3,192,896]{2,1,0:T(8,128)(2,1)S(1)}, u32[]{:S(2)}, u32[]{:S(2)}) %collective-permute-start.7) | collective-permute-done | bytes 1032224 | tf_op jit(solution)/shard_map/ppermute | solution.py:490
  54.1 2.5 %collective-permute-done.8 = bf16[3,192,896]{2,1,0:T(8,128)(2,1)S(1)} collective-permute-done((bf16[3,192,896]{2,1,0:T(8,128)(2,1)S(1)}, bf16[3,192,896]{2,1,0:T(8,128)(2,1)S(1)}, u32[]{:S(2)}, u32[]{:S(2)}) %collective-permute-start.8) | collective-permute-done | bytes 1032224 | tf_op jit(solution)/shard_map/ppermute | solution.py:490
  56.6 8.6 %collective-permute-done.12 = bf16[3,192,896]{2,1,0:T(8,128)(2,1)S(1)} collective-permute-done((bf16[3,192,896]{2,1,0:T(8,128)(2,1)S(1)}, bf16[3,192,896]{2,1,0:T(8,128)(2,1)S(1)}, u32[]{:S(2)}, u32[]{:S(2)}) %collective-permute-start.12) | collective-permute-done | bytes 1032224 | tf_op jit(solution)/shard_map/ppermute | solution.py:490
  65.2 2.5 %collective-permute-done.11 = bf16[3,192,896]{2,1,0:T(8,128)(2,1)S(1)} collective-permute-done((bf16[3,192,896]{2,1,0:T(8,128)(2,1)S(1)}, bf16[3,192,896]{2,1,0:T(8,128)(2,1)S(1)}, u32[]{:S(2)}, u32[]{:S(2)}) %collective-permute-start.11) | collective-permute-done | bytes 1032224 | tf_op jit(solution)/shard_map/ppermute | solution.py:490
  67.7 0.7 convert_add_fusion
  68.4 1.2 collective-permute-start.13
  69.7 1.9 %collective-permute-start.17 = (bf16[3,2,1,48,896]{4,3,2,1,0:T(8,128)(2,1)S(1)}, bf16[3,2,1,48,896]{4,3,2,1,0:T(8,128)(2,1)S(1)}, u32[]{:S(2)}, u32[]{:S(2)}) collective-permute-start(bf16[3,2,1,48,896]{4,3,2,1,0:T(8,128)(2,1)S(1)} %slice.186), channel_id=1, source_target_pairs={{0,3},{1,2},{2,1},{3,0},{4,7},{5,6},{6,5},{7,4},{8,11},{9,10},{10,... | collective-permute-start | bytes 1548296 | tf_op jit(solution)/shard_map/ppermute | solution.py:490
  71.5 5.4 %collective-permute-done.13 = bf16[3,1,2,48,896]{4,3,2,1,0:T(8,128)(2,1)S(1)} collective-permute-done((bf16[3,1,2,48,896]{4,3,2,1,0:T(8,128)(2,1)S(1)}, bf16[3,1,2,48,896]{4,3,2,1,0:T(8,128)(2,1)S(1)}, u32[]{:S(2)}, u32[]{:S(2)}) %collective-permute-start.13) | collective-permute-done | bytes 516128 | tf_op jit(solution)/shard_map/ppermute | solution.py:490
  77.0 2.6 %collective-permute-start.14 = (bf16[3,1,2,48,896]{4,3,2,1,0:T(8,128)(2,1)S(1)}, bf16[3,1,2,48,896]{4,3,2,1,0:T(8,128)(2,1)S(1)}, u32[]{:S(2)}, u32[]{:S(2)}) collective-permute-start(bf16[3,1,2,48,896]{4,3,2,1,0:T(8,128)(2,1)S(1)} %fusion.1), channel_id=1, source_target_pairs={{0,3},{1,2},{2,1},{3,0},{4,7},{5,6},{6,5},{7,4},{8,11},{9,10},{10,... | collective-permute-start | bytes 1548296 | tf_op jit(solution)/shard_map/ppermute | solution.py:490
  79.8 6.7 %collective-permute-done.14 = bf16[3,1,2,48,896]{4,3,2,1,0:T(8,128)(2,1)S(1)} collective-permute-done((bf16[3,1,2,48,896]{4,3,2,1,0:T(8,128)(2,1)S(1)}, bf16[3,1,2,48,896]{4,3,2,1,0:T(8,128)(2,1)S(1)}, u32[]{:S(2)}, u32[]{:S(2)}) %collective-permute-start.14) | collective-permute-done | bytes 516128 | tf_op jit(solution)/shard_map/ppermute | solution.py:490
  87.1 0.9 collective-permute-done.18
  88.2 0.2 multiply_convert_fusion.2
  88.5 1.6 %collective-permute-start.19 = (bf16[3,2,1,48,896]{4,3,2,1,0:T(8,128)(2,1)S(1)}, bf16[3,2,1,48,896]{4,3,2,1,0:T(8,128)(2,1)S(1)}, u32[]{:S(2)}, u32[]{:S(2)}) collective-permute-start(bf16[3,2,1,48,896]{4,3,2,1,0:T(8,128)(2,1)S(1)} %pad_maximum_fusion.7), channel_id=1, source_target_pairs={{0,3},{1,2},{2,1},{3,0},{4,7},{5,6},{6,5},{7,4},{8,11},{9,10},{10,... | collective-permute-start | bytes 1548296 | tf_op jit(solution)/shard_map/ppermute | solution.py:490
  90.1 5.2 %collective-permute-done.15 = bf16[3,1,2,48,896]{4,3,2,1,0:T(8,128)(2,1)S(1)} collective-permute-done((bf16[3,1,2,48,896]{4,3,2,1,0:T(8,128)(2,1)S(1)}, bf16[3,1,2,48,896]{4,3,2,1,0:T(8,128)(2,1)S(1)}, u32[]{:S(2)}, u32[]{:S(2)}) %collective-permute-start.15) | collective-permute-done | bytes 516128 | tf_op jit(solution)/shard_map/ppermute | solution.py:490
  95.5 2.0 %collective-permute-start.16 = (bf16[3,192,896]{2,1,0:T(8,128)(2,1)S(1)}, bf16[3,192,896]{2,1,0:T(8,128)(2,1)S(1)}, u32[]{:S(2)}, u32[]{:S(2)}) collective-permute-start(bf16[3,192,896]{2,1,0:T(8,128)(2,1)S(1)} %bitcast.25), channel_id=1, source_target_pairs={{0,12},{1,13},{2,14},{3,15},{4,8},{5,9},{6,10},{7,11},{8,4},{9,5},... | collective-permute-start | bytes 3096584 | tf_op jit(solution)/shard_map/ppermute | solution.py:490
  97.4 0.6 collective-permute-done.19
  98.3 14.9 %collective-permute-done.16 = bf16[3,192,896]{2,1,0:T(8,128)(2,1)S(1)} collective-permute-done((bf16[3,192,896]{2,1,0:T(8,128)(2,1)S(1)}, bf16[3,192,896]{2,1,0:T(8,128)(2,1)S(1)}, u32[]{:S(2)}, u32[]{:S(2)}) %collective-permute-start.16) | collective-permute-done | bytes 1032224 | tf_op jit(solution)/shard_map/ppermute | solution.py:490
  113.5 1.8 %collective-permute-start.22 = (bf16[1,384,896]{2,1,0:T(8,128)(2,1)S(1)}, bf16[1,384,896]{2,1,0:T(8,128)(2,1)S(1)}, u32[]{:S(2)}, u32[]{:S(2)}) collective-permute-start(bf16[1,384,896]{2,1,0:T(8,128)(2,1)S(1)} %pad_maximum_fusion.5.own1), channel_id=1, source_target_pairs={{0,12},{1,13},{2,14},{3,15},{4,8},{5,9},{6,10},{7,11},{8,4},{9,5},... | collective-permute-start | bytes 2064392 | tf_op jit(solution)/shard_map/ppermute | solution.py:490
  115.6 1.0 collective-permute-start.28
  116.8 0.3 collective-permute-start.27
  117.1 1.2 first_output.1.early_ref
  118.4 2.1 %first_grad.1 = (f32[512,1792]{1,0:T(8,128)S(1)}, f32[512,1792]{1,0:T(8,128)S(1)}) custom-call(bf16[512,768]{1,0:T(8,128)(2,1)S(1)} %get-tuple-element.88.xt0, bf16[512,768]{1,0:T(8,128)(2,1)S(1)} %get-tuple-element.89.xt1, bf16[2,384,896]{2,1,0:T(8,128)(2,1)S(1)} %pad_maximum_fusion.own0, bf16[2,384,896]{2,1,0:T(8,128)(2,1)S(1)} %pad_maximum_fusion.1.own1), custom_call_target="tpu_custom_call" | custom-call | flops 1409286144 | bytes 13631488 | tf_op jit(solution)/shard_map/first_grad/pallas_call | solution.py:431
  120.4 3.0 %collective-permute-done.21.come0 = bf16[1,384,896]{2,1,0:T(8,128)(2,1)S(1)} collective-permute-done((bf16[1,384,896]{2,1,0:T(8,128)(2,1)S(1)}, bf16[1,384,896]{2,1,0:T(8,128)(2,1)S(1)}, u32[]{:S(2)}, u32[]{:S(2)}) %collective-permute-start.21) | collective-permute-done | bytes 688160 | tf_op jit(solution)/shard_map/ppermute | solution.py:490
  123.5 1.4 collective-permute-done.22.come1
  124.9 2.3 %last_output.1 = (bf16[4,128,512]{2,1,0:T(8,128)(2,1)S(1)}, bf16[4,128,512]{2,1,0:T(8,128)(2,1)S(1)}) custom-call(s32[1,768]{1,0:T(1,128)S(1)} %fusion.18.rows_ref, s32[8,8,128]{2,1,0:T(8,128)S(1)} %get-tuple-element.63.offs, s32[8,8,128]{2,1,0:T(8,128)S(1)} %get-tuple-element.64.cnts, f32[3,192,512]{2,1,0:T(8,128)S(1)} %first_output.1.early_ref, ...), custom_call_target="tpu_custom_call" | custom-call | flops 1 | bytes 4096 | tf_op jit(solution)/shard_map/last_output/pallas_call | solution.py:334
  127.2 7.5 %collective-permute-start.23 = (bf16[4,128,512]{2,1,0:T(8,128)(2,1)S(1)}, bf16[4,128,512]{2,1,0:T(8,128)(2,1)S(1)}, u32[]{:S(2)}, u32[]{:S(2)}) collective-permute-start(bf16[4,128,512]{2,1,0:T(8,128)(2,1)S(1)} %get-tuple-element.94), channel_id=1, source_target_pairs={{0,16},{16,0},{32,48},{48,32},{64,80},{80,64},{96,112},{112,96},{1... | collective-permute-start | bytes 1572872 | tf_op jit(solution)/shard_map/ppermute | solution.py:558
  134.7 5.4 %down_gradient.1 = f32[1792,512]{1,0:T(8,128)} custom-call(s32[14,4]{1,0:T(8,128)S(1)} %copy.13.dm, bf16[768,512]{1,0:T(8,128)(2,1)S(1)} %get-tuple-element.73.g_ref, bf16[1,384,896]{2,1,0:T(8,128)(2,1)S(1)} %pad_maximum_fusion.4.own0, bf16[1,384,896]{2,1,0:T(8,128)(2,1)S(1)} %pad_maximum_fusion.5.own1, ...), custom_call_target="tpu_custom_call" | custom-call | flops 1 | bytes 4096 | tf_op jit(solution)/shard_map/down_gradient/pallas_call | solution.py:395
  140.4 2.4 %collective-permute-start.26 = (bf16[128,512]{1,0:T(8,128)(2,1)S(1)}, bf16[128,512]{1,0:T(8,128)(2,1)S(1)}, u32[]{:S(2)}, u32[]{:S(2)}) collective-permute-start(bf16[128,512]{1,0:T(8,128)(2,1)S(1)} %get-tuple-element.112), channel_id=1, source_target_pairs={{0,96},{16,112},{32,0},{48,16},{64,32},{80,48},{96,64},{112,80},{1... | collective-permute-start | bytes 393224 | tf_op jit(solution)/shard_map/ppermute | solution.py:563
  142.9 0.5 collective-permute-start.24
  143.5 6.3 %last_grad.1 = (f32[512,1792]{1,0:T(8,128)}, f32[512,1792]{1,0:T(8,128)}) custom-call(s32[4,14]{1,0:T(4,128)S(1)} %copy-done.6, s32[4,14]{1,0:T(4,128)S(1)} %copy-done.8, bf16[512,768]{1,0:T(8,128)(2,1)S(1)} %get-tuple-element.88.xt0, bf16[512,768]{1,0:T(8,128)(2,1)S(1)} %get-tuple-element.89.xt1, f32[512,1792]{1,0:T(8,128)S(1)} %get-tuple-element.96.gate_in, ...), custom_call_target="tpu_custom_call" | custom-call | flops 1409286144 | bytes 13631488 | tf_op jit(solution)/shard_map/last_grad/pallas_call | solution.py:459
  149.8 2.5 %collective-permute-done.24 = bf16[128,512]{1,0:T(8,128)(2,1)S(1)} collective-permute-done((bf16[128,512]{1,0:T(8,128)(2,1)S(1)}, bf16[128,512]{1,0:T(8,128)(2,1)S(1)}, u32[]{:S(2)}, u32[]{:S(2)}) %collective-permute-start.24) | collective-permute-done | bytes 131104 | tf_op jit(solution)/shard_map/ppermute | solution.py:563
  152.3 0.7 fusion.17
  (60 shorter events, 3.1 us)
Async XLA Ops:
  1.3 0.9 copy-start.3
  2.2 0.9 copy-start.4
  3.2 20.8 %collective-permute-start.3 = (bf16[144,1024]{1,0:T(8,128)(2,1)S(1)}, bf16[144,1024]{1,0:T(8,128)(2,1)S(1)}, u32[]{:S(2)}, u32[]{:S(2)}) collective-permute-start(bf16[144,1024]{1,0:T(8,128)(2,1)S(1)} %pack.1.refs_0_), channel_id=1, source_target_pairs={{0,16},{16,0},{32,48},{48,32},{64,80},{80,64},{96,112},{112,96},{1... | collective-permute-start | bytes 884744 | tf_op jit(solution)/shard_map/ppermute | solution.py:503
  4.7 18.8 %collective-permute-start.2 = (bf16[144,1024]{1,0:T(8,128)(2,1)S(1)}, bf16[144,1024]{1,0:T(8,128)(2,1)S(1)}, u32[]{:S(2)}, u32[]{:S(2)}) collective-permute-start(bf16[144,1024]{1,0:T(8,128)(2,1)S(1)} %pack.1.refs_0_), channel_id=1, source_target_pairs={{0,64},{16,80},{32,96},{48,112},{64,0},{80,16},{96,32},{112,48},{1... | collective-permute-start | bytes 884744 | tf_op jit(solution)/shard_map/ppermute | solution.py:502
  8.3 13.8 %collective-permute-start.1 = (bf16[144,1024]{1,0:T(8,128)(2,1)S(1)}, bf16[144,1024]{1,0:T(8,128)(2,1)S(1)}, u32[]{:S(2)}, u32[]{:S(2)}) collective-permute-start(bf16[144,1024]{1,0:T(8,128)(2,1)S(1)} %pack.1.refs_0_), channel_id=1, source_target_pairs={{0,32},{16,48},{32,64},{48,80},{64,96},{80,112},{96,0},{112,16},{1... | collective-permute-start | bytes 884744 | tf_op jit(solution)/shard_map/ppermute | solution.py:502
  9.1 13.4 %collective-permute-start = (bf16[144,1024]{1,0:T(8,128)(2,1)S(1)}, bf16[144,1024]{1,0:T(8,128)(2,1)S(1)}, u32[]{:S(2)}, u32[]{:S(2)}) collective-permute-start(bf16[144,1024]{1,0:T(8,128)(2,1)S(1)} %pack.1.refs_0_), channel_id=1, source_target_pairs={{0,96},{16,112},{32,0},{48,16},{64,32},{80,48},{96,64},{112,80},{1... | collective-permute-start | bytes 884744 | tf_op jit(solution)/shard_map/ppermute | solution.py:502
  11.8 1.5 copy-start
  13.3 1.5 copy-start.1
  14.8 1.5 copy-start.2
  16.3 0.7 copy-start.5
  17.0 0.7 copy-start.7
  22.5 2.5 %collective-permute-start.4 = (bf16[144,1024]{1,0:T(8,128)(2,1)S(1)}, bf16[144,1024]{1,0:T(8,128)(2,1)S(1)}, u32[]{:S(2)}, u32[]{:S(2)}) collective-permute-start(bf16[144,1024]{1,0:T(8,128)(2,1)S(1)} %collective-permute-done.refs_1_), channel_id=1, source_target_pairs={{0,16},{16,0},{32,48},{48,32},{64,80},{80,64},{96,112},{112,96},{1... | collective-permute-start | bytes 884744 | tf_op jit(solution)/shard_map/ppermute | solution.py:509
  23.4 1.6 %collective-permute-start.5 = (bf16[144,1024]{1,0:T(8,128)(2,1)S(1)}, bf16[144,1024]{1,0:T(8,128)(2,1)S(1)}, u32[]{:S(2)}, u32[]{:S(2)}) collective-permute-start(bf16[144,1024]{1,0:T(8,128)(2,1)S(1)} %collective-permute-done.2.refs_2_), channel_id=1, source_target_pairs={{0,16},{16,0},{32,48},{48,32},{64,80},{80,64},{96,112},{112,96},{1... | collective-permute-start | bytes 884744 | tf_op jit(solution)/shard_map/ppermute | solution.py:509
  23.4 2.0 %collective-permute-start.6 = (bf16[144,1024]{1,0:T(8,128)(2,1)S(1)}, bf16[144,1024]{1,0:T(8,128)(2,1)S(1)}, u32[]{:S(2)}, u32[]{:S(2)}) collective-permute-start(bf16[144,1024]{1,0:T(8,128)(2,1)S(1)} %collective-permute-done.1.refs_3_), channel_id=1, source_target_pairs={{0,16},{16,0},{32,48},{48,32},{64,80},{80,64},{96,112},{112,96},{1... | collective-permute-start | bytes 884744 | tf_op jit(solution)/shard_map/ppermute | solution.py:509
  29.2 13.8 %collective-permute-start.9 = (bf16[3,192,896]{2,1,0:T(8,128)(2,1)S(1)}, bf16[3,192,896]{2,1,0:T(8,128)(2,1)S(1)}, u32[]{:S(2)}, u32[]{:S(2)}) collective-permute-start(bf16[3,192,896]{2,1,0:T(8,128)(2,1)S(1)} %get-tuple-element.70), channel_id=1, source_target_pairs={{0,4},{1,5},{2,6},{3,7},{4,0},{5,1},{6,2},{7,3},{8,12},{9,13},{10,... | collective-permute-start | bytes 3096584 | tf_op jit(solution)/shard_map/ppermute | solution.py:490
  30.6 15.0 %collective-permute-start.10 = (bf16[3,192,896]{2,1,0:T(8,128)(2,1)S(1)}, bf16[3,192,896]{2,1,0:T(8,128)(2,1)S(1)}, u32[]{:S(2)}, u32[]{:S(2)}) collective-permute-start(bf16[3,192,896]{2,1,0:T(8,128)(2,1)S(1)} %get-tuple-element.71), channel_id=1, source_target_pairs={{0,12},{1,13},{2,14},{3,15},{4,8},{5,9},{6,10},{7,11},{8,4},{9,5},... | collective-permute-start | bytes 3096584 | tf_op jit(solution)/shard_map/ppermute | solution.py:490
  36.4 17.7 %collective-permute-start.7 = (bf16[3,192,896]{2,1,0:T(8,128)(2,1)S(1)}, bf16[3,192,896]{2,1,0:T(8,128)(2,1)S(1)}, u32[]{:S(2)}, u32[]{:S(2)}) collective-permute-start(bf16[3,192,896]{2,1,0:T(8,128)(2,1)S(1)} %get-tuple-element.75), channel_id=1, source_target_pairs={{0,4},{1,5},{2,6},{3,7},{4,0},{5,1},{6,2},{7,3},{8,12},{9,13},{10,... | collective-permute-start | bytes 3096584 | tf_op jit(solution)/shard_map/ppermute | solution.py:490
  36.9 19.8 %collective-permute-start.8 = (bf16[3,192,896]{2,1,0:T(8,128)(2,1)S(1)}, bf16[3,192,896]{2,1,0:T(8,128)(2,1)S(1)}, u32[]{:S(2)}, u32[]{:S(2)}) collective-permute-start(bf16[3,192,896]{2,1,0:T(8,128)(2,1)S(1)} %get-tuple-element.76), channel_id=1, source_target_pairs={{0,12},{1,13},{2,14},{3,15},{4,8},{5,9},{6,10},{7,11},{8,4},{9,5},... | collective-permute-start | bytes 3096584 | tf_op jit(solution)/shard_map/ppermute | solution.py:490
  45.8 19.4 %collective-permute-start.12 = (bf16[3,192,896]{2,1,0:T(8,128)(2,1)S(1)}, bf16[3,192,896]{2,1,0:T(8,128)(2,1)S(1)}, u32[]{:S(2)}, u32[]{:S(2)}) collective-permute-start(bf16[3,192,896]{2,1,0:T(8,128)(2,1)S(1)} %add_convert_fusion), channel_id=1, source_target_pairs={{0,4},{1,5},{2,6},{3,7},{4,0},{5,1},{6,2},{7,3},{8,12},{9,13},{10,... | collective-permute-start | bytes 3096584 | tf_op jit(solution)/shard_map/ppermute | solution.py:490
  46.2 21.5 %collective-permute-start.11 = (bf16[3,192,896]{2,1,0:T(8,128)(2,1)S(1)}, bf16[3,192,896]{2,1,0:T(8,128)(2,1)S(1)}, u32[]{:S(2)}, u32[]{:S(2)}) collective-permute-start(bf16[3,192,896]{2,1,0:T(8,128)(2,1)S(1)} %add_convert_fusion.1), channel_id=1, source_target_pairs={{0,12},{1,13},{2,14},{3,15},{4,8},{5,9},{6,10},{7,11},{8,4},{9,5},... | collective-permute-start | bytes 3096584 | tf_op jit(solution)/shard_map/ppermute | solution.py:490
  68.4 8.5 %collective-permute-start.13 = (bf16[3,1,2,48,896]{4,3,2,1,0:T(8,128)(2,1)S(1)}, bf16[3,1,2,48,896]{4,3,2,1,0:T(8,128)(2,1)S(1)}, u32[]{:S(2)}, u32[]{:S(2)}) collective-permute-start(bf16[3,1,2,48,896]{4,3,2,1,0:T(8,128)(2,1)S(1)} %slice.187), channel_id=1, source_target_pairs={{0,1},{1,0},{2,3},{3,2},{4,5},{5,4},{6,7},{7,6},{8,9},{9,8},{10,11... | collective-permute-start | bytes 1548296 | tf_op jit(solution)/shard_map/ppermute | solution.py:490
  69.7 9.9 %collective-permute-start.17 = (bf16[3,2,1,48,896]{4,3,2,1,0:T(8,128)(2,1)S(1)}, bf16[3,2,1,48,896]{4,3,2,1,0:T(8,128)(2,1)S(1)}, u32[]{:S(2)}, u32[]{:S(2)}) collective-permute-start(bf16[3,2,1,48,896]{4,3,2,1,0:T(8,128)(2,1)S(1)} %slice.186), channel_id=1, source_target_pairs={{0,3},{1,2},{2,1},{3,0},{4,7},{5,6},{6,5},{7,4},{8,11},{9,10},{10,... | collective-permute-start | bytes 1548296 | tf_op jit(solution)/shard_map/ppermute | solution.py:490
  77.0 9.5 %collective-permute-start.14 = (bf16[3,1,2,48,896]{4,3,2,1,0:T(8,128)(2,1)S(1)}, bf16[3,1,2,48,896]{4,3,2,1,0:T(8,128)(2,1)S(1)}, u32[]{:S(2)}, u32[]{:S(2)}) collective-permute-start(bf16[3,1,2,48,896]{4,3,2,1,0:T(8,128)(2,1)S(1)} %fusion.1), channel_id=1, source_target_pairs={{0,3},{1,2},{2,1},{3,0},{4,7},{5,6},{6,5},{7,4},{8,11},{9,10},{10,... | collective-permute-start | bytes 1548296 | tf_op jit(solution)/shard_map/ppermute | solution.py:490
  79.7 8.3 %collective-permute-start.18 = (bf16[3,2,1,48,896]{4,3,2,1,0:T(8,128)(2,1)S(1)}, bf16[3,2,1,48,896]{4,3,2,1,0:T(8,128)(2,1)S(1)}, u32[]{:S(2)}, u32[]{:S(2)}) collective-permute-start(bf16[3,2,1,48,896]{4,3,2,1,0:T(8,128)(2,1)S(1)} %fusion), channel_id=1, source_target_pairs={{0,1},{1,0},{2,3},{3,2},{4,5},{5,4},{6,7},{7,6},{8,9},{9,8},{10,11... | collective-permute-start | bytes 1548296 | tf_op jit(solution)/shard_map/ppermute | solution.py:490
  87.0 8.3 %collective-permute-start.15 = (bf16[3,1,2,48,896]{4,3,2,1,0:T(8,128)(2,1)S(1)}, bf16[3,1,2,48,896]{4,3,2,1,0:T(8,128)(2,1)S(1)}, u32[]{:S(2)}, u32[]{:S(2)}) collective-permute-start(bf16[3,1,2,48,896]{4,3,2,1,0:T(8,128)(2,1)S(1)} %pad_maximum_fusion.6), channel_id=1, source_target_pairs={{0,1},{1,0},{2,3},{3,2},{4,5},{5,4},{6,7},{7,6},{8,9},{9,8},{10,11... | collective-permute-start | bytes 1548296 | tf_op jit(solution)/shard_map/ppermute | solution.py:490
  88.5 9.5 %collective-permute-start.19 = (bf16[3,2,1,48,896]{4,3,2,1,0:T(8,128)(2,1)S(1)}, bf16[3,2,1,48,896]{4,3,2,1,0:T(8,128)(2,1)S(1)}, u32[]{:S(2)}, u32[]{:S(2)}) collective-permute-start(bf16[3,2,1,48,896]{4,3,2,1,0:T(8,128)(2,1)S(1)} %pad_maximum_fusion.7), channel_id=1, source_target_pairs={{0,3},{1,2},{2,1},{3,0},{4,7},{5,6},{6,5},{7,4},{8,11},{9,10},{10,... | collective-permute-start | bytes 1548296 | tf_op jit(solution)/shard_map/ppermute | solution.py:490
  95.5 17.7 %collective-permute-start.16 = (bf16[3,192,896]{2,1,0:T(8,128)(2,1)S(1)}, bf16[3,192,896]{2,1,0:T(8,128)(2,1)S(1)}, u32[]{:S(2)}, u32[]{:S(2)}) collective-permute-start(bf16[3,192,896]{2,1,0:T(8,128)(2,1)S(1)} %bitcast.25), channel_id=1, source_target_pairs={{0,12},{1,13},{2,14},{3,15},{4,8},{5,9},{6,10},{7,11},{8,4},{9,5},... | collective-permute-start | bytes 3096584 | tf_op jit(solution)/shard_map/ppermute | solution.py:490
  98.1 15.3 %collective-permute-start.20 = (bf16[3,192,896]{2,1,0:T(8,128)(2,1)S(1)}, bf16[3,192,896]{2,1,0:T(8,128)(2,1)S(1)}, u32[]{:S(2)}, u32[]{:S(2)}) collective-permute-start(bf16[3,192,896]{2,1,0:T(8,128)(2,1)S(1)} %bitcast.26), channel_id=1, source_target_pairs={{0,4},{1,5},{2,6},{3,7},{4,0},{5,1},{6,2},{7,3},{8,12},{9,13},{10,... | collective-permute-start | bytes 3096584 | tf_op jit(solution)/shard_map/ppermute | solution.py:490
  113.3 10.2 %collective-permute-start.21 = (bf16[1,384,896]{2,1,0:T(8,128)(2,1)S(1)}, bf16[1,384,896]{2,1,0:T(8,128)(2,1)S(1)}, u32[]{:S(2)}, u32[]{:S(2)}) collective-permute-start(bf16[1,384,896]{2,1,0:T(8,128)(2,1)S(1)} %pad_maximum_fusion.4.own0), channel_id=1, source_target_pairs={{0,4},{1,5},{2,6},{3,7},{4,0},{5,1},{6,2},{7,3},{8,12},{9,13},{10,... | collective-permute-start | bytes 2064392 | tf_op jit(solution)/shard_map/ppermute | solution.py:490
  113.5 11.4 %collective-permute-start.22 = (bf16[1,384,896]{2,1,0:T(8,128)(2,1)S(1)}, bf16[1,384,896]{2,1,0:T(8,128)(2,1)S(1)}, u32[]{:S(2)}, u32[]{:S(2)}) collective-permute-start(bf16[1,384,896]{2,1,0:T(8,128)(2,1)S(1)} %pad_maximum_fusion.5.own1), channel_id=1, source_target_pairs={{0,12},{1,13},{2,14},{3,15},{4,8},{5,9},{6,10},{7,11},{8,4},{9,5},... | collective-permute-start | bytes 2064392 | tf_op jit(solution)/shard_map/ppermute | solution.py:490
  115.6 27.8 %collective-permute-start.28 = (bf16[2,384,896]{2,1,0:T(8,128)(2,1)S(1)}, bf16[2,384,896]{2,1,0:T(8,128)(2,1)S(1)}, u32[]{:S(2)}, u32[]{:S(2)}) collective-permute-start(bf16[2,384,896]{2,1,0:T(8,128)(2,1)S(1)} %pad_maximum_fusion.1.own1), channel_id=1, source_target_pairs={{0,12},{1,13},{2,14},{3,15},{4,8},{5,9},{6,10},{7,11},{8,4},{9,5},... | collective-permute-start | bytes 4128776 | tf_op jit(solution)/shard_map/ppermute | solution.py:490
  116.8 26.6 %collective-permute-start.27 = (bf16[2,384,896]{2,1,0:T(8,128)(2,1)S(1)}, bf16[2,384,896]{2,1,0:T(8,128)(2,1)S(1)}, u32[]{:S(2)}, u32[]{:S(2)}) collective-permute-start(bf16[2,384,896]{2,1,0:T(8,128)(2,1)S(1)} %pad_maximum_fusion.own0), channel_id=1, source_target_pairs={{0,4},{1,5},{2,6},{3,7},{4,0},{5,1},{6,2},{7,3},{8,12},{9,13},{10,... | collective-permute-start | bytes 4128776 | tf_op jit(solution)/shard_map/ppermute | solution.py:490
  127.2 13.0 %collective-permute-start.23 = (bf16[4,128,512]{2,1,0:T(8,128)(2,1)S(1)}, bf16[4,128,512]{2,1,0:T(8,128)(2,1)S(1)}, u32[]{:S(2)}, u32[]{:S(2)}) collective-permute-start(bf16[4,128,512]{2,1,0:T(8,128)(2,1)S(1)} %get-tuple-element.94), channel_id=1, source_target_pairs={{0,16},{16,0},{32,48},{48,32},{64,80},{80,64},{96,112},{112,96},{1... | collective-permute-start | bytes 1572872 | tf_op jit(solution)/shard_map/ppermute | solution.py:558
  140.1 3.3 %copy-start.6 = (s32[4,14]{1,0:T(4,128)S(1)}, s32[4,14]{1,0:T(4,128)}, u32[]{:S(2)}) copy-start(s32[4,14]{1,0:T(4,128)} %gm.3) | copy-start | bytes 676
  140.2 3.3 %copy-start.8 = (s32[4,14]{1,0:T(4,128)S(1)}, s32[4,14]{1,0:T(4,128)}, u32[]{:S(2)}) copy-start(s32[4,14]{1,0:T(4,128)} %um.3) | copy-start | bytes 676
  140.4 9.4 %collective-permute-start.26 = (bf16[128,512]{1,0:T(8,128)(2,1)S(1)}, bf16[128,512]{1,0:T(8,128)(2,1)S(1)}, u32[]{:S(2)}, u32[]{:S(2)}) collective-permute-start(bf16[128,512]{1,0:T(8,128)(2,1)S(1)} %get-tuple-element.112), channel_id=1, source_target_pairs={{0,96},{16,112},{32,0},{48,16},{64,32},{80,48},{96,64},{112,80},{1... | collective-permute-start | bytes 393224 | tf_op jit(solution)/shard_map/ppermute | solution.py:563
  142.8 7.0 %collective-permute-start.25 = (bf16[128,512]{1,0:T(8,128)(2,1)S(1)}, bf16[128,512]{1,0:T(8,128)(2,1)S(1)}, u32[]{:S(2)}, u32[]{:S(2)}) collective-permute-start(bf16[128,512]{1,0:T(8,128)(2,1)S(1)} %get-tuple-element.113), channel_id=1, source_target_pairs={{0,64},{16,80},{32,96},{48,112},{64,0},{80,16},{96,32},{112,48},{1... | collective-permute-start | bytes 393224 | tf_op jit(solution)/shard_map/ppermute | solution.py:563
  142.9 9.3 %collective-permute-start.24 = (bf16[128,512]{1,0:T(8,128)(2,1)S(1)}, bf16[128,512]{1,0:T(8,128)(2,1)S(1)}, u32[]{:S(2)}, u32[]{:S(2)}) collective-permute-start(bf16[128,512]{1,0:T(8,128)(2,1)S(1)} %get-tuple-element.114), channel_id=1, source_target_pairs={{0,32},{16,48},{32,64},{48,80},{64,96},{80,112},{96,0},{112,16},{1... | collective-permute-start | bytes 393224 | tf_op jit(solution)/shard_map/ppermute | solution.py:563

commit v10 on v9

--- a/solution.py
+++ b/solution.py
@@ -351,22 +351,15 @@
 
 
 def store(block_of, scratch, outs, sems):
-    copies = [None, None]
+    copies = []
     for j in range(STEPS):
-        slot = j % 2
-        if copies[slot] is not None:
-            for copy in copies[slot]:
-                copy.wait()
-        places = block_of(j, [ref.at[slot] for ref in scratch])
-        copies[slot] = [
-            pltpu.make_async_copy(ref.at[slot], out.at[place], sems.at[i, slot])
-            for i, (ref, out, place) in enumerate(zip(scratch, outs, places))
-        ]
-        for copy in copies[slot]:
+        places = block_of(j, [ref.at[j] for ref in scratch])
+        for i, (ref, out, place) in enumerate(zip(scratch, outs, places)):
+            copy = pltpu.make_async_copy(ref.at[j], out.at[place], sems.at[i, j])
             copy.start()
-    for pair in copies:
-        for copy in pair:
-            copy.wait()
+            copies.append(copy)
+    for copy in copies:
+        copy.wait()
 
 
 def down_kernel(dm, g_ref, own0, own1, come0, come1, out, scratch, sems):
@@ -401,8 +394,8 @@
         in_specs=[smem()] + [vmem()] * 5,
         out_specs=pl.BlockSpec(memory_space=pl.ANY),
         scratch_shapes=[
-            pltpu.VMEM((2, PAIR, FEAT), F32),
-            pltpu.SemaphoreType.DMA((1, 2)),
+            pltpu.VMEM((STEPS, PAIR, FEAT), F32),
+            pltpu.SemaphoreType.DMA((1, STEPS)),
         ],
     )(dm, g, *parts)
 
@@ -464,8 +457,8 @@
         out_shape=(jax.ShapeDtypeStruct((FEAT, UNITS), F32),) * 2,
         in_specs=[smem()] * 2 + [vmem()] * 6,
         out_specs=(pl.BlockSpec(memory_space=pl.ANY),) * 2,
-        scratch_shapes=[pltpu.VMEM((2, FEAT, PAIR), F32)] * 2
-        + [pltpu.SemaphoreType.DMA((2, 2))],
+        scratch_shapes=[pltpu.VMEM((STEPS, FEAT, PAIR), F32)] * 2
+        + [pltpu.SemaphoreType.DMA((2, STEPS))],
     )(gm, um, *turns, *begun, *derived_come)
 
 

time: 153 us -> 151 us (0.987)
  Pallas kernels: 27.4 us -> 22.9 us
  waiting for transfers between devices: 72.1 us -> 74.2 us
    pallas_call x1, Pallas kernels: 5.45 us -> 3.15 us  [down_gradient(): call(down_kernel, 'down_gradient', 1, 1 << 12, out_shape=jax.ShapeDtypeSt...]
    ppermute x3, waiting for transfers between devices: 2.49 us -> 4.64 us  [on_device(): arrived = [lax.ppermute(terms[dz], 'col', shift(dz, 0)) for dz in (1, 2, 3)]]
    pallas_call x1, Pallas kernels: 6.28 us -> 4.14 us  [last_grad(): call(last_grad_kernel, 'last_grad', 2 * LIVE * FEAT * UNITS, 13 << 20, ou...]
  transfers between devices with their start and end apart: 29 -> 29, of which waited for: 19 -> 21; matrix products, arithmetic and copies ran while one was open for 2% -> 2% of each run, Pallas kernels for 15% -> 13%
where the time goes in v10:
time: 151 us
  waiting for transfers between devices  74.2 us (49%)
  starting transfers between devices  39 us (26%)
  Pallas kernels  22.9 us (15%)
  local copies, waits for them, and re-layouts  9.01 us (6%)
  other arithmetic  3.89 us (3%)
  between operations  1.67 us (1%)
    ppermute x18, waiting for transfers between devices, exchange(): lax.ppermute(values[q], ('col', 'dp'), partners(ROUNDS[q][number][1]))  65.8 us
    ppermute x18, starting transfers between devices, exchange(): lax.ppermute(values[q], ('col', 'dp'), partners(ROUNDS[q][number][1]))  19.2 us
    unnamed x19, local copies, waits for them, and re-layouts  8.44 us
    ppermute x1, starting transfers between devices, on_device(): other = lax.ppermute(away, 'col', shift(0, 1))  7.51 us
    ppermute x3, starting transfers between devices, on_device(): lax.ppermute(own, 'col', shift(-dz, 0))  6.37 us
    pallas_call x2, Pallas kernels, partials(): call(functools.partial(partial_kernel, start, pieces), 'partials', 2 * co...  4.7 us
    ppermute x3, waiting for transfers between devices, on_device(): arrived = [lax.ppermute(terms[dz], 'col', shift(dz, 0)) for dz in (1, 2, 3)]  4.64 us
    pallas_call x1, Pallas kernels, last_grad(): call(last_grad_kernel, 'last_grad', 2 * LIVE * FEAT * UNITS, 13 << 20, ou...  4.14 us
  transfers between devices with their start and end apart: 29, of which 21 were waited for; matrix products, arithmetic and copies ran while one was open for 2% of the time, Pallas kernels for 13%

profile of v10, /device:TPU:1, one launch (start us, length us, event | category | flops | bytes accessed | tf_op | source)
XLA Modules:
  0.0 150.7 jit_solution(18014711006053031030)
XLA Ops:
  1.3 0.9 copy-done.3
  2.2 0.9 copy-done.4
  3.2 1.5 collective-permute-start.3
  4.7 3.7 %collective-permute-start.2 = (bf16[144,1024]{1,0:T(8,128)(2,1)S(1)}, bf16[144,1024]{1,0:T(8,128)(2,1)S(1)}, u32[]{:S(2)}, u32[]{:S(2)}) collective-permute-start(bf16[144,1024]{1,0:T(8,128)(2,1)S(1)} %pack.1.refs_0_), channel_id=1, source_target_pairs={{0,64},{16,80},{32,96},{48,112},{64,0},{80,16},{96,32},{112,48},{1... | collective-permute-start | bytes 884744 | tf_op jit(solution)/shard_map/ppermute | solution.py:495
  8.3 0.7 collective-permute-start.1
  9.1 1.9 %collective-permute-start = (bf16[144,1024]{1,0:T(8,128)(2,1)S(1)}, bf16[144,1024]{1,0:T(8,128)(2,1)S(1)}, u32[]{:S(2)}, u32[]{:S(2)}) collective-permute-start(bf16[144,1024]{1,0:T(8,128)(2,1)S(1)} %pack.1.refs_0_), channel_id=1, source_target_pairs={{0,96},{16,112},{32,0},{48,16},{64,32},{80,48},{96,64},{112,80},{1... | collective-permute-start | bytes 884744 | tf_op jit(solution)/shard_map/ppermute | solution.py:495
  11.0 0.8 copy.13.dm
  11.8 1.5 copy-done
  13.3 1.5 copy-done.1
  14.8 1.5 copy-done.2
  16.3 0.7 copy-done.5
  17.0 0.7 copy-done.7
  17.7 2.4 %prepare.1 = (bf16[7,512,512]{2,1,0:T(8,128)(2,1)S(1)}, bf16[7,512,256]{2,1,0:T(8,128)(2,1)S(1)}, bf16[1792,512]{1,0:T(8,128)(2,1)S(1)}) custom-call(s32[4,14]{1,0:T(4,128)S(1)} %copy-done.5, s32[4,14]{1,0:T(4,128)S(1)} %copy-done.7, s32[14,4]{1,0:T(8,128)S(1)} %copy.13.dm, bf16[512,1792]{1,0:T(8,128)(2,1)S(1)} %copy-done, bf16[512,1792]{1,0:T(8,128)(2,1)S(1)} %copy-done.1, ...), custom_call_target="tpu_custom_call" | custom-call | bytes 13631488 | tf_op jit(solution)/shard_map/prepare/pallas_call | solution.py:154
  20.3 1.8 %collective-permute-done.1.refs_3_ = bf16[144,1024]{1,0:T(8,128)(2,1)S(1)} collective-permute-done((bf16[144,1024]{1,0:T(8,128)(2,1)S(1)}, bf16[144,1024]{1,0:T(8,128)(2,1)S(1)}, u32[]{:S(2)}, u32[]{:S(2)}) %collective-permute-start.1) | collective-permute-done | bytes 294944 | tf_op jit(solution)/shard_map/ppermute | solution.py:495
  22.1 0.4 collective-permute-done.refs_1_
  22.5 0.9 collective-permute-start.4
  23.4 0.5 collective-permute-start.6
  23.9 1.1 collective-permute-done.5.refs_6_
  25.0 0.4 collective-permute-done.6.refs_7_
  25.5 2.4 %compact.1 = (bf16[768,512]{1,0:T(8,128)(2,1)S(1)}, bf16[768,512]{1,0:T(8,128)(2,1)S(1)}, s32[8,8,128]{2,1,0:T(8,128)S(1)}, s32[8,8,128]{2,1,0:T(8,128)S(1)}) custom-call(s32[8]{0:T(128)S(1)} %fusion.23.shard, s32[768,1]{1,0:T(8,128)S(1)} %fusion.10.rows_ref, bf16[144,1024]{1,0:T(8,128)(2,1)S(1)} %pack.1.refs_0_, ...), custom_call_target="tpu_custom_call" | custom-call | flops 1610612736 | bytes 5242880 | tf_op jit(solution)/shard_map/compact/pallas_call | solution.py:209
  27.9 1.3 partials.2
  29.2 1.4 collective-permute-start.9
  30.6 1.9 %collective-permute-start.10 = (bf16[3,192,896]{2,1,0:T(8,128)(2,1)S(1)}, bf16[3,192,896]{2,1,0:T(8,128)(2,1)S(1)}, u32[]{:S(2)}, u32[]{:S(2)}) collective-permute-start(bf16[3,192,896]{2,1,0:T(8,128)(2,1)S(1)} %get-tuple-element.71), channel_id=1, source_target_pairs={{0,12},{1,13},{2,14},{3,15},{4,8},{5,9},{6,10},{7,11},{8,4},{9,5},... | collective-permute-start | bytes 3096584 | tf_op jit(solution)/shard_map/ppermute | solution.py:483
  32.5 0.5 turned.1
  33.0 3.4 %partials.3 = (bf16[3,192,896]{2,1,0:T(8,128)(2,1)S(1)}, bf16[3,192,896]{2,1,0:T(8,128)(2,1)S(1)}, bf16[3,192,896]{2,1,0:T(8,128)(2,1)S(1)}, bf16[3,192,896]{2,1...) custom-call(bf16[768,512]{1,0:T(8,128)(2,1)S(1)} %get-tuple-element.72.x_ref, ...), custom_call_target="tpu_custom_call" | custom-call | flops 3170893824 | bytes 7340032 | tf_op jit(solution)/shard_map/partials/pallas_call | solution.py:262
  36.4 0.5 collective-permute-start.7
  36.9 0.6 collective-permute-start.8
  37.5 5.6 %collective-permute-done.9 = bf16[3,192,896]{2,1,0:T(8,128)(2,1)S(1)} collective-permute-done((bf16[3,192,896]{2,1,0:T(8,128)(2,1)S(1)}, bf16[3,192,896]{2,1,0:T(8,128)(2,1)S(1)}, u32[]{:S(2)}, u32[]{:S(2)}) %collective-permute-start.9) | collective-permute-done | bytes 1032224 | tf_op jit(solution)/shard_map/ppermute | solution.py:483
  43.0 2.5 %collective-permute-done.10 = bf16[3,192,896]{2,1,0:T(8,128)(2,1)S(1)} collective-permute-done((bf16[3,192,896]{2,1,0:T(8,128)(2,1)S(1)}, bf16[3,192,896]{2,1,0:T(8,128)(2,1)S(1)}, u32[]{:S(2)}, u32[]{:S(2)}) %collective-permute-start.10) | collective-permute-done | bytes 1032224 | tf_op jit(solution)/shard_map/ppermute | solution.py:483
  45.9 0.3 add_convert_fusion.1
  46.2 2.0 %collective-permute-start.11 = (bf16[3,192,896]{2,1,0:T(8,128)(2,1)S(1)}, bf16[3,192,896]{2,1,0:T(8,128)(2,1)S(1)}, u32[]{:S(2)}, u32[]{:S(2)}) collective-permute-start(bf16[3,192,896]{2,1,0:T(8,128)(2,1)S(1)} %add_convert_fusion.1), channel_id=1, source_target_pairs={{0,12},{1,13},{2,14},{3,15},{4,8},{5,9},{6,10},{7,11},{8,4},{9,5},... | collective-permute-start | bytes 3096584 | tf_op jit(solution)/shard_map/ppermute | solution.py:483
  48.1 6.0 %collective-permute-done.7 = bf16[3,192,896]{2,1,0:T(8,128)(2,1)S(1)} collective-permute-done((bf16[3,192,896]{2,1,0:T(8,128)(2,1)S(1)}, bf16[3,192,896]{2,1,0:T(8,128)(2,1)S(1)}, u32[]{:S(2)}, u32[]{:S(2)}) %collective-permute-start.7) | collective-permute-done | bytes 1032224 | tf_op jit(solution)/shard_map/ppermute | solution.py:483
  54.1 2.5 %collective-permute-done.8 = bf16[3,192,896]{2,1,0:T(8,128)(2,1)S(1)} collective-permute-done((bf16[3,192,896]{2,1,0:T(8,128)(2,1)S(1)}, bf16[3,192,896]{2,1,0:T(8,128)(2,1)S(1)}, u32[]{:S(2)}, u32[]{:S(2)}) %collective-permute-start.8) | collective-permute-done | bytes 1032224 | tf_op jit(solution)/shard_map/ppermute | solution.py:483
  56.6 8.6 %collective-permute-done.12 = bf16[3,192,896]{2,1,0:T(8,128)(2,1)S(1)} collective-permute-done((bf16[3,192,896]{2,1,0:T(8,128)(2,1)S(1)}, bf16[3,192,896]{2,1,0:T(8,128)(2,1)S(1)}, u32[]{:S(2)}, u32[]{:S(2)}) %collective-permute-start.12) | collective-permute-done | bytes 1032224 | tf_op jit(solution)/shard_map/ppermute | solution.py:483
  65.2 2.5 %collective-permute-done.11 = bf16[3,192,896]{2,1,0:T(8,128)(2,1)S(1)} collective-permute-done((bf16[3,192,896]{2,1,0:T(8,128)(2,1)S(1)}, bf16[3,192,896]{2,1,0:T(8,128)(2,1)S(1)}, u32[]{:S(2)}, u32[]{:S(2)}) %collective-permute-start.11) | collective-permute-done | bytes 1032224 | tf_op jit(solution)/shard_map/ppermute | solution.py:483
  67.7 0.7 convert_add_fusion
  68.4 1.2 collective-permute-start.13
  69.7 1.9 %collective-permute-start.17 = (bf16[3,2,1,48,896]{4,3,2,1,0:T(8,128)(2,1)S(1)}, bf16[3,2,1,48,896]{4,3,2,1,0:T(8,128)(2,1)S(1)}, u32[]{:S(2)}, u32[]{:S(2)}) collective-permute-start(bf16[3,2,1,48,896]{4,3,2,1,0:T(8,128)(2,1)S(1)} %slice.186), channel_id=1, source_target_pairs={{0,3},{1,2},{2,1},{3,0},{4,7},{5,6},{6,5},{7,4},{8,11},{9,10},{10,... | collective-permute-start | bytes 1548296 | tf_op jit(solution)/shard_map/ppermute | solution.py:483
  71.5 5.4 %collective-permute-done.13 = bf16[3,1,2,48,896]{4,3,2,1,0:T(8,128)(2,1)S(1)} collective-permute-done((bf16[3,1,2,48,896]{4,3,2,1,0:T(8,128)(2,1)S(1)}, bf16[3,1,2,48,896]{4,3,2,1,0:T(8,128)(2,1)S(1)}, u32[]{:S(2)}, u32[]{:S(2)}) %collective-permute-start.13) | collective-permute-done | bytes 516128 | tf_op jit(solution)/shard_map/ppermute | solution.py:483
  77.0 2.6 %collective-permute-start.14 = (bf16[3,1,2,48,896]{4,3,2,1,0:T(8,128)(2,1)S(1)}, bf16[3,1,2,48,896]{4,3,2,1,0:T(8,128)(2,1)S(1)}, u32[]{:S(2)}, u32[]{:S(2)}) collective-permute-start(bf16[3,1,2,48,896]{4,3,2,1,0:T(8,128)(2,1)S(1)} %fusion.1), channel_id=1, source_target_pairs={{0,3},{1,2},{2,1},{3,0},{4,7},{5,6},{6,5},{7,4},{8,11},{9,10},{10,... | collective-permute-start | bytes 1548296 | tf_op jit(solution)/shard_map/ppermute | solution.py:483
  79.8 6.7 %collective-permute-done.14 = bf16[3,1,2,48,896]{4,3,2,1,0:T(8,128)(2,1)S(1)} collective-permute-done((bf16[3,1,2,48,896]{4,3,2,1,0:T(8,128)(2,1)S(1)}, bf16[3,1,2,48,896]{4,3,2,1,0:T(8,128)(2,1)S(1)}, u32[]{:S(2)}, u32[]{:S(2)}) %collective-permute-start.14) | collective-permute-done | bytes 516128 | tf_op jit(solution)/shard_map/ppermute | solution.py:483
  87.1 0.9 collective-permute-done.18
  88.5 1.6 %collective-permute-start.19 = (bf16[3,2,1,48,896]{4,3,2,1,0:T(8,128)(2,1)S(1)}, bf16[3,2,1,48,896]{4,3,2,1,0:T(8,128)(2,1)S(1)}, u32[]{:S(2)}, u32[]{:S(2)}) collective-permute-start(bf16[3,2,1,48,896]{4,3,2,1,0:T(8,128)(2,1)S(1)} %pad_maximum_fusion.7), channel_id=1, source_target_pairs={{0,3},{1,2},{2,1},{3,0},{4,7},{5,6},{6,5},{7,4},{8,11},{9,10},{10,... | collective-permute-start | bytes 1548296 | tf_op jit(solution)/shard_map/ppermute | solution.py:483
  90.1 5.2 %collective-permute-done.15 = bf16[3,1,2,48,896]{4,3,2,1,0:T(8,128)(2,1)S(1)} collective-permute-done((bf16[3,1,2,48,896]{4,3,2,1,0:T(8,128)(2,1)S(1)}, bf16[3,1,2,48,896]{4,3,2,1,0:T(8,128)(2,1)S(1)}, u32[]{:S(2)}, u32[]{:S(2)}) %collective-permute-start.15) | collective-permute-done | bytes 516128 | tf_op jit(solution)/shard_map/ppermute | solution.py:483
  95.5 2.0 %collective-permute-start.16 = (bf16[3,192,896]{2,1,0:T(8,128)(2,1)S(1)}, bf16[3,192,896]{2,1,0:T(8,128)(2,1)S(1)}, u32[]{:S(2)}, u32[]{:S(2)}) collective-permute-start(bf16[3,192,896]{2,1,0:T(8,128)(2,1)S(1)} %bitcast.25), channel_id=1, source_target_pairs={{0,12},{1,13},{2,14},{3,15},{4,8},{5,9},{6,10},{7,11},{8,4},{9,5},... | collective-permute-start | bytes 3096584 | tf_op jit(solution)/shard_map/ppermute | solution.py:483
  97.4 0.6 collective-permute-done.19
  98.3 14.9 %collective-permute-done.16 = bf16[3,192,896]{2,1,0:T(8,128)(2,1)S(1)} collective-permute-done((bf16[3,192,896]{2,1,0:T(8,128)(2,1)S(1)}, bf16[3,192,896]{2,1,0:T(8,128)(2,1)S(1)}, u32[]{:S(2)}, u32[]{:S(2)}) %collective-permute-start.16) | collective-permute-done | bytes 1032224 | tf_op jit(solution)/shard_map/ppermute | solution.py:483
  113.5 1.8 %collective-permute-start.22 = (bf16[1,384,896]{2,1,0:T(8,128)(2,1)S(1)}, bf16[1,384,896]{2,1,0:T(8,128)(2,1)S(1)}, u32[]{:S(2)}, u32[]{:S(2)}) collective-permute-start(bf16[1,384,896]{2,1,0:T(8,128)(2,1)S(1)} %pad_maximum_fusion.5.own1), channel_id=1, source_target_pairs={{0,12},{1,13},{2,14},{3,15},{4,8},{5,9},{6,10},{7,11},{8,4},{9,5},... | collective-permute-start | bytes 2064392 | tf_op jit(solution)/shard_map/ppermute | solution.py:483
  115.6 1.0 collective-permute-start.28
  116.8 0.3 collective-permute-start.27
  117.1 1.2 first_output.1.early_ref
  118.4 2.1 %first_grad.1 = (f32[512,1792]{1,0:T(8,128)S(1)}, f32[512,1792]{1,0:T(8,128)S(1)}) custom-call(bf16[512,768]{1,0:T(8,128)(2,1)S(1)} %get-tuple-element.88.xt0, bf16[512,768]{1,0:T(8,128)(2,1)S(1)} %get-tuple-element.89.xt1, bf16[2,384,896]{2,1,0:T(8,128)(2,1)S(1)} %pad_maximum_fusion.own0, bf16[2,384,896]{2,1,0:T(8,128)(2,1)S(1)} %pad_maximum_fusion.1.own1), custom_call_target="tpu_custom_call" | custom-call | flops 1409286144 | bytes 13631488 | tf_op jit(solution)/shard_map/first_grad/pallas_call | solution.py:424
  120.4 3.0 %collective-permute-done.21.come0 = bf16[1,384,896]{2,1,0:T(8,128)(2,1)S(1)} collective-permute-done((bf16[1,384,896]{2,1,0:T(8,128)(2,1)S(1)}, bf16[1,384,896]{2,1,0:T(8,128)(2,1)S(1)}, u32[]{:S(2)}, u32[]{:S(2)}) %collective-permute-start.21) | collective-permute-done | bytes 688160 | tf_op jit(solution)/shard_map/ppermute | solution.py:483
  123.5 1.4 collective-permute-done.22.come1
  124.9 2.3 %last_output.1 = (bf16[4,128,512]{2,1,0:T(8,128)(2,1)S(1)}, bf16[4,128,512]{2,1,0:T(8,128)(2,1)S(1)}) custom-call(s32[1,768]{1,0:T(1,128)S(1)} %fusion.18.rows_ref, s32[8,8,128]{2,1,0:T(8,128)S(1)} %get-tuple-element.63.offs, s32[8,8,128]{2,1,0:T(8,128)S(1)} %get-tuple-element.64.cnts, f32[3,192,512]{2,1,0:T(8,128)S(1)} %first_output.1.early_ref, ...), custom_call_target="tpu_custom_call" | custom-call | flops 1 | bytes 4096 | tf_op jit(solution)/shard_map/last_output/pallas_call | solution.py:334
  127.2 7.5 %collective-permute-start.23 = (bf16[4,128,512]{2,1,0:T(8,128)(2,1)S(1)}, bf16[4,128,512]{2,1,0:T(8,128)(2,1)S(1)}, u32[]{:S(2)}, u32[]{:S(2)}) collective-permute-start(bf16[4,128,512]{2,1,0:T(8,128)(2,1)S(1)} %get-tuple-element.94), channel_id=1, source_target_pairs={{0,16},{16,0},{32,48},{48,32},{64,80},{80,64},{96,112},{112,96},{1... | collective-permute-start | bytes 1572872 | tf_op jit(solution)/shard_map/ppermute | solution.py:551
  134.7 3.2 %down_gradient.1 = f32[1792,512]{1,0:T(8,128)} custom-call(s32[14,4]{1,0:T(8,128)S(1)} %copy.13.dm, bf16[768,512]{1,0:T(8,128)(2,1)S(1)} %get-tuple-element.73.g_ref, bf16[1,384,896]{2,1,0:T(8,128)(2,1)S(1)} %pad_maximum_fusion.4.own0, bf16[1,384,896]{2,1,0:T(8,128)(2,1)S(1)} %pad_maximum_fusion.5.own1, ...), custom_call_target="tpu_custom_call" | custom-call | flops 1 | bytes 4096 | tf_op jit(solution)/shard_map/down_gradient/pallas_call | solution.py:388
  138.1 2.4 %collective-permute-start.26 = (bf16[128,512]{1,0:T(8,128)(2,1)S(1)}, bf16[128,512]{1,0:T(8,128)(2,1)S(1)}, u32[]{:S(2)}, u32[]{:S(2)}) collective-permute-start(bf16[128,512]{1,0:T(8,128)(2,1)S(1)} %get-tuple-element.112), channel_id=1, source_target_pairs={{0,96},{16,112},{32,0},{48,16},{64,32},{80,48},{96,64},{112,80},{1... | collective-permute-start | bytes 393224 | tf_op jit(solution)/shard_map/ppermute | solution.py:556
  140.7 0.5 collective-permute-start.24
  141.2 4.1 %last_grad.1 = (f32[512,1792]{1,0:T(8,128)}, f32[512,1792]{1,0:T(8,128)}) custom-call(s32[4,14]{1,0:T(4,128)S(1)} %copy-done.6, s32[4,14]{1,0:T(4,128)S(1)} %copy-done.8, bf16[512,768]{1,0:T(8,128)(2,1)S(1)} %get-tuple-element.88.xt0, bf16[512,768]{1,0:T(8,128)(2,1)S(1)} %get-tuple-element.89.xt1, f32[512,1792]{1,0:T(8,128)S(1)} %get-tuple-element.96.gate_in, ...), custom_call_target="tpu_custom_call" | custom-call | flops 1409286144 | bytes 13631488 | tf_op jit(solution)/shard_map/last_grad/pallas_call | solution.py:452
  145.3 0.7 collective-permute-done.26
  146.1 0.8 collective-permute-done.25
  146.8 3.1 %collective-permute-done.24 = bf16[128,512]{1,0:T(8,128)(2,1)S(1)} collective-permute-done((bf16[128,512]{1,0:T(8,128)(2,1)S(1)}, bf16[128,512]{1,0:T(8,128)(2,1)S(1)}, u32[]{:S(2)}, u32[]{:S(2)}) %collective-permute-start.24) | collective-permute-done | bytes 131104 | tf_op jit(solution)/shard_map/ppermute | solution.py:556
  150.0 0.7 fusion.17
  (60 shorter events, 3.5 us)
Async XLA Ops:
  1.3 0.9 copy-start.3
  2.2 0.9 copy-start.4
  3.2 20.8 %collective-permute-start.3 = (bf16[144,1024]{1,0:T(8,128)(2,1)S(1)}, bf16[144,1024]{1,0:T(8,128)(2,1)S(1)}, u32[]{:S(2)}, u32[]{:S(2)}) collective-permute-start(bf16[144,1024]{1,0:T(8,128)(2,1)S(1)} %pack.1.refs_0_), channel_id=1, source_target_pairs={{0,16},{16,0},{32,48},{48,32},{64,80},{80,64},{96,112},{112,96},{1... | collective-permute-start | bytes 884744 | tf_op jit(solution)/shard_map/ppermute | solution.py:496
  4.7 18.8 %collective-permute-start.2 = (bf16[144,1024]{1,0:T(8,128)(2,1)S(1)}, bf16[144,1024]{1,0:T(8,128)(2,1)S(1)}, u32[]{:S(2)}, u32[]{:S(2)}) collective-permute-start(bf16[144,1024]{1,0:T(8,128)(2,1)S(1)} %pack.1.refs_0_), channel_id=1, source_target_pairs={{0,64},{16,80},{32,96},{48,112},{64,0},{80,16},{96,32},{112,48},{1... | collective-permute-start | bytes 884744 | tf_op jit(solution)/shard_map/ppermute | solution.py:495
  8.3 13.8 %collective-permute-start.1 = (bf16[144,1024]{1,0:T(8,128)(2,1)S(1)}, bf16[144,1024]{1,0:T(8,128)(2,1)S(1)}, u32[]{:S(2)}, u32[]{:S(2)}) collective-permute-start(bf16[144,1024]{1,0:T(8,128)(2,1)S(1)} %pack.1.refs_0_), channel_id=1, source_target_pairs={{0,32},{16,48},{32,64},{48,80},{64,96},{80,112},{96,0},{112,16},{1... | collective-permute-start | bytes 884744 | tf_op jit(solution)/shard_map/ppermute | solution.py:495
  9.1 13.4 %collective-permute-start = (bf16[144,1024]{1,0:T(8,128)(2,1)S(1)}, bf16[144,1024]{1,0:T(8,128)(2,1)S(1)}, u32[]{:S(2)}, u32[]{:S(2)}) collective-permute-start(bf16[144,1024]{1,0:T(8,128)(2,1)S(1)} %pack.1.refs_0_), channel_id=1, source_target_pairs={{0,96},{16,112},{32,0},{48,16},{64,32},{80,48},{96,64},{112,80},{1... | collective-permute-start | bytes 884744 | tf_op jit(solution)/shard_map/ppermute | solution.py:495
  11.8 1.5 copy-start
  13.3 1.5 copy-start.1
  14.8 1.5 copy-start.2
  16.3 0.7 copy-start.5
  17.0 0.7 copy-start.7
  22.5 2.5 %collective-permute-start.4 = (bf16[144,1024]{1,0:T(8,128)(2,1)S(1)}, bf16[144,1024]{1,0:T(8,128)(2,1)S(1)}, u32[]{:S(2)}, u32[]{:S(2)}) collective-permute-start(bf16[144,1024]{1,0:T(8,128)(2,1)S(1)} %collective-permute-done.refs_1_), channel_id=1, source_target_pairs={{0,16},{16,0},{32,48},{48,32},{64,80},{80,64},{96,112},{112,96},{1... | collective-permute-start | bytes 884744 | tf_op jit(solution)/shard_map/ppermute | solution.py:502
  23.4 1.6 %collective-permute-start.5 = (bf16[144,1024]{1,0:T(8,128)(2,1)S(1)}, bf16[144,1024]{1,0:T(8,128)(2,1)S(1)}, u32[]{:S(2)}, u32[]{:S(2)}) collective-permute-start(bf16[144,1024]{1,0:T(8,128)(2,1)S(1)} %collective-permute-done.2.refs_2_), channel_id=1, source_target_pairs={{0,16},{16,0},{32,48},{48,32},{64,80},{80,64},{96,112},{112,96},{1... | collective-permute-start | bytes 884744 | tf_op jit(solution)/shard_map/ppermute | solution.py:502
  23.4 2.0 %collective-permute-start.6 = (bf16[144,1024]{1,0:T(8,128)(2,1)S(1)}, bf16[144,1024]{1,0:T(8,128)(2,1)S(1)}, u32[]{:S(2)}, u32[]{:S(2)}) collective-permute-start(bf16[144,1024]{1,0:T(8,128)(2,1)S(1)} %collective-permute-done.1.refs_3_), channel_id=1, source_target_pairs={{0,16},{16,0},{32,48},{48,32},{64,80},{80,64},{96,112},{112,96},{1... | collective-permute-start | bytes 884744 | tf_op jit(solution)/shard_map/ppermute | solution.py:502
  29.2 13.8 %collective-permute-start.9 = (bf16[3,192,896]{2,1,0:T(8,128)(2,1)S(1)}, bf16[3,192,896]{2,1,0:T(8,128)(2,1)S(1)}, u32[]{:S(2)}, u32[]{:S(2)}) collective-permute-start(bf16[3,192,896]{2,1,0:T(8,128)(2,1)S(1)} %get-tuple-element.70), channel_id=1, source_target_pairs={{0,4},{1,5},{2,6},{3,7},{4,0},{5,1},{6,2},{7,3},{8,12},{9,13},{10,... | collective-permute-start | bytes 3096584 | tf_op jit(solution)/shard_map/ppermute | solution.py:483
  30.6 15.0 %collective-permute-start.10 = (bf16[3,192,896]{2,1,0:T(8,128)(2,1)S(1)}, bf16[3,192,896]{2,1,0:T(8,128)(2,1)S(1)}, u32[]{:S(2)}, u32[]{:S(2)}) collective-permute-start(bf16[3,192,896]{2,1,0:T(8,128)(2,1)S(1)} %get-tuple-element.71), channel_id=1, source_target_pairs={{0,12},{1,13},{2,14},{3,15},{4,8},{5,9},{6,10},{7,11},{8,4},{9,5},... | collective-permute-start | bytes 3096584 | tf_op jit(solution)/shard_map/ppermute | solution.py:483
  36.4 17.7 %collective-permute-start.7 = (bf16[3,192,896]{2,1,0:T(8,128)(2,1)S(1)}, bf16[3,192,896]{2,1,0:T(8,128)(2,1)S(1)}, u32[]{:S(2)}, u32[]{:S(2)}) collective-permute-start(bf16[3,192,896]{2,1,0:T(8,128)(2,1)S(1)} %get-tuple-element.75), channel_id=1, source_target_pairs={{0,4},{1,5},{2,6},{3,7},{4,0},{5,1},{6,2},{7,3},{8,12},{9,13},{10,... | collective-permute-start | bytes 3096584 | tf_op jit(solution)/shard_map/ppermute | solution.py:483
  36.9 19.8 %collective-permute-start.8 = (bf16[3,192,896]{2,1,0:T(8,128)(2,1)S(1)}, bf16[3,192,896]{2,1,0:T(8,128)(2,1)S(1)}, u32[]{:S(2)}, u32[]{:S(2)}) collective-permute-start(bf16[3,192,896]{2,1,0:T(8,128)(2,1)S(1)} %get-tuple-element.76), channel_id=1, source_target_pairs={{0,12},{1,13},{2,14},{3,15},{4,8},{5,9},{6,10},{7,11},{8,4},{9,5},... | collective-permute-start | bytes 3096584 | tf_op jit(solution)/shard_map/ppermute | solution.py:483
  45.8 19.4 %collective-permute-start.12 = (bf16[3,192,896]{2,1,0:T(8,128)(2,1)S(1)}, bf16[3,192,896]{2,1,0:T(8,128)(2,1)S(1)}, u32[]{:S(2)}, u32[]{:S(2)}) collective-permute-start(bf16[3,192,896]{2,1,0:T(8,128)(2,1)S(1)} %add_convert_fusion), channel_id=1, source_target_pairs={{0,4},{1,5},{2,6},{3,7},{4,0},{5,1},{6,2},{7,3},{8,12},{9,13},{10,... | collective-permute-start | bytes 3096584 | tf_op jit(solution)/shard_map/ppermute | solution.py:483
  46.2 21.5 %collective-permute-start.11 = (bf16[3,192,896]{2,1,0:T(8,128)(2,1)S(1)}, bf16[3,192,896]{2,1,0:T(8,128)(2,1)S(1)}, u32[]{:S(2)}, u32[]{:S(2)}) collective-permute-start(bf16[3,192,896]{2,1,0:T(8,128)(2,1)S(1)} %add_convert_fusion.1), channel_id=1, source_target_pairs={{0,12},{1,13},{2,14},{3,15},{4,8},{5,9},{6,10},{7,11},{8,4},{9,5},... | collective-permute-start | bytes 3096584 | tf_op jit(solution)/shard_map/ppermute | solution.py:483
  68.4 8.5 %collective-permute-start.13 = (bf16[3,1,2,48,896]{4,3,2,1,0:T(8,128)(2,1)S(1)}, bf16[3,1,2,48,896]{4,3,2,1,0:T(8,128)(2,1)S(1)}, u32[]{:S(2)}, u32[]{:S(2)}) collective-permute-start(bf16[3,1,2,48,896]{4,3,2,1,0:T(8,128)(2,1)S(1)} %slice.187), channel_id=1, source_target_pairs={{0,1},{1,0},{2,3},{3,2},{4,5},{5,4},{6,7},{7,6},{8,9},{9,8},{10,11... | collective-permute-start | bytes 1548296 | tf_op jit(solution)/shard_map/ppermute | solution.py:483
  69.7 9.9 %collective-permute-start.17 = (bf16[3,2,1,48,896]{4,3,2,1,0:T(8,128)(2,1)S(1)}, bf16[3,2,1,48,896]{4,3,2,1,0:T(8,128)(2,1)S(1)}, u32[]{:S(2)}, u32[]{:S(2)}) collective-permute-start(bf16[3,2,1,48,896]{4,3,2,1,0:T(8,128)(2,1)S(1)} %slice.186), channel_id=1, source_target_pairs={{0,3},{1,2},{2,1},{3,0},{4,7},{5,6},{6,5},{7,4},{8,11},{9,10},{10,... | collective-permute-start | bytes 1548296 | tf_op jit(solution)/shard_map/ppermute | solution.py:483
  77.0 9.5 %collective-permute-start.14 = (bf16[3,1,2,48,896]{4,3,2,1,0:T(8,128)(2,1)S(1)}, bf16[3,1,2,48,896]{4,3,2,1,0:T(8,128)(2,1)S(1)}, u32[]{:S(2)}, u32[]{:S(2)}) collective-permute-start(bf16[3,1,2,48,896]{4,3,2,1,0:T(8,128)(2,1)S(1)} %fusion.1), channel_id=1, source_target_pairs={{0,3},{1,2},{2,1},{3,0},{4,7},{5,6},{6,5},{7,4},{8,11},{9,10},{10,... | collective-permute-start | bytes 1548296 | tf_op jit(solution)/shard_map/ppermute | solution.py:483
  79.7 8.3 %collective-permute-start.18 = (bf16[3,2,1,48,896]{4,3,2,1,0:T(8,128)(2,1)S(1)}, bf16[3,2,1,48,896]{4,3,2,1,0:T(8,128)(2,1)S(1)}, u32[]{:S(2)}, u32[]{:S(2)}) collective-permute-start(bf16[3,2,1,48,896]{4,3,2,1,0:T(8,128)(2,1)S(1)} %fusion), channel_id=1, source_target_pairs={{0,1},{1,0},{2,3},{3,2},{4,5},{5,4},{6,7},{7,6},{8,9},{9,8},{10,11... | collective-permute-start | bytes 1548296 | tf_op jit(solution)/shard_map/ppermute | solution.py:483
  87.0 8.3 %collective-permute-start.15 = (bf16[3,1,2,48,896]{4,3,2,1,0:T(8,128)(2,1)S(1)}, bf16[3,1,2,48,896]{4,3,2,1,0:T(8,128)(2,1)S(1)}, u32[]{:S(2)}, u32[]{:S(2)}) collective-permute-start(bf16[3,1,2,48,896]{4,3,2,1,0:T(8,128)(2,1)S(1)} %pad_maximum_fusion.6), channel_id=1, source_target_pairs={{0,1},{1,0},{2,3},{3,2},{4,5},{5,4},{6,7},{7,6},{8,9},{9,8},{10,11... | collective-permute-start | bytes 1548296 | tf_op jit(solution)/shard_map/ppermute | solution.py:483
  88.5 9.5 %collective-permute-start.19 = (bf16[3,2,1,48,896]{4,3,2,1,0:T(8,128)(2,1)S(1)}, bf16[3,2,1,48,896]{4,3,2,1,0:T(8,128)(2,1)S(1)}, u32[]{:S(2)}, u32[]{:S(2)}) collective-permute-start(bf16[3,2,1,48,896]{4,3,2,1,0:T(8,128)(2,1)S(1)} %pad_maximum_fusion.7), channel_id=1, source_target_pairs={{0,3},{1,2},{2,1},{3,0},{4,7},{5,6},{6,5},{7,4},{8,11},{9,10},{10,... | collective-permute-start | bytes 1548296 | tf_op jit(solution)/shard_map/ppermute | solution.py:483
  95.5 17.7 %collective-permute-start.16 = (bf16[3,192,896]{2,1,0:T(8,128)(2,1)S(1)}, bf16[3,192,896]{2,1,0:T(8,128)(2,1)S(1)}, u32[]{:S(2)}, u32[]{:S(2)}) collective-permute-start(bf16[3,192,896]{2,1,0:T(8,128)(2,1)S(1)} %bitcast.25), channel_id=1, source_target_pairs={{0,12},{1,13},{2,14},{3,15},{4,8},{5,9},{6,10},{7,11},{8,4},{9,5},... | collective-permute-start | bytes 3096584 | tf_op jit(solution)/shard_map/ppermute | solution.py:483
  98.1 15.3 %collective-permute-start.20 = (bf16[3,192,896]{2,1,0:T(8,128)(2,1)S(1)}, bf16[3,192,896]{2,1,0:T(8,128)(2,1)S(1)}, u32[]{:S(2)}, u32[]{:S(2)}) collective-permute-start(bf16[3,192,896]{2,1,0:T(8,128)(2,1)S(1)} %bitcast.26), channel_id=1, source_target_pairs={{0,4},{1,5},{2,6},{3,7},{4,0},{5,1},{6,2},{7,3},{8,12},{9,13},{10,... | collective-permute-start | bytes 3096584 | tf_op jit(solution)/shard_map/ppermute | solution.py:483
  113.3 10.2 %collective-permute-start.21 = (bf16[1,384,896]{2,1,0:T(8,128)(2,1)S(1)}, bf16[1,384,896]{2,1,0:T(8,128)(2,1)S(1)}, u32[]{:S(2)}, u32[]{:S(2)}) collective-permute-start(bf16[1,384,896]{2,1,0:T(8,128)(2,1)S(1)} %pad_maximum_fusion.4.own0), channel_id=1, source_target_pairs={{0,4},{1,5},{2,6},{3,7},{4,0},{5,1},{6,2},{7,3},{8,12},{9,13},{10,... | collective-permute-start | bytes 2064392 | tf_op jit(solution)/shard_map/ppermute | solution.py:483
  113.5 11.4 %collective-permute-start.22 = (bf16[1,384,896]{2,1,0:T(8,128)(2,1)S(1)}, bf16[1,384,896]{2,1,0:T(8,128)(2,1)S(1)}, u32[]{:S(2)}, u32[]{:S(2)}) collective-permute-start(bf16[1,384,896]{2,1,0:T(8,128)(2,1)S(1)} %pad_maximum_fusion.5.own1), channel_id=1, source_target_pairs={{0,12},{1,13},{2,14},{3,15},{4,8},{5,9},{6,10},{7,11},{8,4},{9,5},... | collective-permute-start | bytes 2064392 | tf_op jit(solution)/shard_map/ppermute | solution.py:483
  115.6 25.5 %collective-permute-start.28 = (bf16[2,384,896]{2,1,0:T(8,128)(2,1)S(1)}, bf16[2,384,896]{2,1,0:T(8,128)(2,1)S(1)}, u32[]{:S(2)}, u32[]{:S(2)}) collective-permute-start(bf16[2,384,896]{2,1,0:T(8,128)(2,1)S(1)} %pad_maximum_fusion.1.own1), channel_id=1, source_target_pairs={{0,12},{1,13},{2,14},{3,15},{4,8},{5,9},{6,10},{7,11},{8,4},{9,5},... | collective-permute-start | bytes 4128776 | tf_op jit(solution)/shard_map/ppermute | solution.py:483
  116.8 24.3 %collective-permute-start.27 = (bf16[2,384,896]{2,1,0:T(8,128)(2,1)S(1)}, bf16[2,384,896]{2,1,0:T(8,128)(2,1)S(1)}, u32[]{:S(2)}, u32[]{:S(2)}) collective-permute-start(bf16[2,384,896]{2,1,0:T(8,128)(2,1)S(1)} %pad_maximum_fusion.own0), channel_id=1, source_target_pairs={{0,4},{1,5},{2,6},{3,7},{4,0},{5,1},{6,2},{7,3},{8,12},{9,13},{10,... | collective-permute-start | bytes 4128776 | tf_op jit(solution)/shard_map/ppermute | solution.py:483
  127.2 10.7 %collective-permute-start.23 = (bf16[4,128,512]{2,1,0:T(8,128)(2,1)S(1)}, bf16[4,128,512]{2,1,0:T(8,128)(2,1)S(1)}, u32[]{:S(2)}, u32[]{:S(2)}) collective-permute-start(bf16[4,128,512]{2,1,0:T(8,128)(2,1)S(1)} %get-tuple-element.94), channel_id=1, source_target_pairs={{0,16},{16,0},{32,48},{48,32},{64,80},{80,64},{96,112},{112,96},{1... | collective-permute-start | bytes 1572872 | tf_op jit(solution)/shard_map/ppermute | solution.py:551
  137.8 3.3 %copy-start.6 = (s32[4,14]{1,0:T(4,128)S(1)}, s32[4,14]{1,0:T(4,128)}, u32[]{:S(2)}) copy-start(s32[4,14]{1,0:T(4,128)} %gm.3) | copy-start | bytes 676
  137.9 3.3 %copy-start.8 = (s32[4,14]{1,0:T(4,128)S(1)}, s32[4,14]{1,0:T(4,128)}, u32[]{:S(2)}) copy-start(s32[4,14]{1,0:T(4,128)} %um.3) | copy-start | bytes 676
  138.1 8.0 %collective-permute-start.26 = (bf16[128,512]{1,0:T(8,128)(2,1)S(1)}, bf16[128,512]{1,0:T(8,128)(2,1)S(1)}, u32[]{:S(2)}, u32[]{:S(2)}) collective-permute-start(bf16[128,512]{1,0:T(8,128)(2,1)S(1)} %get-tuple-element.112), channel_id=1, source_target_pairs={{0,96},{16,112},{32,0},{48,16},{64,32},{80,48},{96,64},{112,80},{1... | collective-permute-start | bytes 393224 | tf_op jit(solution)/shard_map/ppermute | solution.py:556
  140.5 6.3 %collective-permute-start.25 = (bf16[128,512]{1,0:T(8,128)(2,1)S(1)}, bf16[128,512]{1,0:T(8,128)(2,1)S(1)}, u32[]{:S(2)}, u32[]{:S(2)}) collective-permute-start(bf16[128,512]{1,0:T(8,128)(2,1)S(1)} %get-tuple-element.113), channel_id=1, source_target_pairs={{0,64},{16,80},{32,96},{48,112},{64,0},{80,16},{96,32},{112,48},{1... | collective-permute-start | bytes 393224 | tf_op jit(solution)/shard_map/ppermute | solution.py:556
  140.7 9.3 %collective-permute-start.24 = (bf16[128,512]{1,0:T(8,128)(2,1)S(1)}, bf16[128,512]{1,0:T(8,128)(2,1)S(1)}, u32[]{:S(2)}, u32[]{:S(2)}) collective-permute-start(bf16[128,512]{1,0:T(8,128)(2,1)S(1)} %get-tuple-element.114), channel_id=1, source_target_pairs={{0,32},{16,48},{32,64},{48,80},{64,96},{80,112},{96,0},{112,16},{1... | collective-permute-start | bytes 393224 | tf_op jit(solution)/shard_map/ppermute | solution.py:556

commit v11 on v10

--- a/solution.py
+++ b/solution.py
@@ -183,23 +183,18 @@
     rows = rows_ref[...]
     slot = lax.broadcasted_iota(jnp.int32, (LIVE, BLK), 1)
     cnts = [ref[BLK : BLK + 1, 0:1].astype(F32).astype(jnp.int32) for ref in sources]
-    total = None
-    for pair in range(4):
-        picks = []
-        for k in (2 * pair, 2 * pair + 1):
-            offset = jnp.zeros((1, 1), jnp.int32)
-            for other in range(8):
-                if other != k:
-                    offset += jnp.where(shard[other] < shard[k], cnts[other], 0)
-            offs_ref[k] = jnp.broadcast_to(offset, (8, BLK))
-            cnts_ref[k] = jnp.broadcast_to(cnts[k], (8, BLK))
-            hit = (rows - offset == slot) & (slot < cnts[k])
-            picks.append(jnp.where(hit, 1.0, 0.0).astype(BF))
-        source = jnp.concatenate(
-            [sources[2 * pair][:BLK, :], sources[2 * pair + 1][:BLK, :]], axis=0
-        )
-        part = jnp.dot(jnp.concatenate(picks, axis=1), source, preferred_element_type=F32)
-        total = part if total is None else total + part
+    picks = []
+    for k in range(8):
+        offset = jnp.zeros((1, 1), jnp.int32)
+        for other in range(8):
+            if other != k:
+                offset += jnp.where(shard[other] < shard[k], cnts[other], 0)
+        offs_ref[k] = jnp.broadcast_to(offset, (8, BLK))
+        cnts_ref[k] = jnp.broadcast_to(cnts[k], (8, BLK))
+        hit = (rows - offset == slot) & (slot < cnts[k])
+        picks.append(jnp.where(hit, 1.0, 0.0).astype(BF))
+    source = jnp.concatenate([ref[:BLK, :] for ref in sources], axis=0)
+    total = jnp.dot(jnp.concatenate(picks, axis=1), source, preferred_element_type=F32)
     x_ref[...] = total[:, :FEAT].astype(BF)
     g_ref[...] = total[:, FEAT:].astype(BF)
 

time: 151 us -> 151 us (level)
  no operation moved by 1% of the time
where the time goes in v11:
time: 151 us
  waiting for transfers between devices  73.9 us (49%)
  starting transfers between devices  39.1 us (26%)
  Pallas kernels  22.9 us (15%)
  local copies, waits for them, and re-layouts  9.01 us (6%)
  other arithmetic  3.89 us (3%)
  between operations  1.67 us (1%)
    ppermute x18, waiting for transfers between devices, exchange(): lax.ppermute(values[q], ('col', 'dp'), partners(ROUNDS[q][number][1]))  65.6 us
    ppermute x18, starting transfers between devices, exchange(): lax.ppermute(values[q], ('col', 'dp'), partners(ROUNDS[q][number][1]))  19.2 us
    unnamed x19, local copies, waits for them, and re-layouts  8.44 us
    ppermute x1, starting transfers between devices, on_device(): other = lax.ppermute(away, 'col', shift(0, 1))  7.52 us
    ppermute x3, starting transfers between devices, on_device(): lax.ppermute(own, 'col', shift(-dz, 0))  6.37 us
    pallas_call x2, Pallas kernels, partials(): call(functools.partial(partial_kernel, start, pieces), 'partials', 2 * co...  4.7 us
    ppermute x3, waiting for transfers between devices, on_device(): arrived = [lax.ppermute(terms[dz], 'col', shift(dz, 0)) for dz in (1, 2, 3)]  4.56 us
    pallas_call x1, Pallas kernels, last_grad(): call(last_grad_kernel, 'last_grad', 2 * LIVE * FEAT * UNITS, 13 << 20, ou...  4.14 us
  transfers between devices with their start and end apart: 29, of which 21 were waited for; matrix products, arithmetic and copies ran while one was open for 2% of the time, Pallas kernels for 13%

profile of v11, /device:TPU:1, one launch (start us, length us, event | category | flops | bytes accessed | tf_op | source)
XLA Modules:
  0.0 150.5 jit_solution(7403055109006722488)
XLA Ops:
  1.3 0.9 copy-done.3
  2.2 0.9 copy-done.4
  3.2 1.5 collective-permute-start.3
  4.7 3.7 %collective-permute-start.2 = (bf16[144,1024]{1,0:T(8,128)(2,1)S(1)}, bf16[144,1024]{1,0:T(8,128)(2,1)S(1)}, u32[]{:S(2)}, u32[]{:S(2)}) collective-permute-start(bf16[144,1024]{1,0:T(8,128)(2,1)S(1)} %pack.1.refs_0_), channel_id=1, source_target_pairs={{0,64},{16,80},{32,96},{48,112},{64,0},{80,16},{96,32},{112,48},{1... | collective-permute-start | bytes 884744 | tf_op jit(solution)/shard_map/ppermute | solution.py:490
  8.3 0.7 collective-permute-start.1
  9.1 1.9 %collective-permute-start = (bf16[144,1024]{1,0:T(8,128)(2,1)S(1)}, bf16[144,1024]{1,0:T(8,128)(2,1)S(1)}, u32[]{:S(2)}, u32[]{:S(2)}) collective-permute-start(bf16[144,1024]{1,0:T(8,128)(2,1)S(1)} %pack.1.refs_0_), channel_id=1, source_target_pairs={{0,96},{16,112},{32,0},{48,16},{64,32},{80,48},{96,64},{112,80},{1... | collective-permute-start | bytes 884744 | tf_op jit(solution)/shard_map/ppermute | solution.py:490
  11.0 0.8 copy.13.dm
  11.8 1.5 copy-done
  13.3 1.5 copy-done.1
  14.8 1.5 copy-done.2
  16.3 0.7 copy-done.5
  17.0 0.7 copy-done.7
  17.7 2.4 %prepare.1 = (bf16[7,512,512]{2,1,0:T(8,128)(2,1)S(1)}, bf16[7,512,256]{2,1,0:T(8,128)(2,1)S(1)}, bf16[1792,512]{1,0:T(8,128)(2,1)S(1)}) custom-call(s32[4,14]{1,0:T(4,128)S(1)} %copy-done.5, s32[4,14]{1,0:T(4,128)S(1)} %copy-done.7, s32[14,4]{1,0:T(8,128)S(1)} %copy.13.dm, bf16[512,1792]{1,0:T(8,128)(2,1)S(1)} %copy-done, bf16[512,1792]{1,0:T(8,128)(2,1)S(1)} %copy-done.1, ...), custom_call_target="tpu_custom_call" | custom-call | bytes 13631488 | tf_op jit(solution)/shard_map/prepare/pallas_call | solution.py:154
  20.3 1.8 %collective-permute-done.1.refs_3_ = bf16[144,1024]{1,0:T(8,128)(2,1)S(1)} collective-permute-done((bf16[144,1024]{1,0:T(8,128)(2,1)S(1)}, bf16[144,1024]{1,0:T(8,128)(2,1)S(1)}, u32[]{:S(2)}, u32[]{:S(2)}) %collective-permute-start.1) | collective-permute-done | bytes 294944 | tf_op jit(solution)/shard_map/ppermute | solution.py:490
  22.1 0.4 collective-permute-done.refs_1_
  22.5 0.9 collective-permute-start.4
  23.4 0.5 collective-permute-start.6
  23.9 1.1 collective-permute-done.5.refs_6_
  25.0 0.4 collective-permute-done.6.refs_7_
  25.5 2.4 %compact.1 = (bf16[768,512]{1,0:T(8,128)(2,1)S(1)}, bf16[768,512]{1,0:T(8,128)(2,1)S(1)}, s32[8,8,128]{2,1,0:T(8,128)S(1)}, s32[8,8,128]{2,1,0:T(8,128)S(1)}) custom-call(s32[8]{0:T(128)S(1)} %fusion.23.shard, s32[768,1]{1,0:T(8,128)S(1)} %fusion.10.rows_ref, bf16[144,1024]{1,0:T(8,128)(2,1)S(1)} %pack.1.refs_0_, ...), custom_call_target="tpu_custom_call" | custom-call | flops 1610612736 | bytes 5242880 | tf_op jit(solution)/shard_map/compact/pallas_call | solution.py:204
  27.9 1.3 partials.2
  29.2 1.4 collective-permute-start.9
  30.6 1.9 %collective-permute-start.10 = (bf16[3,192,896]{2,1,0:T(8,128)(2,1)S(1)}, bf16[3,192,896]{2,1,0:T(8,128)(2,1)S(1)}, u32[]{:S(2)}, u32[]{:S(2)}) collective-permute-start(bf16[3,192,896]{2,1,0:T(8,128)(2,1)S(1)} %get-tuple-element.71), channel_id=1, source_target_pairs={{0,12},{1,13},{2,14},{3,15},{4,8},{5,9},{6,10},{7,11},{8,4},{9,5},... | collective-permute-start | bytes 3096584 | tf_op jit(solution)/shard_map/ppermute | solution.py:478
  32.5 0.5 turned.1
  33.0 3.4 %partials.3 = (bf16[3,192,896]{2,1,0:T(8,128)(2,1)S(1)}, bf16[3,192,896]{2,1,0:T(8,128)(2,1)S(1)}, bf16[3,192,896]{2,1,0:T(8,128)(2,1)S(1)}, bf16[3,192,896]{2,1...) custom-call(bf16[768,512]{1,0:T(8,128)(2,1)S(1)} %get-tuple-element.72.x_ref, ...), custom_call_target="tpu_custom_call" | custom-call | flops 3170893824 | bytes 7340032 | tf_op jit(solution)/shard_map/partials/pallas_call | solution.py:257
  36.4 0.5 collective-permute-start.7
  36.9 0.6 collective-permute-start.8
  37.5 5.6 %collective-permute-done.9 = bf16[3,192,896]{2,1,0:T(8,128)(2,1)S(1)} collective-permute-done((bf16[3,192,896]{2,1,0:T(8,128)(2,1)S(1)}, bf16[3,192,896]{2,1,0:T(8,128)(2,1)S(1)}, u32[]{:S(2)}, u32[]{:S(2)}) %collective-permute-start.9) | collective-permute-done | bytes 1032224 | tf_op jit(solution)/shard_map/ppermute | solution.py:478
  43.1 2.5 %collective-permute-done.10 = bf16[3,192,896]{2,1,0:T(8,128)(2,1)S(1)} collective-permute-done((bf16[3,192,896]{2,1,0:T(8,128)(2,1)S(1)}, bf16[3,192,896]{2,1,0:T(8,128)(2,1)S(1)}, u32[]{:S(2)}, u32[]{:S(2)}) %collective-permute-start.10) | collective-permute-done | bytes 1032224 | tf_op jit(solution)/shard_map/ppermute | solution.py:478
  45.9 0.3 add_convert_fusion.1
  46.2 2.0 %collective-permute-start.11 = (bf16[3,192,896]{2,1,0:T(8,128)(2,1)S(1)}, bf16[3,192,896]{2,1,0:T(8,128)(2,1)S(1)}, u32[]{:S(2)}, u32[]{:S(2)}) collective-permute-start(bf16[3,192,896]{2,1,0:T(8,128)(2,1)S(1)} %add_convert_fusion.1), channel_id=1, source_target_pairs={{0,12},{1,13},{2,14},{3,15},{4,8},{5,9},{6,10},{7,11},{8,4},{9,5},... | collective-permute-start | bytes 3096584 | tf_op jit(solution)/shard_map/ppermute | solution.py:478
  48.1 6.0 %collective-permute-done.7 = bf16[3,192,896]{2,1,0:T(8,128)(2,1)S(1)} collective-permute-done((bf16[3,192,896]{2,1,0:T(8,128)(2,1)S(1)}, bf16[3,192,896]{2,1,0:T(8,128)(2,1)S(1)}, u32[]{:S(2)}, u32[]{:S(2)}) %collective-permute-start.7) | collective-permute-done | bytes 1032224 | tf_op jit(solution)/shard_map/ppermute | solution.py:478
  54.1 2.5 %collective-permute-done.8 = bf16[3,192,896]{2,1,0:T(8,128)(2,1)S(1)} collective-permute-done((bf16[3,192,896]{2,1,0:T(8,128)(2,1)S(1)}, bf16[3,192,896]{2,1,0:T(8,128)(2,1)S(1)}, u32[]{:S(2)}, u32[]{:S(2)}) %collective-permute-start.8) | collective-permute-done | bytes 1032224 | tf_op jit(solution)/shard_map/ppermute | solution.py:478
  56.6 8.6 %collective-permute-done.12 = bf16[3,192,896]{2,1,0:T(8,128)(2,1)S(1)} collective-permute-done((bf16[3,192,896]{2,1,0:T(8,128)(2,1)S(1)}, bf16[3,192,896]{2,1,0:T(8,128)(2,1)S(1)}, u32[]{:S(2)}, u32[]{:S(2)}) %collective-permute-start.12) | collective-permute-done | bytes 1032224 | tf_op jit(solution)/shard_map/ppermute | solution.py:478
  65.2 2.5 %collective-permute-done.11 = bf16[3,192,896]{2,1,0:T(8,128)(2,1)S(1)} collective-permute-done((bf16[3,192,896]{2,1,0:T(8,128)(2,1)S(1)}, bf16[3,192,896]{2,1,0:T(8,128)(2,1)S(1)}, u32[]{:S(2)}, u32[]{:S(2)}) %collective-permute-start.11) | collective-permute-done | bytes 1032224 | tf_op jit(solution)/shard_map/ppermute | solution.py:478
  67.7 0.7 convert_add_fusion
  68.4 1.0 collective-permute-start.13
  69.5 2.1 %collective-permute-start.17 = (bf16[3,2,1,48,896]{4,3,2,1,0:T(8,128)(2,1)S(1)}, bf16[3,2,1,48,896]{4,3,2,1,0:T(8,128)(2,1)S(1)}, u32[]{:S(2)}, u32[]{:S(2)}) collective-permute-start(bf16[3,2,1,48,896]{4,3,2,1,0:T(8,128)(2,1)S(1)} %slice.186), channel_id=1, source_target_pairs={{0,3},{1,2},{2,1},{3,0},{4,7},{5,6},{6,5},{7,4},{8,11},{9,10},{10,... | collective-permute-start | bytes 1548296 | tf_op jit(solution)/shard_map/ppermute | solution.py:478
  71.6 5.2 %collective-permute-done.13 = bf16[3,1,2,48,896]{4,3,2,1,0:T(8,128)(2,1)S(1)} collective-permute-done((bf16[3,1,2,48,896]{4,3,2,1,0:T(8,128)(2,1)S(1)}, bf16[3,1,2,48,896]{4,3,2,1,0:T(8,128)(2,1)S(1)}, u32[]{:S(2)}, u32[]{:S(2)}) %collective-permute-start.13) | collective-permute-done | bytes 516128 | tf_op jit(solution)/shard_map/ppermute | solution.py:478
  76.9 2.6 %collective-permute-start.14 = (bf16[3,1,2,48,896]{4,3,2,1,0:T(8,128)(2,1)S(1)}, bf16[3,1,2,48,896]{4,3,2,1,0:T(8,128)(2,1)S(1)}, u32[]{:S(2)}, u32[]{:S(2)}) collective-permute-start(bf16[3,1,2,48,896]{4,3,2,1,0:T(8,128)(2,1)S(1)} %fusion.1), channel_id=1, source_target_pairs={{0,3},{1,2},{2,1},{3,0},{4,7},{5,6},{6,5},{7,4},{8,11},{9,10},{10,... | collective-permute-start | bytes 1548296 | tf_op jit(solution)/shard_map/ppermute | solution.py:478
  79.6 6.7 %collective-permute-done.14 = bf16[3,1,2,48,896]{4,3,2,1,0:T(8,128)(2,1)S(1)} collective-permute-done((bf16[3,1,2,48,896]{4,3,2,1,0:T(8,128)(2,1)S(1)}, bf16[3,1,2,48,896]{4,3,2,1,0:T(8,128)(2,1)S(1)}, u32[]{:S(2)}, u32[]{:S(2)}) %collective-permute-start.14) | collective-permute-done | bytes 516128 | tf_op jit(solution)/shard_map/ppermute | solution.py:478
  86.9 0.9 collective-permute-done.18
  88.3 1.7 %collective-permute-start.19 = (bf16[3,2,1,48,896]{4,3,2,1,0:T(8,128)(2,1)S(1)}, bf16[3,2,1,48,896]{4,3,2,1,0:T(8,128)(2,1)S(1)}, u32[]{:S(2)}, u32[]{:S(2)}) collective-permute-start(bf16[3,2,1,48,896]{4,3,2,1,0:T(8,128)(2,1)S(1)} %pad_maximum_fusion.7), channel_id=1, source_target_pairs={{0,3},{1,2},{2,1},{3,0},{4,7},{5,6},{6,5},{7,4},{8,11},{9,10},{10,... | collective-permute-start | bytes 1548296 | tf_op jit(solution)/shard_map/ppermute | solution.py:478
  90.0 5.2 %collective-permute-done.15 = bf16[3,1,2,48,896]{4,3,2,1,0:T(8,128)(2,1)S(1)} collective-permute-done((bf16[3,1,2,48,896]{4,3,2,1,0:T(8,128)(2,1)S(1)}, bf16[3,1,2,48,896]{4,3,2,1,0:T(8,128)(2,1)S(1)}, u32[]{:S(2)}, u32[]{:S(2)}) %collective-permute-start.15) | collective-permute-done | bytes 516128 | tf_op jit(solution)/shard_map/ppermute | solution.py:478
  95.3 2.0 %collective-permute-start.16 = (bf16[3,192,896]{2,1,0:T(8,128)(2,1)S(1)}, bf16[3,192,896]{2,1,0:T(8,128)(2,1)S(1)}, u32[]{:S(2)}, u32[]{:S(2)}) collective-permute-start(bf16[3,192,896]{2,1,0:T(8,128)(2,1)S(1)} %bitcast.25), channel_id=1, source_target_pairs={{0,12},{1,13},{2,14},{3,15},{4,8},{5,9},{6,10},{7,11},{8,4},{9,5},... | collective-permute-start | bytes 3096584 | tf_op jit(solution)/shard_map/ppermute | solution.py:478
  97.3 0.6 collective-permute-done.19
  98.1 14.9 %collective-permute-done.16 = bf16[3,192,896]{2,1,0:T(8,128)(2,1)S(1)} collective-permute-done((bf16[3,192,896]{2,1,0:T(8,128)(2,1)S(1)}, bf16[3,192,896]{2,1,0:T(8,128)(2,1)S(1)}, u32[]{:S(2)}, u32[]{:S(2)}) %collective-permute-start.16) | collective-permute-done | bytes 1032224 | tf_op jit(solution)/shard_map/ppermute | solution.py:478
  113.3 1.9 %collective-permute-start.22 = (bf16[1,384,896]{2,1,0:T(8,128)(2,1)S(1)}, bf16[1,384,896]{2,1,0:T(8,128)(2,1)S(1)}, u32[]{:S(2)}, u32[]{:S(2)}) collective-permute-start(bf16[1,384,896]{2,1,0:T(8,128)(2,1)S(1)} %pad_maximum_fusion.5.own1), channel_id=1, source_target_pairs={{0,12},{1,13},{2,14},{3,15},{4,8},{5,9},{6,10},{7,11},{8,4},{9,5},... | collective-permute-start | bytes 2064392 | tf_op jit(solution)/shard_map/ppermute | solution.py:478
  115.5 1.0 collective-permute-start.28
  116.7 0.3 collective-permute-start.27
  117.0 1.2 first_output.1.early_ref
  118.2 2.1 %first_grad.1 = (f32[512,1792]{1,0:T(8,128)S(1)}, f32[512,1792]{1,0:T(8,128)S(1)}) custom-call(bf16[512,768]{1,0:T(8,128)(2,1)S(1)} %get-tuple-element.88.xt0, bf16[512,768]{1,0:T(8,128)(2,1)S(1)} %get-tuple-element.89.xt1, bf16[2,384,896]{2,1,0:T(8,128)(2,1)S(1)} %pad_maximum_fusion.own0, bf16[2,384,896]{2,1,0:T(8,128)(2,1)S(1)} %pad_maximum_fusion.1.own1), custom_call_target="tpu_custom_call" | custom-call | flops 1409286144 | bytes 13631488 | tf_op jit(solution)/shard_map/first_grad/pallas_call | solution.py:419
  120.3 3.0 %collective-permute-done.21.come0 = bf16[1,384,896]{2,1,0:T(8,128)(2,1)S(1)} collective-permute-done((bf16[1,384,896]{2,1,0:T(8,128)(2,1)S(1)}, bf16[1,384,896]{2,1,0:T(8,128)(2,1)S(1)}, u32[]{:S(2)}, u32[]{:S(2)}) %collective-permute-start.21) | collective-permute-done | bytes 688160 | tf_op jit(solution)/shard_map/ppermute | solution.py:478
  123.3 1.4 collective-permute-done.22.come1
  124.7 2.3 %last_output.1 = (bf16[4,128,512]{2,1,0:T(8,128)(2,1)S(1)}, bf16[4,128,512]{2,1,0:T(8,128)(2,1)S(1)}) custom-call(s32[1,768]{1,0:T(1,128)S(1)} %fusion.18.rows_ref, s32[8,8,128]{2,1,0:T(8,128)S(1)} %get-tuple-element.63.offs, s32[8,8,128]{2,1,0:T(8,128)S(1)} %get-tuple-element.64.cnts, f32[3,192,512]{2,1,0:T(8,128)S(1)} %first_output.1.early_ref, ...), custom_call_target="tpu_custom_call" | custom-call | flops 1 | bytes 4096 | tf_op jit(solution)/shard_map/last_output/pallas_call | solution.py:329
  127.0 7.5 %collective-permute-start.23 = (bf16[4,128,512]{2,1,0:T(8,128)(2,1)S(1)}, bf16[4,128,512]{2,1,0:T(8,128)(2,1)S(1)}, u32[]{:S(2)}, u32[]{:S(2)}) collective-permute-start(bf16[4,128,512]{2,1,0:T(8,128)(2,1)S(1)} %get-tuple-element.94), channel_id=1, source_target_pairs={{0,16},{16,0},{32,48},{48,32},{64,80},{80,64},{96,112},{112,96},{1... | collective-permute-start | bytes 1572872 | tf_op jit(solution)/shard_map/ppermute | solution.py:546
  134.5 3.2 %down_gradient.1 = f32[1792,512]{1,0:T(8,128)} custom-call(s32[14,4]{1,0:T(8,128)S(1)} %copy.13.dm, bf16[768,512]{1,0:T(8,128)(2,1)S(1)} %get-tuple-element.73.g_ref, bf16[1,384,896]{2,1,0:T(8,128)(2,1)S(1)} %pad_maximum_fusion.4.own0, bf16[1,384,896]{2,1,0:T(8,128)(2,1)S(1)} %pad_maximum_fusion.5.own1, ...), custom_call_target="tpu_custom_call" | custom-call | flops 1 | bytes 4096 | tf_op jit(solution)/shard_map/down_gradient/pallas_call | solution.py:383
  137.9 2.5 %collective-permute-start.26 = (bf16[128,512]{1,0:T(8,128)(2,1)S(1)}, bf16[128,512]{1,0:T(8,128)(2,1)S(1)}, u32[]{:S(2)}, u32[]{:S(2)}) collective-permute-start(bf16[128,512]{1,0:T(8,128)(2,1)S(1)} %get-tuple-element.112), channel_id=1, source_target_pairs={{0,96},{16,112},{32,0},{48,16},{64,32},{80,48},{96,64},{112,80},{1... | collective-permute-start | bytes 393224 | tf_op jit(solution)/shard_map/ppermute | solution.py:551
  140.5 0.5 collective-permute-start.24
  141.0 4.1 %last_grad.1 = (f32[512,1792]{1,0:T(8,128)}, f32[512,1792]{1,0:T(8,128)}) custom-call(s32[4,14]{1,0:T(4,128)S(1)} %copy-done.6, s32[4,14]{1,0:T(4,128)S(1)} %copy-done.8, bf16[512,768]{1,0:T(8,128)(2,1)S(1)} %get-tuple-element.88.xt0, bf16[512,768]{1,0:T(8,128)(2,1)S(1)} %get-tuple-element.89.xt1, f32[512,1792]{1,0:T(8,128)S(1)} %get-tuple-element.96.gate_in, ...), custom_call_target="tpu_custom_call" | custom-call | flops 1409286144 | bytes 13631488 | tf_op jit(solution)/shard_map/last_grad/pallas_call | solution.py:447
  145.2 0.7 collective-permute-done.26
  145.9 0.8 collective-permute-done.25
  146.7 3.1 %collective-permute-done.24 = bf16[128,512]{1,0:T(8,128)(2,1)S(1)} collective-permute-done((bf16[128,512]{1,0:T(8,128)(2,1)S(1)}, bf16[128,512]{1,0:T(8,128)(2,1)S(1)}, u32[]{:S(2)}, u32[]{:S(2)}) %collective-permute-start.24) | collective-permute-done | bytes 131104 | tf_op jit(solution)/shard_map/ppermute | solution.py:551
  149.8 0.7 fusion.17
  (60 shorter events, 3.4 us)
Async XLA Ops:
  1.3 0.9 copy-start.3
  2.2 0.9 copy-start.4
  3.2 20.8 %collective-permute-start.3 = (bf16[144,1024]{1,0:T(8,128)(2,1)S(1)}, bf16[144,1024]{1,0:T(8,128)(2,1)S(1)}, u32[]{:S(2)}, u32[]{:S(2)}) collective-permute-start(bf16[144,1024]{1,0:T(8,128)(2,1)S(1)} %pack.1.refs_0_), channel_id=1, source_target_pairs={{0,16},{16,0},{32,48},{48,32},{64,80},{80,64},{96,112},{112,96},{1... | collective-permute-start | bytes 884744 | tf_op jit(solution)/shard_map/ppermute | solution.py:491
  4.7 18.8 %collective-permute-start.2 = (bf16[144,1024]{1,0:T(8,128)(2,1)S(1)}, bf16[144,1024]{1,0:T(8,128)(2,1)S(1)}, u32[]{:S(2)}, u32[]{:S(2)}) collective-permute-start(bf16[144,1024]{1,0:T(8,128)(2,1)S(1)} %pack.1.refs_0_), channel_id=1, source_target_pairs={{0,64},{16,80},{32,96},{48,112},{64,0},{80,16},{96,32},{112,48},{1... | collective-permute-start | bytes 884744 | tf_op jit(solution)/shard_map/ppermute | solution.py:490
  8.3 13.8 %collective-permute-start.1 = (bf16[144,1024]{1,0:T(8,128)(2,1)S(1)}, bf16[144,1024]{1,0:T(8,128)(2,1)S(1)}, u32[]{:S(2)}, u32[]{:S(2)}) collective-permute-start(bf16[144,1024]{1,0:T(8,128)(2,1)S(1)} %pack.1.refs_0_), channel_id=1, source_target_pairs={{0,32},{16,48},{32,64},{48,80},{64,96},{80,112},{96,0},{112,16},{1... | collective-permute-start | bytes 884744 | tf_op jit(solution)/shard_map/ppermute | solution.py:490
  9.1 13.4 %collective-permute-start = (bf16[144,1024]{1,0:T(8,128)(2,1)S(1)}, bf16[144,1024]{1,0:T(8,128)(2,1)S(1)}, u32[]{:S(2)}, u32[]{:S(2)}) collective-permute-start(bf16[144,1024]{1,0:T(8,128)(2,1)S(1)} %pack.1.refs_0_), channel_id=1, source_target_pairs={{0,96},{16,112},{32,0},{48,16},{64,32},{80,48},{96,64},{112,80},{1... | collective-permute-start | bytes 884744 | tf_op jit(solution)/shard_map/ppermute | solution.py:490
  11.8 1.5 copy-start
  13.3 1.5 copy-start.1
  14.8 1.5 copy-start.2
  16.3 0.7 copy-start.5
  17.0 0.7 copy-start.7
  22.5 2.5 %collective-permute-start.4 = (bf16[144,1024]{1,0:T(8,128)(2,1)S(1)}, bf16[144,1024]{1,0:T(8,128)(2,1)S(1)}, u32[]{:S(2)}, u32[]{:S(2)}) collective-permute-start(bf16[144,1024]{1,0:T(8,128)(2,1)S(1)} %collective-permute-done.refs_1_), channel_id=1, source_target_pairs={{0,16},{16,0},{32,48},{48,32},{64,80},{80,64},{96,112},{112,96},{1... | collective-permute-start | bytes 884744 | tf_op jit(solution)/shard_map/ppermute | solution.py:497
  23.4 1.6 %collective-permute-start.5 = (bf16[144,1024]{1,0:T(8,128)(2,1)S(1)}, bf16[144,1024]{1,0:T(8,128)(2,1)S(1)}, u32[]{:S(2)}, u32[]{:S(2)}) collective-permute-start(bf16[144,1024]{1,0:T(8,128)(2,1)S(1)} %collective-permute-done.2.refs_2_), channel_id=1, source_target_pairs={{0,16},{16,0},{32,48},{48,32},{64,80},{80,64},{96,112},{112,96},{1... | collective-permute-start | bytes 884744 | tf_op jit(solution)/shard_map/ppermute | solution.py:497
  23.4 2.0 %collective-permute-start.6 = (bf16[144,1024]{1,0:T(8,128)(2,1)S(1)}, bf16[144,1024]{1,0:T(8,128)(2,1)S(1)}, u32[]{:S(2)}, u32[]{:S(2)}) collective-permute-start(bf16[144,1024]{1,0:T(8,128)(2,1)S(1)} %collective-permute-done.1.refs_3_), channel_id=1, source_target_pairs={{0,16},{16,0},{32,48},{48,32},{64,80},{80,64},{96,112},{112,96},{1... | collective-permute-start | bytes 884744 | tf_op jit(solution)/shard_map/ppermute | solution.py:497
  29.2 13.8 %collective-permute-start.9 = (bf16[3,192,896]{2,1,0:T(8,128)(2,1)S(1)}, bf16[3,192,896]{2,1,0:T(8,128)(2,1)S(1)}, u32[]{:S(2)}, u32[]{:S(2)}) collective-permute-start(bf16[3,192,896]{2,1,0:T(8,128)(2,1)S(1)} %get-tuple-element.70), channel_id=1, source_target_pairs={{0,4},{1,5},{2,6},{3,7},{4,0},{5,1},{6,2},{7,3},{8,12},{9,13},{10,... | collective-permute-start | bytes 3096584 | tf_op jit(solution)/shard_map/ppermute | solution.py:478
  30.6 15.0 %collective-permute-start.10 = (bf16[3,192,896]{2,1,0:T(8,128)(2,1)S(1)}, bf16[3,192,896]{2,1,0:T(8,128)(2,1)S(1)}, u32[]{:S(2)}, u32[]{:S(2)}) collective-permute-start(bf16[3,192,896]{2,1,0:T(8,128)(2,1)S(1)} %get-tuple-element.71), channel_id=1, source_target_pairs={{0,12},{1,13},{2,14},{3,15},{4,8},{5,9},{6,10},{7,11},{8,4},{9,5},... | collective-permute-start | bytes 3096584 | tf_op jit(solution)/shard_map/ppermute | solution.py:478
  36.4 17.7 %collective-permute-start.7 = (bf16[3,192,896]{2,1,0:T(8,128)(2,1)S(1)}, bf16[3,192,896]{2,1,0:T(8,128)(2,1)S(1)}, u32[]{:S(2)}, u32[]{:S(2)}) collective-permute-start(bf16[3,192,896]{2,1,0:T(8,128)(2,1)S(1)} %get-tuple-element.75), channel_id=1, source_target_pairs={{0,4},{1,5},{2,6},{3,7},{4,0},{5,1},{6,2},{7,3},{8,12},{9,13},{10,... | collective-permute-start | bytes 3096584 | tf_op jit(solution)/shard_map/ppermute | solution.py:478
  36.9 19.8 %collective-permute-start.8 = (bf16[3,192,896]{2,1,0:T(8,128)(2,1)S(1)}, bf16[3,192,896]{2,1,0:T(8,128)(2,1)S(1)}, u32[]{:S(2)}, u32[]{:S(2)}) collective-permute-start(bf16[3,192,896]{2,1,0:T(8,128)(2,1)S(1)} %get-tuple-element.76), channel_id=1, source_target_pairs={{0,12},{1,13},{2,14},{3,15},{4,8},{5,9},{6,10},{7,11},{8,4},{9,5},... | collective-permute-start | bytes 3096584 | tf_op jit(solution)/shard_map/ppermute | solution.py:478
  45.8 19.4 %collective-permute-start.12 = (bf16[3,192,896]{2,1,0:T(8,128)(2,1)S(1)}, bf16[3,192,896]{2,1,0:T(8,128)(2,1)S(1)}, u32[]{:S(2)}, u32[]{:S(2)}) collective-permute-start(bf16[3,192,896]{2,1,0:T(8,128)(2,1)S(1)} %add_convert_fusion), channel_id=1, source_target_pairs={{0,4},{1,5},{2,6},{3,7},{4,0},{5,1},{6,2},{7,3},{8,12},{9,13},{10,... | collective-permute-start | bytes 3096584 | tf_op jit(solution)/shard_map/ppermute | solution.py:478
  46.2 21.5 %collective-permute-start.11 = (bf16[3,192,896]{2,1,0:T(8,128)(2,1)S(1)}, bf16[3,192,896]{2,1,0:T(8,128)(2,1)S(1)}, u32[]{:S(2)}, u32[]{:S(2)}) collective-permute-start(bf16[3,192,896]{2,1,0:T(8,128)(2,1)S(1)} %add_convert_fusion.1), channel_id=1, source_target_pairs={{0,12},{1,13},{2,14},{3,15},{4,8},{5,9},{6,10},{7,11},{8,4},{9,5},... | collective-permute-start | bytes 3096584 | tf_op jit(solution)/shard_map/ppermute | solution.py:478
  68.4 8.3 %collective-permute-start.13 = (bf16[3,1,2,48,896]{4,3,2,1,0:T(8,128)(2,1)S(1)}, bf16[3,1,2,48,896]{4,3,2,1,0:T(8,128)(2,1)S(1)}, u32[]{:S(2)}, u32[]{:S(2)}) collective-permute-start(bf16[3,1,2,48,896]{4,3,2,1,0:T(8,128)(2,1)S(1)} %slice.187), channel_id=1, source_target_pairs={{0,1},{1,0},{2,3},{3,2},{4,5},{5,4},{6,7},{7,6},{8,9},{9,8},{10,11... | collective-permute-start | bytes 1548296 | tf_op jit(solution)/shard_map/ppermute | solution.py:478
  69.5 9.9 %collective-permute-start.17 = (bf16[3,2,1,48,896]{4,3,2,1,0:T(8,128)(2,1)S(1)}, bf16[3,2,1,48,896]{4,3,2,1,0:T(8,128)(2,1)S(1)}, u32[]{:S(2)}, u32[]{:S(2)}) collective-permute-start(bf16[3,2,1,48,896]{4,3,2,1,0:T(8,128)(2,1)S(1)} %slice.186), channel_id=1, source_target_pairs={{0,3},{1,2},{2,1},{3,0},{4,7},{5,6},{6,5},{7,4},{8,11},{9,10},{10,... | collective-permute-start | bytes 1548296 | tf_op jit(solution)/shard_map/ppermute | solution.py:478
  76.9 9.5 %collective-permute-start.14 = (bf16[3,1,2,48,896]{4,3,2,1,0:T(8,128)(2,1)S(1)}, bf16[3,1,2,48,896]{4,3,2,1,0:T(8,128)(2,1)S(1)}, u32[]{:S(2)}, u32[]{:S(2)}) collective-permute-start(bf16[3,1,2,48,896]{4,3,2,1,0:T(8,128)(2,1)S(1)} %fusion.1), channel_id=1, source_target_pairs={{0,3},{1,2},{2,1},{3,0},{4,7},{5,6},{6,5},{7,4},{8,11},{9,10},{10,... | collective-permute-start | bytes 1548296 | tf_op jit(solution)/shard_map/ppermute | solution.py:478
  79.6 8.3 %collective-permute-start.18 = (bf16[3,2,1,48,896]{4,3,2,1,0:T(8,128)(2,1)S(1)}, bf16[3,2,1,48,896]{4,3,2,1,0:T(8,128)(2,1)S(1)}, u32[]{:S(2)}, u32[]{:S(2)}) collective-permute-start(bf16[3,2,1,48,896]{4,3,2,1,0:T(8,128)(2,1)S(1)} %fusion), channel_id=1, source_target_pairs={{0,1},{1,0},{2,3},{3,2},{4,5},{5,4},{6,7},{7,6},{8,9},{9,8},{10,11... | collective-permute-start | bytes 1548296 | tf_op jit(solution)/shard_map/ppermute | solution.py:478
  86.8 8.3 %collective-permute-start.15 = (bf16[3,1,2,48,896]{4,3,2,1,0:T(8,128)(2,1)S(1)}, bf16[3,1,2,48,896]{4,3,2,1,0:T(8,128)(2,1)S(1)}, u32[]{:S(2)}, u32[]{:S(2)}) collective-permute-start(bf16[3,1,2,48,896]{4,3,2,1,0:T(8,128)(2,1)S(1)} %pad_maximum_fusion.6), channel_id=1, source_target_pairs={{0,1},{1,0},{2,3},{3,2},{4,5},{5,4},{6,7},{7,6},{8,9},{9,8},{10,11... | collective-permute-start | bytes 1548296 | tf_op jit(solution)/shard_map/ppermute | solution.py:478
  88.3 9.5 %collective-permute-start.19 = (bf16[3,2,1,48,896]{4,3,2,1,0:T(8,128)(2,1)S(1)}, bf16[3,2,1,48,896]{4,3,2,1,0:T(8,128)(2,1)S(1)}, u32[]{:S(2)}, u32[]{:S(2)}) collective-permute-start(bf16[3,2,1,48,896]{4,3,2,1,0:T(8,128)(2,1)S(1)} %pad_maximum_fusion.7), channel_id=1, source_target_pairs={{0,3},{1,2},{2,1},{3,0},{4,7},{5,6},{6,5},{7,4},{8,11},{9,10},{10,... | collective-permute-start | bytes 1548296 | tf_op jit(solution)/shard_map/ppermute | solution.py:478
  95.3 17.7 %collective-permute-start.16 = (bf16[3,192,896]{2,1,0:T(8,128)(2,1)S(1)}, bf16[3,192,896]{2,1,0:T(8,128)(2,1)S(1)}, u32[]{:S(2)}, u32[]{:S(2)}) collective-permute-start(bf16[3,192,896]{2,1,0:T(8,128)(2,1)S(1)} %bitcast.25), channel_id=1, source_target_pairs={{0,12},{1,13},{2,14},{3,15},{4,8},{5,9},{6,10},{7,11},{8,4},{9,5},... | collective-permute-start | bytes 3096584 | tf_op jit(solution)/shard_map/ppermute | solution.py:478
  98.0 15.2 %collective-permute-start.20 = (bf16[3,192,896]{2,1,0:T(8,128)(2,1)S(1)}, bf16[3,192,896]{2,1,0:T(8,128)(2,1)S(1)}, u32[]{:S(2)}, u32[]{:S(2)}) collective-permute-start(bf16[3,192,896]{2,1,0:T(8,128)(2,1)S(1)} %bitcast.26), channel_id=1, source_target_pairs={{0,4},{1,5},{2,6},{3,7},{4,0},{5,1},{6,2},{7,3},{8,12},{9,13},{10,... | collective-permute-start | bytes 3096584 | tf_op jit(solution)/shard_map/ppermute | solution.py:478
  113.1 10.2 %collective-permute-start.21 = (bf16[1,384,896]{2,1,0:T(8,128)(2,1)S(1)}, bf16[1,384,896]{2,1,0:T(8,128)(2,1)S(1)}, u32[]{:S(2)}, u32[]{:S(2)}) collective-permute-start(bf16[1,384,896]{2,1,0:T(8,128)(2,1)S(1)} %pad_maximum_fusion.4.own0), channel_id=1, source_target_pairs={{0,4},{1,5},{2,6},{3,7},{4,0},{5,1},{6,2},{7,3},{8,12},{9,13},{10,... | collective-permute-start | bytes 2064392 | tf_op jit(solution)/shard_map/ppermute | solution.py:478
  113.3 11.4 %collective-permute-start.22 = (bf16[1,384,896]{2,1,0:T(8,128)(2,1)S(1)}, bf16[1,384,896]{2,1,0:T(8,128)(2,1)S(1)}, u32[]{:S(2)}, u32[]{:S(2)}) collective-permute-start(bf16[1,384,896]{2,1,0:T(8,128)(2,1)S(1)} %pad_maximum_fusion.5.own1), channel_id=1, source_target_pairs={{0,12},{1,13},{2,14},{3,15},{4,8},{5,9},{6,10},{7,11},{8,4},{9,5},... | collective-permute-start | bytes 2064392 | tf_op jit(solution)/shard_map/ppermute | solution.py:478
  115.5 25.5 %collective-permute-start.28 = (bf16[2,384,896]{2,1,0:T(8,128)(2,1)S(1)}, bf16[2,384,896]{2,1,0:T(8,128)(2,1)S(1)}, u32[]{:S(2)}, u32[]{:S(2)}) collective-permute-start(bf16[2,384,896]{2,1,0:T(8,128)(2,1)S(1)} %pad_maximum_fusion.1.own1), channel_id=1, source_target_pairs={{0,12},{1,13},{2,14},{3,15},{4,8},{5,9},{6,10},{7,11},{8,4},{9,5},... | collective-permute-start | bytes 4128776 | tf_op jit(solution)/shard_map/ppermute | solution.py:478
  116.7 24.4 %collective-permute-start.27 = (bf16[2,384,896]{2,1,0:T(8,128)(2,1)S(1)}, bf16[2,384,896]{2,1,0:T(8,128)(2,1)S(1)}, u32[]{:S(2)}, u32[]{:S(2)}) collective-permute-start(bf16[2,384,896]{2,1,0:T(8,128)(2,1)S(1)} %pad_maximum_fusion.own0), channel_id=1, source_target_pairs={{0,4},{1,5},{2,6},{3,7},{4,0},{5,1},{6,2},{7,3},{8,12},{9,13},{10,... | collective-permute-start | bytes 4128776 | tf_op jit(solution)/shard_map/ppermute | solution.py:478
  127.0 10.7 %collective-permute-start.23 = (bf16[4,128,512]{2,1,0:T(8,128)(2,1)S(1)}, bf16[4,128,512]{2,1,0:T(8,128)(2,1)S(1)}, u32[]{:S(2)}, u32[]{:S(2)}) collective-permute-start(bf16[4,128,512]{2,1,0:T(8,128)(2,1)S(1)} %get-tuple-element.94), channel_id=1, source_target_pairs={{0,16},{16,0},{32,48},{48,32},{64,80},{80,64},{96,112},{112,96},{1... | collective-permute-start | bytes 1572872 | tf_op jit(solution)/shard_map/ppermute | solution.py:546
  137.7 3.4 %copy-start.6 = (s32[4,14]{1,0:T(4,128)S(1)}, s32[4,14]{1,0:T(4,128)}, u32[]{:S(2)}) copy-start(s32[4,14]{1,0:T(4,128)} %gm.3) | copy-start | bytes 676
  137.7 3.3 %copy-start.8 = (s32[4,14]{1,0:T(4,128)S(1)}, s32[4,14]{1,0:T(4,128)}, u32[]{:S(2)}) copy-start(s32[4,14]{1,0:T(4,128)} %um.3) | copy-start | bytes 676
  137.9 8.0 %collective-permute-start.26 = (bf16[128,512]{1,0:T(8,128)(2,1)S(1)}, bf16[128,512]{1,0:T(8,128)(2,1)S(1)}, u32[]{:S(2)}, u32[]{:S(2)}) collective-permute-start(bf16[128,512]{1,0:T(8,128)(2,1)S(1)} %get-tuple-element.112), channel_id=1, source_target_pairs={{0,96},{16,112},{32,0},{48,16},{64,32},{80,48},{96,64},{112,80},{1... | collective-permute-start | bytes 393224 | tf_op jit(solution)/shard_map/ppermute | solution.py:551
  140.4 6.3 %collective-permute-start.25 = (bf16[128,512]{1,0:T(8,128)(2,1)S(1)}, bf16[128,512]{1,0:T(8,128)(2,1)S(1)}, u32[]{:S(2)}, u32[]{:S(2)}) collective-permute-start(bf16[128,512]{1,0:T(8,128)(2,1)S(1)} %get-tuple-element.113), channel_id=1, source_target_pairs={{0,64},{16,80},{32,96},{48,112},{64,0},{80,16},{96,32},{112,48},{1... | collective-permute-start | bytes 393224 | tf_op jit(solution)/shard_map/ppermute | solution.py:551
  140.5 9.3 %collective-permute-start.24 = (bf16[128,512]{1,0:T(8,128)(2,1)S(1)}, bf16[128,512]{1,0:T(8,128)(2,1)S(1)}, u32[]{:S(2)}, u32[]{:S(2)}) collective-permute-start(bf16[128,512]{1,0:T(8,128)(2,1)S(1)} %get-tuple-element.114), channel_id=1, source_target_pairs={{0,32},{16,48},{32,64},{48,80},{64,96},{80,112},{96,0},{112,16},{1... | collective-permute-start | bytes 393224 | tf_op jit(solution)/shard_map/ppermute | solution.py:551
